TPU v7x, 32 devices: a whole 2x2x4 slice. The times are simulated.
32 devices in a mesh: pipe: 4 (over y, x), tensor: 4 (over z), dp: 2 (over core).
Axes of the slice: x: 2, y: 2, z: 4, core: 2. Of those that a mesh axis runs over, the one named last changes fastest.
Arguments:
- weight_main: bfloat16 [4, 4096, 2, 1024], P('pipe', None, None, 'tensor'), may hold values from -0.09375 to 0.09375
- weight_state: bfloat16 [4, 4096, 2, 128], P('pipe', None, None, 'tensor'), may hold values from -0.09375 to 0.09375
- weight_step: bfloat16 [4, 16, 4096], P('pipe', 'tensor'), may hold values from -0.09375 to 0.09375
- weight_out: bfloat16 [4, 1024, 4096], P('pipe', 'tensor'), may hold values from -0.1875 to 0.1875
- conv_main: float32 [4, 4, 1024], P('pipe', None, 'tensor'), may hold values from -3 to 3
- conv_state: float32 [4, 4, 2, 128], P('pipe'), may hold values from -3 to 3
- step_bias: float32 [4, 16], P('pipe', 'tensor'), may hold values from -3 to 0
- decay_log: float32 [4, 16], P('pipe', 'tensor'), may hold values from -5 to 0.5
- skip_gain: float32 [4, 16], P('pipe', 'tensor'), may hold values from 1 to 6
- norm_gain: float32 [4, 1024], P('pipe', 'tensor'), may hold values from 0.5 to 1.5
- saved_main: bfloat16 [4, 256, 2, 1024], P('pipe', 'dp', None, 'tensor'), parts along dimension 1, may hold values from -6 to 6
- saved_state: bfloat16 [4, 256, 2, 128], P('pipe', 'dp'), parts along dimension 1, may hold values from -6 to 6
- saved_step: bfloat16 [4, 16, 256], P('pipe', 'tensor', 'dp'), parts along dimension 2, may hold values from -6 to 6
- output_grad: bfloat16 [256, 4096], P('dp', 'tensor'), parts along dimension 0, may hold values from -6 to 6
Outputs:
- input_grads: bfloat16 [4, 256, 4096], P('pipe', 'dp', 'tensor'), parts along dimension 1
There are 2 independent parts, one for each index of `dp`. A program takes and returns all parts, laid end to end along the dimension named above; an argument that names none is the same for every part. Nothing has to cross between parts.
All inputs are finite; a program needn't handle non-finite values.
Results may differ from a plain program's by a relative error of at most 0.02.
Values may be sent and summed in bfloat16 or wider, within the bound.
No kernel may reach another device: no remote copies, remote signals or barrier semaphores. Data moves between devices by JAX's collectives and lax.ppermute only.
A program may use at most 64 MiB of HBM per device.

v0:
```python
import jax
import jax.numpy as jnp
from jax import lax
from jax.sharding import PartitionSpec as P

NSTATE = 128
GROUP_SPAN = 4
STRETCH = 128


EPSILON = 1e-05
HIGHEST = lax.Precision.HIGHEST


def from_partner(value, axis, bit):
    mask = 2**bit
    pairs = [(source, source ^ mask) for source in range(lax.axis_size(axis))]
    return lax.ppermute(value, axis, pairs)


def passed_along(value, axis, steps):
    count = lax.axis_size(axis)
    leading, last = (max(0, -steps), min(count, count - steps))
    return lax.ppermute(value, axis, [(source, source + steps) for source in range(leading, last)])


def causal_conv(signal, kernel):
    taps = kernel.shape[0]
    length = signal.shape[0]
    padded = jnp.pad(signal, ((taps - 1, 0), (0, 0)))
    summed = kernel[0] * padded[0:length]
    for offset in range(1, taps):
        summed = summed + kernel[offset] * padded[offset : offset + length]
    return summed


def state_space(values, step_sizes, decay_rates, inputs, readout):
    length, head_count, head_size = values.shape
    blocks = length // STRETCH
    state_width = inputs.shape[1]
    decays = (step_sizes * decay_rates[:, None]).reshape(head_count, blocks, STRETCH)
    running = jnp.cumsum(decays, axis=2)
    scaled = (values * step_sizes.T[:, :, None]).reshape(blocks, STRETCH, head_count, head_size)
    inputs_blocked = inputs.reshape(blocks, STRETCH, state_width)
    readout_blocked = readout.reshape(blocks, STRETCH, state_width)
    scores = jnp.einsum("cin,cjn->cij", readout_blocked, inputs_blocked, precision=HIGHEST)
    position = jnp.arange(STRETCH)
    causal = position[:, None] >= position[None, :]
    differ = running[:, :, :, None] - running[:, :, None, :]
    weights = jnp.where(causal, jnp.exp(jnp.where(causal, differ, 0.0)), 0.0) * scores[None]
    within = jnp.einsum("hcij,cjhp->cihp", weights, scaled, precision=HIGHEST)
    tail_decay = jnp.exp(running[:, :, -1:] - running)
    weighted = scaled * jnp.transpose(tail_decay, (1, 2, 0))[:, :, :, None]
    block_sums = jnp.einsum("cjhp,cjn->chpn", weighted, inputs_blocked, precision=HIGHEST)
    shrinks = jnp.exp(running[:, :, -1]).T

    def advance(carried, item):
        newest, shrink = item
        return (carried * shrink[:, None, None] + newest, carried)

    anchor = jnp.zeros((head_count, head_size, state_width), jnp.float32)
    _, entering = lax.scan(advance, anchor, (block_sums, shrinks))
    across = jnp.einsum("cin,chpn->cihp", readout_blocked, entering, precision=HIGHEST)
    across = across * jnp.transpose(jnp.exp(running), (1, 2, 0))[:, :, :, None]
    return (within + across).reshape(length, head_count, head_size)


def mamba_mixer(
    main_proj,
    state_proj,
    step_proj,
    conv_main,
    conv_state,
    step_bias,
    decay_log,
    skip_gain,
    norm_gain,
):
    length = main_proj.shape[0]
    head_count = step_proj.shape[0]
    gating = main_proj[:, 0]
    mixed_in = jax.nn.silu(causal_conv(main_proj[:, 1], conv_main))
    flat_state = state_proj.reshape(length, -1)
    state_conv = jax.nn.silu(
        causal_conv(flat_state, conv_state.reshape(conv_state.shape[0], -1))
    ).reshape(length, 2, -1)
    step_sizes = jax.nn.softplus(step_proj + step_bias[:, None])
    decay_rates = -jnp.exp(decay_log)
    values = mixed_in.reshape(length, head_count, -1)
    scanned = state_space(values, step_sizes, decay_rates, state_conv[:, 0], state_conv[:, 1])
    scanned = scanned + skip_gain[None, :, None] * values
    gated = scanned.reshape(length, -1) * jax.nn.silu(gating)
    inverse = lax.rsqrt(jnp.mean(gated * gated, axis=1, keepdims=True) + EPSILON)
    return gated * inverse * norm_gain


def body(
    weight_main,
    weight_state,
    weight_step,
    weight_out,
    conv_main,
    conv_state,
    step_bias,
    decay_log,
    skip_gain,
    norm_gain,
    saved_main,
    saved_state,
    saved_step,
    output_grad,
):
    sections = lax.axis_size("pipe")
    section = lax.axis_index("pipe")
    tensor_index = lax.axis_index("tensor")
    member = tensor_index % GROUP_SPAN
    group = tensor_index // GROUP_SPAN
    span_bits = GROUP_SPAN.bit_length() - 1
    length = saved_main.shape[1]
    col_count = output_grad.shape[1]
    model_width = weight_out.shape[2]
    main_cols = weight_main[0].reshape(model_width, -1)
    state_cols = weight_state[0].reshape(model_width, -1)
    step_rows = weight_step[0]
    out_rows = weight_out[0]
    state_group = lax.dynamic_slice_in_dim(saved_state[0], group * NSTATE, NSTATE, 2)
    conv_group = lax.dynamic_slice_in_dim(conv_state[0], group * NSTATE, NSTATE, 2)

    def local_mixer(first_in, second_in, third_in):
        return mamba_mixer(
            first_in,
            second_in,
            third_in,
            conv_main[0],
            conv_group,
            step_bias[0],
            decay_log[0],
            skip_gain[0],
            norm_gain[0],
        )

    _, pullback = jax.vjp(
        local_mixer,
        saved_main[0].astype(jnp.float32),
        state_group.astype(jnp.float32),
        saved_step[0].astype(jnp.float32),
    )
    result = jnp.zeros((length, col_count), jnp.bfloat16)
    incoming = output_grad
    for moment in range(sections):
        back_grad_main, back_grad_state, back_grad_step = pullback(
            lax.dot_general(
                lax.all_gather(incoming, "tensor", axis=1, tiled=True),
                out_rows,
                (((1,), (1,)), ((), ())),
                preferred_element_type=jnp.float32,
            )
        )
        kept = back_grad_state
        for bit in range(span_bits - 1, -1, -1):
            half = kept.shape[2] // 2
            lower = kept[:, :, :half]
            upper = kept[:, :, half:]
            high = member // 2**bit % 2 == 1
            own = jnp.where(high, upper, lower)
            other = jnp.where(high, lower, upper)
            kept = own + from_partner(other, "tensor", bit)
        grad_main = back_grad_main.astype(jnp.bfloat16).reshape(length, -1)
        grad_state = kept.astype(jnp.bfloat16).reshape(length, -1)
        grad_step = back_grad_step.astype(jnp.bfloat16)
        summed = lax.dot_general(
            main_cols, grad_main, (((1,), (1,)), ((), ())), preferred_element_type=jnp.float32
        )
        summed = summed + lax.dot_general(
            state_cols, grad_state, (((1,), (1,)), ((), ())), preferred_element_type=jnp.float32
        )
        owned = lax.psum_scatter(
            summed
            + lax.dot_general(
                step_rows, grad_step, (((0,), (0,)), ((), ())), preferred_element_type=jnp.float32
            ),
            "tensor",
            scatter_dimension=0,
            tiled=True,
        ).T.astype(jnp.bfloat16)
        result = jnp.where(section == sections - 1 - moment, owned, result)
        if moment + 1 < sections:
            incoming = passed_along(owned, "pipe", -1)
    return result[None]


def solution(mesh):
    return jax.shard_map(
        body,
        mesh=mesh,
        in_specs=(
            P("pipe", None, None, "tensor"),
            P("pipe", None, None, "tensor"),
            P("pipe", "tensor", None),
            P("pipe", "tensor", None),
            P("pipe", None, "tensor"),
            P("pipe", None, None, None),
            P("pipe", "tensor"),
            P("pipe", "tensor"),
            P("pipe", "tensor"),
            P("pipe", "tensor"),
            P("pipe", "dp", None, "tensor"),
            P("pipe", "dp", None, None),
            P("pipe", "tensor", "dp"),
            P("dp", "tensor"),
        ),
        out_specs=P("pipe", "dp", "tensor"),
        check_vma=False,
    )
```

profile of v0, /device:TPU:11, one launch (start us, length us, event | category | flops | bytes accessed | tf_op | source)
XLA Modules:
  0.0 514.1 jit_solution(10231602153734534701)
XLA Ops:
  17.4 5.1 copy.113
  22.4 15.3 %all-gather.5.cloned.1.call-done = bf16[128,4096]{1,0:T(8,128)(2,1)} async-done(((bf16[128,1024]{1,0:T(8,128)(2,1)}), bf16[128,4096]{1,0:T(8,128)(2,1)}) %all-gather.5.cloned.1.call-update) | async-done | bytes 1048592 | tf_op jit(solution)/shard_map/all_gather | solution.py:153
  37.8 2.1 multiply_reduce_fusion.13
  42.2 2.3 fusion.50
  45.1 2.8 fusion.64
  47.9 1.7 copy.58
  49.5 1.8 broadcast_multiply_fusion.31
  61.5 1.7 copy.60
  63.2 5.2 %fusion.189 = f32[128,4096]{1,0:T(8,128)} fusion(bf16[128,512]{0,1:T(8,128)(2,1)} %bitcast.543, bf16[4096,512]{1,0:T(8,128)(2,1)} %bitcast.512), kind=kOutput, calls=%fused_computation.360 | convolution fusion | flops 536870912 | bytes 6422528 | tf_op jit(solution)/shard_map/dot_general | solution.py:171
  72.2 2.5 reduce_window_sum.50
  75.6 2.0 convolution_add_fusion.7
  77.7 1.9 fusion.3
  79.7 42.1 %reduce-scatter.5.cloned.1.call-done = f32[1024,128]{0,1:T(8,128)} async-done(((f32[4096,128]{0,1:T(8,128)}), f32[1024,128]{0,1:T(8,128)}) %reduce-scatter.5.cloned.1.call-update) | async-done | bytes 524304 | tf_op jit(solution)/shard_map/reduce_scatter | solution.py:177
  122.9 2.2 collective-permute-start.2
  125.1 7.7 %collective-permute-done.2 = bf16[128,1024]{1,0:T(8,128)(2,1)} collective-permute-done((bf16[128,1024]{1,0:T(8,128)(2,1)S(1)}, bf16[128,1024]{1,0:T(8,128)(2,1)}, u32[]{:S(2)}, u32[]{:S(2)}) %collective-permute-start.2) | collective-permute-done | bytes 262176 | tf_op jit(solution)/shard_map/ppermute | solution.py:24
  133.1 29.5 %all-gather.7.cloned.1.call-done = bf16[128,4096]{1,0:T(8,128)(2,1)} async-done(((bf16[128,1024]{1,0:T(8,128)(2,1)}), bf16[128,4096]{1,0:T(8,128)(2,1)}) %all-gather.7.cloned.1.call-update) | async-done | bytes 1048592 | tf_op jit(solution)/shard_map/all_gather | solution.py:153
  162.6 2.2 multiply_reduce_fusion.9
  165.4 1.5 fusion.181
  166.9 1.7 copy.72
  168.6 2.3 fusion.52
  170.9 2.8 fusion.63
  174.3 1.7 copy.77
  180.1 1.6 copy.103
  184.1 1.7 copy.107
  185.8 1.5 slice_select_fusion.2
  188.4 1.7 copy.73
  191.9 1.6 add_convert_fusion.2
  193.4 1.7 copy.75
  195.1 5.1 %fusion.190 = f32[128,4096]{1,0:T(8,128)} fusion(bf16[128,512]{0,1:T(8,128)(2,1)} %bitcast.544, bf16[4096,512]{1,0:T(8,128)(2,1)} %bitcast.513), kind=kOutput, calls=%fused_computation.361 | convolution fusion | flops 536870912 | bytes 6422528 | tf_op jit(solution)/shard_map/dot_general | solution.py:171
  204.1 2.5 reduce_window_sum.52
  207.5 2.0 convolution_add_fusion.5
  209.6 2.0 fusion.2
  211.7 42.1 %reduce-scatter.7.cloned.1.call-done = f32[1024,128]{0,1:T(8,128)} async-done(((f32[4096,128]{0,1:T(8,128)}), f32[1024,128]{0,1:T(8,128)}) %reduce-scatter.7.cloned.1.call-update) | async-done | bytes 524304 | tf_op jit(solution)/shard_map/reduce_scatter | solution.py:177
  254.9 2.2 collective-permute-start.5
  257.1 7.7 %collective-permute-done.5 = bf16[128,1024]{1,0:T(8,128)(2,1)} collective-permute-done((bf16[128,1024]{1,0:T(8,128)(2,1)S(1)}, bf16[128,1024]{1,0:T(8,128)(2,1)}, u32[]{:S(2)}, u32[]{:S(2)}) %collective-permute-start.5) | collective-permute-done | bytes 262176 | tf_op jit(solution)/shard_map/ppermute | solution.py:24
  265.1 29.5 %all-gather.9.cloned.1.call-done = bf16[128,4096]{1,0:T(8,128)(2,1)} async-done(((bf16[128,1024]{1,0:T(8,128)(2,1)}), bf16[128,4096]{1,0:T(8,128)(2,1)}) %all-gather.9.cloned.1.call-update) | async-done | bytes 1048592 | tf_op jit(solution)/shard_map/all_gather | solution.py:153
  294.6 2.2 multiply_reduce_fusion.7
  298.8 1.7 copy.82
  300.5 2.4 fusion.54
  302.9 2.8 fusion.62
  306.2 1.7 copy.87
  312.0 1.7 copy.104
  316.1 1.7 copy.108
  317.7 1.5 slice_select_fusion.1
  320.4 1.7 copy.83
  323.8 1.6 add_convert_fusion.1
  325.4 1.7 copy.85
  327.1 5.2 %fusion.191 = f32[128,4096]{1,0:T(8,128)} fusion(bf16[128,512]{0,1:T(8,128)(2,1)} %bitcast.545, bf16[4096,512]{1,0:T(8,128)(2,1)} %bitcast.514), kind=kOutput, calls=%fused_computation.362 | convolution fusion | flops 536870912 | bytes 6422528 | tf_op jit(solution)/shard_map/dot_general | solution.py:171
  336.2 2.5 reduce_window_sum.54
  339.5 2.0 convolution_add_fusion.3
  341.6 2.0 fusion.1
  343.7 42.1 %reduce-scatter.9.cloned.1.call-done = f32[1024,128]{0,1:T(8,128)} async-done(((f32[4096,128]{0,1:T(8,128)}), f32[1024,128]{0,1:T(8,128)}) %reduce-scatter.9.cloned.1.call-update) | async-done | bytes 524304 | tf_op jit(solution)/shard_map/reduce_scatter | solution.py:177
  386.9 2.2 collective-permute-start.8
  389.1 7.8 %collective-permute-done.8 = bf16[128,1024]{1,0:T(8,128)(2,1)} collective-permute-done((bf16[128,1024]{1,0:T(8,128)(2,1)S(1)}, bf16[128,1024]{1,0:T(8,128)(2,1)}, u32[]{:S(2)}, u32[]{:S(2)}) %collective-permute-start.8) | collective-permute-done | bytes 262176 | tf_op jit(solution)/shard_map/ppermute | solution.py:24
  397.2 29.4 %all-gather.11.cloned.1.call-done = bf16[128,4096]{1,0:T(8,128)(2,1)} async-done(((bf16[128,1024]{1,0:T(8,128)(2,1)}), bf16[128,4096]{1,0:T(8,128)(2,1)}) %all-gather.11.cloned.1.call-update) | async-done | bytes 1048592 | tf_op jit(solution)/shard_map/all_gather | solution.py:153
  426.6 2.2 multiply_reduce_fusion.5
  431.8 2.3 fusion.56
  434.1 2.7 fusion.61
  445.5 1.7 copy.93
  449.0 5.1 fusion.192
  458.0 2.0 convolution_add_fusion.1
  460.1 1.9 fusion
  462.0 43.3 %reduce-scatter.11.cloned.1.call-done = f32[1024,128]{0,1:T(8,128)} async-done(((f32[4096,128]{0,1:T(8,128)}), f32[1024,128]{0,1:T(8,128)}) %reduce-scatter.11.cloned.1.call-update) | async-done | bytes 524304 | tf_op jit(solution)/shard_map/reduce_scatter | solution.py:177
  505.3 2.0 fusion.41
  (324 shorter events, 81.5 us)
Async XLA Ops:
  6.5 31.3 %copy-start = (bf16[1,256,4096]{2,1,0:T(8,128)(2,1)S(1)}, bf16[1,256,4096]{2,1,0:T(8,128)(2,1)}, u32[]{:S(2)}) copy-start(bf16[1,256,4096]{2,1,0:T(8,128)(2,1)} %param.17) | copy-start | bytes 6291460
  6.5 4.7 copy-start.85
  6.5 4.8 copy-start.52
  6.5 4.8 copy-start.43
  6.5 31.2 %all-gather.5.cloned.1.call-start = ((), (), s32[]{:S(2)}) async-start(), calls=%async_computation.4 | async-start | bytes 1310720 | tf_op jit(solution)/shard_map/all_gather | solution.py:153
  7.3 114.6 %reduce-scatter.5.cloned.1.call-start = ((), (), s32[]{:S(2)}) async-start(), calls=%async_computation.5 | async-start | bytes 2621440 | tf_op jit(solution)/shard_map/reduce_scatter | solution.py:177
  7.3 8.2 %copy-start.84 = (f32[1,4]{1,0:T(1,128)S(1)}, f32[1,4]{1,0:T(1,128)}, u32[]{:S(2)}) copy-start(f32[1,4]{1,0:T(1,128)} %param.22) | copy-start | bytes 52
  8.2 4.5 copy-start.48
  9.2 31.4 %copy-start.2 = (f32[128,2,256]{2,0,1:T(8,128)}, f32[128,2,256]{2,0,1:T(8,128)S(1)}, u32[]{:S(2)}) copy-start(f32[128,2,256]{2,0,1:T(8,128)S(1)} %bitcast_convert_fusion) | copy-start | bytes 786436
  9.4 6.2 %copy-start.33 = (f32[128,256]{0,1:T(8,128)}, f32[128,256]{0,1:T(8,128)S(1)}, u32[]{:S(2)}) copy-start(f32[128,256]{0,1:T(8,128)S(1)} %copy.52) | copy-start | bytes 393220
  11.4 11.0 %copy-start.59 = (f32[128,4]{0,1:T(4,128)}, f32[128,4]{0,1:T(4,128)S(1)}, u32[]{:S(2)}) copy-start(f32[128,4]{0,1:T(4,128)S(1)} %fusion.171) | copy-start | bytes 6148
  14.2 8.3 %copy-start.57 = (f32[4,1,128]{2,1,0:T(1,128)}, f32[4,1,128]{2,1,0:T(1,128)S(1)}, u32[]{:S(2)}) copy-start(f32[4,1,128]{2,1,0:T(1,128)S(1)} %get-tuple-element.142) | copy-start | bytes 6148
  39.9 11.4 %copy-start.6 = (f32[128,256]{1,0:T(8,128)}, f32[128,256]{1,0:T(8,128)S(1)}, u32[]{:S(2)}) copy-start(f32[128,256]{1,0:T(8,128)S(1)} %get-tuple-element.152) | copy-start | bytes 393220
  41.4 11.3 %copy-start.27 = (f32[128,256]{1,0:T(8,128)S(1)}, f32[128,256]{1,0:T(8,128)}, u32[]{:S(2)}) copy-start(f32[128,256]{1,0:T(8,128)} %get-tuple-element.145) | copy-start | bytes 393220
  51.3 7.5 %copy-start.36 = (f32[1,1,256]{2,1,0:T(1,128)S(1)}, f32[1,1,256]{2,1,0:T(1,128)}, u32[]{:S(2)}) copy-start(f32[1,1,256]{2,1,0:T(1,128)} %copy-done.35) | copy-start | bytes 3076
  51.3 7.5 %copy-start.38 = (f32[1,1,256]{2,1,0:T(1,128)S(1)}, f32[1,1,256]{2,1,0:T(1,128)}, u32[]{:S(2)}) copy-start(f32[1,1,256]{2,1,0:T(1,128)} %copy-done.37) | copy-start | bytes 3076
  52.6 7.2 %copy-start.12 = (f32[1,128,128]{1,2,0:T(8,128)}, f32[1,128,128]{1,2,0:T(8,128)S(1)}, u32[]{:S(2)}) copy-start(f32[1,128,128]{1,2,0:T(8,128)S(1)} %convolution_bitcast_fusion.13) | copy-start | bytes 196612
  54.2 6.6 %copy-start.26 = (f32[128,1,256]{2,0,1:T(8,128)S(1)}, f32[128,1,256]{2,0,1:T(8,128)}, u32[]{:S(2)}) copy-start(f32[128,1,256]{2,0,1:T(8,128)} %get-tuple-element.160) | copy-start | bytes 393220
  57.1 6.1 %copy-start.16 = (f32[128,256]{0,1:T(8,128)}, f32[128,256]{0,1:T(8,128)S(1)}, u32[]{:S(2)}) copy-start(f32[128,256]{0,1:T(8,128)S(1)} %copy.106) | copy-start | bytes 393220
  57.8 10.6 %collective-permute-start = (f32[128,2,64]{0,2,1:T(8,128)}, f32[128,2,64]{0,2,1:T(8,128)}, u32[]{:S(2)}, u32[]{:S(2)}) collective-permute-start(f32[128,2,64]{0,2,1:T(8,128)} %slice_select_fusion.3), channel_id=1, source_target_pairs={{0,4},{2,6},{4,0},{6,2},{1,5},{3,7},{5,1},{7,3},{8,12},{10,14},{12... | collective-permute-start | bytes 196616 | tf_op jit(solution)/shard_map/ppermute | solution.py:18
  63.1 5.2 %copy-start.30 = (f32[128,256]{0,1:T(8,128)S(1)}, f32[128,256]{0,1:T(8,128)}, u32[]{:S(2)}) copy-start(f32[128,256]{0,1:T(8,128)} %copy.57) | copy-start | bytes 393220
  63.1 5.2 %copy-start.17 = (f32[128,256]{0,1:T(8,128)S(1)}, f32[128,256]{0,1:T(8,128)}, u32[]{:S(2)}) copy-start(f32[128,256]{0,1:T(8,128)} %copy-done.16) | copy-start | bytes 393220
  63.1 8.4 %copy-start.58 = (f32[4,1,128]{2,1,0:T(1,128)S(1)}, f32[4,1,128]{2,1,0:T(1,128)}, u32[]{:S(2)}) copy-start(f32[4,1,128]{2,1,0:T(1,128)} %copy-done.57) | copy-start | bytes 6148
  63.2 8.4 %copy-start.61 = (f32[128,4]{0,1:T(4,128)S(1)}, f32[128,4]{0,1:T(4,128)}, u32[]{:S(2)}) copy-start(f32[128,4]{0,1:T(4,128)} %copy-done.60) | copy-start | bytes 6148
  63.2 8.4 %copy-start.72 = (f32[4,128]{1,0:T(4,128)S(1)}, f32[4,128]{1,0:T(4,128)}, u32[]{:S(2)}) copy-start(f32[4,128]{1,0:T(4,128)} %neg.67) | copy-start | bytes 6148
  63.2 8.4 %copy-start.80 = (f32[4,128]{1,0:T(4,128)S(1)}, f32[4,128]{1,0:T(4,128)}, u32[]{:S(2)}) copy-start(f32[4,128]{1,0:T(4,128)} %get-tuple-element.84) | copy-start | bytes 6148
  63.2 12.4 %copy-start.1 = (bf16[1,4096,2,32]{1,3,2,0:T(8,128)(2,1)S(1)}, bf16[1,4096,2,32]{1,3,2,0:T(8,128)(2,1)}, u32[]{:S(2)}) copy-start(bf16[1,4096,2,32]{1,3,2,0:T(8,128)(2,1)} %param.15) | copy-start | bytes 1572868
  70.5 4.2 collective-permute-start.1
  79.7 82.9 %all-gather.7.cloned.1.call-start = ((), (), s32[]{:S(2)}) async-start(), calls=%async_computation.6 | async-start | bytes 1310720 | tf_op jit(solution)/shard_map/all_gather | solution.py:153
  122.9 9.9 %collective-permute-start.2 = (bf16[128,1024]{1,0:T(8,128)(2,1)S(1)}, bf16[128,1024]{1,0:T(8,128)(2,1)}, u32[]{:S(2)}, u32[]{:S(2)}) collective-permute-start(bf16[128,1024]{1,0:T(8,128)(2,1)S(1)} %convert_bitcast_fusion.2), channel_id=1, source_target_pairs={{8,0},{16,8},{24,16},{9,1},{17,9},{25,17},{10,2},{18,10},{26,18},{... | collective-permute-start | bytes 786440 | tf_op jit(solution)/shard_map/ppermute | solution.py:24
  132.9 120.9 %reduce-scatter.7.cloned.1.call-start = ((), (), s32[]{:S(2)}) async-start(), calls=%async_computation.7 | async-start | bytes 2621440 | tf_op jit(solution)/shard_map/reduce_scatter | solution.py:177
  162.6 2.8 copy-start.3
  162.6 2.8 copy-start.7
  187.3 13.0 %collective-permute-start.3 = (f32[128,2,64]{0,2,1:T(8,128)}, f32[128,2,64]{0,2,1:T(8,128)}, u32[]{:S(2)}, u32[]{:S(2)}) collective-permute-start(f32[128,2,64]{0,2,1:T(8,128)} %slice_select_fusion.2), channel_id=1, source_target_pairs={{0,4},{2,6},{4,0},{6,2},{1,5},{3,7},{5,1},{7,3},{8,12},{10,14},{12... | collective-permute-start | bytes 196616 | tf_op jit(solution)/shard_map/ppermute | solution.py:18
  195.1 5.2 %copy-start.31 = (f32[128,256]{0,1:T(8,128)S(1)}, f32[128,256]{0,1:T(8,128)}, u32[]{:S(2)}) copy-start(f32[128,256]{0,1:T(8,128)} %copy.72) | copy-start | bytes 393220
  195.1 5.2 %copy-start.14 = (f32[128,256]{0,1:T(8,128)S(1)}, f32[128,256]{0,1:T(8,128)}, u32[]{:S(2)}) copy-start(f32[128,256]{0,1:T(8,128)} %copy.107) | copy-start | bytes 393220
  195.1 8.4 %copy-start.49 = (f32[4,1,128]{2,1,0:T(1,128)S(1)}, f32[4,1,128]{2,1,0:T(1,128)}, u32[]{:S(2)}) copy-start(f32[4,1,128]{2,1,0:T(1,128)} %get-tuple-element.140) | copy-start | bytes 6148
  195.1 8.4 %copy-start.74 = (f32[4,128]{1,0:T(4,128)S(1)}, f32[4,128]{1,0:T(4,128)}, u32[]{:S(2)}) copy-start(f32[4,128]{1,0:T(4,128)} %neg.69) | copy-start | bytes 6148
  195.1 8.4 %copy-start.82 = (f32[4,128]{1,0:T(4,128)S(1)}, f32[4,128]{1,0:T(4,128)}, u32[]{:S(2)}) copy-start(f32[4,128]{1,0:T(4,128)} %get-tuple-element.82) | copy-start | bytes 6148
  202.4 4.2 collective-permute-start.4
  211.6 82.9 %all-gather.9.cloned.1.call-start = ((), (), s32[]{:S(2)}) async-start(), calls=%async_computation.8 | async-start | bytes 1310720 | tf_op jit(solution)/shard_map/all_gather | solution.py:153
  254.9 9.9 %collective-permute-start.5 = (bf16[128,1024]{1,0:T(8,128)(2,1)S(1)}, bf16[128,1024]{1,0:T(8,128)(2,1)}, u32[]{:S(2)}, u32[]{:S(2)}) collective-permute-start(bf16[128,1024]{1,0:T(8,128)(2,1)S(1)} %convert_bitcast_fusion.1), channel_id=1, source_target_pairs={{8,0},{16,8},{24,16},{9,1},{17,9},{25,17},{10,2},{18,10},{26,18},{... | collective-permute-start | bytes 786440 | tf_op jit(solution)/shard_map/ppermute | solution.py:24
  264.8 121.0 %reduce-scatter.9.cloned.1.call-start = ((), (), s32[]{:S(2)}) async-start(), calls=%async_computation.9 | async-start | bytes 2621440 | tf_op jit(solution)/shard_map/reduce_scatter | solution.py:177
  319.3 13.1 %collective-permute-start.6 = (f32[128,2,64]{0,2,1:T(8,128)}, f32[128,2,64]{0,2,1:T(8,128)}, u32[]{:S(2)}, u32[]{:S(2)}) collective-permute-start(f32[128,2,64]{0,2,1:T(8,128)} %slice_select_fusion.1), channel_id=1, source_target_pairs={{0,4},{2,6},{4,0},{6,2},{1,5},{3,7},{5,1},{7,3},{8,12},{10,14},{12... | collective-permute-start | bytes 196616 | tf_op jit(solution)/shard_map/ppermute | solution.py:18
  327.1 5.2 %copy-start.32 = (f32[128,256]{0,1:T(8,128)S(1)}, f32[128,256]{0,1:T(8,128)}, u32[]{:S(2)}) copy-start(f32[128,256]{0,1:T(8,128)} %copy.82) | copy-start | bytes 393220
  327.1 5.3 %copy-start.15 = (f32[128,256]{0,1:T(8,128)S(1)}, f32[128,256]{0,1:T(8,128)}, u32[]{:S(2)}) copy-start(f32[128,256]{0,1:T(8,128)} %copy.108) | copy-start | bytes 393220
  327.1 8.4 %copy-start.50 = (f32[4,1,128]{2,1,0:T(1,128)S(1)}, f32[4,1,128]{2,1,0:T(1,128)}, u32[]{:S(2)}) copy-start(f32[4,1,128]{2,1,0:T(1,128)} %get-tuple-element.140) | copy-start | bytes 6148
  327.1 8.4 %copy-start.75 = (f32[4,128]{1,0:T(4,128)S(1)}, f32[4,128]{1,0:T(4,128)}, u32[]{:S(2)}) copy-start(f32[4,128]{1,0:T(4,128)} %neg.71) | copy-start | bytes 6148
  327.1 8.4 %copy-start.83 = (f32[4,128]{1,0:T(4,128)S(1)}, f32[4,128]{1,0:T(4,128)}, u32[]{:S(2)}) copy-start(f32[4,128]{1,0:T(4,128)} %get-tuple-element.80) | copy-start | bytes 6148
  334.4 4.2 collective-permute-start.7
  343.6 82.9 %all-gather.11.cloned.1.call-start = ((), (), s32[]{:S(2)}) async-start(), calls=%async_computation.10 | async-start | bytes 1310720 | tf_op jit(solution)/shard_map/all_gather | solution.py:153
  386.9 9.9 %collective-permute-start.8 = (bf16[128,1024]{1,0:T(8,128)(2,1)S(1)}, bf16[128,1024]{1,0:T(8,128)(2,1)}, u32[]{:S(2)}, u32[]{:S(2)}) collective-permute-start(bf16[128,1024]{1,0:T(8,128)(2,1)S(1)} %convert_bitcast_fusion), channel_id=1, source_target_pairs={{8,0},{16,8},{24,16},{9,1},{17,9},{25,17},{10,2},{18,10},{26,18},{... | collective-permute-start | bytes 786440 | tf_op jit(solution)/shard_map/ppermute | solution.py:24
  396.9 108.4 %reduce-scatter.11.cloned.1.call-start = ((), (), s32[]{:S(2)}) async-start(), calls=%async_computation.11 | async-start | bytes 2621440 | tf_op jit(solution)/shard_map/reduce_scatter | solution.py:177
  426.6 2.8 copy-start.9
  436.9 10.2 %copy-start.13 = (f32[128,256]{1,0:T(8,128)S(1)}, f32[128,256]{1,0:T(8,128)}, u32[]{:S(2)}) copy-start(f32[128,256]{1,0:T(8,128)} %get-tuple-element.108) | copy-start | bytes 393220
  441.8 7.0 %copy-start.25 = (f32[128,1,256]{2,0,1:T(8,128)S(1)}, f32[128,1,256]{2,0,1:T(8,128)}, u32[]{:S(2)}) copy-start(f32[128,1,256]{2,0,1:T(8,128)} %get-tuple-element.157) | copy-start | bytes 393220
  444.3 9.9 %collective-permute-start.9 = (f32[128,2,64]{0,2,1:T(8,128)}, f32[128,2,64]{0,2,1:T(8,128)}, u32[]{:S(2)}, u32[]{:S(2)}) collective-permute-start(f32[128,2,64]{0,2,1:T(8,128)} %slice_select_fusion), channel_id=1, source_target_pairs={{0,4},{2,6},{4,0},{6,2},{1,5},{3,7},{5,1},{7,3},{8,12},{10,14},{12... | collective-permute-start | bytes 196616 | tf_op jit(solution)/shard_map/ppermute | solution.py:18
  449.0 5.1 %copy-start.29 = (f32[128,256]{0,1:T(8,128)S(1)}, f32[128,256]{0,1:T(8,128)}, u32[]{:S(2)}) copy-start(f32[128,256]{0,1:T(8,128)} %copy-done.28) | copy-start | bytes 393220
  449.0 7.1 %copy-start.51 = (f32[4,1,128]{2,1,0:T(1,128)S(1)}, f32[4,1,128]{2,1,0:T(1,128)}, u32[]{:S(2)}) copy-start(f32[4,1,128]{2,1,0:T(1,128)} %get-tuple-element.140) | copy-start | bytes 6148
  449.0 7.1 %copy-start.73 = (f32[4,128]{1,0:T(4,128)S(1)}, f32[4,128]{1,0:T(4,128)}, u32[]{:S(2)}) copy-start(f32[4,128]{1,0:T(4,128)} %neg.73) | copy-start | bytes 6148
  449.0 7.1 %copy-start.81 = (f32[4,128]{1,0:T(4,128)S(1)}, f32[4,128]{1,0:T(4,128)}, u32[]{:S(2)}) copy-start(f32[4,128]{1,0:T(4,128)} %get-tuple-element.71) | copy-start | bytes 6148
  455.1 2.8 collective-permute-start.10
  462.0 43.3 %copy-start.10 = (f32[1024,128]{0,1:T(8,128)S(1)}, f32[1024,128]{0,1:T(8,128)}, u32[]{:S(2)}) copy-start(f32[1024,128]{0,1:T(8,128)} %reduce-scatter.5.cloned.1.call-done) | copy-start | bytes 1572868
  462.0 43.3 %copy-start.11 = (f32[1024,128]{0,1:T(8,128)S(1)}, f32[1024,128]{0,1:T(8,128)}, u32[]{:S(2)}) copy-start(f32[1024,128]{0,1:T(8,128)} %reduce-scatter.7.cloned.1.call-done) | copy-start | bytes 1572868
  (41 other events, 81.7 us)
Sparse Core Ops, SparseCore 0:
  8.9 28.8 all-gather.4
  79.8 41.9 reduce-scatter.4
  133.0 29.5 all-gather.6
  211.7 42.0 reduce-scatter.6
  264.9 29.5 all-gather.8
  343.7 42.0 reduce-scatter.8
  397.0 29.5 all-gather.10
  462.1 43.1 reduce-scatter.10
where the time goes:
time: 521 us; the launch traced here: 514 us
  waiting for transfers between devices  298 us (57%)
  matrix products  80.2 us (15%)
  other arithmetic  63.4 us (12%)
  local copies, waits for them, and re-layouts  41.7 us (8%)
  starting transfers between devices  16.2 us (3%)
  between operations  14.9 us (3%)
    reduce_scatter x4, waiting for transfers between devices, body(): lax.psum_scatter(summed + lax.dot_general(step_rows, grad_step, (((0,), (...  170 us
    all_gather x4, waiting for transfers between devices, body(): lax.all_gather(incoming, 'tensor', axis=1, tiled=True)  104 us
    ppermute x3, waiting for transfers between devices, passed_along(): lax.ppermute(value, axis, [(source, source + steps) for source in range(l...  23.2 us
    dot_general x9, matrix products, state_space(): within = jnp.einsum('hcij,cjhp->cihp', weights, scaled, precision=HIGHEST)  21.1 us
    dot_general x4, matrix products, body(): lax.dot_general(main_cols, grad_main, (((1,), (1,)), ((), ())), preferred...  20.6 us
    mul x16, other arithmetic, causal_conv(): summed = summed + kernel[offset] * padded[offset:offset + length]  14.4 us
  transfers between devices with their start and end apart: 19, of which 12 were waited for; matrix products, arithmetic and copies ran while one was open for 13% of the time, Pallas kernels for 0%

commit v1 on v0

--- a/solution.py
+++ b/solution.py
@@ -1,6 +1,8 @@
 import jax
 import jax.numpy as jnp
 from jax import lax
+from jax.experimental import pallas as pl
+from jax.experimental.pallas import tpu as pltpu
 from jax.sharding import PartitionSpec as P
 
 NSTATE = 128
@@ -94,7 +96,7 @@
     return gated * inverse * norm_gain
 
 
-def body(
+def wide_body(
     weight_main,
     weight_state,
     weight_step,
@@ -189,9 +191,465 @@
     return result[None]
 
 
+BF16 = jnp.bfloat16
+F32 = jnp.float32
+SPACE = pltpu.VMEM
+VMEM_BYTES = 48 * 2**20
+
+
+def dot_nt(left, right, **options):
+    return lax.dot_general(
+        left, right, (((1,), (1,)), ((), ())), preferred_element_type=F32, **options
+    )
+
+
+def dot_tn(left, right):
+    return lax.dot_general(left, right, (((0,), (0,)), ((), ())), preferred_element_type=F32)
+
+
+def dot_nn(left, right, **options):
+    return jnp.dot(left, right, preferred_element_type=F32, **options)
+
+
+def iota(shape, dim):
+    return lax.broadcasted_iota(jnp.int32, shape, dim)
+
+
+def head_lanes(shape, head, size):
+    lane = iota(shape, 1)
+    return (lane >= head * size) & (lane < (head + 1) * size)
+
+
+def conv_taps(signal, taps):
+    count = taps.shape[0]
+    row = iota(signal.shape, 0)
+    total = taps[count - 1 : count] * signal
+    for back in range(1, count):
+        moved = jnp.where(row >= back, pltpu.roll(signal, back, 0), 0.0)
+        total = total + taps[count - 1 - back : count - back] * moved
+    return total
+
+
+def conv_taps_back(grad, taps):
+    count = taps.shape[0]
+    length = grad.shape[0]
+    row = iota(grad.shape, 0)
+    total = taps[count - 1 : count] * grad
+    for ahead in range(1, count):
+        moved = jnp.where(row < length - ahead, pltpu.roll(grad, length - ahead, 0), 0.0)
+        total = total + taps[count - 1 - ahead : count - ahead] * moved
+    return total
+
+
+def silu_and_slope(value):
+    gate = jax.nn.sigmoid(value)
+    return value * gate, gate * (1.0 + value * (1.0 - gate))
+
+
+def forward_kernel(
+    heads,
+    gate_ref,
+    mixer_ref,
+    state_ref,
+    step_ref,
+    taps_main_ref,
+    taps_state_ref,
+    heads_ref,
+    gain_ref,
+    maps_ref,
+    decay_ref,
+    decayed_ref,
+    values_ref,
+    state_out_ref,
+    slope_ref,
+):
+    length, channels = gate_ref.shape
+    size = channels // heads
+    states = state_ref.shape[1] // 2
+    gate, gate_slope = silu_and_slope(gate_ref[...].astype(F32))
+    value, value_slope = silu_and_slope(
+        conv_taps(mixer_ref[...].astype(F32), taps_main_ref[...])
+    )
+    state, state_slope = silu_and_slope(
+        conv_taps(state_ref[...].astype(F32), taps_state_ref[...])
+    )
+    inputs = state[:, :states]
+    readout = state[:, states:]
+    raw_step = step_ref[...] + heads_ref[0:1]
+    step = jnp.maximum(raw_step, 0.0) + jnp.log1p(jnp.exp(-jnp.abs(raw_step)))
+    slope_ref[...] = jax.nn.sigmoid(raw_step)
+    rate = -jnp.exp(heads_ref[1:2])
+    square = (length, length)
+    later = iota(square, 0) >= iota(square, 1)
+    earlier = iota(square, 0) <= iota(square, 1)
+    running = dot_nn(later.astype(F32), step * rate, precision=HIGHEST)
+    running_row = running.T
+    scores = dot_nt(readout, inputs, precision=HIGHEST)
+    scores_back = dot_nt(inputs, readout, precision=HIGHEST)
+    wide = (length, channels)
+    step_wide = jnp.zeros(wide, F32)
+    skip_wide = jnp.zeros(wide, F32)
+    for head in range(heads):
+        lanes = head_lanes(wide, head, size)
+        step_wide = jnp.where(lanes, step[:, head : head + 1], step_wide)
+        skip_wide = jnp.where(lanes, heads_ref[2:3, head : head + 1], skip_wide)
+    scaled = value * step_wide
+    output = skip_wide * value
+    for head in range(heads):
+        lanes = head_lanes(wide, head, size)
+        columns = pl.ds(head * length, length)
+        column = running[:, head : head + 1]
+        row = running_row[head : head + 1, :]
+        decay = jnp.where(later, jnp.exp(jnp.where(later, column - row, 0.0)), 0.0)
+        back = jnp.where(earlier, jnp.exp(jnp.where(earlier, row - column, 0.0)), 0.0)
+        weights = decay * scores
+        own = jnp.where(lanes, scaled, 0.0)
+        output = output + dot_nn(weights, own, precision=HIGHEST)
+        decay_ref[0, :, columns] = decay
+        decay_ref[1, :, columns] = weights
+        decayed_ref[:, columns] = (back * scores_back).astype(BF16)
+        values_ref[columns, :] = own.astype(BF16)
+    gated = output * gate
+    inverse = lax.rsqrt(jnp.mean(gated * gated, axis=1, keepdims=True) + EPSILON)
+    gain = gain_ref[...]
+    normal = gated * inverse
+    maps_ref[0] = gain * inverse
+    maps_ref[1] = normal * inverse
+    maps_ref[2] = gain * normal * (1.0 / channels)
+    maps_ref[3] = gate
+    maps_ref[4] = output * gate_slope
+    maps_ref[5] = skip_wide * value_slope
+    maps_ref[6] = step_wide * value_slope
+    maps_ref[7] = value
+    maps_ref[8] = state_slope
+    state_out_ref[0] = inputs.astype(BF16)
+    state_out_ref[1] = readout.astype(BF16)
+
+
+def mixer_back(heads, dnormed, residuals):
+    (
+        maps_ref,
+        decay_ref,
+        decayed_ref,
+        values_ref,
+        state_ref,
+        slope_ref,
+        taps_main_ref,
+        taps_state_ref,
+        heads_ref,
+    ) = residuals
+    length, channels = dnormed.shape
+    size = channels // heads
+    shared = jnp.sum(dnormed * maps_ref[2], axis=1, keepdims=True)
+    d_gated = dnormed * maps_ref[0] - maps_ref[1] * shared
+    d_output = d_gated * maps_ref[3]
+    d_gate = d_gated * maps_ref[4]
+    by_head = jnp.concatenate(
+        [
+            jnp.where(head_lanes(d_output.shape, head, size), d_output, 0.0).astype(BF16)
+            for head in range(heads)
+        ],
+        axis=0,
+    )
+    d_scaled = dot_nn(decayed_ref[...], by_head)
+    d_weights = dot_nt(d_output.astype(BF16), values_ref[...])
+    d_decayed = d_weights * decay_ref[0]
+    d_scores = d_decayed[:, :length]
+    for head in range(1, heads):
+        d_scores = d_scores + d_decayed[:, head * length : (head + 1) * length]
+    d_exponent = d_weights * decay_ref[1]
+    square = (length, length)
+    onward = (iota(square, 0) <= iota(square, 1)).astype(BF16)
+    spanning = dot_nn(onward, d_exponent.astype(BF16))
+    row = iota(spanning.shape, 0)
+    source = iota(spanning.shape, 1) % length
+    spanning = jnp.where(source < row, spanning, 0.0)
+    lane = iota((channels, 128), 1)
+    of_channel = (iota((channels, 128), 0) // size == lane).astype(BF16)
+    of_source = (
+        iota((heads * length, 128), 0) // length == iota((heads * length, 128), 1)
+    ).astype(BF16)
+    rate = -jnp.exp(heads_ref[1:2])
+    d_step = dot_nn((d_scaled * maps_ref[7]).astype(BF16), of_channel)
+    d_step = d_step + rate * dot_nn(spanning.astype(BF16), of_source)
+    d_step = d_step * slope_ref[...]
+    rounded = d_scores.astype(BF16)
+    d_readout = dot_nn(rounded, state_ref[0])
+    d_inputs = dot_tn(rounded, state_ref[1])
+    d_state = jnp.concatenate([d_inputs, d_readout], axis=1) * maps_ref[8]
+    d_mixer = d_output * maps_ref[5] + d_scaled * maps_ref[6]
+    main = jnp.concatenate(
+        [
+            d_gate.astype(BF16),
+            conv_taps_back(d_mixer, taps_main_ref[...]).astype(BF16),
+            d_step.astype(BF16),
+        ],
+        axis=1,
+    )
+    return main, conv_taps_back(d_state, taps_state_ref[...]).astype(BF16)
+
+
+def section_kernel(heads, chunks, first, *refs):
+    count = chunks
+    incoming = refs[:count]
+    refs = refs[count:]
+    out_rows_ref = None
+    if first:
+        out_rows_ref, refs = refs[0], refs[1:]
+    residuals, refs = refs[:9], refs[9:]
+    cols_ref, refs = refs[0], refs[1:]
+    outs, refs = refs[:chunks], refs[chunks:]
+    cols, cols_sems = refs[0], refs[1]
+    me = lax.axis_index("tensor")
+    width = cols.shape[1]
+    copies = []
+    if first:
+        rows, rows_sem = refs[2], refs[3]
+        rows_copy = pltpu.make_async_copy(out_rows_ref, rows, rows_sem)
+        rows_copy.start()
+    for hop in range(chunks):
+        chunk = lax.rem(me + hop, chunks)
+        copy = pltpu.make_async_copy(
+            cols_ref.at[pl.ds(pl.multiple_of(chunk * width, width), width), :],
+            cols.at[hop],
+            cols_sems.at[hop],
+        )
+        copy.start()
+        copies.append(copy)
+    if first:
+        rows_copy.wait()
+        dnormed = None
+        for hop in range(chunks):
+            chunk = lax.rem(me + chunks - hop, chunks)
+            term = dot_nt(
+                incoming[hop][...], rows[:, pl.ds(pl.multiple_of(chunk * width, width), width)]
+            )
+            dnormed = term if dnormed is None else dnormed + term
+    else:
+        dnormed = incoming[0][...].astype(F32)
+        for hop in range(1, chunks):
+            dnormed = dnormed + incoming[hop][...].astype(F32)
+    main, state = mixer_back(heads, dnormed, residuals)
+    for hop in range(chunks):
+        copies[hop].wait()
+        outs[hop][:, :width] = dot_nt(main, cols[hop]).astype(BF16)
+        outs[hop][:, width:] = state
+
+
+def carry_kernel(chunks, last, *refs):
+    parts = refs[:chunks]
+    state_ref, refs = refs[chunks], refs[chunks + 1 :]
+    if not last:
+        own_ref, other_ref, refs = refs[0], refs[1], refs[2:]
+        carry_ref, outs, refs = refs[0], refs[1 : 1 + chunks], refs[1 + chunks :]
+        own, other, sems = refs
+        copies = [
+            pltpu.make_async_copy(own_ref, own, sems.at[0]),
+            pltpu.make_async_copy(other_ref, other, sems.at[1]),
+        ]
+        for copy in copies:
+            copy.start()
+    else:
+        carry_ref = refs[0]
+    width = carry_ref.shape[1]
+    total = parts[0][...].astype(F32)
+    for part in parts[1:]:
+        total = total + part[...].astype(F32)
+    carry = total[:, :width] + dot_nn(total[:, width:].astype(BF16), state_ref[...])
+    carry = carry.astype(BF16)
+    carry_ref[...] = carry
+    if not last:
+        half = own.shape[0] // chunks
+        core = lax.axis_index("dp")
+        for copy, held, place in ((copies[0], own, core), (copies[1], other, 1 - core)):
+            copy.wait()
+            product = dot_nt(carry, held[...]).astype(BF16)
+            lanes = pl.ds(pl.multiple_of(place * half, half), half)
+            for hop in range(chunks):
+                outs[hop][:, lanes] = product[:, hop * half : (hop + 1) * half]
+
+
+def kernel_params():
+    return pltpu.CompilerParams(vmem_limit_bytes=VMEM_BYTES)
+
+
+def whole(count):
+    return [pl.BlockSpec(memory_space=SPACE)] * count
+
+
+def section_pairs(sections, chunks, source, target, hop):
+    return [
+        (source * chunks + index, target * chunks + (index + hop) % chunks)
+        for index in range(chunks)
+    ]
+
+
+def relay_body(
+    weight_main,
+    weight_state,
+    weight_step,
+    weight_out,
+    conv_main,
+    conv_state,
+    step_bias,
+    decay_log,
+    skip_gain,
+    norm_gain,
+    saved_main,
+    saved_state,
+    saved_step,
+    output_grad,
+):
+    sections = lax.axis_size("pipe")
+    chunks = lax.axis_size("tensor")
+    section = lax.axis_index("pipe")
+    me = lax.axis_index("tensor")
+    core = lax.axis_index("dp")
+    length, width = output_grad.shape
+    model_width = weight_out.shape[2]
+    heads = step_bias.shape[1]
+    channels = weight_out.shape[1]
+    half_rows = channels // 2
+    half_width = width // 2
+    place = ("pipe", "tensor")
+
+    last_own = jnp.where(section == sections - 1, output_grad, jnp.zeros_like(output_grad))
+    incoming = [last_own]
+    for hop in range(1, chunks):
+        pairs = section_pairs(sections, chunks, sections - 1, sections - 1, hop)
+        incoming.append(lax.ppermute(output_grad, place, pairs))
+
+    own_half = []
+    for hop in range(chunks):
+        chunk = (me + hop) % chunks
+        piece = lax.dynamic_slice(
+            weight_out[0], (core * half_rows, chunk * width), (half_rows, width)
+        )
+        pairs = []
+        for source in range(sections - 1):
+            pairs += section_pairs(sections, chunks, source, source + 1, hop)
+        own_half.append(lax.ppermute(piece, place, pairs))
+    own_half = jnp.concatenate(own_half, axis=0)
+    other_half = lax.ppermute(own_half, "dp", [(0, 1), (1, 0)])
+
+    state_cols = weight_state[0].reshape(model_width, -1).T
+    pieces = []
+    for hop in range(chunks):
+        chunk = (me + hop) % chunks
+        piece = lax.dynamic_slice(
+            state_cols,
+            (0, chunk * width + core * half_width),
+            (state_cols.shape[0], half_width),
+        )
+        if hop:
+            pairs = [(index, (index + hop) % chunks) for index in range(chunks)]
+            piece = lax.ppermute(piece, "tensor", pairs)
+        pieces.append(piece)
+    state_own = jnp.stack(pieces)
+    state_other = lax.ppermute(state_own, "dp", [(0, 1), (1, 0)])
+    lower = jnp.where(core == 0, state_own, state_other)
+    upper = jnp.where(core == 0, state_other, state_own)
+    state_rows = jnp.concatenate([lower, upper], axis=2)
+    order = (me - jnp.arange(chunks)) % chunks
+    state_rows = jnp.take(state_rows, order, axis=0)
+    state_rows = state_rows.reshape(chunks, 2, -1, width).transpose(1, 0, 2, 3)
+    state_rows = state_rows.reshape(-1, width)
+
+    step_cols = jnp.pad(weight_step[0].T, ((0, 0), (0, 128 - heads)))
+    cols = jnp.concatenate([weight_main[0].reshape(model_width, -1), step_cols], axis=1)
+
+    lanes = ((0, 0), (0, 128 - heads))
+    by_head = jnp.pad(
+        jnp.stack([step_bias[0], decay_log[0], skip_gain[0]]), ((0, 5), (0, 128 - heads))
+    )
+    steps = jnp.pad(saved_step[0].astype(F32).T, lanes)
+    taps_main = conv_main[0]
+    taps_state = conv_state[0].reshape(conv_state.shape[1], -1)
+    state_width = taps_state.shape[1]
+    residual_shapes = (
+        jax.ShapeDtypeStruct((9, length, channels), F32),
+        jax.ShapeDtypeStruct((2, length, heads * length), F32),
+        jax.ShapeDtypeStruct((length, heads * length), BF16),
+        jax.ShapeDtypeStruct((heads * length, channels), BF16),
+        jax.ShapeDtypeStruct((2, length, state_width // 2), BF16),
+        jax.ShapeDtypeStruct((length, 128), F32),
+    )
+    residuals = pl.pallas_call(
+        lambda *refs: forward_kernel(heads, *refs),
+        out_shape=residual_shapes,
+        in_specs=whole(8),
+        out_specs=whole(6),
+        compiler_params=kernel_params(),
+        name="forward_residuals",
+    )(
+        saved_main[0, :, 0],
+        saved_main[0, :, 1],
+        saved_state[0].reshape(length, -1),
+        steps,
+        taps_main,
+        taps_state,
+        by_head,
+        norm_gain,
+    )
+    residuals = tuple(residuals) + (taps_main, taps_state, by_head)
+    message = jax.ShapeDtypeStruct((length, width + state_width), BF16)
+    slice_out = jax.ShapeDtypeStruct((length, channels), BF16)
+    hbm = pl.BlockSpec(memory_space=pl.ANY)
+
+    result = jnp.zeros((length, width), BF16)
+    for moment in range(sections):
+        active = sections - 1 - moment
+        first = moment == 0
+        last = moment + 1 == sections
+        scratch = [
+            pltpu.VMEM((chunks, width, cols.shape[1]), BF16),
+            pltpu.SemaphoreType.DMA((chunks,)),
+        ]
+        if first:
+            scratch += [pltpu.VMEM((channels, model_width), BF16), pltpu.SemaphoreType.DMA]
+        parts = pl.pallas_call(
+            lambda *refs, first=first: section_kernel(heads, chunks, first, *refs),
+            out_shape=(message,) * chunks,
+            in_specs=whole(chunks) + [hbm] * first + whole(9) + [hbm],
+            out_specs=whole(chunks),
+            scratch_shapes=scratch,
+            compiler_params=kernel_params(),
+            name="section_first" if first else "section_next",
+        )(*incoming, *((weight_out[0],) if first else ()), *residuals, cols)
+        gathered = [parts[0]]
+        for hop in range(1, chunks):
+            pairs = section_pairs(sections, chunks, active, active, hop)
+            gathered.append(lax.ppermute(parts[hop], place, pairs))
+        carry_shape = jax.ShapeDtypeStruct((length, width), BF16)
+        scratch = []
+        if not last:
+            scratch = [
+                pltpu.VMEM(own_half.shape, BF16),
+                pltpu.VMEM(own_half.shape, BF16),
+                pltpu.SemaphoreType.DMA((2,)),
+            ]
+        outs = pl.pallas_call(
+            lambda *refs, last=last: carry_kernel(chunks, last, *refs),
+            out_shape=(carry_shape,) + (() if last else (slice_out,) * chunks),
+            in_specs=whole(chunks + 1) + ([] if last else [hbm] * 2),
+            out_specs=whole(1 if last else 1 + chunks),
+            scratch_shapes=scratch,
+            compiler_params=kernel_params(),
+            name="carry_last" if last else "carry_next",
+        )(*gathered, state_rows, *(() if last else (own_half, other_half)))
+        result = jnp.where(section == active, outs[0], result)
+        if not last:
+            incoming = []
+            for hop in range(chunks):
+                pairs = section_pairs(sections, chunks, active, active - 1, chunks - hop)
+                incoming.append(lax.ppermute(outs[1 + hop], place, pairs))
+    return result[None]
+
+
 def solution(mesh):
+    narrow = mesh.shape["tensor"] == GROUP_SPAN
     return jax.shard_map(
-        body,
+        relay_body if narrow else wide_body,
         mesh=mesh,
         in_specs=(
             P("pipe", None, None, "tensor"),

time: 521 us -> 249 us (0.48)
  the two profiles are of different devices: /device:TPU:11 before, /device:TPU:9 now
where the time goes in v1:
time: 249 us; the launch traced here: 248 us
  waiting for transfers between devices  140 us (56%)
  starting transfers between devices  56.5 us (23%)
  Pallas kernels  29.4 us (12%)
  local copies, waits for them, and re-layouts  12.7 us (5%)
  other arithmetic  8 us (3%)
    ppermute x12, waiting for transfers between devices, relay_body(): incoming.append(lax.ppermute(outs[1 + hop], place, pairs))  107 us
    ppermute x12, waiting for transfers between devices, relay_body(): gathered.append(lax.ppermute(parts[hop], place, pairs))  25.6 us
    pallas_call x4, Pallas kernels, relay_body(): pl.pallas_call(lambda *refs, first=first: section_kernel(heads, chunks, f...  21.2 us
    ppermute x12, starting transfers between devices, relay_body(): gathered.append(lax.ppermute(parts[hop], place, pairs))  19.5 us
    ppermute x4, starting transfers between devices, relay_body(): own_half.append(lax.ppermute(piece, place, pairs))  17.1 us
    ppermute x12, starting transfers between devices, relay_body(): incoming.append(lax.ppermute(outs[1 + hop], place, pairs))  10.8 us
    unnamed x60, local copies, waits for them, and re-layouts  7.71 us
    pallas_call x4, Pallas kernels, relay_body(): pl.pallas_call(lambda *refs, last=last: carry_kernel(chunks, last, *refs)...  6.96 us
  transfers between devices with their start and end apart: 36, of which 7 were waited for; matrix products, arithmetic and copies ran while one was open for 7% of the time, Pallas kernels for 4%

profile of v1, /device:TPU:9, one launch (start us, length us, event | category | flops | bytes accessed | tf_op | source)
XLA Modules:
  0.0 247.7 jit_solution(17651144061631204064)
XLA Ops:
  0.0 1.4 collective-permute-start
  1.4 1.4 collective-permute-start.1
  2.8 1.3 dynamic-slice_bitcast_fusion
  4.0 3.1 %collective-permute-start.10 = (bf16[128,1024]{1,0:T(8,128)(2,1)S(1)}, bf16[128,1024]{1,0:T(8,128)(2,1)S(1)}, u32[]{:S(2)}, u32[]{:S(2)}) collective-permute-start(bf16[128,1024]{1,0:T(8,128)(2,1)S(1)} %get-tuple-element.81), channel_id=1, source_target_pairs={{0,8},{2,10},{4,12},{6,14},{8,16},{10,18},{12,20},{14,22},{16,24},... | collective-permute-start | bytes 786440 | tf_op jit(solution)/shard_map/ppermute | solution.py:531
  7.2 4.1 %collective-permute-start.11 = (bf16[128,1024]{1,0:T(8,128)(2,1)S(1)}, bf16[128,1024]{1,0:T(8,128)(2,1)S(1)}, u32[]{:S(2)}, u32[]{:S(2)}) collective-permute-start(bf16[128,1024]{1,0:T(8,128)(2,1)S(1)} %get-tuple-element.80), channel_id=1, source_target_pairs={{0,10},{2,12},{4,14},{6,8},{8,18},{10,20},{12,22},{14,16},{16,26},... | collective-permute-start | bytes 786440 | tf_op jit(solution)/shard_map/ppermute | solution.py:531
  11.3 8.6 %collective-permute-start.12 = (bf16[128,1024]{1,0:T(8,128)(2,1)S(1)}, bf16[128,1024]{1,0:T(8,128)(2,1)S(1)}, u32[]{:S(2)}, u32[]{:S(2)}) collective-permute-start(bf16[128,1024]{1,0:T(8,128)(2,1)S(1)} %get-tuple-element.82), channel_id=1, source_target_pairs={{0,12},{2,14},{4,8},{6,10},{8,20},{10,22},{12,16},{14,18},{16,28},... | collective-permute-start | bytes 786440 | tf_op jit(solution)/shard_map/ppermute | solution.py:531
  19.9 1.2 fusion.5
  21.1 0.8 copy.21
  21.9 1.4 copy.22
  23.3 2.9 %copy.28 = bf16[512,8,2,256]{3,1,2,0:T(8,128)(2,1)S(1)} copy(bf16[512,8,2,256]{3,2,1,0:T(2,128)(2,1)} %bitcast.73) | data formatting | bytes 8388608
  26.3 3.0 %fusion.1.refs_14_.refs_13_ = bf16[4096,640]{1,0:T(8,128)(2,1)} fusion(bf16[4096,4]{1,0:T(8,128)(2,1)S(1)} %bitcast.72, bf16[4096,512]{1,0:T(8,128)(2,1)S(1)} %bitcast.70), kind=kLoop, calls=%fused_computation.3 | loop fusion | flops 15728640 | bytes 9469952 | tf_op jit(solution)/shard_map/concatenate | solution.py:559
  29.4 1.0 dynamic-slice_bitcast_fusion.7
  31.0 1.3 collective-permute-start.13
  32.3 1.8 collective-permute-start.8
  34.9 1.2 collective-permute-done.13
  36.1 1.2 collective-permute-start.6
  37.3 2.1 collective-permute-done.8
  39.3 0.7 collective-permute-start.2
  40.0 3.9 %collective-permute-done.7 = bf16[64,512]{1,0:T(8,128)(2,1)S(1)} collective-permute-done((bf16[64,512]{1,0:T(8,128)(2,1)S(1)}, bf16[64,512]{1,0:T(8,128)(2,1)S(1)}, u32[]{:S(2)}, u32[]{:S(2)}) %collective-permute-start.7) | collective-permute-done | bytes 65568 | tf_op jit(solution)/shard_map/ppermute | solution.py:546
  43.9 1.7 collective-permute-start.14
  45.7 0.7 pad_maximum_fusion.1
  47.3 1.2 forward_residuals.1
  48.6 8.0 %section_first.1 = (bf16[128,1280]{1,0:T(8,128)(2,1)S(1)}, bf16[128,1280]{1,0:T(8,128)(2,1)}, bf16[128,1280]{1,0:T(8,128)(2,1)}, bf16[128,1280]{1,0:T(8,128)(2,1)}) custom-call(bf16[128,1024]{1,0:T(8,128)(2,1)S(1)} %broadcast_select_fusion.2.refs_0_, bf16[128,1024]{1,0:T(8,128)(2,1)} %collective-permute-done.refs_1_, ...), custom_call_target="tpu_custom_call" | custom-call | tf_op jit(solution)/shard_map/section_first/pallas_call | solution.py:610
  56.7 0.7 copy-done.6
  57.4 1.4 collective-permute-start.3
  58.8 1.4 collective-permute-start.4
  60.2 1.4 collective-permute-start.5
  61.6 1.0 broadcast_select_fusion.1
  62.7 1.5 gather_fusion
  64.2 1.2 select_bitcast_fusion
  65.5 1.0 copy-done.7
  66.5 3.0 %carry_next.3 = (bf16[128,1024]{1,0:T(8,128)(2,1)S(1)}, bf16[128,256]{1,0:T(8,128)(2,1)S(1)}, bf16[128,256]{1,0:T(8,128)(2,1)S(1)}, bf16[128,256]{1,0:T(8,128)(2,1)S(1)}, bf16[128,256]{1,0:T(8,128)(2,1)S(1)}) custom-call(bf16[128,1280]{1,0:T(8,128)(2,1)S(1)} %copy-done.7, bf16[128,1280]{1,0:T(8,128)(2,1)} %collective-permute-done.3.refs_1_, ...), custom_call_target="tpu_custom_call" | custom-call | tf_op jit(solution)/shard_map/carry_next/pallas_call | solution.py:631
  69.5 0.7 collective-permute-start.15
  70.2 0.7 collective-permute-start.16
  70.9 0.7 collective-permute-start.17
  71.5 0.7 collective-permute-start.18
  72.3 4.2 %section_next.3 = (bf16[128,1280]{1,0:T(8,128)(2,1)S(1)}, bf16[128,1280]{1,0:T(8,128)(2,1)S(1)}, bf16[128,1280]{1,0:T(8,128)(2,1)S(1)}, bf16[128,1280]{1,0:T(8,128)(2,1)S(1)}) custom-call(bf16[128,256]{1,0:T(8,128)(2,1)S(1)} %collective-permute-done.15.refs_0_, bf16[128,256]{1,0:T(8,128)(2,1)S(1)} %collective-permute-done.16.refs_1_, ...), custom_call_target="tpu_custom_call" | custom-call | tf_op jit(solution)/shard_map/section_next/pallas_call | solution.py:610
  76.5 0.7 collective-permute-start.19
  77.2 0.7 collective-permute-start.20
  77.8 0.7 collective-permute-start.21
  78.6 1.8 carry_next.4
  80.4 0.7 copy-done.10
  81.1 0.7 collective-permute-start.22
  81.8 0.7 collective-permute-start.23
  82.5 0.7 collective-permute-start.24
  83.1 0.8 collective-permute-start.25
  84.0 4.2 %section_next.4 = (bf16[128,1280]{1,0:T(8,128)(2,1)S(1)}, bf16[128,1280]{1,0:T(8,128)(2,1)S(1)}, bf16[128,1280]{1,0:T(8,128)(2,1)S(1)}, bf16[128,1280]{1,0:T(8,128)(2,1)S(1)}) custom-call(bf16[128,256]{1,0:T(8,128)(2,1)S(1)} %collective-permute-done.22.refs_0_, bf16[128,256]{1,0:T(8,128)(2,1)S(1)} %collective-permute-done.23.refs_1_, ...), custom_call_target="tpu_custom_call" | custom-call | tf_op jit(solution)/shard_map/section_next/pallas_call | solution.py:610
  88.2 0.7 collective-permute-start.26
  88.9 0.7 collective-permute-start.27
  89.6 0.7 collective-permute-start.28
  90.3 1.8 carry_next.5
  92.2 1.4 collective-permute-start.29
  93.6 1.3 collective-permute-start.30
  94.9 1.3 collective-permute-start.31
  96.2 1.3 collective-permute-start.32
  97.5 107.3 %collective-permute-done.29.refs_0_ = bf16[128,256]{1,0:T(8,128)(2,1)S(1)} collective-permute-done((bf16[128,256]{1,0:T(8,128)(2,1)S(1)}, bf16[128,256]{1,0:T(8,128)(2,1)S(1)}, u32[]{:S(2)}, u32[]{:S(2)}) %collective-permute-start.29) | collective-permute-done | bytes 65568 | tf_op jit(solution)/shard_map/ppermute | solution.py:645
  204.8 4.9 %section_next.5 = (bf16[128,1280]{1,0:T(8,128)(2,1)S(1)}, bf16[128,1280]{1,0:T(8,128)(2,1)}, bf16[128,1280]{1,0:T(8,128)(2,1)}, bf16[128,1280]{1,0:T(8,128)(2,1)}) custom-call(bf16[128,256]{1,0:T(8,128)(2,1)S(1)} %collective-permute-done.29.refs_0_, bf16[128,256]{1,0:T(8,128)(2,1)S(1)} %collective-permute-done.30.refs_1_, ...), custom_call_target="tpu_custom_call" | custom-call | tf_op jit(solution)/shard_map/section_next/pallas_call | solution.py:610
  209.7 4.8 %collective-permute-start.33 = (bf16[128,1280]{1,0:T(8,128)(2,1)}, bf16[128,1280]{1,0:T(8,128)(2,1)S(1)}, u32[]{:S(2)}, u32[]{:S(2)}) collective-permute-start(bf16[128,1280]{1,0:T(8,128)(2,1)} %get-tuple-element.73), channel_id=1, source_target_pairs={{0,2},{2,4},{4,6},{6,0},{1,3},{3,5},{5,7},{7,1}} | collective-permute-start | bytes 983048 | tf_op jit(solution)/shard_map/ppermute | solution.py:622
  214.5 4.5 %collective-permute-start.34 = (bf16[128,1280]{1,0:T(8,128)(2,1)}, bf16[128,1280]{1,0:T(8,128)(2,1)S(1)}, u32[]{:S(2)}, u32[]{:S(2)}) collective-permute-start(bf16[128,1280]{1,0:T(8,128)(2,1)} %get-tuple-element.74), channel_id=1, source_target_pairs={{0,4},{2,6},{4,0},{6,2},{1,5},{3,7},{5,1},{7,3}} | collective-permute-start | bytes 983048 | tf_op jit(solution)/shard_map/ppermute | solution.py:622
  219.1 1.9 collective-permute-start.35
  221.0 1.5 collective-permute-done.33.refs_1_
  222.6 19.5 %collective-permute-done.34.refs_2_ = bf16[128,1280]{1,0:T(8,128)(2,1)S(1)} collective-permute-done((bf16[128,1280]{1,0:T(8,128)(2,1)}, bf16[128,1280]{1,0:T(8,128)(2,1)S(1)}, u32[]{:S(2)}, u32[]{:S(2)}) %collective-permute-start.34) | collective-permute-done | bytes 327712 | tf_op jit(solution)/shard_map/ppermute | solution.py:622
  242.0 4.6 %collective-permute-done.35.refs_3_ = bf16[128,1280]{1,0:T(8,128)(2,1)S(1)} collective-permute-done((bf16[128,1280]{1,0:T(8,128)(2,1)}, bf16[128,1280]{1,0:T(8,128)(2,1)S(1)}, u32[]{:S(2)}, u32[]{:S(2)}) %collective-permute-start.35) | collective-permute-done | bytes 327712 | tf_op jit(solution)/shard_map/ppermute | solution.py:622
  246.9 0.8 select_bitcast_fusion.1
  (96 shorter events, 2.7 us)
Async XLA Ops:
  0.0 48.6 %collective-permute-start = (bf16[128,1024]{1,0:T(8,128)(2,1)}, bf16[128,1024]{1,0:T(8,128)(2,1)}, u32[]{:S(2)}, u32[]{:S(2)}) collective-permute-start(bf16[128,1024]{1,0:T(8,128)(2,1)} %param.27), channel_id=1, source_target_pairs={{24,26},{26,28},{28,30},{30,24},{25,27},{27,29},{29,31},{31,25}} | collective-permute-start | bytes 786440 | tf_op jit(solution)/shard_map/ppermute | solution.py:520
  1.4 47.2 %collective-permute-start.1 = (bf16[128,1024]{1,0:T(8,128)(2,1)}, bf16[128,1024]{1,0:T(8,128)(2,1)}, u32[]{:S(2)}, u32[]{:S(2)}) collective-permute-start(bf16[128,1024]{1,0:T(8,128)(2,1)} %param.27), channel_id=1, source_target_pairs={{24,28},{26,30},{28,24},{30,26},{25,29},{27,31},{29,25},{31,27}} | collective-permute-start | bytes 786440 | tf_op jit(solution)/shard_map/ppermute | solution.py:520
  4.0 27.0 %collective-permute-start.10 = (bf16[128,1024]{1,0:T(8,128)(2,1)S(1)}, bf16[128,1024]{1,0:T(8,128)(2,1)S(1)}, u32[]{:S(2)}, u32[]{:S(2)}) collective-permute-start(bf16[128,1024]{1,0:T(8,128)(2,1)S(1)} %get-tuple-element.81), channel_id=1, source_target_pairs={{0,8},{2,10},{4,12},{6,14},{8,16},{10,18},{12,20},{14,22},{16,24},... | collective-permute-start | bytes 786440 | tf_op jit(solution)/shard_map/ppermute | solution.py:531
  7.2 25.2 %collective-permute-start.11 = (bf16[128,1024]{1,0:T(8,128)(2,1)S(1)}, bf16[128,1024]{1,0:T(8,128)(2,1)S(1)}, u32[]{:S(2)}, u32[]{:S(2)}) collective-permute-start(bf16[128,1024]{1,0:T(8,128)(2,1)S(1)} %get-tuple-element.80), channel_id=1, source_target_pairs={{0,10},{2,12},{4,14},{6,8},{8,18},{10,20},{12,22},{14,16},{16,26},... | collective-permute-start | bytes 786440 | tf_op jit(solution)/shard_map/ppermute | solution.py:531
  11.3 22.9 %collective-permute-start.12 = (bf16[128,1024]{1,0:T(8,128)(2,1)S(1)}, bf16[128,1024]{1,0:T(8,128)(2,1)S(1)}, u32[]{:S(2)}, u32[]{:S(2)}) collective-permute-start(bf16[128,1024]{1,0:T(8,128)(2,1)S(1)} %get-tuple-element.82), channel_id=1, source_target_pairs={{0,12},{2,14},{4,8},{6,10},{8,20},{10,22},{12,16},{14,18},{16,28},... | collective-permute-start | bytes 786440 | tf_op jit(solution)/shard_map/ppermute | solution.py:531
  26.3 4.7 %copy-start.23 = (f32[1,4]{1,0:T(1,128)S(1)}, f32[1,4]{1,0:T(1,128)}, u32[]{:S(2)}) copy-start(f32[1,4]{1,0:T(1,128)} %param.22) | copy-start | bytes 52
  26.3 4.7 %copy-start.24 = (f32[1,4]{1,0:T(1,128)S(1)}, f32[1,4]{1,0:T(1,128)}, u32[]{:S(2)}) copy-start(f32[1,4]{1,0:T(1,128)} %param.21) | copy-start | bytes 52
  26.3 4.7 %copy-start.25 = (f32[1,4]{1,0:T(1,128)S(1)}, f32[1,4]{1,0:T(1,128)}, u32[]{:S(2)}) copy-start(f32[1,4]{1,0:T(1,128)} %param.20) | copy-start | bytes 52
  26.3 20.9 %copy-start.21 = (bf16[1,128,2,128]{3,2,1,0:T(2,128)(2,1)S(1)}, bf16[1,128,2,128]{3,2,1,0:T(2,128)(2,1)}, u32[]{:S(2)}) copy-start(bf16[1,128,2,128]{3,2,1,0:T(2,128)(2,1)} %param.25) | copy-start | bytes 196612
  26.3 20.9 %copy-start.22 = (f32[1,4,2,128]{3,2,1,0:T(2,128)S(1)}, f32[1,4,2,128]{3,2,1,0:T(2,128)}, u32[]{:S(2)}) copy-start(f32[1,4,2,128]{3,2,1,0:T(2,128)} %param.19) | copy-start | bytes 12292
  26.3 21.0 %copy-start.13 = (f32[1,4,256]{2,1,0:T(4,128)S(1)}, f32[1,4,256]{2,1,0:T(4,128)}, u32[]{:S(2)}) copy-start(f32[1,4,256]{2,1,0:T(4,128)} %param.18) | copy-start | bytes 12292
  26.3 21.0 %copy-start.14 = (f32[1,256]{1,0:T(1,128)S(1)}, f32[1,256]{1,0:T(1,128)}, u32[]{:S(2)}) copy-start(f32[1,256]{1,0:T(1,128)} %refs_7_.1) | copy-start | bytes 3076
  31.0 5.1 %collective-permute-start.13 = (bf16[128,1024]{1,0:T(8,128)(2,1)S(1)}, bf16[128,1024]{1,0:T(8,128)(2,1)S(1)}, u32[]{:S(2)}, u32[]{:S(2)}) collective-permute-start(bf16[128,1024]{1,0:T(8,128)(2,1)S(1)} %get-tuple-element.79), channel_id=1, source_target_pairs={{0,14},{2,8},{4,10},{6,12},{8,22},{10,16},{12,18},{14,20},{16,30},... | collective-permute-start | bytes 786440 | tf_op jit(solution)/shard_map/ppermute | solution.py:531
  32.3 7.0 %collective-permute-start.8 = (bf16[64,512]{1,0:T(8,128)(2,1)S(1)}, bf16[64,512]{1,0:T(8,128)(2,1)S(1)}, u32[]{:S(2)}, u32[]{:S(2)}) collective-permute-start(bf16[64,512]{1,0:T(8,128)(2,1)S(1)} %get-tuple-element.86), channel_id=1, source_target_pairs={{0,6},{2,0},{4,2},{6,4},{1,7},{3,1},{5,3},{7,5},{8,14},{10,8},{12,... | collective-permute-start | bytes 196616 | tf_op jit(solution)/shard_map/ppermute | solution.py:546
  34.2 9.7 %collective-permute-start.7 = (bf16[64,512]{1,0:T(8,128)(2,1)S(1)}, bf16[64,512]{1,0:T(8,128)(2,1)S(1)}, u32[]{:S(2)}, u32[]{:S(2)}) collective-permute-start(bf16[64,512]{1,0:T(8,128)(2,1)S(1)} %get-tuple-element.87), channel_id=1, source_target_pairs={{0,4},{2,6},{4,0},{6,2},{1,5},{3,7},{5,1},{7,3},{8,12},{10,14},{12... | collective-permute-start | bytes 196616 | tf_op jit(solution)/shard_map/ppermute | solution.py:546
  36.1 9.6 %collective-permute-start.6 = (bf16[64,512]{1,0:T(8,128)(2,1)S(1)}, bf16[64,512]{1,0:T(8,128)(2,1)S(1)}, u32[]{:S(2)}, u32[]{:S(2)}) collective-permute-start(bf16[64,512]{1,0:T(8,128)(2,1)S(1)} %get-tuple-element.88), channel_id=1, source_target_pairs={{0,2},{2,4},{4,6},{6,0},{1,3},{3,5},{5,7},{7,1},{8,10},{10,12},{12... | collective-permute-start | bytes 196616 | tf_op jit(solution)/shard_map/ppermute | solution.py:546
  39.3 7.9 %copy-start.15 = (bf16[64,512]{1,0:T(8,128)(2,1)}, bf16[64,512]{1,0:T(8,128)(2,1)S(1)}, u32[]{:S(2)}) copy-start(bf16[64,512]{1,0:T(8,128)(2,1)S(1)} %collective-permute-done.8) | copy-start | bytes 196612
  39.3 9.3 %collective-permute-start.2 = (bf16[128,1024]{1,0:T(8,128)(2,1)}, bf16[128,1024]{1,0:T(8,128)(2,1)S(1)}, u32[]{:S(2)}, u32[]{:S(2)}) collective-permute-start(bf16[128,1024]{1,0:T(8,128)(2,1)} %param.27), channel_id=1, source_target_pairs={{24,30},{26,24},{28,26},{30,28},{25,31},{27,25},{29,27},{31,29}} | collective-permute-start | bytes 786440 | tf_op jit(solution)/shard_map/ppermute | solution.py:520
  43.9 3.3 %copy-start.17 = (bf16[64,512]{1,0:T(8,128)(2,1)}, bf16[64,512]{1,0:T(8,128)(2,1)S(1)}, u32[]{:S(2)}) copy-start(bf16[64,512]{1,0:T(8,128)(2,1)S(1)} %collective-permute-done.7) | copy-start | bytes 196612
  43.9 21.6 %collective-permute-start.14 = (bf16[512,1024]{1,0:T(8,128)(2,1)S(1)}, bf16[512,1024]{1,0:T(8,128)(2,1)}, u32[]{:S(2)}, u32[]{:S(2)}) collective-permute-start(bf16[512,1024]{1,0:T(8,128)(2,1)S(1)} %constant_dynamic-update-slice_fusion.refs_5_), channel_id=1, source_target_pairs={{0,1},{1,0},{2,3},{3,2},{4,5},{5,4},{6,7},{7,6},{8,9},{9,8},{10,11... | collective-permute-start | bytes 3145736 | tf_op jit(solution)/shard_map/ppermute | solution.py:533
  45.7 1.6 copy-start.19
  46.4 15.2 %collective-permute-start.9 = (bf16[4,64,512]{2,1,0:T(8,128)(2,1)}, bf16[4,64,512]{2,1,0:T(8,128)(2,1)}, u32[]{:S(2)}, u32[]{:S(2)}) collective-permute-start(bf16[4,64,512]{2,1,0:T(8,128)(2,1)} %pad_maximum_fusion.1), channel_id=1, source_target_pairs={{0,1},{1,0},{2,3},{3,2},{4,5},{5,4},{6,7},{7,6},{8,9},{9,8},{10,11... | collective-permute-start | bytes 786440 | tf_op jit(solution)/shard_map/ppermute | solution.py:549
  48.5 8.2 %copy-start = (bf16[128,512]{1,0:T(8,128)(2,1)}, bf16[128,512]{1,0:T(8,128)(2,1)S(1)}, u32[]{:S(2)}) copy-start(bf16[128,512]{1,0:T(8,128)(2,1)S(1)} %get-tuple-element.44.refs_7_.refs_6_) | copy-start | bytes 393220
  48.5 8.2 %copy-start.2 = (bf16[2,128,128]{2,1,0:T(8,128)(2,1)}, bf16[2,128,128]{2,1,0:T(8,128)(2,1)S(1)}, u32[]{:S(2)}) copy-start(bf16[2,128,128]{2,1,0:T(8,128)(2,1)S(1)} %get-tuple-element.46.refs_9_.refs_8_) | copy-start | bytes 196612
  48.5 8.2 %copy-start.4 = (f32[128,128]{1,0:T(8,128)}, f32[128,128]{1,0:T(8,128)S(1)}, u32[]{:S(2)}) copy-start(f32[128,128]{1,0:T(8,128)S(1)} %get-tuple-element.47.refs_10_.refs_9_) | copy-start | bytes 196612
  48.6 13.0 %copy-start.16 = (bf16[64,512]{1,0:T(8,128)(2,1)S(1)}, bf16[64,512]{1,0:T(8,128)(2,1)}, u32[]{:S(2)}) copy-start(bf16[64,512]{1,0:T(8,128)(2,1)} %copy-done.15) | copy-start | bytes 196612
  48.6 13.0 %copy-start.18 = (bf16[64,512]{1,0:T(8,128)(2,1)S(1)}, bf16[64,512]{1,0:T(8,128)(2,1)}, u32[]{:S(2)}) copy-start(bf16[64,512]{1,0:T(8,128)(2,1)} %copy-done.17) | copy-start | bytes 196612
  48.6 13.0 %copy-start.20 = (bf16[64,512]{1,0:T(8,128)(2,1)S(1)}, bf16[64,512]{1,0:T(8,128)(2,1)}, u32[]{:S(2)}) copy-start(bf16[64,512]{1,0:T(8,128)(2,1)} %copy-done.19) | copy-start | bytes 196612
  56.7 0.8 copy-start.6
  57.4 8.0 %collective-permute-start.3 = (bf16[128,1280]{1,0:T(8,128)(2,1)}, bf16[128,1280]{1,0:T(8,128)(2,1)}, u32[]{:S(2)}, u32[]{:S(2)}) collective-permute-start(bf16[128,1280]{1,0:T(8,128)(2,1)} %get-tuple-element.49), channel_id=1, source_target_pairs={{24,26},{26,28},{28,30},{30,24},{25,27},{27,29},{29,31},{31,25}} | collective-permute-start | bytes 983048 | tf_op jit(solution)/shard_map/ppermute | solution.py:622
  58.8 6.6 %collective-permute-start.4 = (bf16[128,1280]{1,0:T(8,128)(2,1)}, bf16[128,1280]{1,0:T(8,128)(2,1)}, u32[]{:S(2)}, u32[]{:S(2)}) collective-permute-start(bf16[128,1280]{1,0:T(8,128)(2,1)} %get-tuple-element.50), channel_id=1, source_target_pairs={{24,28},{26,30},{28,24},{30,26},{25,29},{27,31},{29,25},{31,27}} | collective-permute-start | bytes 983048 | tf_op jit(solution)/shard_map/ppermute | solution.py:622
  60.2 5.3 %collective-permute-start.5 = (bf16[128,1280]{1,0:T(8,128)(2,1)}, bf16[128,1280]{1,0:T(8,128)(2,1)}, u32[]{:S(2)}, u32[]{:S(2)}) collective-permute-start(bf16[128,1280]{1,0:T(8,128)(2,1)} %get-tuple-element.51), channel_id=1, source_target_pairs={{24,30},{26,24},{28,26},{30,28},{25,31},{27,25},{29,27},{31,29}} | collective-permute-start | bytes 983048 | tf_op jit(solution)/shard_map/ppermute | solution.py:622
  64.2 8.1 %copy-start.1 = (bf16[128,512]{1,0:T(8,128)(2,1)S(1)}, bf16[128,512]{1,0:T(8,128)(2,1)}, u32[]{:S(2)}) copy-start(bf16[128,512]{1,0:T(8,128)(2,1)} %copy-done) | copy-start | bytes 393220
  64.2 8.1 %copy-start.3 = (bf16[2,128,128]{2,1,0:T(8,128)(2,1)S(1)}, bf16[2,128,128]{2,1,0:T(8,128)(2,1)}, u32[]{:S(2)}) copy-start(bf16[2,128,128]{2,1,0:T(8,128)(2,1)} %copy-done.2) | copy-start | bytes 196612
  64.2 8.1 %copy-start.5 = (f32[128,128]{1,0:T(8,128)S(1)}, f32[128,128]{1,0:T(8,128)}, u32[]{:S(2)}) copy-start(f32[128,128]{1,0:T(8,128)} %copy-done.4) | copy-start | bytes 196612
  65.5 1.0 copy-start.7
  69.5 9.0 %copy-start.8 = (bf16[128,1024]{1,0:T(8,128)(2,1)}, bf16[128,1024]{1,0:T(8,128)(2,1)S(1)}, u32[]{:S(2)}) copy-start(bf16[128,1024]{1,0:T(8,128)(2,1)S(1)} %get-tuple-element.78) | copy-start | bytes 786436
  69.5 2.7 %collective-permute-start.15 = (bf16[128,256]{1,0:T(8,128)(2,1)S(1)}, bf16[128,256]{1,0:T(8,128)(2,1)S(1)}, u32[]{:S(2)}, u32[]{:S(2)}) collective-permute-start(bf16[128,256]{1,0:T(8,128)(2,1)S(1)} %get-tuple-element.52), channel_id=1, source_target_pairs={{24,16},{26,18},{28,20},{30,22},{25,17},{27,19},{29,21},{31,23}} | collective-permute-start | bytes 196616 | tf_op jit(solution)/shard_map/ppermute | solution.py:645
  70.2 2.0 collective-permute-start.16
  70.9 1.4 collective-permute-start.17
  71.5 0.7 collective-permute-start.18
  76.5 2.1 collective-permute-start.19
  77.2 1.4 collective-permute-start.20
  77.8 0.7 collective-permute-start.21
  80.4 0.7 copy-start.10
  81.1 2.9 %collective-permute-start.22 = (bf16[128,256]{1,0:T(8,128)(2,1)S(1)}, bf16[128,256]{1,0:T(8,128)(2,1)S(1)}, u32[]{:S(2)}, u32[]{:S(2)}) collective-permute-start(bf16[128,256]{1,0:T(8,128)(2,1)S(1)} %get-tuple-element.60), channel_id=1, source_target_pairs={{16,8},{18,10},{20,12},{22,14},{17,9},{19,11},{21,13},{23,15}} | collective-permute-start | bytes 196616 | tf_op jit(solution)/shard_map/ppermute | solution.py:645
  81.8 2.2 collective-permute-start.23
  82.5 1.5 collective-permute-start.24
  83.1 0.9 collective-permute-start.25
  88.2 2.1 collective-permute-start.26
  88.9 1.4 collective-permute-start.27
  89.6 0.7 collective-permute-start.28
  92.1 126.9 %copy-start.12 = (bf16[128,1024]{1,0:T(8,128)(2,1)}, bf16[128,1024]{1,0:T(8,128)(2,1)S(1)}, u32[]{:S(2)}) copy-start(bf16[128,1024]{1,0:T(8,128)(2,1)S(1)} %get-tuple-element.76) | copy-start | bytes 786436
  92.2 154.7 %copy-start.9 = (bf16[128,1024]{1,0:T(8,128)(2,1)S(1)}, bf16[128,1024]{1,0:T(8,128)(2,1)}, u32[]{:S(2)}) copy-start(bf16[128,1024]{1,0:T(8,128)(2,1)} %copy-done.8) | copy-start | bytes 786436
  92.2 154.7 %copy-start.11 = (bf16[128,1024]{1,0:T(8,128)(2,1)S(1)}, bf16[128,1024]{1,0:T(8,128)(2,1)}, u32[]{:S(2)}) copy-start(bf16[128,1024]{1,0:T(8,128)(2,1)} %copy-done.10) | copy-start | bytes 786436
  92.2 112.7 %collective-permute-start.29 = (bf16[128,256]{1,0:T(8,128)(2,1)S(1)}, bf16[128,256]{1,0:T(8,128)(2,1)S(1)}, u32[]{:S(2)}, u32[]{:S(2)}) collective-permute-start(bf16[128,256]{1,0:T(8,128)(2,1)S(1)} %get-tuple-element.68), channel_id=1, source_target_pairs={{8,0},{10,2},{12,4},{14,6},{9,1},{11,3},{13,5},{15,7}} | collective-permute-start | bytes 196616 | tf_op jit(solution)/shard_map/ppermute | solution.py:645
  93.6 111.2 %collective-permute-start.30 = (bf16[128,256]{1,0:T(8,128)(2,1)S(1)}, bf16[128,256]{1,0:T(8,128)(2,1)S(1)}, u32[]{:S(2)}, u32[]{:S(2)}) collective-permute-start(bf16[128,256]{1,0:T(8,128)(2,1)S(1)} %get-tuple-element.69), channel_id=1, source_target_pairs={{8,6},{10,0},{12,2},{14,4},{9,7},{11,1},{13,3},{15,5}} | collective-permute-start | bytes 196616 | tf_op jit(solution)/shard_map/ppermute | solution.py:645
  94.9 109.9 %collective-permute-start.31 = (bf16[128,256]{1,0:T(8,128)(2,1)S(1)}, bf16[128,256]{1,0:T(8,128)(2,1)S(1)}, u32[]{:S(2)}, u32[]{:S(2)}) collective-permute-start(bf16[128,256]{1,0:T(8,128)(2,1)S(1)} %get-tuple-element.70), channel_id=1, source_target_pairs={{8,4},{10,6},{12,0},{14,2},{9,5},{11,7},{13,1},{15,3}} | collective-permute-start | bytes 196616 | tf_op jit(solution)/shard_map/ppermute | solution.py:645
  96.2 108.6 %collective-permute-start.32 = (bf16[128,256]{1,0:T(8,128)(2,1)S(1)}, bf16[128,256]{1,0:T(8,128)(2,1)S(1)}, u32[]{:S(2)}, u32[]{:S(2)}) collective-permute-start(bf16[128,256]{1,0:T(8,128)(2,1)S(1)} %get-tuple-element.71), channel_id=1, source_target_pairs={{8,2},{10,4},{12,6},{14,0},{9,3},{11,5},{13,7},{15,1}} | collective-permute-start | bytes 196616 | tf_op jit(solution)/shard_map/ppermute | solution.py:645
  209.7 12.8 %collective-permute-start.33 = (bf16[128,1280]{1,0:T(8,128)(2,1)}, bf16[128,1280]{1,0:T(8,128)(2,1)S(1)}, u32[]{:S(2)}, u32[]{:S(2)}) collective-permute-start(bf16[128,1280]{1,0:T(8,128)(2,1)} %get-tuple-element.73), channel_id=1, source_target_pairs={{0,2},{2,4},{4,6},{6,0},{1,3},{3,5},{5,7},{7,1}} | collective-permute-start | bytes 983048 | tf_op jit(solution)/shard_map/ppermute | solution.py:622
  214.5 27.5 %collective-permute-start.34 = (bf16[128,1280]{1,0:T(8,128)(2,1)}, bf16[128,1280]{1,0:T(8,128)(2,1)S(1)}, u32[]{:S(2)}, u32[]{:S(2)}) collective-permute-start(bf16[128,1280]{1,0:T(8,128)(2,1)} %get-tuple-element.74), channel_id=1, source_target_pairs={{0,4},{2,6},{4,0},{6,2},{1,5},{3,7},{5,1},{7,3}} | collective-permute-start | bytes 983048 | tf_op jit(solution)/shard_map/ppermute | solution.py:622
  219.1 27.5 %collective-permute-start.35 = (bf16[128,1280]{1,0:T(8,128)(2,1)}, bf16[128,1280]{1,0:T(8,128)(2,1)S(1)}, u32[]{:S(2)}, u32[]{:S(2)}) collective-permute-start(bf16[128,1280]{1,0:T(8,128)(2,1)} %get-tuple-element.75), channel_id=1, source_target_pairs={{0,6},{2,0},{4,2},{6,4},{1,7},{3,1},{5,3},{7,5}} | collective-permute-start | bytes 983048 | tf_op jit(solution)/shard_map/ppermute | solution.py:622

commit v2 on v1

--- a/solution.py
+++ b/solution.py
@@ -389,24 +389,34 @@
     return main, conv_taps_back(d_state, taps_state_ref[...]).astype(BF16)
 
 
-def section_kernel(heads, chunks, first, *refs):
-    count = chunks
-    incoming = refs[:count]
-    refs = refs[count:]
-    out_rows_ref = None
-    if first:
-        out_rows_ref, refs = refs[0], refs[1:]
+def first_kernel(heads, chunks, *refs):
+    incoming, refs = refs[:chunks], refs[chunks:]
+    out_rows_ref, refs = refs[0], refs[1:]
     residuals, refs = refs[:9], refs[9:]
     cols_ref, refs = refs[0], refs[1:]
     outs, refs = refs[:chunks], refs[chunks:]
-    cols, cols_sems = refs[0], refs[1]
+    cols, cols_sems, rows, rows_sem = refs
+    me = lax.axis_index("tensor")
+    width = cols.shape[1]
+    rows_copy = pltpu.make_async_copy(out_rows_ref, rows, rows_sem)
+    rows_copy.start()
+    copies = start_cols(chunks, cols_ref, cols, cols_sems)
+    rows_copy.wait()
+    dnormed = None
+    for hop in range(chunks):
+        chunk = lax.rem(me + chunks - hop, chunks)
+        term = dot_nt(
+            incoming[hop][...], rows[:, pl.ds(pl.multiple_of(chunk * width, width), width)]
+        )
+        dnormed = term if dnormed is None else dnormed + term
+    main, state = mixer_back(heads, dnormed, residuals)
+    project(chunks, main, state, copies, cols, outs)
+
+
+def start_cols(chunks, cols_ref, cols, cols_sems):
     me = lax.axis_index("tensor")
     width = cols.shape[1]
     copies = []
-    if first:
-        rows, rows_sem = refs[2], refs[3]
-        rows_copy = pltpu.make_async_copy(out_rows_ref, rows, rows_sem)
-        rows_copy.start()
     for hop in range(chunks):
         chunk = lax.rem(me + hop, chunks)
         copy = pltpu.make_async_copy(
@@ -416,24 +426,74 @@
         )
         copy.start()
         copies.append(copy)
-    if first:
-        rows_copy.wait()
-        dnormed = None
-        for hop in range(chunks):
-            chunk = lax.rem(me + chunks - hop, chunks)
-            term = dot_nt(
-                incoming[hop][...], rows[:, pl.ds(pl.multiple_of(chunk * width, width), width)]
-            )
-            dnormed = term if dnormed is None else dnormed + term
-    else:
-        dnormed = incoming[0][...].astype(F32)
-        for hop in range(1, chunks):
-            dnormed = dnormed + incoming[hop][...].astype(F32)
-    main, state = mixer_back(heads, dnormed, residuals)
+    return copies
+
+
+def project(chunks, main, state, copies, cols, outs):
+    width = cols.shape[1]
     for hop in range(chunks):
         copies[hop].wait()
         outs[hop][:, :width] = dot_nt(main, cols[hop]).astype(BF16)
         outs[hop][:, width:] = state
+
+
+def project_kernel(chunks, main_ref, state_ref, cols_ref, *refs):
+    outs, refs = refs[:chunks], refs[chunks:]
+    cols, cols_sems = refs
+    copies = start_cols(chunks, cols_ref, cols, cols_sems)
+    project(chunks, main_ref[...], state_ref[...], copies, cols, outs)
+
+
+def next_kernel(heads, chunks, *refs):
+    incoming, refs = refs[:chunks], refs[chunks:]
+    residuals, refs = refs[:9], refs[9:]
+    main_ref, state_ref = refs
+    dnormed = incoming[0][...].astype(F32)
+    for hop in range(1, chunks):
+        dnormed = dnormed + incoming[hop][...].astype(F32)
+    main, state = mixer_back(heads, dnormed, residuals)
+    main_ref[...] = main
+    state_ref[...] = state
+
+
+def compose_kernel(chunks, *refs):
+    rows, refs = refs[:chunks], refs[chunks:]
+    cols_ref, state_cols_ref, main_ref, state_ref, main_sum, state_sum = refs
+    step = pl.program_id(0)
+
+    @pl.when(step == 0)
+    def _():
+        main_sum[...] = jnp.zeros_like(main_sum)
+        state_sum[...] = jnp.zeros_like(state_sum)
+
+    size = rows[0].shape[0]
+    for hop in range(chunks):
+        place = pl.ds(hop * size, size)
+        main_sum[place, :] += dot_nn(rows[hop][...], cols_ref[...])
+        state_sum[:, place] += dot_nt(state_cols_ref[...], rows[hop][...])
+
+    @pl.when(step == pl.num_programs(0) - 1)
+    def _():
+        main_ref[...] = main_sum[...].astype(BF16)
+        state_ref[...] = state_sum[...].astype(BF16)
+
+
+def send_kernel(
+    chunks, main_ref, state_ref, main_own_ref, main_other_ref, state_own_ref, state_other_ref, *outs
+):
+    core = lax.axis_index("dp")
+    size = main_own_ref.shape[0] // chunks
+    main = main_ref[...]
+    state = state_ref[...]
+    for main_map, state_map, place in (
+        (main_own_ref, state_own_ref, core),
+        (main_other_ref, state_other_ref, 1 - core),
+    ):
+        product = dot_nt(main, main_map[...]) + dot_nn(state, state_map[...])
+        product = product.astype(BF16)
+        lanes = pl.ds(pl.multiple_of(place * size, size), size)
+        for hop in range(chunks):
+            outs[hop][:, lanes] = product[:, hop * size : (hop + 1) * size]
 
 
 def carry_kernel(chunks, last, *refs):
@@ -469,6 +529,19 @@
                 outs[hop][:, lanes] = product[:, hop * half : (hop + 1) * half]
 
 
+SWAP = [(0, 1), (1, 0)]
+
+
+def after(value, dependency):
+    return lax.optimization_barrier((value, dependency))[0]
+
+
+def by_member(pieces, order):
+    count, _, width = pieces.shape
+    pieces = jnp.take(pieces, order, axis=0).reshape(count, 2, -1, width)
+    return pieces.transpose(1, 0, 2, 3).reshape(-1, width)
+
+
 def kernel_params():
     return pltpu.CompilerParams(vmem_limit_bytes=VMEM_BYTES)
 
@@ -513,47 +586,18 @@
     half_width = width // 2
     place = ("pipe", "tensor")
 
-    last_own = jnp.where(section == sections - 1, output_grad, jnp.zeros_like(output_grad))
-    incoming = [last_own]
+    incoming = [jnp.where(section == sections - 1, output_grad, jnp.zeros_like(output_grad))]
     for hop in range(1, chunks):
         pairs = section_pairs(sections, chunks, sections - 1, sections - 1, hop)
         incoming.append(lax.ppermute(output_grad, place, pairs))
 
-    own_half = []
+    out_half = lax.dynamic_slice_in_dim(weight_out[0], core * half_rows, half_rows, 0)
+    gathered_rows = []
     for hop in range(chunks):
-        chunk = (me + hop) % chunks
-        piece = lax.dynamic_slice(
-            weight_out[0], (core * half_rows, chunk * width), (half_rows, width)
-        )
         pairs = []
-        for source in range(sections - 1):
+        for source in range(sections - 2):
             pairs += section_pairs(sections, chunks, source, source + 1, hop)
-        own_half.append(lax.ppermute(piece, place, pairs))
-    own_half = jnp.concatenate(own_half, axis=0)
-    other_half = lax.ppermute(own_half, "dp", [(0, 1), (1, 0)])
-
-    state_cols = weight_state[0].reshape(model_width, -1).T
-    pieces = []
-    for hop in range(chunks):
-        chunk = (me + hop) % chunks
-        piece = lax.dynamic_slice(
-            state_cols,
-            (0, chunk * width + core * half_width),
-            (state_cols.shape[0], half_width),
-        )
-        if hop:
-            pairs = [(index, (index + hop) % chunks) for index in range(chunks)]
-            piece = lax.ppermute(piece, "tensor", pairs)
-        pieces.append(piece)
-    state_own = jnp.stack(pieces)
-    state_other = lax.ppermute(state_own, "dp", [(0, 1), (1, 0)])
-    lower = jnp.where(core == 0, state_own, state_other)
-    upper = jnp.where(core == 0, state_other, state_own)
-    state_rows = jnp.concatenate([lower, upper], axis=2)
-    order = (me - jnp.arange(chunks)) % chunks
-    state_rows = jnp.take(state_rows, order, axis=0)
-    state_rows = state_rows.reshape(chunks, 2, -1, width).transpose(1, 0, 2, 3)
-    state_rows = state_rows.reshape(-1, width)
+        gathered_rows.append(lax.ppermute(out_half, place, pairs))
 
     step_cols = jnp.pad(weight_step[0].T, ((0, 0), (0, 128 - heads)))
     cols = jnp.concatenate([weight_main[0].reshape(model_width, -1), step_cols], axis=1)
@@ -594,33 +638,65 @@
     residuals = tuple(residuals) + (taps_main, taps_state, by_head)
     message = jax.ShapeDtypeStruct((length, width + state_width), BF16)
     slice_out = jax.ShapeDtypeStruct((length, channels), BF16)
+    carry_shape = jax.ShapeDtypeStruct((length, width), BF16)
+    main_shape = jax.ShapeDtypeStruct((length, cols.shape[1]), BF16)
+    state_shape = jax.ShapeDtypeStruct((length, state_width), BF16)
     hbm = pl.BlockSpec(memory_space=pl.ANY)
 
-    result = jnp.zeros((length, width), BF16)
-    for moment in range(sections):
-        active = sections - 1 - moment
-        first = moment == 0
-        last = moment + 1 == sections
-        scratch = [
-            pltpu.VMEM((chunks, width, cols.shape[1]), BF16),
-            pltpu.SemaphoreType.DMA((chunks,)),
-        ]
-        if first:
-            scratch += [pltpu.VMEM((channels, model_width), BF16), pltpu.SemaphoreType.DMA]
-        parts = pl.pallas_call(
-            lambda *refs, first=first: section_kernel(heads, chunks, first, *refs),
-            out_shape=(message,) * chunks,
-            in_specs=whole(chunks) + [hbm] * first + whole(9) + [hbm],
-            out_specs=whole(chunks),
-            scratch_shapes=scratch,
-            compiler_params=kernel_params(),
-            name="section_first" if first else "section_next",
-        )(*incoming, *((weight_out[0],) if first else ()), *residuals, cols)
-        gathered = [parts[0]]
-        for hop in range(1, chunks):
-            pairs = section_pairs(sections, chunks, active, active, hop)
-            gathered.append(lax.ppermute(parts[hop], place, pairs))
-        carry_shape = jax.ShapeDtypeStruct((length, width), BF16)
+    incoming[1:] = lax.optimization_barrier(tuple(incoming[1:]))
+    weight_late = after(weight_out[0], incoming[1])
+    own_half = []
+    for hop in range(chunks):
+        chunk = (me + hop) % chunks
+        piece = lax.dynamic_slice(
+            weight_late, (core * half_rows, chunk * width), (half_rows, width)
+        )
+        pairs = section_pairs(sections, chunks, sections - 2, sections - 1, hop)
+        own_half.append(lax.ppermute(piece, place, pairs))
+
+    cols_scratch = [
+        pltpu.VMEM((chunks, width, cols.shape[1]), BF16),
+        pltpu.SemaphoreType.DMA((chunks,)),
+    ]
+    parts = pl.pallas_call(
+        lambda *refs: first_kernel(heads, chunks, *refs),
+        out_shape=(message,) * chunks,
+        in_specs=whole(chunks) + [hbm] + whole(9) + [hbm],
+        out_specs=whole(chunks),
+        scratch_shapes=cols_scratch
+        + [pltpu.VMEM((channels, model_width), BF16), pltpu.SemaphoreType.DMA],
+        compiler_params=kernel_params(),
+        name="section_first",
+    )(*incoming, weight_out[0], *residuals, cols)
+    exchanged = [parts[0]]
+    for hop in range(1, chunks):
+        pairs = section_pairs(sections, chunks, sections - 1, sections - 1, hop)
+        exchanged.append(lax.ppermute(parts[hop], place, pairs))
+
+    state_cols = weight_state[0].reshape(model_width, -1).T
+    state_late = after(state_cols, parts[0])
+    pieces = []
+    for hop in range(chunks):
+        chunk = (me + hop) % chunks
+        piece = lax.dynamic_slice(
+            state_late,
+            (0, chunk * width + core * half_width),
+            (state_cols.shape[0], half_width),
+        )
+        if hop:
+            pairs = [(index, (index + hop) % chunks) for index in range(chunks)]
+            piece = lax.ppermute(piece, "tensor", pairs)
+        pieces.append(piece)
+    own_half = jnp.concatenate(own_half, axis=0)
+    other_half = lax.ppermute(own_half, "dp", SWAP)
+    state_own = jnp.stack(pieces)
+    state_other = lax.ppermute(state_own, "dp", SWAP)
+    lower = jnp.where(core == 0, state_own, state_other)
+    upper = jnp.where(core == 0, state_other, state_own)
+    order = (me - jnp.arange(chunks)) % chunks
+    state_rows = by_member(jnp.concatenate([lower, upper], axis=2), order)
+
+    def carry_call(last, *operands):
         scratch = []
         if not last:
             scratch = [
@@ -628,22 +704,114 @@
                 pltpu.VMEM(own_half.shape, BF16),
                 pltpu.SemaphoreType.DMA((2,)),
             ]
-        outs = pl.pallas_call(
-            lambda *refs, last=last: carry_kernel(chunks, last, *refs),
+        return pl.pallas_call(
+            lambda *refs: carry_kernel(chunks, last, *refs),
             out_shape=(carry_shape,) + (() if last else (slice_out,) * chunks),
             in_specs=whole(chunks + 1) + ([] if last else [hbm] * 2),
             out_specs=whole(1 if last else 1 + chunks),
             scratch_shapes=scratch,
             compiler_params=kernel_params(),
             name="carry_last" if last else "carry_next",
-        )(*gathered, state_rows, *(() if last else (own_half, other_half)))
-        result = jnp.where(section == active, outs[0], result)
-        if not last:
-            incoming = []
-            for hop in range(chunks):
-                pairs = section_pairs(sections, chunks, active, active - 1, chunks - hop)
-                incoming.append(lax.ppermute(outs[1 + hop], place, pairs))
-    return result[None]
+        )(*operands)
+
+    def pass_back(messages, active):
+        moved = []
+        for hop in range(chunks):
+            pairs = section_pairs(sections, chunks, active, active - 1, chunks - hop)
+            moved.append(lax.ppermute(messages[hop], place, pairs))
+        return moved
+
+    carry, *messages = carry_call(False, *exchanged, state_rows, own_half, other_half)
+    result = carry
+    incoming = pass_back(messages, sections - 1)
+
+    kept = None
+    composed = None
+    for active in range(sections - 2, -1, -1):
+        main, state = pl.pallas_call(
+            lambda *refs: next_kernel(heads, chunks, *refs),
+            out_shape=(main_shape, state_shape),
+            in_specs=whole(chunks + 9),
+            out_specs=whole(2),
+            compiler_params=kernel_params(),
+            name="section_next",
+        )(*incoming, *residuals)
+        if kept is None:
+            kept = (main, state)
+        else:
+            kept = tuple(
+                jnp.where(section == active, new, old) for new, old in zip((main, state), kept)
+            )
+        if active == 0:
+            break
+        if composed is None:
+            depth = model_width // 8
+            total = chunks * half_rows
+            late_rows = after(tuple(gathered_rows), main)
+            main_map, state_map = pl.pallas_call(
+                lambda *refs: compose_kernel(chunks, *refs),
+                grid=(8,),
+                out_shape=(
+                    jax.ShapeDtypeStruct((total, cols.shape[1]), BF16),
+                    jax.ShapeDtypeStruct((state_cols.shape[0], total), BF16),
+                ),
+                in_specs=[pl.BlockSpec((half_rows, depth), lambda step: (0, step))] * chunks
+                + [
+                    pl.BlockSpec((depth, cols.shape[1]), lambda step: (step, 0)),
+                    pl.BlockSpec((state_cols.shape[0], depth), lambda step: (0, step)),
+                ],
+                out_specs=[
+                    pl.BlockSpec((total, cols.shape[1]), lambda step: (0, 0)),
+                    pl.BlockSpec((state_cols.shape[0], total), lambda step: (0, 0)),
+                ],
+                scratch_shapes=[
+                    pltpu.VMEM((total, cols.shape[1]), F32),
+                    pltpu.VMEM((state_cols.shape[0], total), F32),
+                ],
+                compiler_params=kernel_params(),
+                name="compose_weights",
+            )(*late_rows, cols, state_cols)
+            shared = [state_map]
+            for hop in range(1, chunks):
+                pairs = []
+                for target in range(1, sections - 1):
+                    pairs += section_pairs(sections, chunks, target, target, hop)
+                moved = lax.ppermute(state_map, place, pairs)
+                shared.append(jnp.roll(moved, hop * half_rows, axis=1))
+            state_map = by_member(jnp.stack(shared), order)
+            composed = (
+                main_map,
+                lax.ppermute(main_map, "dp", SWAP),
+                state_map,
+                lax.ppermute(state_map, "dp", SWAP),
+            )
+        messages = pl.pallas_call(
+            lambda *refs: send_kernel(chunks, *refs),
+            out_shape=(slice_out,) * chunks,
+            in_specs=whole(6),
+            out_specs=whole(chunks),
+            compiler_params=kernel_params(),
+            name="send_back",
+        )(main, state, *composed)
+        incoming = pass_back(messages, active)
+
+    parts = pl.pallas_call(
+        lambda *refs: project_kernel(chunks, *refs),
+        out_shape=(message,) * chunks,
+        in_specs=whole(2) + [hbm],
+        out_specs=whole(chunks),
+        scratch_shapes=cols_scratch,
+        compiler_params=kernel_params(),
+        name="project",
+    )(*kept, cols)
+    exchanged = [parts[0]]
+    for hop in range(1, chunks):
+        pairs = []
+        for source in range(sections - 1):
+            pairs += section_pairs(sections, chunks, source, source, hop)
+        exchanged.append(lax.ppermute(parts[hop], place, pairs))
+    carry = carry_call(True, *exchanged, state_rows)[0]
+    return jnp.where(section == sections - 1, result, carry)[None]
 
 
 def solution(mesh):

time: 249 us -> 271 us (1.088)
  the two profiles are of different devices: /device:TPU:9 before, /device:TPU:11 now
where the time goes in v2:
time: 271 us; the launch traced here: 266 us
  waiting for transfers between devices  111 us (41%)
  starting transfers between devices  93.1 us (34%)
  Pallas kernels  29.6 us (11%)
  local copies, waits for them, and re-layouts  21.1 us (8%)
  other arithmetic  10.2 us (4%)
    ppermute x4, waiting for transfers between devices, relay_body(): gathered_rows.append(lax.ppermute(out_half, place, pairs))  70.7 us
    ppermute x4, starting transfers between devices, relay_body(): gathered_rows.append(lax.ppermute(out_half, place, pairs))  43.5 us
    ppermute x6, waiting for transfers between devices, relay_body(): exchanged.append(lax.ppermute(parts[hop], place, pairs))  25.4 us
    unnamed x48, local copies, waits for them, and re-layouts  13.3 us
    ppermute x12, starting transfers between devices, pass_back(): moved.append(lax.ppermute(messages[hop], place, pairs))  13.2 us
    ppermute x12, waiting for transfers between devices, pass_back(): moved.append(lax.ppermute(messages[hop], place, pairs))  12.7 us
    ppermute x3, starting transfers between devices, relay_body(): moved = lax.ppermute(state_map, place, pairs)  12 us
    ppermute x6, starting transfers between devices, relay_body(): exchanged.append(lax.ppermute(parts[hop], place, pairs))  9.89 us
  transfers between devices with their start and end apart: 39, of which 14 were waited for; matrix products, arithmetic and copies ran while one was open for 9% of the time, Pallas kernels for 2%

profile of v2, /device:TPU:11, one launch (start us, length us, event | category | flops | bytes accessed | tf_op | source)
XLA Modules:
  0.0 266.3 jit_solution(10036370123993904199)
XLA Ops:
  2.0 1.2 fusion.6
  3.3 0.8 copy.17
  4.1 1.3 copy.18
  5.4 2.9 %copy.25 = bf16[512,8,2,256]{3,1,2,0:T(8,128)(2,1)S(1)} copy(bf16[512,8,2,256]{3,2,1,0:T(2,128)(2,1)} %bitcast.77) | data formatting | bytes 8388608
  8.4 3.0 %fusion.1.refs_14_.refs_4_.refs_2_ = bf16[4096,640]{1,0:T(8,128)(2,1)} fusion(bf16[4096,4]{1,0:T(8,128)(2,1)S(1)} %bitcast.76, bf16[4096,512]{1,0:T(8,128)(2,1)S(1)} %bitcast.73), kind=kLoop, calls=%fused_computation.4 | loop fusion | flops 15728640 | bytes 9469952 | tf_op jit(solution)/shard_map/concatenate | solution.py:603
  11.6 1.2 forward_residuals.1
  12.9 6.3 %section_first.1 = (bf16[128,1280]{1,0:T(8,128)(2,1)S(1)}, bf16[128,1280]{1,0:T(8,128)(2,1)S(1)}, bf16[128,1280]{1,0:T(8,128)(2,1)S(1)}, bf16[128,1280]{1,0:T(8,128)(2,1)S(1)}) custom-call(bf16[128,1024]{1,0:T(8,128)(2,1)S(1)} %broadcast_select_fusion.2.refs_0_, bf16[128,1024]{1,0:T(8,128)(2,1)S(1)} %collective-permute-done.refs_1_, ...), custom_call_target="tpu_custom_call" | custom-call | tf_op jit(solution)/shard_map/section_first/pallas_call | solution.py:661
  20.3 2.3 collective-permute-start.7
  22.6 2.2 collective-permute-start.6
  26.9 1.3 collective-permute-done.6
  31.7 1.3 collective-permute-start.9
  33.0 0.7 constant_dynamic-update-slice_fusion.1
  34.5 1.1 dynamic-slice_bitcast_fusion
  35.6 37.8 %collective-permute-start.19 = (bf16[128,4096]{1,0:T(8,128)(2,1)}, bf16[128,4096]{1,0:T(8,128)(2,1)}, u32[]{:S(2)}, u32[]{:S(2)}) collective-permute-start(bf16[128,4096]{1,0:T(8,128)(2,1)} %dynamic-slice_bitcast_fusion), channel_id=1, source_target_pairs={{0,8},{2,10},{4,12},{6,14},{8,16},{10,18},{12,20},{14,22},{1,9},{3... | collective-permute-start | bytes 3145736 | tf_op jit(solution)/shard_map/ppermute | solution.py:600
  73.5 1.9 collective-permute-start.20
  76.1 1.9 collective-permute-start.21
  78.8 1.9 collective-permute-start.22
  81.3 1.0 broadcast_select_fusion.1
  82.3 0.9 pad_maximum_fusion
  83.2 2.4 gather_fusion
  85.6 1.2 copy_select_fusion
  86.8 1.0 copy-done.6
  87.7 1.0 copy-done.8
  88.7 2.2 carry_next.1
  93.7 0.7 section_next.3
  95.1 45.6 %collective-permute-done.19.refs_0_ = bf16[128,4096]{1,0:T(8,128)(2,1)} collective-permute-done((bf16[128,4096]{1,0:T(8,128)(2,1)}, bf16[128,4096]{1,0:T(8,128)(2,1)}, u32[]{:S(2)}, u32[]{:S(2)}) %collective-permute-start.19) | collective-permute-done | bytes 1048608 | tf_op jit(solution)/shard_map/ppermute | solution.py:600
  140.7 24.5 %collective-permute-done.21.refs_2_ = bf16[128,4096]{1,0:T(8,128)(2,1)} collective-permute-done((bf16[128,4096]{1,0:T(8,128)(2,1)}, bf16[128,4096]{1,0:T(8,128)(2,1)}, u32[]{:S(2)}, u32[]{:S(2)}) %collective-permute-start.21) | collective-permute-done | bytes 1048608 | tf_op jit(solution)/shard_map/ppermute | solution.py:600
  165.8 1.0 copy-done.1
  166.8 9.6 %compose_weights.1 = (bf16[512,640]{1,0:T(8,128)(2,1)S(1)}, bf16[64,512]{1,0:T(8,128)(2,1)S(1)}) custom-call(bf16[128,4096]{1,0:T(8,128)(2,1)} %collective-permute-done.19.refs_0_, bf16[128,4096]{1,0:T(8,128)(2,1)} %collective-permute-done.20.refs_1_, bf16[128,4096]{1,0:T(8,128)(2,1)} %collective-permute-done.21.refs_2_, ...), custom_call_target="tpu_custom_call" | custom-call | tf_op jit(solution)/shard_map/compose_weights/pallas_call | solution.py:751
  176.4 1.9 collective-permute-start.26
  178.4 5.8 %collective-permute-start.25 = (bf16[64,512]{1,0:T(8,128)(2,1)S(1)}, bf16[64,512]{1,0:T(8,128)(2,1)S(1)}, u32[]{:S(2)}, u32[]{:S(2)}) collective-permute-start(bf16[64,512]{1,0:T(8,128)(2,1)S(1)} %get-tuple-element.76), channel_id=1, source_target_pairs={{8,12},{10,14},{12,8},{14,10},{16,20},{18,22},{20,16},{22,18},{9,1... | collective-permute-start | bytes 196616 | tf_op jit(solution)/shard_map/ppermute | solution.py:779
  184.2 4.3 %collective-permute-start.24 = (bf16[64,512]{1,0:T(8,128)(2,1)S(1)}, bf16[64,512]{1,0:T(8,128)(2,1)S(1)}, u32[]{:S(2)}, u32[]{:S(2)}) collective-permute-start(bf16[64,512]{1,0:T(8,128)(2,1)S(1)} %get-tuple-element.76), channel_id=1, source_target_pairs={{8,10},{10,12},{12,14},{14,8},{16,18},{18,20},{20,22},{22,16},{9,1... | collective-permute-start | bytes 196616 | tf_op jit(solution)/shard_map/ppermute | solution.py:779
  188.4 2.0 collective-permute-start.23
  190.6 0.7 pad_maximum_fusion.2
  191.3 2.2 gather_fusion.1
  193.5 1.0 copy_select_fusion.1
  194.6 1.8 collective-permute-start.27
  196.4 1.2 collective-permute-done.27.refs_5_
  197.5 0.9 copy-done.3
  198.5 1.7 send_back.2
  200.2 1.3 collective-permute-start.28
  201.5 1.3 collective-permute-start.29
  202.8 1.3 collective-permute-start.30
  204.1 1.5 collective-permute-start.31
  206.1 3.1 %collective-permute-done.29.refs_1_ = bf16[128,256]{1,0:T(8,128)(2,1)S(1)} collective-permute-done((bf16[128,256]{1,0:T(8,128)(2,1)S(1)}, bf16[128,256]{1,0:T(8,128)(2,1)S(1)}, u32[]{:S(2)}, u32[]{:S(2)}) %collective-permute-start.29) | collective-permute-done | bytes 65568 | tf_op jit(solution)/shard_map/ppermute | solution.py:721
  209.2 2.9 %collective-permute-done.30.refs_2_ = bf16[128,256]{1,0:T(8,128)(2,1)S(1)} collective-permute-done((bf16[128,256]{1,0:T(8,128)(2,1)S(1)}, bf16[128,256]{1,0:T(8,128)(2,1)S(1)}, u32[]{:S(2)}, u32[]{:S(2)}) %collective-permute-start.30) | collective-permute-done | bytes 65568 | tf_op jit(solution)/shard_map/ppermute | solution.py:721
  212.1 1.3 collective-permute-done.31.refs_3_
  213.4 0.7 section_next.4
  214.1 2.5 send_back.3
  216.6 1.3 collective-permute-start.32
  217.9 1.3 collective-permute-start.33
  219.2 1.3 collective-permute-start.34
  220.5 1.3 collective-permute-start.35
  222.1 4.6 %collective-permute-done.35.refs_3_ = bf16[128,256]{1,0:T(8,128)(2,1)S(1)} collective-permute-done((bf16[128,256]{1,0:T(8,128)(2,1)}, bf16[128,256]{1,0:T(8,128)(2,1)S(1)}, u32[]{:S(2)}, u32[]{:S(2)}) %collective-permute-start.35) | collective-permute-done | bytes 65568 | tf_op jit(solution)/shard_map/ppermute | solution.py:721
  226.8 0.7 section_next.5
  227.5 1.0 select_select_fusion.refs_0_
  228.5 3.6 %project.1 = (bf16[128,1280]{1,0:T(8,128)(2,1)S(1)}, bf16[128,1280]{1,0:T(8,128)(2,1)S(1)}, bf16[128,1280]{1,0:T(8,128)(2,1)S(1)}, bf16[128,1280]{1,0:T(8,128)(2,1)S(1)}) custom-call(bf16[128,640]{1,0:T(8,128)(2,1)S(1)} %select_select_fusion.refs_0_, bf16[128,256]{1,0:T(8,128)(2,1)S(1)} %select_select_fusion.1.refs_1_, ...), custom_call_target="tpu_custom_call" | custom-call | tf_op jit(solution)/shard_map/project/pallas_call | solution.py:798
  232.1 2.8 %collective-permute-start.36 = (bf16[128,1280]{1,0:T(8,128)(2,1)S(1)}, bf16[128,1280]{1,0:T(8,128)(2,1)S(1)}, u32[]{:S(2)}, u32[]{:S(2)}) collective-permute-start(bf16[128,1280]{1,0:T(8,128)(2,1)S(1)} %get-tuple-element.90), channel_id=1, source_target_pairs={{0,2},{2,4},{4,6},{6,0},{8,10},{10,12},{12,14},{14,8},{16,18},{18,... | collective-permute-start | bytes 983048 | tf_op jit(solution)/shard_map/ppermute | solution.py:812
  234.9 3.1 %collective-permute-start.37 = (bf16[128,1280]{1,0:T(8,128)(2,1)S(1)}, bf16[128,1280]{1,0:T(8,128)(2,1)S(1)}, u32[]{:S(2)}, u32[]{:S(2)}) collective-permute-start(bf16[128,1280]{1,0:T(8,128)(2,1)S(1)} %get-tuple-element.91), channel_id=1, source_target_pairs={{0,4},{2,6},{4,0},{6,2},{8,12},{10,14},{12,8},{14,10},{16,20},{18,... | collective-permute-start | bytes 983048 | tf_op jit(solution)/shard_map/ppermute | solution.py:812
  238.0 1.9 collective-permute-start.38
  239.9 2.1 collective-permute-done.36.refs_1_
  242.0 20.0 %collective-permute-done.37.refs_2_ = bf16[128,1280]{1,0:T(8,128)(2,1)S(1)} collective-permute-done((bf16[128,1280]{1,0:T(8,128)(2,1)S(1)}, bf16[128,1280]{1,0:T(8,128)(2,1)S(1)}, u32[]{:S(2)}, u32[]{:S(2)}) %collective-permute-start.37) | collective-permute-done | bytes 327712 | tf_op jit(solution)/shard_map/ppermute | solution.py:812
  262.0 3.3 %collective-permute-done.38.refs_3_ = bf16[128,1280]{1,0:T(8,128)(2,1)S(1)} collective-permute-done((bf16[128,1280]{1,0:T(8,128)(2,1)S(1)}, bf16[128,1280]{1,0:T(8,128)(2,1)S(1)}, u32[]{:S(2)}, u32[]{:S(2)}) %collective-permute-start.38) | collective-permute-done | bytes 327712 | tf_op jit(solution)/shard_map/ppermute | solution.py:812
  265.6 0.7 select_bitcast_fusion
  (105 shorter events, 16.6 us)
Async XLA Ops:
  0.0 12.8 %collective-permute-start = (bf16[128,1024]{1,0:T(8,128)(2,1)}, bf16[128,1024]{1,0:T(8,128)(2,1)S(1)}, u32[]{:S(2)}, u32[]{:S(2)}) collective-permute-start(bf16[128,1024]{1,0:T(8,128)(2,1)} %param.27), channel_id=1, source_target_pairs={{24,26},{26,28},{28,30},{30,24},{25,27},{27,29},{29,31},{31,25}} | collective-permute-start | bytes 786440 | tf_op jit(solution)/shard_map/ppermute | solution.py:592
  0.7 12.2 %collective-permute-start.1 = (bf16[128,1024]{1,0:T(8,128)(2,1)}, bf16[128,1024]{1,0:T(8,128)(2,1)S(1)}, u32[]{:S(2)}, u32[]{:S(2)}) collective-permute-start(bf16[128,1024]{1,0:T(8,128)(2,1)} %param.27), channel_id=1, source_target_pairs={{24,28},{26,30},{28,24},{30,26},{25,29},{27,31},{29,25},{31,27}} | collective-permute-start | bytes 786440 | tf_op jit(solution)/shard_map/ppermute | solution.py:592
  1.4 11.5 %collective-permute-start.2 = (bf16[128,1024]{1,0:T(8,128)(2,1)}, bf16[128,1024]{1,0:T(8,128)(2,1)S(1)}, u32[]{:S(2)}, u32[]{:S(2)}) collective-permute-start(bf16[128,1024]{1,0:T(8,128)(2,1)} %param.27), channel_id=1, source_target_pairs={{24,30},{26,24},{28,26},{30,28},{25,31},{27,25},{29,27},{31,29}} | collective-permute-start | bytes 786440 | tf_op jit(solution)/shard_map/ppermute | solution.py:592
  8.3 3.1 %copy-start.17 = (f32[1,4]{1,0:T(1,128)S(1)}, f32[1,4]{1,0:T(1,128)}, u32[]{:S(2)}) copy-start(f32[1,4]{1,0:T(1,128)} %param.22) | copy-start | bytes 52
  8.3 3.1 %copy-start.18 = (f32[1,4]{1,0:T(1,128)S(1)}, f32[1,4]{1,0:T(1,128)}, u32[]{:S(2)}) copy-start(f32[1,4]{1,0:T(1,128)} %param.21) | copy-start | bytes 52
  8.3 3.1 %copy-start.19 = (f32[1,4]{1,0:T(1,128)S(1)}, f32[1,4]{1,0:T(1,128)}, u32[]{:S(2)}) copy-start(f32[1,4]{1,0:T(1,128)} %param.20) | copy-start | bytes 52
  8.3 3.2 %copy-start.15 = (bf16[1,128,2,128]{3,2,1,0:T(2,128)(2,1)S(1)}, bf16[1,128,2,128]{3,2,1,0:T(2,128)(2,1)}, u32[]{:S(2)}) copy-start(bf16[1,128,2,128]{3,2,1,0:T(2,128)(2,1)} %param.25) | copy-start | bytes 196612
  8.4 3.2 %copy-start.16 = (f32[1,4,2,128]{3,2,1,0:T(2,128)S(1)}, f32[1,4,2,128]{3,2,1,0:T(2,128)}, u32[]{:S(2)}) copy-start(f32[1,4,2,128]{3,2,1,0:T(2,128)} %param.19) | copy-start | bytes 12292
  8.4 3.2 %copy-start.11 = (f32[1,4,256]{2,1,0:T(4,128)S(1)}, f32[1,4,256]{2,1,0:T(4,128)}, u32[]{:S(2)}) copy-start(f32[1,4,256]{2,1,0:T(4,128)} %param.18) | copy-start | bytes 12292
  8.4 3.2 %copy-start.12 = (f32[1,256]{1,0:T(1,128)S(1)}, f32[1,256]{1,0:T(1,128)}, u32[]{:S(2)}) copy-start(f32[1,256]{1,0:T(1,128)} %refs_7_.1) | copy-start | bytes 3076
  12.9 6.4 %copy-start.13 = (bf16[1,256,4096]{2,1,0:T(8,128)(2,1)S(1)}, bf16[1,256,4096]{2,1,0:T(8,128)(2,1)}, u32[]{:S(2)}) copy-start(bf16[1,256,4096]{2,1,0:T(8,128)(2,1)} %param.17) | copy-start | bytes 6291460
  12.9 7.2 %copy-start = (bf16[1,4096,2,32]{1,3,2,0:T(8,128)(2,1)S(1)}, bf16[1,4096,2,32]{1,3,2,0:T(8,128)(2,1)}, u32[]{:S(2)}) copy-start(bf16[1,4096,2,32]{1,3,2,0:T(8,128)(2,1)} %param.15) | copy-start | bytes 1572868
  19.4 9.5 %collective-permute-start.10 = (bf16[128,1024]{1,0:T(8,128)(2,1)S(1)}, bf16[128,1024]{1,0:T(8,128)(2,1)S(1)}, u32[]{:S(2)}, u32[]{:S(2)}) collective-permute-start(bf16[128,1024]{1,0:T(8,128)(2,1)S(1)} %get-tuple-element.96), channel_id=1, source_target_pairs={{16,24},{18,26},{20,28},{22,30},{17,25},{19,27},{21,29},{23,31}} | collective-permute-start | bytes 786440 | tf_op jit(solution)/shard_map/ppermute | solution.py:655
  20.1 5.4 %collective-permute-start.8 = (bf16[64,512]{1,0:T(8,128)(2,1)S(1)}, bf16[64,512]{1,0:T(8,128)(2,1)S(1)}, u32[]{:S(2)}, u32[]{:S(2)}) collective-permute-start(bf16[64,512]{1,0:T(8,128)(2,1)S(1)} %get-tuple-element.100), channel_id=1, source_target_pairs={{0,6},{2,0},{4,2},{6,4},{1,7},{3,1},{5,3},{7,5},{8,14},{10,8},{12,... | collective-permute-start | bytes 196616 | tf_op jit(solution)/shard_map/ppermute | solution.py:688
  20.3 5.9 %collective-permute-start.7 = (bf16[64,512]{1,0:T(8,128)(2,1)S(1)}, bf16[64,512]{1,0:T(8,128)(2,1)S(1)}, u32[]{:S(2)}, u32[]{:S(2)}) collective-permute-start(bf16[64,512]{1,0:T(8,128)(2,1)S(1)} %get-tuple-element.101), channel_id=1, source_target_pairs={{0,4},{2,6},{4,0},{6,2},{1,5},{3,7},{5,1},{7,3},{8,12},{10,14},{12... | collective-permute-start | bytes 196616 | tf_op jit(solution)/shard_map/ppermute | solution.py:688
  22.6 5.5 %collective-permute-start.6 = (bf16[64,512]{1,0:T(8,128)(2,1)S(1)}, bf16[64,512]{1,0:T(8,128)(2,1)S(1)}, u32[]{:S(2)}, u32[]{:S(2)}) collective-permute-start(bf16[64,512]{1,0:T(8,128)(2,1)S(1)} %get-tuple-element.102), channel_id=1, source_target_pairs={{0,2},{2,4},{4,6},{6,0},{1,3},{3,5},{5,7},{7,1},{8,10},{10,12},{12... | collective-permute-start | bytes 196616 | tf_op jit(solution)/shard_map/ppermute | solution.py:688
  24.8 5.5 %collective-permute-start.11 = (bf16[128,1024]{1,0:T(8,128)(2,1)S(1)}, bf16[128,1024]{1,0:T(8,128)(2,1)S(1)}, u32[]{:S(2)}, u32[]{:S(2)}) collective-permute-start(bf16[128,1024]{1,0:T(8,128)(2,1)S(1)} %get-tuple-element.95), channel_id=1, source_target_pairs={{16,26},{18,28},{20,30},{22,24},{17,27},{19,29},{21,31},{23,25}} | collective-permute-start | bytes 786440 | tf_op jit(solution)/shard_map/ppermute | solution.py:655
  25.5 10.1 %collective-permute-start.3 = (bf16[128,1280]{1,0:T(8,128)(2,1)S(1)}, bf16[128,1280]{1,0:T(8,128)(2,1)S(1)}, u32[]{:S(2)}, u32[]{:S(2)}) collective-permute-start(bf16[128,1280]{1,0:T(8,128)(2,1)S(1)} %get-tuple-element.59), channel_id=1, source_target_pairs={{24,26},{26,28},{28,30},{30,24},{25,27},{27,29},{29,31},{31,25}} | collective-permute-start | bytes 983048 | tf_op jit(solution)/shard_map/ppermute | solution.py:674
  26.2 47.2 %collective-permute-start.4 = (bf16[128,1280]{1,0:T(8,128)(2,1)S(1)}, bf16[128,1280]{1,0:T(8,128)(2,1)S(1)}, u32[]{:S(2)}, u32[]{:S(2)}) collective-permute-start(bf16[128,1280]{1,0:T(8,128)(2,1)S(1)} %get-tuple-element.60), channel_id=1, source_target_pairs={{24,28},{26,30},{28,24},{30,26},{25,29},{27,31},{29,25},{31,27}} | collective-permute-start | bytes 983048 | tf_op jit(solution)/shard_map/ppermute | solution.py:674
  28.2 3.5 %collective-permute-start.12 = (bf16[128,1024]{1,0:T(8,128)(2,1)S(1)}, bf16[128,1024]{1,0:T(8,128)(2,1)S(1)}, u32[]{:S(2)}, u32[]{:S(2)}) collective-permute-start(bf16[128,1024]{1,0:T(8,128)(2,1)S(1)} %get-tuple-element.94), channel_id=1, source_target_pairs={{16,28},{18,30},{20,24},{22,26},{17,29},{19,31},{21,25},{23,27}} | collective-permute-start | bytes 786440 | tf_op jit(solution)/shard_map/ppermute | solution.py:655
  28.9 4.9 %collective-permute-start.13 = (bf16[128,1024]{1,0:T(8,128)(2,1)S(1)}, bf16[128,1024]{1,0:T(8,128)(2,1)S(1)}, u32[]{:S(2)}, u32[]{:S(2)}) collective-permute-start(bf16[128,1024]{1,0:T(8,128)(2,1)S(1)} %get-tuple-element.93), channel_id=1, source_target_pairs={{16,30},{18,24},{20,26},{22,28},{17,31},{19,25},{21,27},{23,29}} | collective-permute-start | bytes 786440 | tf_op jit(solution)/shard_map/ppermute | solution.py:655
  30.3 45.1 %collective-permute-start.5 = (bf16[128,1280]{1,0:T(8,128)(2,1)S(1)}, bf16[128,1280]{1,0:T(8,128)(2,1)S(1)}, u32[]{:S(2)}, u32[]{:S(2)}) collective-permute-start(bf16[128,1280]{1,0:T(8,128)(2,1)S(1)} %get-tuple-element.61), channel_id=1, source_target_pairs={{24,30},{26,24},{28,26},{30,28},{25,31},{27,25},{29,27},{31,29}} | collective-permute-start | bytes 983048 | tf_op jit(solution)/shard_map/ppermute | solution.py:674
  31.7 46.4 %collective-permute-start.9 = (bf16[4,64,512]{2,1,0:T(8,128)(2,1)S(1)}, bf16[4,64,512]{2,1,0:T(8,128)(2,1)S(1)}, u32[]{:S(2)}, u32[]{:S(2)}) collective-permute-start(bf16[4,64,512]{2,1,0:T(8,128)(2,1)S(1)} %pad_maximum_fusion.1), channel_id=1, source_target_pairs={{0,1},{1,0},{2,3},{3,2},{4,5},{5,4},{6,7},{7,6},{8,9},{9,8},{10,11... | collective-permute-start | bytes 786440 | tf_op jit(solution)/shard_map/ppermute | solution.py:693
  34.5 52.2 %collective-permute-start.14 = (bf16[512,1024]{1,0:T(8,128)(2,1)}, bf16[512,1024]{1,0:T(8,128)(2,1)}, u32[]{:S(2)}, u32[]{:S(2)}) collective-permute-start(bf16[512,1024]{1,0:T(8,128)(2,1)} %constant_dynamic-update-slice_fusion.refs_5_), channel_id=1, source_target_pairs={{0,1},{1,0},{2,3},{3,2},{4,5},{5,4},{6,7},{7,6},{8,9},{9,8},{10,11... | collective-permute-start | bytes 3145736 | tf_op jit(solution)/shard_map/ppermute | solution.py:691
  35.6 105.1 %collective-permute-start.19 = (bf16[128,4096]{1,0:T(8,128)(2,1)}, bf16[128,4096]{1,0:T(8,128)(2,1)}, u32[]{:S(2)}, u32[]{:S(2)}) collective-permute-start(bf16[128,4096]{1,0:T(8,128)(2,1)} %dynamic-slice_bitcast_fusion), channel_id=1, source_target_pairs={{0,8},{2,10},{4,12},{6,14},{8,16},{10,18},{12,20},{14,22},{1,9},{3... | collective-permute-start | bytes 3145736 | tf_op jit(solution)/shard_map/ppermute | solution.py:600
  73.4 12.1 %copy-start.5 = (bf16[128,1280]{1,0:T(8,128)(2,1)}, bf16[128,1280]{1,0:T(8,128)(2,1)S(1)}, u32[]{:S(2)}) copy-start(bf16[128,1280]{1,0:T(8,128)(2,1)S(1)} %collective-permute-done.4.refs_2_) | copy-start | bytes 983044
  73.5 67.2 %collective-permute-start.20 = (bf16[128,4096]{1,0:T(8,128)(2,1)}, bf16[128,4096]{1,0:T(8,128)(2,1)}, u32[]{:S(2)}, u32[]{:S(2)}) collective-permute-start(bf16[128,4096]{1,0:T(8,128)(2,1)} %dynamic-slice_bitcast_fusion), channel_id=1, source_target_pairs={{0,10},{2,12},{4,14},{6,8},{8,18},{10,20},{12,22},{14,16},{1,11},{... | collective-permute-start | bytes 3145736 | tf_op jit(solution)/shard_map/ppermute | solution.py:600
  75.4 0.7 copy-start.7
  76.1 89.0 %collective-permute-start.21 = (bf16[128,4096]{1,0:T(8,128)(2,1)}, bf16[128,4096]{1,0:T(8,128)(2,1)}, u32[]{:S(2)}, u32[]{:S(2)}) collective-permute-start(bf16[128,4096]{1,0:T(8,128)(2,1)} %dynamic-slice_bitcast_fusion), channel_id=1, source_target_pairs={{0,12},{2,14},{4,8},{6,10},{8,20},{10,22},{12,16},{14,18},{1,13},{... | collective-permute-start | bytes 3145736 | tf_op jit(solution)/shard_map/ppermute | solution.py:600
  78.1 0.7 copy-start.14
  78.8 87.0 %collective-permute-start.22 = (bf16[128,4096]{1,0:T(8,128)(2,1)}, bf16[128,4096]{1,0:T(8,128)(2,1)}, u32[]{:S(2)}, u32[]{:S(2)}) collective-permute-start(bf16[128,4096]{1,0:T(8,128)(2,1)} %dynamic-slice_bitcast_fusion), channel_id=1, source_target_pairs={{0,14},{2,8},{4,10},{6,12},{8,22},{10,16},{12,18},{14,20},{1,15},{... | collective-permute-start | bytes 3145736 | tf_op jit(solution)/shard_map/ppermute | solution.py:600
  86.8 1.0 copy-start.6
  87.7 1.0 copy-start.8
  90.9 74.8 %copy-start.9 = (bf16[128,1024]{1,0:T(8,128)(2,1)}, bf16[128,1024]{1,0:T(8,128)(2,1)S(1)}, u32[]{:S(2)}) copy-start(bf16[128,1024]{1,0:T(8,128)(2,1)S(1)} %get-tuple-element.64) | copy-start | bytes 786436
  90.9 0.7 collective-permute-start.15
  91.6 0.7 collective-permute-start.16
  92.3 0.7 collective-permute-start.17
  93.0 0.7 collective-permute-start.18
  94.4 0.7 copy-start.2
  165.8 1.0 copy-start.1
  176.4 14.0 %collective-permute-start.26 = (bf16[64,512]{1,0:T(8,128)(2,1)S(1)}, bf16[64,512]{1,0:T(8,128)(2,1)S(1)}, u32[]{:S(2)}, u32[]{:S(2)}) collective-permute-start(bf16[64,512]{1,0:T(8,128)(2,1)S(1)} %get-tuple-element.76), channel_id=1, source_target_pairs={{8,14},{10,8},{12,10},{14,12},{16,22},{18,16},{20,18},{22,20},{9,1... | collective-permute-start | bytes 196616 | tf_op jit(solution)/shard_map/ppermute | solution.py:779
  178.4 12.1 %collective-permute-start.25 = (bf16[64,512]{1,0:T(8,128)(2,1)S(1)}, bf16[64,512]{1,0:T(8,128)(2,1)S(1)}, u32[]{:S(2)}, u32[]{:S(2)}) collective-permute-start(bf16[64,512]{1,0:T(8,128)(2,1)S(1)} %get-tuple-element.76), channel_id=1, source_target_pairs={{8,12},{10,14},{12,8},{14,10},{16,20},{18,22},{20,16},{22,18},{9,1... | collective-permute-start | bytes 196616 | tf_op jit(solution)/shard_map/ppermute | solution.py:779
  184.2 6.3 %collective-permute-start.24 = (bf16[64,512]{1,0:T(8,128)(2,1)S(1)}, bf16[64,512]{1,0:T(8,128)(2,1)S(1)}, u32[]{:S(2)}, u32[]{:S(2)}) collective-permute-start(bf16[64,512]{1,0:T(8,128)(2,1)S(1)} %get-tuple-element.76), channel_id=1, source_target_pairs={{8,10},{10,12},{12,14},{14,8},{16,18},{18,20},{20,22},{22,16},{9,1... | collective-permute-start | bytes 196616 | tf_op jit(solution)/shard_map/ppermute | solution.py:779
  188.4 9.1 %collective-permute-start.23 = (bf16[512,640]{1,0:T(8,128)(2,1)S(1)}, bf16[512,640]{1,0:T(8,128)(2,1)}, u32[]{:S(2)}, u32[]{:S(2)}) collective-permute-start(bf16[512,640]{1,0:T(8,128)(2,1)S(1)} %get-tuple-element.75.refs_2_), channel_id=1, source_target_pairs={{0,1},{1,0},{2,3},{3,2},{4,5},{5,4},{6,7},{7,6},{8,9},{9,8},{10,11... | collective-permute-start | bytes 1966088 | tf_op jit(solution)/shard_map/ppermute | solution.py:784
  194.6 2.9 %collective-permute-start.27 = (bf16[256,512]{1,0:T(8,128)(2,1)S(1)}, bf16[256,512]{1,0:T(8,128)(2,1)S(1)}, u32[]{:S(2)}, u32[]{:S(2)}) collective-permute-start(bf16[256,512]{1,0:T(8,128)(2,1)S(1)} %bitcast.56), channel_id=1, source_target_pairs={{0,1},{1,0},{2,3},{3,2},{4,5},{5,4},{6,7},{7,6},{8,9},{9,8},{10,11... | collective-permute-start | bytes 786440 | tf_op jit(solution)/shard_map/ppermute | solution.py:786
  197.5 0.9 copy-start.3
  200.2 5.9 %collective-permute-start.28 = (bf16[128,256]{1,0:T(8,128)(2,1)S(1)}, bf16[128,256]{1,0:T(8,128)(2,1)S(1)}, u32[]{:S(2)}, u32[]{:S(2)}) collective-permute-start(bf16[128,256]{1,0:T(8,128)(2,1)S(1)} %get-tuple-element.77), channel_id=1, source_target_pairs={{16,8},{18,10},{20,12},{22,14},{17,9},{19,11},{21,13},{23,15}} | collective-permute-start | bytes 196616 | tf_op jit(solution)/shard_map/ppermute | solution.py:721
  201.5 7.7 %collective-permute-start.29 = (bf16[128,256]{1,0:T(8,128)(2,1)S(1)}, bf16[128,256]{1,0:T(8,128)(2,1)S(1)}, u32[]{:S(2)}, u32[]{:S(2)}) collective-permute-start(bf16[128,256]{1,0:T(8,128)(2,1)S(1)} %get-tuple-element.78), channel_id=1, source_target_pairs={{16,14},{18,8},{20,10},{22,12},{17,15},{19,9},{21,11},{23,13}} | collective-permute-start | bytes 196616 | tf_op jit(solution)/shard_map/ppermute | solution.py:721
  202.8 9.3 %collective-permute-start.30 = (bf16[128,256]{1,0:T(8,128)(2,1)S(1)}, bf16[128,256]{1,0:T(8,128)(2,1)S(1)}, u32[]{:S(2)}, u32[]{:S(2)}) collective-permute-start(bf16[128,256]{1,0:T(8,128)(2,1)S(1)} %get-tuple-element.79), channel_id=1, source_target_pairs={{16,12},{18,14},{20,8},{22,10},{17,13},{19,15},{21,9},{23,11}} | collective-permute-start | bytes 196616 | tf_op jit(solution)/shard_map/ppermute | solution.py:721
  204.1 9.3 %collective-permute-start.31 = (bf16[128,256]{1,0:T(8,128)(2,1)S(1)}, bf16[128,256]{1,0:T(8,128)(2,1)S(1)}, u32[]{:S(2)}, u32[]{:S(2)}) collective-permute-start(bf16[128,256]{1,0:T(8,128)(2,1)S(1)} %get-tuple-element.80), channel_id=1, source_target_pairs={{16,10},{18,12},{20,14},{22,8},{17,11},{19,13},{21,15},{23,9}} | collective-permute-start | bytes 196616 | tf_op jit(solution)/shard_map/ppermute | solution.py:721
  214.1 2.5 copy-start.4
  216.6 5.2 %collective-permute-start.32 = (bf16[128,256]{1,0:T(8,128)(2,1)}, bf16[128,256]{1,0:T(8,128)(2,1)S(1)}, u32[]{:S(2)}, u32[]{:S(2)}) collective-permute-start(bf16[128,256]{1,0:T(8,128)(2,1)} %get-tuple-element.83), channel_id=1, source_target_pairs={{8,0},{10,2},{12,4},{14,6},{9,1},{11,3},{13,5},{15,7}} | collective-permute-start | bytes 196616 | tf_op jit(solution)/shard_map/ppermute | solution.py:721
  217.9 3.9 %collective-permute-start.33 = (bf16[128,256]{1,0:T(8,128)(2,1)}, bf16[128,256]{1,0:T(8,128)(2,1)S(1)}, u32[]{:S(2)}, u32[]{:S(2)}) collective-permute-start(bf16[128,256]{1,0:T(8,128)(2,1)} %get-tuple-element.84), channel_id=1, source_target_pairs={{8,6},{10,0},{12,2},{14,4},{9,7},{11,1},{13,3},{15,5}} | collective-permute-start | bytes 196616 | tf_op jit(solution)/shard_map/ppermute | solution.py:721
  219.2 2.9 %collective-permute-start.34 = (bf16[128,256]{1,0:T(8,128)(2,1)}, bf16[128,256]{1,0:T(8,128)(2,1)S(1)}, u32[]{:S(2)}, u32[]{:S(2)}) collective-permute-start(bf16[128,256]{1,0:T(8,128)(2,1)} %get-tuple-element.85), channel_id=1, source_target_pairs={{8,4},{10,6},{12,0},{14,2},{9,5},{11,7},{13,1},{15,3}} | collective-permute-start | bytes 196616 | tf_op jit(solution)/shard_map/ppermute | solution.py:721
  220.5 6.3 %collective-permute-start.35 = (bf16[128,256]{1,0:T(8,128)(2,1)}, bf16[128,256]{1,0:T(8,128)(2,1)S(1)}, u32[]{:S(2)}, u32[]{:S(2)}) collective-permute-start(bf16[128,256]{1,0:T(8,128)(2,1)} %get-tuple-element.86), channel_id=1, source_target_pairs={{8,2},{10,4},{12,6},{14,0},{9,3},{11,5},{13,7},{15,1}} | collective-permute-start | bytes 196616 | tf_op jit(solution)/shard_map/ppermute | solution.py:721
  221.8 43.8 %copy-start.10 = (bf16[128,1024]{1,0:T(8,128)(2,1)S(1)}, bf16[128,1024]{1,0:T(8,128)(2,1)}, u32[]{:S(2)}) copy-start(bf16[128,1024]{1,0:T(8,128)(2,1)} %copy-done.9) | copy-start | bytes 786436
  232.1 9.9 %collective-permute-start.36 = (bf16[128,1280]{1,0:T(8,128)(2,1)S(1)}, bf16[128,1280]{1,0:T(8,128)(2,1)S(1)}, u32[]{:S(2)}, u32[]{:S(2)}) collective-permute-start(bf16[128,1280]{1,0:T(8,128)(2,1)S(1)} %get-tuple-element.90), channel_id=1, source_target_pairs={{0,2},{2,4},{4,6},{6,0},{8,10},{10,12},{12,14},{14,8},{16,18},{18,... | collective-permute-start | bytes 983048 | tf_op jit(solution)/shard_map/ppermute | solution.py:812
  234.9 27.1 %collective-permute-start.37 = (bf16[128,1280]{1,0:T(8,128)(2,1)S(1)}, bf16[128,1280]{1,0:T(8,128)(2,1)S(1)}, u32[]{:S(2)}, u32[]{:S(2)}) collective-permute-start(bf16[128,1280]{1,0:T(8,128)(2,1)S(1)} %get-tuple-element.91), channel_id=1, source_target_pairs={{0,4},{2,6},{4,0},{6,2},{8,12},{10,14},{12,8},{14,10},{16,20},{18,... | collective-permute-start | bytes 983048 | tf_op jit(solution)/shard_map/ppermute | solution.py:812
  238.0 27.3 %collective-permute-start.38 = (bf16[128,1280]{1,0:T(8,128)(2,1)S(1)}, bf16[128,1280]{1,0:T(8,128)(2,1)S(1)}, u32[]{:S(2)}, u32[]{:S(2)}) collective-permute-start(bf16[128,1280]{1,0:T(8,128)(2,1)S(1)} %get-tuple-element.92), channel_id=1, source_target_pairs={{0,6},{2,0},{4,2},{6,4},{8,14},{10,8},{12,10},{14,12},{16,22},{18,... | collective-permute-start | bytes 983048 | tf_op jit(solution)/shard_map/ppermute | solution.py:812

commit v3 on v1

--- a/solution.py
+++ b/solution.py
@@ -389,84 +389,224 @@
     return main, conv_taps_back(d_state, taps_state_ref[...]).astype(BF16)
 
 
-def section_kernel(heads, chunks, first, *refs):
-    count = chunks
-    incoming = refs[:count]
-    refs = refs[count:]
-    out_rows_ref = None
-    if first:
-        out_rows_ref, refs = refs[0], refs[1:]
+def picked_members(chunks, state):
+    me = lax.axis_index("tensor")
+    states = state.shape[1] // 2
+    share = states // chunks
+    shape = (state.shape[1], 128)
+    row = iota(shape, 0)
+    lane = iota(shape, 1)
+    source = jnp.where(lane < share, lane, lane + states - share)
+    pieces = []
+    for hop in range(chunks):
+        member = lax.rem(me + hop, chunks)
+        picked = (row == source + member * share) & (lane < 2 * share)
+        pieces.append(dot_nn(state, picked.astype(BF16)).astype(BF16))
+    return pieces
+
+
+def first_kernel(heads, chunks, *refs):
+    incoming, refs = refs[:chunks], refs[chunks:]
+    rows_ref, refs = refs[0], refs[1:]
     residuals, refs = refs[:9], refs[9:]
-    cols_ref, refs = refs[0], refs[1:]
+    main_ref, outs = refs[0], refs[1:]
+    me = lax.axis_index("tensor")
+    width = incoming[0].shape[1]
+    dnormed = None
+    for hop in range(chunks):
+        chunk = lax.rem(me + chunks - hop, chunks)
+        term = dot_nt(
+            incoming[hop][...], rows_ref[:, pl.ds(pl.multiple_of(chunk * width, width), width)]
+        )
+        dnormed = term if dnormed is None else dnormed + term
+    main, state = mixer_back(heads, dnormed, residuals)
+    main_ref[...] = main
+    for out, piece in zip(outs, picked_members(chunks, state)):
+        out[...] = piece
+
+
+def next_kernel(heads, chunks, active, *refs):
+    incoming, refs = refs[:chunks], refs[chunks:]
+    residuals, refs = refs[:9], refs[9:]
+    channels = residuals[0].shape[2]
+    dnormed = incoming[0][:, :channels].astype(F32)
+    for hop in range(1, chunks):
+        dnormed = dnormed + incoming[hop][:, :channels].astype(F32)
+    states = residuals[4].shape[2] * 2
+    joined = incoming[0].shape[1] > channels
+    if joined:
+        place = slice(channels, channels + states)
+        state = incoming[0][:, place].astype(F32)
+        for hop in range(1, chunks):
+            state = state + incoming[hop][:, place].astype(F32)
+        share = states // chunks
+        pieces = picked_members(chunks, state.astype(BF16))
+        place = slice(channels + states, channels + states + channels // 2)
+        for hop in range(chunks):
+            piece = pieces[hop][:, :share]
+            halves = [incoming[hop][start : start + share, place] for start in (0, share)]
+            dnormed = dnormed + jnp.concatenate([dot_nn(piece, half) for half in halves], axis=1)
+    main, state = mixer_back(heads, dnormed, residuals)
+    if joined:
+        done = lax.axis_index("pipe") > active
+        main = jnp.where(done, refs[0][...], main)
+        state = jnp.where(done, refs[1][...], state)
+        refs = refs[2:]
+    refs[0][...] = main
+    refs[1][...] = state
+    if active == 0:
+        for ref, piece in zip(refs[2:], picked_members(chunks, state)):
+            ref[...] = piece
+
+
+def sum_pieces(pieces, width):
+    total = pieces[0][...].astype(F32)
+    for piece in pieces[1:]:
+        total = total + piece[...].astype(F32)
+    return total.astype(BF16)[:, :width]
+
+
+def project_kernel(chunks, *refs):
+    main_ref, refs = refs[0], refs[1:]
+    pieces, refs = refs[:chunks], refs[chunks:]
+    state_cols_ref, cols_ref, refs = refs[0], refs[1], refs[2:]
     outs, refs = refs[:chunks], refs[chunks:]
-    cols, cols_sems = refs[0], refs[1]
+    cols, sems = refs
     me = lax.axis_index("tensor")
     width = cols.shape[1]
+    places = []
     copies = []
-    if first:
-        rows, rows_sem = refs[2], refs[3]
-        rows_copy = pltpu.make_async_copy(out_rows_ref, rows, rows_sem)
-        rows_copy.start()
     for hop in range(chunks):
-        chunk = lax.rem(me + hop, chunks)
-        copy = pltpu.make_async_copy(
-            cols_ref.at[pl.ds(pl.multiple_of(chunk * width, width), width), :],
-            cols.at[hop],
-            cols_sems.at[hop],
-        )
+        place = pl.ds(pl.multiple_of(lax.rem(me + hop, chunks) * width, width), width)
+        copy = pltpu.make_async_copy(cols_ref.at[place, :], cols.at[hop], sems.at[hop])
         copy.start()
+        places.append(place)
         copies.append(copy)
-    if first:
-        rows_copy.wait()
-        dnormed = None
-        for hop in range(chunks):
-            chunk = lax.rem(me + chunks - hop, chunks)
-            term = dot_nt(
-                incoming[hop][...], rows[:, pl.ds(pl.multiple_of(chunk * width, width), width)]
-            )
-            dnormed = term if dnormed is None else dnormed + term
+    main = main_ref[...]
+    state = sum_pieces(pieces, pieces[0].shape[1])
+    state = state[:, : state_cols_ref.shape[0]]
+    for hop in range(chunks):
+        product = dot_nn(state, state_cols_ref[:, places[hop]])
+        copies[hop].wait()
+        outs[hop][...] = (product + dot_nt(main, cols[hop])).astype(BF16)
+
+
+def compose_kernel(rows_ref, cols_ref, main_ref, main_sum):
+    step = pl.program_id(0)
+    main = dot_nn(rows_ref[...], cols_ref[...])
+
+    @pl.when(step == 0)
+    def _():
+        main_sum[...] = main
+
+    @pl.when(step > 0)
+    def _():
+        main_sum[...] += main
+
+    @pl.when(step == pl.num_programs(0) - 1)
+    def _():
+        main_ref[...] = main_sum[...].astype(BF16)
+
+
+def compose_last_kernel(half, *refs):
+    rows, refs = refs[:half], refs[half:]
+    done, refs = refs[: half - 1], refs[half - 1 :]
+    cols_ref, state_ref, joint_ref, main_sum, maps_sum = refs
+    step = pl.program_id(0)
+    size = rows[0].shape[0]
+    map_width = main_sum.shape[1]
+
+    @pl.when(step == 0)
+    def _():
+        main_sum[...] = jnp.zeros_like(main_sum)
+        maps_sum[...] = jnp.zeros_like(maps_sum)
+
+    main_sum[...] += dot_nn(rows[-1][...], cols_ref[...])
+    for hop in range(half):
+        maps_sum[:, hop * size : (hop + 1) * size] += dot_nt(state_ref[...], rows[hop][...])
+
+    @pl.when(step == pl.num_programs(0) - 1)
+    def _():
+        joint_ref[...] = jnp.zeros_like(joint_ref)
+        for hop in range(half - 1):
+            joint_ref[:size, hop * map_width : (hop + 1) * map_width] = done[hop][...]
+        joint_ref[:size, (half - 1) * map_width :] = main_sum[...].astype(BF16)
+        joint_ref[size:, : half * size] = maps_sum[...].astype(BF16)
+
+
+def by_hop(chunks, own, other):
+    core = lax.axis_index("dp")
+    half = chunks // 2
+    return [
+        jnp.where((core == 0) == (hop < half), own[hop % half], other[hop % half])
+        for hop in range(chunks)
+    ]
+
+
+def send_kernel(chunks, main_ref, state_ref, *refs):
+    sources, refs = refs[:2], refs[2:]
+    outs, held, sems = refs[:chunks], refs[chunks:-1], refs[-1]
+    half = chunks // 2
+    map_width = main_ref.shape[1]
+    states = state_ref.shape[1]
+    share = states // chunks
+    size = held[0].shape[0] - share
+    copies = [
+        pltpu.make_async_copy(source, place, sems.at[index])
+        for index, (source, place) in enumerate(zip(sources, held))
+    ]
+    for copy in copies:
+        copy.start()
+    main = main_ref[...]
+    for copy in copies:
+        copy.wait()
+
+    def terms(joint):
+        return [
+            dot_nt(main, joint[:size, hop * map_width : (hop + 1) * map_width])
+            for hop in range(half)
+        ]
+
+    def maps(joint):
+        return [joint[size:, hop * size : (hop + 1) * size] for hop in range(half)]
+
+    total = by_hop(chunks, terms(held[0]), terms(held[1]))
+    kept = by_hop(chunks, maps(held[0]), maps(held[1]))
+    for hop in range(chunks):
+        outs[hop][:, :size] = total[hop].astype(BF16)
+        outs[hop][:, size : size + states] = state_ref[...]
+        for part in range(2):
+            outs[hop][part * share : (part + 1) * share, size + states :] = kept[hop][
+                :, part * (size // 2) : (part + 1) * (size // 2)
+            ]
+
+
+def carry_kernel(chunks, last, *refs):
+    parts, refs = refs[:chunks], refs[chunks:]
+    if last:
+        done_ref, out_ref = refs
     else:
-        dnormed = incoming[0][...].astype(F32)
-        for hop in range(1, chunks):
-            dnormed = dnormed + incoming[hop][...].astype(F32)
-    main, state = mixer_back(heads, dnormed, residuals)
+        refs = refs[1:]
+    carry = sum_pieces(parts, parts[0].shape[1])
+    if last:
+        is_last = lax.axis_index("pipe") == lax.axis_size("pipe") - 1
+        out_ref[0] = jnp.where(is_last, done_ref[...], carry)
+        return
+    half = chunks // 2
+    own, other = refs[:half], refs[half : 2 * half]
+    refs[2 * half][...] = carry
+
+    terms = by_hop(
+        chunks,
+        [dot_nt(carry, row[...]) for row in own],
+        [dot_nt(carry, row[...]) for row in other],
+    )
     for hop in range(chunks):
-        copies[hop].wait()
-        outs[hop][:, :width] = dot_nt(main, cols[hop]).astype(BF16)
-        outs[hop][:, width:] = state
-
-
-def carry_kernel(chunks, last, *refs):
-    parts = refs[:chunks]
-    state_ref, refs = refs[chunks], refs[chunks + 1 :]
-    if not last:
-        own_ref, other_ref, refs = refs[0], refs[1], refs[2:]
-        carry_ref, outs, refs = refs[0], refs[1 : 1 + chunks], refs[1 + chunks :]
-        own, other, sems = refs
-        copies = [
-            pltpu.make_async_copy(own_ref, own, sems.at[0]),
-            pltpu.make_async_copy(other_ref, other, sems.at[1]),
-        ]
-        for copy in copies:
-            copy.start()
-    else:
-        carry_ref = refs[0]
-    width = carry_ref.shape[1]
-    total = parts[0][...].astype(F32)
-    for part in parts[1:]:
-        total = total + part[...].astype(F32)
-    carry = total[:, :width] + dot_nn(total[:, width:].astype(BF16), state_ref[...])
-    carry = carry.astype(BF16)
-    carry_ref[...] = carry
-    if not last:
-        half = own.shape[0] // chunks
-        core = lax.axis_index("dp")
-        for copy, held, place in ((copies[0], own, core), (copies[1], other, 1 - core)):
-            copy.wait()
-            product = dot_nt(carry, held[...]).astype(BF16)
-            lanes = pl.ds(pl.multiple_of(place * half, half), half)
-            for hop in range(chunks):
-                outs[hop][:, lanes] = product[:, hop * half : (hop + 1) * half]
+        refs[2 * half + 1 + hop][...] = terms[hop].astype(BF16)
+
+
+def after(value, dependency):
+    return lax.optimization_barrier((value, dependency))[0]
 
 
 def kernel_params():
@@ -509,60 +649,47 @@
     model_width = weight_out.shape[2]
     heads = step_bias.shape[1]
     channels = weight_out.shape[1]
-    half_rows = channels // 2
-    half_width = width // 2
     place = ("pipe", "tensor")
 
-    last_own = jnp.where(section == sections - 1, output_grad, jnp.zeros_like(output_grad))
-    incoming = [last_own]
+    def within(active, hop):
+        return section_pairs(sections, chunks, active, active, hop)
+
+    half = chunks // 2
+
+    def by_core(sources, hop):
+        pairs = []
+        for source in sources:
+            for index in range(chunks):
+                for lane in range(2):
+                    target = (index + hop + lane * half) % chunks
+                    start = (source * chunks + index) * 2 + lane
+                    pairs.append((start, ((source + 1) * chunks + target) * 2 + lane))
+        return pairs
+
+    everywhere = ("pipe", "tensor", "dp")
+
+    def swap(value, sections_in):
+        pairs = []
+        for source in sections_in:
+            for start in range(source * chunks * 2, (source + 1) * chunks * 2):
+                pairs.append((start, start ^ 1))
+        return lax.ppermute(value, everywhere, pairs)
+
+    incoming = [output_grad]
     for hop in range(1, chunks):
-        pairs = section_pairs(sections, chunks, sections - 1, sections - 1, hop)
-        incoming.append(lax.ppermute(output_grad, place, pairs))
-
-    own_half = []
-    for hop in range(chunks):
-        chunk = (me + hop) % chunks
-        piece = lax.dynamic_slice(
-            weight_out[0], (core * half_rows, chunk * width), (half_rows, width)
-        )
-        pairs = []
-        for source in range(sections - 1):
-            pairs += section_pairs(sections, chunks, source, source + 1, hop)
-        own_half.append(lax.ppermute(piece, place, pairs))
-    own_half = jnp.concatenate(own_half, axis=0)
-    other_half = lax.ppermute(own_half, "dp", [(0, 1), (1, 0)])
-
-    state_cols = weight_state[0].reshape(model_width, -1).T
-    pieces = []
-    for hop in range(chunks):
-        chunk = (me + hop) % chunks
-        piece = lax.dynamic_slice(
-            state_cols,
-            (0, chunk * width + core * half_width),
-            (state_cols.shape[0], half_width),
-        )
-        if hop:
-            pairs = [(index, (index + hop) % chunks) for index in range(chunks)]
-            piece = lax.ppermute(piece, "tensor", pairs)
-        pieces.append(piece)
-    state_own = jnp.stack(pieces)
-    state_other = lax.ppermute(state_own, "dp", [(0, 1), (1, 0)])
-    lower = jnp.where(core == 0, state_own, state_other)
-    upper = jnp.where(core == 0, state_other, state_own)
-    state_rows = jnp.concatenate([lower, upper], axis=2)
-    order = (me - jnp.arange(chunks)) % chunks
-    state_rows = jnp.take(state_rows, order, axis=0)
-    state_rows = state_rows.reshape(chunks, 2, -1, width).transpose(1, 0, 2, 3)
-    state_rows = state_rows.reshape(-1, width)
-
-    step_cols = jnp.pad(weight_step[0].T, ((0, 0), (0, 128 - heads)))
-    cols = jnp.concatenate([weight_main[0].reshape(model_width, -1), step_cols], axis=1)
-
+        incoming.append(lax.ppermute(output_grad, place, within(sections - 1, hop)))
+
+    rows = [lax.ppermute(weight_out[0], everywhere, by_core(range(sections - 2), 0))]
     lanes = ((0, 0), (0, 128 - heads))
     by_head = jnp.pad(
         jnp.stack([step_bias[0], decay_log[0], skip_gain[0]]), ((0, 5), (0, 128 - heads))
     )
     steps = jnp.pad(saved_step[0].astype(F32).T, lanes)
+    chunk_rows = []
+    for hop in range(half):
+        chunk = (me + hop + core * half) % chunks
+        chunk_rows.append(lax.dynamic_slice_in_dim(weight_out[0], chunk * width, width, 1))
+    steps, chunk_rows = lax.optimization_barrier((steps, chunk_rows))
     taps_main = conv_main[0]
     taps_state = conv_state[0].reshape(conv_state.shape[1], -1)
     state_width = taps_state.shape[1]
@@ -592,58 +719,174 @@
         norm_gain,
     )
     residuals = tuple(residuals) + (taps_main, taps_state, by_head)
-    message = jax.ShapeDtypeStruct((length, width + state_width), BF16)
     slice_out = jax.ShapeDtypeStruct((length, channels), BF16)
+    message = jax.ShapeDtypeStruct((length, width), BF16)
+    map_width = 2 * channels + 128
+    main_shape = jax.ShapeDtypeStruct((length, map_width), BF16)
+    piece_shape = jax.ShapeDtypeStruct((length, 128), BF16)
     hbm = pl.BlockSpec(memory_space=pl.ANY)
-
-    result = jnp.zeros((length, width), BF16)
-    for moment in range(sections):
-        active = sections - 1 - moment
-        first = moment == 0
-        last = moment + 1 == sections
-        scratch = [
-            pltpu.VMEM((chunks, width, cols.shape[1]), BF16),
-            pltpu.SemaphoreType.DMA((chunks,)),
-        ]
-        if first:
-            scratch += [pltpu.VMEM((channels, model_width), BF16), pltpu.SemaphoreType.DMA]
-        parts = pl.pallas_call(
-            lambda *refs, first=first: section_kernel(heads, chunks, first, *refs),
+    step_cols, main_cols = after((weight_step[0], weight_main[0]), incoming[1])
+    step_cols = jnp.pad(step_cols.T, ((0, 0), (0, 128 - heads)))
+    main_cols = main_cols.reshape(model_width, -1)
+    cols = jnp.concatenate([main_cols, step_cols], axis=1)
+    residuals = residuals[:-1] + (after(by_head, main_cols),)
+
+    for hop, piece in enumerate(chunk_rows):
+        piece = after(piece, (residuals[0], main_cols, step_cols, *incoming[1:]))
+        chunk_rows[hop] = lax.ppermute(piece, everywhere, by_core([sections - 2], hop))
+    main, *pieces = pl.pallas_call(
+        lambda *refs: first_kernel(heads, chunks, *refs),
+        out_shape=(main_shape,) + (piece_shape,) * chunks,
+        in_specs=whole(chunks + 10),
+        out_specs=whole(1 + chunks),
+        compiler_params=kernel_params(),
+        name="section_first",
+    )(*incoming, weight_out[0], *residuals)
+
+    def share_state(pieces, sections_in):
+        shared = [pieces[0]]
+        for hop in range(1, chunks):
+            pairs = []
+            for source in sections_in:
+                pairs += within(source, hop)
+            shared.append(lax.ppermute(pieces[hop], place, pairs))
+        return shared
+
+    def project_call(main, pieces):
+        return pl.pallas_call(
+            lambda *refs: project_kernel(chunks, *refs),
             out_shape=(message,) * chunks,
-            in_specs=whole(chunks) + [hbm] * first + whole(9) + [hbm],
+            in_specs=whole(2 + chunks) + [hbm],
             out_specs=whole(chunks),
-            scratch_shapes=scratch,
+            scratch_shapes=[
+                pltpu.VMEM((chunks, width, map_width), BF16),
+                pltpu.SemaphoreType.DMA((chunks,)),
+            ],
             compiler_params=kernel_params(),
-            name="section_first" if first else "section_next",
-        )(*incoming, *((weight_out[0],) if first else ()), *residuals, cols)
-        gathered = [parts[0]]
-        for hop in range(1, chunks):
-            pairs = section_pairs(sections, chunks, active, active, hop)
-            gathered.append(lax.ppermute(parts[hop], place, pairs))
-        carry_shape = jax.ShapeDtypeStruct((length, width), BF16)
-        scratch = []
-        if not last:
-            scratch = [
-                pltpu.VMEM(own_half.shape, BF16),
-                pltpu.VMEM(own_half.shape, BF16),
-                pltpu.SemaphoreType.DMA((2,)),
-            ]
-        outs = pl.pallas_call(
-            lambda *refs, last=last: carry_kernel(chunks, last, *refs),
-            out_shape=(carry_shape,) + (() if last else (slice_out,) * chunks),
-            in_specs=whole(chunks + 1) + ([] if last else [hbm] * 2),
-            out_specs=whole(1 if last else 1 + chunks),
-            scratch_shapes=scratch,
+            name="project",
+        )(main, *pieces, state_cols, cols)
+
+    pieces = share_state(after(pieces, rows[0]), [sections - 1])
+    for hop in range(1, half):
+        following = after(weight_out[0], (rows[-1], *chunk_rows, *pieces[1:]))
+        rows.append(lax.ppermute(following, everywhere, by_core(range(sections - 2), hop)))
+    state_cols = after(weight_state[0], main).reshape(model_width, -1).T
+    state_share = state_cols.shape[0]
+    chunk_others = [swap(after(held, tuple(pieces[1:])), [sections - 1]) for held in chunk_rows]
+    pieces[0] = after(pieces[0], chunk_others)
+    parts = project_call(main, pieces)
+    exchanged = [parts[0]]
+    for hop in range(1, chunks):
+        exchanged.append(lax.ppermute(parts[hop], place, within(sections - 1, hop)))
+
+    grid_steps = 4
+    depth = model_width // grid_steps
+    rows_spec = pl.BlockSpec((channels, depth), lambda step: (0, step))
+    cols_spec = pl.BlockSpec((depth, map_width), lambda step: (step, 0))
+    map_spec = pl.BlockSpec((channels, map_width), lambda step: (0, 0))
+    map_shape = jax.ShapeDtypeStruct((channels, map_width), BF16)
+    main_own = [
+        pl.pallas_call(
+            compose_kernel,
+            grid=(grid_steps,),
+            out_shape=map_shape,
+            in_specs=[rows_spec, cols_spec],
+            out_specs=map_spec,
+            scratch_shapes=[pltpu.VMEM((channels, map_width), F32)],
             compiler_params=kernel_params(),
-            name="carry_last" if last else "carry_next",
-        )(*gathered, state_rows, *(() if last else (own_half, other_half)))
-        result = jnp.where(section == active, outs[0], result)
-        if not last:
-            incoming = []
-            for hop in range(chunks):
-                pairs = section_pairs(sections, chunks, active, active - 1, chunks - hop)
-                incoming.append(lax.ppermute(outs[1 + hop], place, pairs))
-    return result[None]
+            name="compose_weights",
+        )(after(held, parts[0]), cols)
+        for held in rows[:-1]
+    ]
+
+
+    def pass_back(messages, active):
+        moved = []
+        for hop in range(chunks):
+            pairs = section_pairs(sections, chunks, active, active - 1, chunks - hop)
+            moved.append(lax.ppermute(messages[hop], place, pairs))
+        return moved
+
+    carry, *messages = pl.pallas_call(
+        lambda *refs: carry_kernel(chunks, False, *refs),
+        out_shape=(message,) + (slice_out,) * chunks,
+        in_specs=whole(2 * chunks + 1),
+        out_specs=whole(1 + chunks),
+        compiler_params=kernel_params(),
+        name="carry_next",
+    )(*exchanged, after(by_head, main_own), *chunk_rows, *chunk_others)
+    result = carry
+    incoming = pass_back(messages, sections - 1)
+    joint_shape = jax.ShapeDtypeStruct((channels + state_share, half * map_width), BF16)
+    joint = pl.pallas_call(
+        lambda *refs: compose_last_kernel(half, *refs),
+        grid=(grid_steps,),
+        out_shape=joint_shape,
+        in_specs=[rows_spec] * half
+        + [map_spec] * (half - 1)
+        + [cols_spec, pl.BlockSpec((state_share, depth), lambda step: (0, step))],
+        out_specs=pl.BlockSpec(joint_shape.shape, lambda step: (0, 0)),
+        scratch_shapes=[
+            pltpu.VMEM((channels, map_width), F32),
+            pltpu.VMEM((state_share, half * channels), F32),
+        ],
+        compiler_params=kernel_params(),
+        name="compose_last",
+    )(*rows[:-1], after(rows[-1], messages[0]), *main_own, cols, state_cols)
+    residuals = residuals[:-1] + (after(by_head, joint),)
+
+    state_shape = jax.ShapeDtypeStruct((length, state_width), BF16)
+    joined = jax.ShapeDtypeStruct((length, channels + state_width + channels // 2), BF16)
+    assert 2 * state_share == length
+
+    def next_call(incoming, kept, active):
+        count = chunks if active == 0 else 0
+        main, state, *pieces = pl.pallas_call(
+            lambda *refs: next_kernel(heads, chunks, active, *refs),
+            out_shape=(main_shape, state_shape) + (piece_shape,) * count,
+            in_specs=whole(chunks + 9 + len(kept)),
+            out_specs=whole(2 + count),
+            compiler_params=kernel_params(),
+            name="section_next",
+        )(*incoming, *residuals, *kept)
+        return (main, state), pieces
+
+    joint_other = None
+    kept = ()
+    for active in range(sections - 2, -1, -1):
+        kept, pieces = next_call(incoming, kept, active)
+        if active == 0:
+            break
+        if joint_other is None:
+            joint_other = swap(after(joint, kept[0]), range(1, sections - 1))
+        messages = pl.pallas_call(
+            lambda *refs: send_kernel(chunks, *refs),
+            out_shape=(joined,) * chunks,
+            in_specs=whole(2) + [hbm] * 2,
+            out_specs=whole(chunks),
+            scratch_shapes=[pltpu.VMEM(joint_shape.shape, BF16)] * 2
+            + [pltpu.SemaphoreType.DMA((2,))],
+            compiler_params=kernel_params(),
+            name="send_back",
+        )(*kept, joint, joint_other)
+        incoming = pass_back(messages, active)
+    pieces = share_state(pieces, range(sections - 1))
+
+    parts = project_call(kept[0], pieces)
+    exchanged = [parts[0]]
+    for hop in range(1, chunks):
+        pairs = []
+        for source in range(sections - 1):
+            pairs += within(source, hop)
+        exchanged.append(lax.ppermute(parts[hop], place, pairs))
+    return pl.pallas_call(
+        lambda *refs: carry_kernel(chunks, True, *refs),
+        out_shape=jax.ShapeDtypeStruct((1, length, width), BF16),
+        in_specs=whole(chunks + 1),
+        out_specs=pl.BlockSpec(memory_space=SPACE),
+        compiler_params=kernel_params(),
+        name="carry_last",
+    )(*exchanged, result)
 
 
 def solution(mesh):

time: 249 us -> 214 us (0.86)
  the two profiles are of different devices: /device:TPU:9 before, /device:TPU:11 now
where the time goes in v3:
time: 214 us; the launch traced here: 210 us
  waiting for transfers between devices  108 us (50%)
  starting transfers between devices  54.5 us (25%)
  Pallas kernels  28.3 us (13%)
  local copies, waits for them, and re-layouts  13.3 us (6%)
  other arithmetic  5.69 us (3%)
    ppermute x1, waiting for transfers between devices, relay_body(): lax.ppermute(following, everywhere, by_core(range(sections - 2), hop))  33.9 us
    ppermute x12, waiting for transfers between devices, pass_back(): moved.append(lax.ppermute(messages[hop], place, pairs))  27.1 us
    ppermute x1, waiting for transfers between devices, relay_body(): lax.ppermute(weight_out[0], everywhere, by_core(range(sections - 2), 0))  24.7 us
    ppermute x3, waiting for transfers between devices, relay_body(): exchanged.append(lax.ppermute(parts[hop], place, pairs))  18.3 us
    ppermute x12, starting transfers between devices, pass_back(): moved.append(lax.ppermute(messages[hop], place, pairs))  13.2 us
    ppermute x6, starting transfers between devices, share_state(): shared.append(lax.ppermute(pieces[hop], place, pairs))  11.4 us
    ppermute x3, starting transfers between devices, relay_body(): exchanged.append(lax.ppermute(parts[hop], place, pairs))  11.4 us
    unnamed x21, local copies, waits for them, and re-layouts  9.67 us
  transfers between devices with their start and end apart: 34, of which 13 were waited for; matrix products, arithmetic and copies ran while one was open for 9% of the time, Pallas kernels for 9%

profile of v3, /device:TPU:11, one launch (start us, length us, event | category | flops | bytes accessed | tf_op | source)
XLA Modules:
  0.0 210.4 jit_solution(2517076045696455244)
XLA Ops:
  0.0 5.3 %collective-permute-start.3 = (bf16[256,4096]{1,0:T(8,128)(2,1)}, bf16[256,4096]{1,0:T(8,128)(2,1)S(1)}, u32[]{:S(2)}, u32[]{:S(2)}) collective-permute-start(bf16[256,4096]{1,0:T(8,128)(2,1)} %bitcast.32), channel_id=1, source_target_pairs={{0,8},{1,13},{2,10},{3,15},{4,12},{5,9},{6,14},{7,11},{8,16},{9,21... | collective-permute-start | bytes 6291464 | tf_op jit(solution)/shard_map/ppermute | solution.py:682
  5.3 0.7 collective-permute-start
  6.0 0.7 collective-permute-start.1
  6.6 0.7 collective-permute-start.2
  7.4 0.8 copy.17
  8.2 2.3 %dynamic-slice_bitcast_fusion = (bf16[256,1024]{1,0:T(8,128)(2,1)}, bf16[256,1024]{1,0:T(8,128)(2,1)}) fusion(bf16[1,256,4096]{2,1,0:T(8,128)(2,1)} %param.17, s32[]{:T(128)S(6)} %select_n.20, s32[]{:T(128)S(6)} %select_n.18), kind=kLoop, calls=%fused_computation.1 | loop fusion | bytes 2097160 | tf_op jit(solution)/shard_map/dynamic_slice | solution.py:691
  10.4 1.2 fusion
  11.7 0.7 select_maximum_fusion.refs_6_.refs_13_.refs_4_.refs_12_
  12.4 0.8 copy.28
  13.2 0.7 copy.29
  13.9 2.2 %copy.18 = bf16[1,4,4096]{1,2,0:T(8,128)(2,1)} copy(bf16[1,4,4096]{2,1,0:T(4,128)(2,1)} %param.16) | data formatting | bytes 65536 | tf_op args[2]
  16.1 1.2 forward_residuals.1
  17.4 5.1 %copy.23 = bf16[512,8,2,256]{3,1,2,0:T(8,128)(2,1)} copy(bf16[512,8,2,256]{3,2,1,0:T(2,128)(2,1)} %bitcast.51) | data formatting | bytes 8388608
  22.7 0.7 collective-permute-start.4
  23.4 0.7 collective-permute-start.9
  24.2 2.1 section_first.1
  26.2 24.7 %collective-permute-done.3.rows_ref.refs_0_ = bf16[256,4096]{1,0:T(8,128)(2,1)S(1)} collective-permute-done((bf16[256,4096]{1,0:T(8,128)(2,1)}, bf16[256,4096]{1,0:T(8,128)(2,1)S(1)}, u32[]{:S(2)}, u32[]{:S(2)}) %collective-permute-start.3) | collective-permute-done | bytes 2097184 | tf_op jit(solution)/shard_map/ppermute | solution.py:682
  53.0 4.4 %collective-permute-start.18 = (bf16[256,4096]{1,0:T(8,128)(2,1)S(1)}, bf16[256,4096]{1,0:T(8,128)(2,1)S(1)}, u32[]{:S(2)}, u32[]{:S(2)}) collective-permute-start(bf16[256,4096]{1,0:T(8,128)(2,1)S(1)} %bitcast.34), channel_id=1, source_target_pairs={{0,10},{1,15},{2,12},{3,9},{4,14},{5,11},{6,8},{7,13},{8,18},{9,23... | collective-permute-start | bytes 6291464 | tf_op jit(solution)/shard_map/ppermute | solution.py:772
  57.4 0.8 collective-permute-start.8
  58.2 0.7 collective-permute-start.10
  58.9 5.0 %pad_maximum_fusion.refs_6_.cols_ref.refs_3_ = bf16[4096,640]{1,0:T(8,128)(2,1)} fusion(bf16[4096,128]{1,0:T(8,128)(2,1)S(1)} %pad.18, bf16[4096,512]{1,0:T(8,128)(2,1)} %bitcast.49), kind=kLoop, calls=%fused_computation | loop fusion | flops 10485760 | bytes 10485760 | tf_op jit(solution)/shard_map/concatenate | solution.py:731
  63.9 3.9 %project.2 = (bf16[128,1024]{1,0:T(8,128)(2,1)S(1)}, bf16[128,1024]{1,0:T(8,128)(2,1)S(1)}, bf16[128,1024]{1,0:T(8,128)(2,1)S(1)}, bf16[128,1024]{1,0:T(8,128)(2,1)S(1)}) custom-call(bf16[128,640]{1,0:T(8,128)(2,1)S(1)} %get-tuple-element.77.refs_0_, bf16[128,128]{1,0:T(8,128)(2,1)S(1)} %get-tuple-element.93.refs_1_, ...), custom_call_target="tpu_custom_call" | custom-call | tf_op jit(solution)/shard_map/project/pallas_call | solution.py:756
  67.8 0.7 collective-permute-start.11
  68.5 0.7 collective-permute-start.12
  69.2 0.7 collective-permute-start.13
  69.8 4.8 %compose_weights.1.refs_2_ = bf16[256,640]{1,0:T(8,128)(2,1)S(1)} custom-call(bf16[256,4096]{1,0:T(8,128)(2,1)S(1)} %collective-permute-done.3.rows_ref.refs_0_, bf16[4096,640]{1,0:T(8,128)(2,1)} %pad_maximum_fusion.refs_6_.cols_ref.refs_3_), custom_call_target="tpu_custom_call" | custom-call | tf_op jit(solution)/shard_map/compose_weights/pallas_call | solution.py:789
  74.7 0.8 carry_next.1
  75.5 0.7 collective-permute-start.14
  76.2 0.7 collective-permute-start.15
  76.9 0.7 collective-permute-start.16
  77.5 0.7 collective-permute-start.17
  78.2 33.9 %collective-permute-done.18.refs_1_ = bf16[256,4096]{1,0:T(8,128)(2,1)S(1)} collective-permute-done((bf16[256,4096]{1,0:T(8,128)(2,1)S(1)}, bf16[256,4096]{1,0:T(8,128)(2,1)S(1)}, u32[]{:S(2)}, u32[]{:S(2)}) %collective-permute-start.18) | collective-permute-done | bytes 2097184 | tf_op jit(solution)/shard_map/ppermute | solution.py:772
  112.2 5.6 %compose_last.1.refs_2_ = bf16[320,1280]{1,0:T(8,128)(2,1)S(1)} custom-call(bf16[256,4096]{1,0:T(8,128)(2,1)S(1)} %collective-permute-done.3.rows_ref.refs_0_, bf16[256,4096]{1,0:T(8,128)(2,1)S(1)} %collective-permute-done.18.refs_1_, bf16[256,640]{1,0:T(8,128)(2,1)S(1)} %compose_weights.1.refs_2_, ...), custom_call_target="tpu_custom_call" | custom-call | tf_op jit(solution)/shard_map/compose_last/pallas_call | solution.py:821
  117.8 0.7 section_next.3
  118.6 1.9 collective-permute-start.19
  120.5 2.3 %collective-permute-done.19.refs_3_ = bf16[320,1280]{1,0:T(8,128)(2,1)S(1)} collective-permute-done((bf16[320,1280]{1,0:T(8,128)(2,1)S(1)}, bf16[320,1280]{1,0:T(8,128)(2,1)S(1)}, u32[]{:S(2)}, u32[]{:S(2)}) %collective-permute-start.19) | collective-permute-done | bytes 819232 | tf_op jit(solution)/shard_map/ppermute | solution.py:676
  122.8 0.8 send_back.2
  123.6 1.3 collective-permute-start.20
  124.9 1.3 collective-permute-start.21
  126.2 1.3 collective-permute-start.22
  127.5 1.5 collective-permute-start.23
  129.0 6.6 %collective-permute-done.20.refs_0_ = bf16[128,640]{1,0:T(8,128)(2,1)S(1)} collective-permute-done((bf16[128,640]{1,0:T(8,128)(2,1)S(1)}, bf16[128,640]{1,0:T(8,128)(2,1)S(1)}, u32[]{:S(2)}, u32[]{:S(2)}) %collective-permute-start.20) | collective-permute-done | bytes 163872 | tf_op jit(solution)/shard_map/ppermute | solution.py:807
  135.6 5.5 %collective-permute-done.22.refs_2_ = bf16[128,640]{1,0:T(8,128)(2,1)S(1)} collective-permute-done((bf16[128,640]{1,0:T(8,128)(2,1)S(1)}, bf16[128,640]{1,0:T(8,128)(2,1)S(1)}, u32[]{:S(2)}, u32[]{:S(2)}) %collective-permute-start.22) | collective-permute-done | bytes 163872 | tf_op jit(solution)/shard_map/ppermute | solution.py:807
  141.0 2.7 %collective-permute-done.23.refs_3_ = bf16[128,640]{1,0:T(8,128)(2,1)S(1)} collective-permute-done((bf16[128,640]{1,0:T(8,128)(2,1)S(1)}, bf16[128,640]{1,0:T(8,128)(2,1)S(1)}, u32[]{:S(2)}, u32[]{:S(2)}) %collective-permute-start.23) | collective-permute-done | bytes 163872 | tf_op jit(solution)/shard_map/ppermute | solution.py:807
  143.7 1.1 section_next.4
  144.8 0.8 send_back.3
  145.6 1.3 collective-permute-start.24
  146.9 1.3 collective-permute-start.25
  148.2 1.3 collective-permute-start.26
  149.5 1.3 collective-permute-start.27
  151.1 8.4 %collective-permute-done.26.refs_2_ = bf16[128,640]{1,0:T(8,128)(2,1)S(1)} collective-permute-done((bf16[128,640]{1,0:T(8,128)(2,1)S(1)}, bf16[128,640]{1,0:T(8,128)(2,1)S(1)}, u32[]{:S(2)}, u32[]{:S(2)}) %collective-permute-start.26) | collective-permute-done | bytes 163872 | tf_op jit(solution)/shard_map/ppermute | solution.py:807
  159.5 3.7 %collective-permute-done.27.refs_3_ = bf16[128,640]{1,0:T(8,128)(2,1)S(1)} collective-permute-done((bf16[128,640]{1,0:T(8,128)(2,1)S(1)}, bf16[128,640]{1,0:T(8,128)(2,1)S(1)}, u32[]{:S(2)}, u32[]{:S(2)}) %collective-permute-start.27) | collective-permute-done | bytes 163872 | tf_op jit(solution)/shard_map/ppermute | solution.py:807
  163.2 1.8 section_next.5
  165.0 4.4 %collective-permute-start.28 = (bf16[128,128]{1,0:T(8,128)(2,1)S(1)}, bf16[128,128]{1,0:T(8,128)(2,1)S(1)}, u32[]{:S(2)}, u32[]{:S(2)}) collective-permute-start(bf16[128,128]{1,0:T(8,128)(2,1)S(1)} %get-tuple-element.123), channel_id=1, source_target_pairs={{0,2},{2,4},{4,6},{6,0},{8,10},{10,12},{12,14},{14,8},{16,18},{18,... | collective-permute-start | bytes 98312 | tf_op jit(solution)/shard_map/ppermute | solution.py:752
  169.4 1.9 collective-permute-start.29
  171.3 3.1 %collective-permute-start.30 = (bf16[128,128]{1,0:T(8,128)(2,1)S(1)}, bf16[128,128]{1,0:T(8,128)(2,1)S(1)}, u32[]{:S(2)}, u32[]{:S(2)}) collective-permute-start(bf16[128,128]{1,0:T(8,128)(2,1)S(1)} %get-tuple-element.125), channel_id=1, source_target_pairs={{0,6},{2,0},{4,2},{6,4},{8,14},{10,8},{12,10},{14,12},{16,22},{18,... | collective-permute-start | bytes 98312 | tf_op jit(solution)/shard_map/ppermute | solution.py:752
  175.1 0.9 collective-permute-done.30.refs_4_
  176.0 3.9 %project.3 = (bf16[128,1024]{1,0:T(8,128)(2,1)S(1)}, bf16[128,1024]{1,0:T(8,128)(2,1)S(1)}, bf16[128,1024]{1,0:T(8,128)(2,1)S(1)}, bf16[128,1024]{1,0:T(8,128)(2,1)S(1)}) custom-call(bf16[128,640]{1,0:T(8,128)(2,1)S(1)} %get-tuple-element.121.refs_0_, bf16[128,128]{1,0:T(8,128)(2,1)S(1)} %get-tuple-element.122.refs_1_, ...), custom_call_target="tpu_custom_call" | custom-call | tf_op jit(solution)/shard_map/project/pallas_call | solution.py:756
  179.8 3.3 %collective-permute-start.31 = (bf16[128,1024]{1,0:T(8,128)(2,1)S(1)}, bf16[128,1024]{1,0:T(8,128)(2,1)S(1)}, u32[]{:S(2)}, u32[]{:S(2)}) collective-permute-start(bf16[128,1024]{1,0:T(8,128)(2,1)S(1)} %get-tuple-element.127), channel_id=1, source_target_pairs={{0,2},{2,4},{4,6},{6,0},{8,10},{10,12},{12,14},{14,8},{16,18},{18,... | collective-permute-start | bytes 786440 | tf_op jit(solution)/shard_map/ppermute | solution.py:881
  183.1 4.7 %collective-permute-start.32 = (bf16[128,1024]{1,0:T(8,128)(2,1)S(1)}, bf16[128,1024]{1,0:T(8,128)(2,1)S(1)}, u32[]{:S(2)}, u32[]{:S(2)}) collective-permute-start(bf16[128,1024]{1,0:T(8,128)(2,1)S(1)} %get-tuple-element.128), channel_id=1, source_target_pairs={{0,4},{2,6},{4,0},{6,2},{8,12},{10,14},{12,8},{14,10},{16,20},{18,... | collective-permute-start | bytes 786440 | tf_op jit(solution)/shard_map/ppermute | solution.py:881
  187.8 3.4 %collective-permute-start.33 = (bf16[128,1024]{1,0:T(8,128)(2,1)S(1)}, bf16[128,1024]{1,0:T(8,128)(2,1)S(1)}, u32[]{:S(2)}, u32[]{:S(2)}) collective-permute-start(bf16[128,1024]{1,0:T(8,128)(2,1)S(1)} %get-tuple-element.129), channel_id=1, source_target_pairs={{0,6},{2,0},{4,2},{6,4},{8,14},{10,8},{12,10},{14,12},{16,22},{18,... | collective-permute-start | bytes 786440 | tf_op jit(solution)/shard_map/ppermute | solution.py:881
  191.2 14.0 %collective-permute-done.32.refs_2_ = bf16[128,1024]{1,0:T(8,128)(2,1)S(1)} collective-permute-done((bf16[128,1024]{1,0:T(8,128)(2,1)S(1)}, bf16[128,1024]{1,0:T(8,128)(2,1)S(1)}, u32[]{:S(2)}, u32[]{:S(2)}) %collective-permute-start.32) | collective-permute-done | bytes 262176 | tf_op jit(solution)/shard_map/ppermute | solution.py:881
  205.2 4.3 %collective-permute-done.33.refs_3_ = bf16[128,1024]{1,0:T(8,128)(2,1)S(1)} collective-permute-done((bf16[128,1024]{1,0:T(8,128)(2,1)S(1)}, bf16[128,1024]{1,0:T(8,128)(2,1)S(1)}, u32[]{:S(2)}, u32[]{:S(2)}) %collective-permute-start.33) | collective-permute-done | bytes 262176 | tf_op jit(solution)/shard_map/ppermute | solution.py:881
  209.5 0.8 carry_last.1
  (45 shorter events, 3.2 us)
Async XLA Ops:
  0.0 16.1 %copy-start.3 = (f32[1,4,256]{2,1,0:T(4,128)S(1)}, f32[1,4,256]{2,1,0:T(4,128)}, u32[]{:S(2)}) copy-start(f32[1,4,256]{2,1,0:T(4,128)} %param.18) | copy-start | bytes 12292
  0.0 16.1 %copy-start.4 = (f32[1,256]{1,0:T(1,128)S(1)}, f32[1,256]{1,0:T(1,128)}, u32[]{:S(2)}) copy-start(f32[1,256]{1,0:T(1,128)} %refs_7_.1) | copy-start | bytes 3076
  0.0 50.9 %collective-permute-start.3 = (bf16[256,4096]{1,0:T(8,128)(2,1)}, bf16[256,4096]{1,0:T(8,128)(2,1)S(1)}, u32[]{:S(2)}, u32[]{:S(2)}) collective-permute-start(bf16[256,4096]{1,0:T(8,128)(2,1)} %bitcast.32), channel_id=1, source_target_pairs={{0,8},{1,13},{2,10},{3,15},{4,12},{5,9},{6,14},{7,11},{8,16},{9,21... | collective-permute-start | bytes 6291464 | tf_op jit(solution)/shard_map/ppermute | solution.py:682
  5.3 12.0 %collective-permute-start = (bf16[128,1024]{1,0:T(8,128)(2,1)}, bf16[128,1024]{1,0:T(8,128)(2,1)S(1)}, u32[]{:S(2)}, u32[]{:S(2)}) collective-permute-start(bf16[128,1024]{1,0:T(8,128)(2,1)} %refs_0_.1), channel_id=1, source_target_pairs={{24,26},{26,28},{28,30},{30,24},{25,27},{27,29},{29,31},{31,25}} | collective-permute-start | bytes 786440 | tf_op jit(solution)/shard_map/ppermute | solution.py:680
  6.0 16.7 %collective-permute-start.1 = (bf16[128,1024]{1,0:T(8,128)(2,1)}, bf16[128,1024]{1,0:T(8,128)(2,1)S(1)}, u32[]{:S(2)}, u32[]{:S(2)}) collective-permute-start(bf16[128,1024]{1,0:T(8,128)(2,1)} %refs_0_.1), channel_id=1, source_target_pairs={{24,28},{26,30},{28,24},{30,26},{25,29},{27,31},{29,25},{31,27}} | collective-permute-start | bytes 786440 | tf_op jit(solution)/shard_map/ppermute | solution.py:680
  6.6 16.1 %collective-permute-start.2 = (bf16[128,1024]{1,0:T(8,128)(2,1)}, bf16[128,1024]{1,0:T(8,128)(2,1)S(1)}, u32[]{:S(2)}, u32[]{:S(2)}) collective-permute-start(bf16[128,1024]{1,0:T(8,128)(2,1)} %refs_0_.1), channel_id=1, source_target_pairs={{24,30},{26,24},{28,26},{30,28},{25,31},{27,25},{29,27},{31,29}} | collective-permute-start | bytes 786440 | tf_op jit(solution)/shard_map/ppermute | solution.py:680
  17.3 5.2 %copy-start.5 = (bf16[1,4,4096]{1,2,0:T(8,128)(2,1)S(1)}, bf16[1,4,4096]{1,2,0:T(8,128)(2,1)}, u32[]{:S(2)}) copy-start(bf16[1,4,4096]{1,2,0:T(8,128)(2,1)} %copy.18) | copy-start | bytes 98308
  17.3 5.4 %copy-start.7 = (bf16[256,1024]{1,0:T(8,128)(2,1)S(1)}, bf16[256,1024]{1,0:T(8,128)(2,1)}, u32[]{:S(2)}) copy-start(bf16[256,1024]{1,0:T(8,128)(2,1)} %get-tuple-element.85) | copy-start | bytes 1572868
  17.3 6.1 %copy-start.6 = (bf16[256,1024]{1,0:T(8,128)(2,1)S(1)}, bf16[256,1024]{1,0:T(8,128)(2,1)}, u32[]{:S(2)}) copy-start(bf16[256,1024]{1,0:T(8,128)(2,1)} %get-tuple-element.91) | copy-start | bytes 1572868
  17.4 6.8 %copy-start = (bf16[1,256,4096]{2,1,0:T(8,128)(2,1)S(1)}, bf16[1,256,4096]{2,1,0:T(8,128)(2,1)}, u32[]{:S(2)}) copy-start(bf16[1,256,4096]{2,1,0:T(8,128)(2,1)} %param.17) | copy-start | bytes 6291460
  17.4 6.8 %copy-start.2 = (bf16[128,1024]{1,0:T(8,128)(2,1)S(1)}, bf16[128,1024]{1,0:T(8,128)(2,1)}, u32[]{:S(2)}) copy-start(bf16[128,1024]{1,0:T(8,128)(2,1)} %refs_0_.1) | copy-start | bytes 786436
  22.7 30.2 %collective-permute-start.4 = (bf16[256,1024]{1,0:T(8,128)(2,1)S(1)}, bf16[256,1024]{1,0:T(8,128)(2,1)S(1)}, u32[]{:S(2)}, u32[]{:S(2)}) collective-permute-start(bf16[256,1024]{1,0:T(8,128)(2,1)S(1)} %copy-done.7), channel_id=1, source_target_pairs={{16,24},{17,29},{18,26},{19,31},{20,28},{21,25},{22,30},{23,27}} | collective-permute-start | bytes 1572872 | tf_op jit(solution)/shard_map/ppermute | solution.py:736
  23.4 29.5 %collective-permute-start.9 = (bf16[256,1024]{1,0:T(8,128)(2,1)S(1)}, bf16[256,1024]{1,0:T(8,128)(2,1)S(1)}, u32[]{:S(2)}, u32[]{:S(2)}) collective-permute-start(bf16[256,1024]{1,0:T(8,128)(2,1)S(1)} %copy-done.6), channel_id=1, source_target_pairs={{16,26},{17,31},{18,28},{19,25},{20,30},{21,27},{22,24},{23,29}} | collective-permute-start | bytes 1572872 | tf_op jit(solution)/shard_map/ppermute | solution.py:736
  50.9 2.0 collective-permute-start.5
  51.6 1.4 collective-permute-start.6
  52.2 0.7 collective-permute-start.7
  53.0 59.2 %collective-permute-start.18 = (bf16[256,4096]{1,0:T(8,128)(2,1)S(1)}, bf16[256,4096]{1,0:T(8,128)(2,1)S(1)}, u32[]{:S(2)}, u32[]{:S(2)}) collective-permute-start(bf16[256,4096]{1,0:T(8,128)(2,1)S(1)} %bitcast.34), channel_id=1, source_target_pairs={{0,10},{1,15},{2,12},{3,9},{4,14},{5,11},{6,8},{7,13},{8,18},{9,23... | collective-permute-start | bytes 6291464 | tf_op jit(solution)/shard_map/ppermute | solution.py:772
  57.4 6.5 %copy-start.1 = (bf16[1,4096,2,32]{1,3,2,0:T(8,128)(2,1)S(1)}, bf16[1,4096,2,32]{1,3,2,0:T(8,128)(2,1)}, u32[]{:S(2)}) copy-start(bf16[1,4096,2,32]{1,3,2,0:T(8,128)(2,1)} %param.15) | copy-start | bytes 1572868
  57.4 6.5 %collective-permute-start.8 = (bf16[256,1024]{1,0:T(8,128)(2,1)S(1)}, bf16[256,1024]{1,0:T(8,128)(2,1)S(1)}, u32[]{:S(2)}, u32[]{:S(2)}) collective-permute-start(bf16[256,1024]{1,0:T(8,128)(2,1)S(1)} %collective-permute-done.4.refs_5_), channel_id=1, source_target_pairs={{24,25},{25,24},{26,27},{27,26},{28,29},{29,28},{30,31},{31,30}} | collective-permute-start | bytes 1572872 | tf_op jit(solution)/shard_map/ppermute | solution.py:676
  58.2 5.7 %collective-permute-start.10 = (bf16[256,1024]{1,0:T(8,128)(2,1)S(1)}, bf16[256,1024]{1,0:T(8,128)(2,1)S(1)}, u32[]{:S(2)}, u32[]{:S(2)}) collective-permute-start(bf16[256,1024]{1,0:T(8,128)(2,1)S(1)} %collective-permute-done.9.refs_6_), channel_id=1, source_target_pairs={{24,25},{25,24},{26,27},{27,26},{28,29},{29,28},{30,31},{31,30}} | collective-permute-start | bytes 1572872 | tf_op jit(solution)/shard_map/ppermute | solution.py:676
  67.8 6.9 %collective-permute-start.11 = (bf16[128,1024]{1,0:T(8,128)(2,1)S(1)}, bf16[128,1024]{1,0:T(8,128)(2,1)S(1)}, u32[]{:S(2)}, u32[]{:S(2)}) collective-permute-start(bf16[128,1024]{1,0:T(8,128)(2,1)S(1)} %get-tuple-element.96), channel_id=1, source_target_pairs={{24,26},{26,28},{28,30},{30,24},{25,27},{27,29},{29,31},{31,25}} | collective-permute-start | bytes 786440 | tf_op jit(solution)/shard_map/ppermute | solution.py:780
  68.5 6.2 %collective-permute-start.12 = (bf16[128,1024]{1,0:T(8,128)(2,1)S(1)}, bf16[128,1024]{1,0:T(8,128)(2,1)S(1)}, u32[]{:S(2)}, u32[]{:S(2)}) collective-permute-start(bf16[128,1024]{1,0:T(8,128)(2,1)S(1)} %get-tuple-element.97), channel_id=1, source_target_pairs={{24,28},{26,30},{28,24},{30,26},{25,29},{27,31},{29,25},{31,27}} | collective-permute-start | bytes 786440 | tf_op jit(solution)/shard_map/ppermute | solution.py:780
  69.2 5.5 %collective-permute-start.13 = (bf16[128,1024]{1,0:T(8,128)(2,1)S(1)}, bf16[128,1024]{1,0:T(8,128)(2,1)S(1)}, u32[]{:S(2)}, u32[]{:S(2)}) collective-permute-start(bf16[128,1024]{1,0:T(8,128)(2,1)S(1)} %get-tuple-element.98), channel_id=1, source_target_pairs={{24,30},{26,24},{28,26},{30,28},{25,31},{27,25},{29,27},{31,29}} | collective-permute-start | bytes 786440 | tf_op jit(solution)/shard_map/ppermute | solution.py:780
  75.5 42.2 %collective-permute-start.14 = (bf16[128,256]{1,0:T(8,128)(2,1)S(1)}, bf16[128,256]{1,0:T(8,128)(2,1)S(1)}, u32[]{:S(2)}, u32[]{:S(2)}) collective-permute-start(bf16[128,256]{1,0:T(8,128)(2,1)S(1)} %get-tuple-element.101), channel_id=1, source_target_pairs={{24,16},{26,18},{28,20},{30,22},{25,17},{27,19},{29,21},{31,23}} | collective-permute-start | bytes 196616 | tf_op jit(solution)/shard_map/ppermute | solution.py:807
  76.2 41.6 %collective-permute-start.15 = (bf16[128,256]{1,0:T(8,128)(2,1)S(1)}, bf16[128,256]{1,0:T(8,128)(2,1)S(1)}, u32[]{:S(2)}, u32[]{:S(2)}) collective-permute-start(bf16[128,256]{1,0:T(8,128)(2,1)S(1)} %get-tuple-element.102), channel_id=1, source_target_pairs={{24,22},{26,16},{28,18},{30,20},{25,23},{27,17},{29,19},{31,21}} | collective-permute-start | bytes 196616 | tf_op jit(solution)/shard_map/ppermute | solution.py:807
  76.9 40.9 %collective-permute-start.16 = (bf16[128,256]{1,0:T(8,128)(2,1)S(1)}, bf16[128,256]{1,0:T(8,128)(2,1)S(1)}, u32[]{:S(2)}, u32[]{:S(2)}) collective-permute-start(bf16[128,256]{1,0:T(8,128)(2,1)S(1)} %get-tuple-element.103), channel_id=1, source_target_pairs={{24,20},{26,22},{28,16},{30,18},{25,21},{27,23},{29,17},{31,19}} | collective-permute-start | bytes 196616 | tf_op jit(solution)/shard_map/ppermute | solution.py:807
  77.5 40.2 %collective-permute-start.17 = (bf16[128,256]{1,0:T(8,128)(2,1)S(1)}, bf16[128,256]{1,0:T(8,128)(2,1)S(1)}, u32[]{:S(2)}, u32[]{:S(2)}) collective-permute-start(bf16[128,256]{1,0:T(8,128)(2,1)S(1)} %get-tuple-element.104), channel_id=1, source_target_pairs={{24,18},{26,20},{28,22},{30,16},{25,19},{27,21},{29,23},{31,17}} | collective-permute-start | bytes 196616 | tf_op jit(solution)/shard_map/ppermute | solution.py:807
  118.6 4.2 %collective-permute-start.19 = (bf16[320,1280]{1,0:T(8,128)(2,1)S(1)}, bf16[320,1280]{1,0:T(8,128)(2,1)S(1)}, u32[]{:S(2)}, u32[]{:S(2)}) collective-permute-start(bf16[320,1280]{1,0:T(8,128)(2,1)S(1)} %compose_last.1.refs_2_), channel_id=1, source_target_pairs={{8,9},{9,8},{10,11},{11,10},{12,13},{13,12},{14,15},{15,14},{16,17... | collective-permute-start | bytes 2457608 | tf_op jit(solution)/shard_map/ppermute | solution.py:676
  123.6 12.0 %collective-permute-start.20 = (bf16[128,640]{1,0:T(8,128)(2,1)S(1)}, bf16[128,640]{1,0:T(8,128)(2,1)S(1)}, u32[]{:S(2)}, u32[]{:S(2)}) collective-permute-start(bf16[128,640]{1,0:T(8,128)(2,1)S(1)} %get-tuple-element.111), channel_id=1, source_target_pairs={{16,8},{18,10},{20,12},{22,14},{17,9},{19,11},{21,13},{23,15}} | collective-permute-start | bytes 491528 | tf_op jit(solution)/shard_map/ppermute | solution.py:807
  124.9 10.7 %collective-permute-start.21 = (bf16[128,640]{1,0:T(8,128)(2,1)S(1)}, bf16[128,640]{1,0:T(8,128)(2,1)S(1)}, u32[]{:S(2)}, u32[]{:S(2)}) collective-permute-start(bf16[128,640]{1,0:T(8,128)(2,1)S(1)} %get-tuple-element.112), channel_id=1, source_target_pairs={{16,14},{18,8},{20,10},{22,12},{17,15},{19,9},{21,11},{23,13}} | collective-permute-start | bytes 491528 | tf_op jit(solution)/shard_map/ppermute | solution.py:807
  126.2 14.8 %collective-permute-start.22 = (bf16[128,640]{1,0:T(8,128)(2,1)S(1)}, bf16[128,640]{1,0:T(8,128)(2,1)S(1)}, u32[]{:S(2)}, u32[]{:S(2)}) collective-permute-start(bf16[128,640]{1,0:T(8,128)(2,1)S(1)} %get-tuple-element.113), channel_id=1, source_target_pairs={{16,12},{18,14},{20,8},{22,10},{17,13},{19,15},{21,9},{23,11}} | collective-permute-start | bytes 491528 | tf_op jit(solution)/shard_map/ppermute | solution.py:807
  127.5 16.2 %collective-permute-start.23 = (bf16[128,640]{1,0:T(8,128)(2,1)S(1)}, bf16[128,640]{1,0:T(8,128)(2,1)S(1)}, u32[]{:S(2)}, u32[]{:S(2)}) collective-permute-start(bf16[128,640]{1,0:T(8,128)(2,1)S(1)} %get-tuple-element.114), channel_id=1, source_target_pairs={{16,10},{18,12},{20,14},{22,8},{17,11},{19,13},{21,15},{23,9}} | collective-permute-start | bytes 491528 | tf_op jit(solution)/shard_map/ppermute | solution.py:807
  145.6 5.2 %collective-permute-start.24 = (bf16[128,640]{1,0:T(8,128)(2,1)S(1)}, bf16[128,640]{1,0:T(8,128)(2,1)S(1)}, u32[]{:S(2)}, u32[]{:S(2)}) collective-permute-start(bf16[128,640]{1,0:T(8,128)(2,1)S(1)} %get-tuple-element.117), channel_id=1, source_target_pairs={{8,0},{10,2},{12,4},{14,6},{9,1},{11,3},{13,5},{15,7}} | collective-permute-start | bytes 491528 | tf_op jit(solution)/shard_map/ppermute | solution.py:807
  146.9 4.2 %collective-permute-start.25 = (bf16[128,640]{1,0:T(8,128)(2,1)S(1)}, bf16[128,640]{1,0:T(8,128)(2,1)S(1)}, u32[]{:S(2)}, u32[]{:S(2)}) collective-permute-start(bf16[128,640]{1,0:T(8,128)(2,1)S(1)} %get-tuple-element.118), channel_id=1, source_target_pairs={{8,6},{10,0},{12,2},{14,4},{9,7},{11,1},{13,3},{15,5}} | collective-permute-start | bytes 491528 | tf_op jit(solution)/shard_map/ppermute | solution.py:807
  148.2 11.3 %collective-permute-start.26 = (bf16[128,640]{1,0:T(8,128)(2,1)S(1)}, bf16[128,640]{1,0:T(8,128)(2,1)S(1)}, u32[]{:S(2)}, u32[]{:S(2)}) collective-permute-start(bf16[128,640]{1,0:T(8,128)(2,1)S(1)} %get-tuple-element.119), channel_id=1, source_target_pairs={{8,4},{10,6},{12,0},{14,2},{9,5},{11,7},{13,1},{15,3}} | collective-permute-start | bytes 491528 | tf_op jit(solution)/shard_map/ppermute | solution.py:807
  149.5 13.6 %collective-permute-start.27 = (bf16[128,640]{1,0:T(8,128)(2,1)S(1)}, bf16[128,640]{1,0:T(8,128)(2,1)S(1)}, u32[]{:S(2)}, u32[]{:S(2)}) collective-permute-start(bf16[128,640]{1,0:T(8,128)(2,1)S(1)} %get-tuple-element.120), channel_id=1, source_target_pairs={{8,2},{10,4},{12,6},{14,0},{9,3},{11,5},{13,7},{15,1}} | collective-permute-start | bytes 491528 | tf_op jit(solution)/shard_map/ppermute | solution.py:807
  165.0 9.5 %collective-permute-start.28 = (bf16[128,128]{1,0:T(8,128)(2,1)S(1)}, bf16[128,128]{1,0:T(8,128)(2,1)S(1)}, u32[]{:S(2)}, u32[]{:S(2)}) collective-permute-start(bf16[128,128]{1,0:T(8,128)(2,1)S(1)} %get-tuple-element.123), channel_id=1, source_target_pairs={{0,2},{2,4},{4,6},{6,0},{8,10},{10,12},{12,14},{14,8},{16,18},{18,... | collective-permute-start | bytes 98312 | tf_op jit(solution)/shard_map/ppermute | solution.py:752
  169.4 5.7 %collective-permute-start.29 = (bf16[128,128]{1,0:T(8,128)(2,1)S(1)}, bf16[128,128]{1,0:T(8,128)(2,1)S(1)}, u32[]{:S(2)}, u32[]{:S(2)}) collective-permute-start(bf16[128,128]{1,0:T(8,128)(2,1)S(1)} %get-tuple-element.124), channel_id=1, source_target_pairs={{0,4},{2,6},{4,0},{6,2},{8,12},{10,14},{12,8},{14,10},{16,20},{18,... | collective-permute-start | bytes 98312 | tf_op jit(solution)/shard_map/ppermute | solution.py:752
  171.3 4.7 %collective-permute-start.30 = (bf16[128,128]{1,0:T(8,128)(2,1)S(1)}, bf16[128,128]{1,0:T(8,128)(2,1)S(1)}, u32[]{:S(2)}, u32[]{:S(2)}) collective-permute-start(bf16[128,128]{1,0:T(8,128)(2,1)S(1)} %get-tuple-element.125), channel_id=1, source_target_pairs={{0,6},{2,0},{4,2},{6,4},{8,14},{10,8},{12,10},{14,12},{16,22},{18,... | collective-permute-start | bytes 98312 | tf_op jit(solution)/shard_map/ppermute | solution.py:752
  179.8 11.4 %collective-permute-start.31 = (bf16[128,1024]{1,0:T(8,128)(2,1)S(1)}, bf16[128,1024]{1,0:T(8,128)(2,1)S(1)}, u32[]{:S(2)}, u32[]{:S(2)}) collective-permute-start(bf16[128,1024]{1,0:T(8,128)(2,1)S(1)} %get-tuple-element.127), channel_id=1, source_target_pairs={{0,2},{2,4},{4,6},{6,0},{8,10},{10,12},{12,14},{14,8},{16,18},{18,... | collective-permute-start | bytes 786440 | tf_op jit(solution)/shard_map/ppermute | solution.py:881
  183.1 22.1 %collective-permute-start.32 = (bf16[128,1024]{1,0:T(8,128)(2,1)S(1)}, bf16[128,1024]{1,0:T(8,128)(2,1)S(1)}, u32[]{:S(2)}, u32[]{:S(2)}) collective-permute-start(bf16[128,1024]{1,0:T(8,128)(2,1)S(1)} %get-tuple-element.128), channel_id=1, source_target_pairs={{0,4},{2,6},{4,0},{6,2},{8,12},{10,14},{12,8},{14,10},{16,20},{18,... | collective-permute-start | bytes 786440 | tf_op jit(solution)/shard_map/ppermute | solution.py:881
  187.8 21.7 %collective-permute-start.33 = (bf16[128,1024]{1,0:T(8,128)(2,1)S(1)}, bf16[128,1024]{1,0:T(8,128)(2,1)S(1)}, u32[]{:S(2)}, u32[]{:S(2)}) collective-permute-start(bf16[128,1024]{1,0:T(8,128)(2,1)S(1)} %get-tuple-element.129), channel_id=1, source_target_pairs={{0,6},{2,0},{4,2},{6,4},{8,14},{10,8},{12,10},{14,12},{16,22},{18,... | collective-permute-start | bytes 786440 | tf_op jit(solution)/shard_map/ppermute | solution.py:881

commit v4 on v3

--- a/solution.py
+++ b/solution.py
@@ -410,30 +410,22 @@
     rows_ref, refs = refs[0], refs[1:]
     residuals, refs = refs[:9], refs[9:]
     main_ref, outs = refs[0], refs[1:]
-    me = lax.axis_index("tensor")
-    width = incoming[0].shape[1]
-    dnormed = None
-    for hop in range(chunks):
-        chunk = lax.rem(me + chunks - hop, chunks)
-        term = dot_nt(
-            incoming[hop][...], rows_ref[:, pl.ds(pl.multiple_of(chunk * width, width), width)]
-        )
-        dnormed = term if dnormed is None else dnormed + term
+    dnormed = gathered_product(chunks, lax.axis_index("tensor"), incoming, rows_ref)
     main, state = mixer_back(heads, dnormed, residuals)
     main_ref[...] = main
     for out, piece in zip(outs, picked_members(chunks, state)):
         out[...] = piece
 
 
-def next_kernel(heads, chunks, active, *refs):
-    incoming, refs = refs[:chunks], refs[chunks:]
+def next_kernel(heads, chunks, count, active, *refs):
+    incoming, refs = refs[:count], refs[count:]
     residuals, refs = refs[:9], refs[9:]
     channels = residuals[0].shape[2]
     dnormed = incoming[0][:, :channels].astype(F32)
-    for hop in range(1, chunks):
-        dnormed = dnormed + incoming[hop][:, :channels].astype(F32)
+    for message in incoming[1:]:
+        dnormed = dnormed + message[:, :channels].astype(F32)
     states = residuals[4].shape[2] * 2
-    joined = incoming[0].shape[1] > channels
+    joined = count > 1
     if joined:
         place = slice(channels, channels + states)
         state = incoming[0][:, place].astype(F32)
@@ -454,7 +446,7 @@
         refs = refs[2:]
     refs[0][...] = main
     refs[1][...] = state
-    if active == 0:
+    if joined:
         for ref, piece in zip(refs[2:], picked_members(chunks, state)):
             ref[...] = piece
 
@@ -466,10 +458,15 @@
     return total.astype(BF16)[:, :width]
 
 
-def project_kernel(chunks, *refs):
+def project_kernel(chunks, final, *refs):
     main_ref, refs = refs[0], refs[1:]
     pieces, refs = refs[:chunks], refs[chunks:]
-    state_cols_ref, cols_ref, refs = refs[0], refs[1], refs[2:]
+    count = chunks if final else 0
+    newest, refs = refs[:count], refs[count:]
+    state_ref, refs = refs[0], refs[1:]
+    if final:
+        own_ref, other_ref, refs = refs[0], refs[1], refs[2:]
+    cols_ref, refs = refs[0], refs[1:]
     outs, refs = refs[:chunks], refs[chunks:]
     cols, sems = refs
     me = lax.axis_index("tensor")
@@ -483,55 +480,62 @@
         places.append(place)
         copies.append(copy)
     main = main_ref[...]
-    state = sum_pieces(pieces, pieces[0].shape[1])
-    state = state[:, : state_cols_ref.shape[0]]
+    state = [sum_pieces(pieces, pieces[0].shape[1])]
+    if final:
+        nothing = jnp.zeros_like(state[0])
+        first = lax.axis_index("pipe") == 0
+        state = [
+            jnp.where(first, piece[...], other)
+            for piece, other in zip(newest, state + [nothing] * (chunks - 1))
+        ]
+    share = state_ref.shape[0]
+    if final:
+        others = jnp.concatenate([piece[:, :share] for piece in state[1:]], axis=1)
+    core = lax.axis_index("dp")
+    half = chunks // 2
     for hop in range(chunks):
-        product = dot_nn(state, state_cols_ref[:, places[hop]])
+        product = dot_nn(state[0][:, :share], state_ref[:, places[hop]])
+        if final:
+            chunk = lax.rem(me + hop, chunks)
+            mine = chunk // half == core
+            place = pl.ds(pl.multiple_of(lax.rem(chunk, half) * width, width), width)
+            held = jnp.where(mine, own_ref[:, place], other_ref[:, place])
+            product = product + dot_nn(others, held)
         copies[hop].wait()
         outs[hop][...] = (product + dot_nt(main, cols[hop])).astype(BF16)
 
 
-def compose_kernel(rows_ref, cols_ref, main_ref, main_sum):
-    step = pl.program_id(0)
-    main = dot_nn(rows_ref[...], cols_ref[...])
-
-    @pl.when(step == 0)
-    def _():
-        main_sum[...] = main
-
-    @pl.when(step > 0)
-    def _():
-        main_sum[...] += main
-
-    @pl.when(step == pl.num_programs(0) - 1)
-    def _():
-        main_ref[...] = main_sum[...].astype(BF16)
-
-
-def compose_last_kernel(half, *refs):
+def compose_kernel(half, *refs):
     rows, refs = refs[:half], refs[half:]
-    done, refs = refs[: half - 1], refs[half - 1 :]
     cols_ref, state_ref, joint_ref, main_sum, maps_sum = refs
     step = pl.program_id(0)
     size = rows[0].shape[0]
     map_width = main_sum.shape[1]
-
-    @pl.when(step == 0)
+    section = lax.axis_index("pipe")
+
+    @pl.when((section > 0) & (section < lax.axis_size("pipe") - 1))
     def _():
-        main_sum[...] = jnp.zeros_like(main_sum)
-        maps_sum[...] = jnp.zeros_like(maps_sum)
-
-    main_sum[...] += dot_nn(rows[-1][...], cols_ref[...])
-    for hop in range(half):
-        maps_sum[:, hop * size : (hop + 1) * size] += dot_nt(state_ref[...], rows[hop][...])
-
-    @pl.when(step == pl.num_programs(0) - 1)
-    def _():
-        joint_ref[...] = jnp.zeros_like(joint_ref)
-        for hop in range(half - 1):
-            joint_ref[:size, hop * map_width : (hop + 1) * map_width] = done[hop][...]
-        joint_ref[:size, (half - 1) * map_width :] = main_sum[...].astype(BF16)
-        joint_ref[size:, : half * size] = maps_sum[...].astype(BF16)
+        stacked = jnp.concatenate([row[...] for row in rows], axis=0)
+        main = dot_nn(stacked, cols_ref[...])
+        maps = dot_nt(state_ref[...], stacked)
+
+        @pl.when(step == 0)
+        def _():
+            main_sum[...] = main
+            maps_sum[...] = maps
+
+        @pl.when(step > 0)
+        def _():
+            main_sum[...] += main
+            maps_sum[...] += maps
+
+        @pl.when(step == pl.num_programs(0) - 1)
+        def _():
+            for hop in range(half):
+                joint_ref[:size, hop * map_width : (hop + 1) * map_width] = main_sum[
+                    hop * size : (hop + 1) * size, :
+                ].astype(BF16)
+            joint_ref[size:, : half * size] = maps_sum[...].astype(BF16)
 
 
 def by_hop(chunks, own, other):
@@ -543,9 +547,18 @@
     ]
 
 
-def send_kernel(chunks, main_ref, state_ref, *refs):
+def send_kernel(chunks, count, main_ref, state_ref, *refs):
+    others, refs = refs[:count], refs[count:]
     sources, refs = refs[:2], refs[2:]
-    outs, held, sems = refs[:chunks], refs[chunks:-1], refs[-1]
+    outs, others_ref, held, sems = refs[:chunks], refs[chunks], refs[chunks + 1 : -1], refs[-1]
+    if count:
+
+        @pl.when(lax.axis_index("pipe") == 0)
+        def _():
+            for index, other in enumerate(others):
+                size = other.shape[0]
+                others_ref[index * size : (index + 1) * size, :] = other[...]
+
     half = chunks // 2
     map_width = main_ref.shape[1]
     states = state_ref.shape[1]
@@ -582,27 +595,38 @@
 
 
 def carry_kernel(chunks, last, *refs):
-    parts, refs = refs[:chunks], refs[chunks:]
+    carry = sum_pieces(refs[:chunks], refs[0].shape[1])
     if last:
-        done_ref, out_ref = refs
-    else:
-        refs = refs[1:]
-    carry = sum_pieces(parts, parts[0].shape[1])
-    if last:
+        done_ref, out_ref = refs[chunks:]
         is_last = lax.axis_index("pipe") == lax.axis_size("pipe") - 1
         out_ref[0] = jnp.where(is_last, done_ref[...], carry)
-        return
-    half = chunks // 2
-    own, other = refs[:half], refs[half : 2 * half]
-    refs[2 * half][...] = carry
-
-    terms = by_hop(
-        chunks,
-        [dot_nt(carry, row[...]) for row in own],
-        [dot_nt(carry, row[...]) for row in other],
-    )
+    else:
+        refs[-1][...] = carry
+
+
+def dnormed_kernel(chunks, *refs):
+    incoming, refs = refs[:chunks], refs[chunks:]
+    *sources, out_ref = refs
+    core = lax.axis_index("dp")
+    last = lax.axis_index("pipe") == lax.axis_size("pipe") - 1
+    for lane, rows in enumerate(sources):
+
+        @pl.when(last & (core == lane))
+        def _():
+            product = gathered_product(chunks, lax.axis_index("tensor"), incoming, rows)
+            out_ref[...] = product.astype(BF16)
+
+
+def gathered_product(chunks, me, incoming, rows):
+    width = incoming[0].shape[1]
+    total = None
     for hop in range(chunks):
-        refs[2 * half + 1 + hop][...] = terms[hop].astype(BF16)
+        chunk = lax.rem(me + chunks - hop, chunks)
+        term = dot_nt(
+            incoming[hop][...], rows[:, pl.ds(pl.multiple_of(chunk * width, width), width)]
+        )
+        total = term if total is None else total + term
+    return total
 
 
 def after(value, dependency):
@@ -656,14 +680,19 @@
 
     half = chunks // 2
 
-    def by_core(sources, hop):
+    def rows_up(hop):
         pairs = []
-        for source in sources:
+        for source in range(sections - 1):
             for index in range(chunks):
                 for lane in range(2):
-                    target = (index + hop + lane * half) % chunks
+                    move = hop + lane * half
+                    if source == sections - 2:
+                        if lane != hop:
+                            continue
+                        move = 0
                     start = (source * chunks + index) * 2 + lane
-                    pairs.append((start, ((source + 1) * chunks + target) * 2 + lane))
+                    target = (source + 1) * chunks + (index + move) % chunks
+                    pairs.append((start, target * 2 + lane))
         return pairs
 
     everywhere = ("pipe", "tensor", "dp")
@@ -679,17 +708,12 @@
     for hop in range(1, chunks):
         incoming.append(lax.ppermute(output_grad, place, within(sections - 1, hop)))
 
-    rows = [lax.ppermute(weight_out[0], everywhere, by_core(range(sections - 2), 0))]
+    rows = [lax.ppermute(weight_out[0], everywhere, rows_up(0))]
     lanes = ((0, 0), (0, 128 - heads))
     by_head = jnp.pad(
         jnp.stack([step_bias[0], decay_log[0], skip_gain[0]]), ((0, 5), (0, 128 - heads))
     )
     steps = jnp.pad(saved_step[0].astype(F32).T, lanes)
-    chunk_rows = []
-    for hop in range(half):
-        chunk = (me + hop + core * half) % chunks
-        chunk_rows.append(lax.dynamic_slice_in_dim(weight_out[0], chunk * width, width, 1))
-    steps, chunk_rows = lax.optimization_barrier((steps, chunk_rows))
     taps_main = conv_main[0]
     taps_state = conv_state[0].reshape(conv_state.shape[1], -1)
     state_width = taps_state.shape[1]
@@ -731,9 +755,6 @@
     cols = jnp.concatenate([main_cols, step_cols], axis=1)
     residuals = residuals[:-1] + (after(by_head, main_cols),)
 
-    for hop, piece in enumerate(chunk_rows):
-        piece = after(piece, (residuals[0], main_cols, step_cols, *incoming[1:]))
-        chunk_rows[hop] = lax.ppermute(piece, everywhere, by_core([sections - 2], hop))
     main, *pieces = pl.pallas_call(
         lambda *refs: first_kernel(heads, chunks, *refs),
         out_shape=(main_shape,) + (piece_shape,) * chunks,
@@ -752,11 +773,11 @@
             shared.append(lax.ppermute(pieces[hop], place, pairs))
         return shared
 
-    def project_call(main, pieces):
+    def project_call(main, pieces, newest=(), others=()):
         return pl.pallas_call(
-            lambda *refs: project_kernel(chunks, *refs),
+            lambda *refs: project_kernel(chunks, bool(others), *refs),
             out_shape=(message,) * chunks,
-            in_specs=whole(2 + chunks) + [hbm],
+            in_specs=whole(2 + chunks + len(newest) + len(others)) + [hbm],
             out_specs=whole(chunks),
             scratch_shapes=[
                 pltpu.VMEM((chunks, width, map_width), BF16),
@@ -764,16 +785,13 @@
             ],
             compiler_params=kernel_params(),
             name="project",
-        )(main, *pieces, state_cols, cols)
-
-    pieces = share_state(after(pieces, rows[0]), [sections - 1])
+        )(main, *pieces, *newest, state_cols, *others, cols)
+
+    pieces = share_state(pieces, [sections - 1])
     for hop in range(1, half):
-        following = after(weight_out[0], (rows[-1], *chunk_rows, *pieces[1:]))
-        rows.append(lax.ppermute(following, everywhere, by_core(range(sections - 2), hop)))
+        rows.append(lax.ppermute(after(weight_out[0], main), everywhere, rows_up(hop)))
     state_cols = after(weight_state[0], main).reshape(model_width, -1).T
     state_share = state_cols.shape[0]
-    chunk_others = [swap(after(held, tuple(pieces[1:])), [sections - 1]) for held in chunk_rows]
-    pieces[0] = after(pieces[0], chunk_others)
     parts = project_call(main, pieces)
     exchanged = [parts[0]]
     for hop in range(1, chunks):
@@ -783,23 +801,6 @@
     depth = model_width // grid_steps
     rows_spec = pl.BlockSpec((channels, depth), lambda step: (0, step))
     cols_spec = pl.BlockSpec((depth, map_width), lambda step: (step, 0))
-    map_spec = pl.BlockSpec((channels, map_width), lambda step: (0, 0))
-    map_shape = jax.ShapeDtypeStruct((channels, map_width), BF16)
-    main_own = [
-        pl.pallas_call(
-            compose_kernel,
-            grid=(grid_steps,),
-            out_shape=map_shape,
-            in_specs=[rows_spec, cols_spec],
-            out_specs=map_spec,
-            scratch_shapes=[pltpu.VMEM((channels, map_width), F32)],
-            compiler_params=kernel_params(),
-            name="compose_weights",
-        )(after(held, parts[0]), cols)
-        for held in rows[:-1]
-    ]
-
-
     def pass_back(messages, active):
         moved = []
         for hop in range(chunks):
@@ -807,44 +808,58 @@
             moved.append(lax.ppermute(messages[hop], place, pairs))
         return moved
 
-    carry, *messages = pl.pallas_call(
+    result = pl.pallas_call(
         lambda *refs: carry_kernel(chunks, False, *refs),
-        out_shape=(message,) + (slice_out,) * chunks,
-        in_specs=whole(2 * chunks + 1),
-        out_specs=whole(1 + chunks),
+        out_shape=message,
+        in_specs=whole(chunks),
+        out_specs=pl.BlockSpec(memory_space=SPACE),
         compiler_params=kernel_params(),
         name="carry_next",
-    )(*exchanged, after(by_head, main_own), *chunk_rows, *chunk_others)
-    result = carry
-    incoming = pass_back(messages, sections - 1)
+    )(*exchanged)
+    exchanged = [result]
+    for hop in range(1, chunks):
+        exchanged.append(lax.ppermute(result, place, within(sections - 1, hop)))
+    dnormed = pl.pallas_call(
+        lambda *refs: dnormed_kernel(chunks, *refs),
+        out_shape=slice_out,
+        in_specs=whole(chunks + 2),
+        out_specs=pl.BlockSpec(memory_space=SPACE),
+        compiler_params=kernel_params(),
+        name="dnormed_back",
+    )(*exchanged, *rows)
+    pairs = section_pairs(sections, chunks, sections - 1, sections - 2, 0)
+    incoming = [lax.ppermute(dnormed, place, pairs)]
     joint_shape = jax.ShapeDtypeStruct((channels + state_share, half * map_width), BF16)
     joint = pl.pallas_call(
-        lambda *refs: compose_last_kernel(half, *refs),
+        lambda *refs: compose_kernel(half, *refs),
         grid=(grid_steps,),
         out_shape=joint_shape,
         in_specs=[rows_spec] * half
-        + [map_spec] * (half - 1)
         + [cols_spec, pl.BlockSpec((state_share, depth), lambda step: (0, step))],
         out_specs=pl.BlockSpec(joint_shape.shape, lambda step: (0, 0)),
         scratch_shapes=[
-            pltpu.VMEM((channels, map_width), F32),
+            pltpu.VMEM((half * channels, map_width), F32),
             pltpu.VMEM((state_share, half * channels), F32),
         ],
         compiler_params=kernel_params(),
-        name="compose_last",
-    )(*rows[:-1], after(rows[-1], messages[0]), *main_own, cols, state_cols)
-    residuals = residuals[:-1] + (after(by_head, joint),)
+        name="compose_weights",
+    )(*rows[:-1], after(rows[-1], dnormed), cols, state_cols)
+
+    half_cols = lax.dynamic_slice_in_dim(
+        after(state_cols, parts[0]), core * (model_width // 2), model_width // 2, 1
+    )
+    residuals = residuals[:-1] + (after(by_head, (joint, half_cols)),)
 
     state_shape = jax.ShapeDtypeStruct((length, state_width), BF16)
     joined = jax.ShapeDtypeStruct((length, channels + state_width + channels // 2), BF16)
     assert 2 * state_share == length
 
     def next_call(incoming, kept, active):
-        count = chunks if active == 0 else 0
+        count = chunks if len(incoming) > 1 else 0
         main, state, *pieces = pl.pallas_call(
-            lambda *refs: next_kernel(heads, chunks, active, *refs),
+            lambda *refs: next_kernel(heads, chunks, len(incoming), active, *refs),
             out_shape=(main_shape, state_shape) + (piece_shape,) * count,
-            in_specs=whole(chunks + 9 + len(kept)),
+            in_specs=whole(len(incoming) + 9 + len(kept)),
             out_specs=whole(2 + count),
             compiler_params=kernel_params(),
             name="section_next",
@@ -853,26 +868,38 @@
 
     joint_other = None
     kept = ()
+    summed = None
     for active in range(sections - 2, -1, -1):
         kept, pieces = next_call(incoming, kept, active)
         if active == 0:
             break
         if joint_other is None:
             joint_other = swap(after(joint, kept[0]), range(1, sections - 1))
-        messages = pl.pallas_call(
-            lambda *refs: send_kernel(chunks, *refs),
-            out_shape=(joined,) * chunks,
-            in_specs=whole(2) + [hbm] * 2,
-            out_specs=whole(chunks),
+        state_others = []
+        if active == sections - 2:
+            late = after(half_cols, kept[0])
+            state_others = [
+                lax.ppermute(late, place, within(0, chunks - away)) for away in range(1, chunks)
+            ]
+        count = len(state_others)
+        others_shape = jax.ShapeDtypeStruct((count * state_share, model_width // 2), BF16)
+        *messages, state_others = pl.pallas_call(
+            lambda *refs: send_kernel(chunks, count, *refs),
+            out_shape=(joined,) * chunks + (others_shape if count else piece_shape,),
+            in_specs=whole(2 + count) + [hbm] * 2,
+            out_specs=whole(chunks + 1),
             scratch_shapes=[pltpu.VMEM(joint_shape.shape, BF16)] * 2
             + [pltpu.SemaphoreType.DMA((2,))],
             compiler_params=kernel_params(),
             name="send_back",
-        )(*kept, joint, joint_other)
+        )(*kept, *state_others, joint, joint_other)
         incoming = pass_back(messages, active)
-    pieces = share_state(pieces, range(sections - 1))
-
-    parts = project_call(kept[0], pieces)
+        if active == sections - 2:
+            shared = (state_others, swap(state_others, [0]))
+        if active == 1:
+            summed = share_state(after(pieces, incoming[0]), range(1, sections - 1))
+
+    parts = project_call(kept[0], summed, pieces, shared)
     exchanged = [parts[0]]
     for hop in range(1, chunks):
         pairs = []

time: 214 us -> 202 us (0.944)
  waiting for transfers between devices: 108 us -> 95.6 us
  starting transfers between devices: 54.5 us -> 60.2 us
  local copies, waits for them, and re-layouts: 13.3 us -> 10.2 us
    ppermute x12 -> x8, waiting for transfers between devices: 27.1 us -> 17.8 us  [pass_back(): moved.append(lax.ppermute(messages[hop], place, pairs))]
    ppermute x12 -> x8, starting transfers between devices: 13.2 us -> 16.9 us  [pass_back(): moved.append(lax.ppermute(messages[hop], place, pairs))]
    ppermute x3 -> x2, waiting for transfers between devices: 2.3 us -> 0.01 us  [swap(): return lax.ppermute(value, everywhere, pairs)]
    ppermute x6, starting transfers between devices: 11.4 us -> 13.7 us  [share_state(): shared.append(lax.ppermute(pieces[hop], place, pairs))]
    dynamic_slice x1, local copies, waits for them, and re-layouts: 2.25 us -> 0.03 us  [relay_body(): lax.dynamic_slice_in_dim(after(state_cols, parts[0]), core * (model_width...]
    ppermute x4 -> x9, starting transfers between devices: 11 us -> 12.5 us  [the longest x1 5.15 us: relay_body(): rows = [lax.ppermute(weight_out[0], everywhere, rows_up(0))]]
    unnamed x21 -> x17, local copies, waits for them, and re-layouts: 9.67 us -> 8.95 us
    ppermute x4 -> x9, waiting for transfers between devices: 58.6 us -> 58.9 us  [the longest x1 58.8 us: relay_body(): rows = [lax.ppermute(weight_out[0], everywhere, rows_up(0))]]
  transfers between devices with their start and end apart: 34 -> 34, of which waited for: 13 -> 9; matrix products, arithmetic and copies ran while one was open for 9% -> 6% of each run, Pallas kernels for 9% -> 10%
where the time goes in v4:
time: 202 us; the launch traced here: 199 us
  waiting for transfers between devices  95.6 us (47%)
  starting transfers between devices  60.2 us (30%)
  Pallas kernels  28.9 us (14%)
  local copies, waits for them, and re-layouts  10.2 us (5%)
  other arithmetic  3.7 us (2%)
    ppermute x1, waiting for transfers between devices, relay_body(): rows = [lax.ppermute(weight_out[0], everywhere, rows_up(0))]  58.8 us
    ppermute x3, waiting for transfers between devices, relay_body(): exchanged.append(lax.ppermute(parts[hop], place, pairs))  18.3 us
    ppermute x8, waiting for transfers between devices, pass_back(): moved.append(lax.ppermute(messages[hop], place, pairs))  17.8 us
    ppermute x8, starting transfers between devices, pass_back(): moved.append(lax.ppermute(messages[hop], place, pairs))  16.9 us
    ppermute x6, starting transfers between devices, share_state(): shared.append(lax.ppermute(pieces[hop], place, pairs))  13.7 us
    ppermute x3, starting transfers between devices, relay_body(): exchanged.append(lax.ppermute(parts[hop], place, pairs))  9.76 us
    unnamed x17, local copies, waits for them, and re-layouts  8.95 us
    pallas_call x1, Pallas kernels, relay_body(): pl.pallas_call(lambda *refs: compose_kernel(half, *refs), grid=(grid_step...  7.66 us
  transfers between devices with their start and end apart: 34, of which 9 were waited for; matrix products, arithmetic and copies ran while one was open for 6% of the time, Pallas kernels for 10%

profile of v4, /device:TPU:11, one launch (start us, length us, event | category | flops | bytes accessed | tf_op | source)
XLA Modules:
  0.0 199.2 jit_solution(13699122699486034479)
XLA Ops:
  0.0 0.7 collective-permute-start
  0.7 0.7 collective-permute-start.1
  1.4 0.7 collective-permute-start.2
  2.0 5.1 %collective-permute-start.12 = (bf16[256,4096]{1,0:T(8,128)(2,1)}, bf16[256,4096]{1,0:T(8,128)(2,1)}, u32[]{:S(2)}, u32[]{:S(2)}) collective-permute-start(bf16[256,4096]{1,0:T(8,128)(2,1)} %bitcast.refs_4_), channel_id=1, source_target_pairs={{0,8},{1,13},{2,10},{3,15},{4,12},{5,9},{6,14},{7,11},{8,16},{9,21... | collective-permute-start | bytes 6291464 | tf_op jit(solution)/shard_map/ppermute | solution.py:711
  7.2 1.2 fusion.2
  8.4 0.9 copy.17
  9.3 0.7 select_maximum_fusion.refs_6_.refs_13_.refs_9_.refs_12_
  10.0 0.7 copy.29
  10.7 0.8 copy.28
  11.5 2.2 %copy.18 = bf16[1,4,4096]{1,2,0:T(8,128)(2,1)} copy(bf16[1,4,4096]{2,1,0:T(4,128)(2,1)} %param.16) | data formatting | bytes 65536 | tf_op args[2]
  13.7 0.7 copy-done.2
  14.4 0.7 copy-done.4
  15.1 1.2 forward_residuals.1
  16.3 3.0 %copy.23 = bf16[512,8,2,256]{3,1,2,0:T(8,128)(2,1)S(1)} copy(bf16[512,8,2,256]{3,2,1,0:T(2,128)(2,1)} %bitcast.45) | data formatting | bytes 8388608
  19.4 3.6 %section_first.1 = (bf16[128,640]{1,0:T(8,128)(2,1)S(1)}, bf16[128,128]{1,0:T(8,128)(2,1)S(1)}, bf16[128,128]{1,0:T(8,128)(2,1)S(1)}, bf16[128,128]{1,0:T(8,128)(2,1)S(1)}, bf16[128,128]{1,0:T(8,128)(2,1)S(1)}) custom-call(bf16[128,1024]{1,0:T(8,128)(2,1)S(1)} %copy-done.1, bf16[128,1024]{1,0:T(8,128)(2,1)S(1)} %collective-permute-done.refs_1_, ...), custom_call_target="tpu_custom_call" | custom-call | tf_op jit(solution)/shard_map/section_first/pallas_call | solution.py:758
  23.0 1.9 collective-permute-start.13
  24.9 0.7 collective-permute-start.3
  25.6 0.7 collective-permute-start.4
  26.3 0.7 collective-permute-start.5
  27.0 3.0 %fusion.1.refs_6_.refs_2_.refs_12_ = bf16[4096,640]{1,0:T(8,128)(2,1)} fusion(bf16[4096,4]{1,0:T(8,128)(2,1)S(1)} %bitcast.44, bf16[4096,512]{1,0:T(8,128)(2,1)S(1)} %bitcast.43), kind=kLoop, calls=%fused_computation.2 | loop fusion | flops 15728640 | bytes 9469952 | tf_op jit(solution)/shard_map/concatenate | solution.py:755
  30.0 3.9 %project.2 = (bf16[128,1024]{1,0:T(8,128)(2,1)S(1)}, bf16[128,1024]{1,0:T(8,128)(2,1)S(1)}, bf16[128,1024]{1,0:T(8,128)(2,1)S(1)}, bf16[128,1024]{1,0:T(8,128)(2,1)S(1)}) custom-call(bf16[128,640]{1,0:T(8,128)(2,1)S(1)} %get-tuple-element.68.refs_0_, bf16[128,128]{1,0:T(8,128)(2,1)S(1)} %get-tuple-element.69.refs_1_, ...), custom_call_target="tpu_custom_call" | custom-call | tf_op jit(solution)/shard_map/project/pallas_call | solution.py:777
  33.9 0.7 collective-permute-start.6
  34.6 0.7 collective-permute-start.7
  35.2 0.7 collective-permute-start.8
  36.1 0.7 collective-permute-start.10
  36.8 0.7 collective-permute-start.11
  37.5 1.4 collective-permute-start.9
  38.8 58.8 %collective-permute-done.12.refs_4_.refs_0_ = bf16[256,4096]{1,0:T(8,128)(2,1)} collective-permute-done((bf16[256,4096]{1,0:T(8,128)(2,1)}, bf16[256,4096]{1,0:T(8,128)(2,1)}, u32[]{:S(2)}, u32[]{:S(2)}) %collective-permute-start.12) | collective-permute-done | bytes 2097184 | tf_op jit(solution)/shard_map/ppermute | solution.py:711
  97.7 2.3 %dnormed_back.1 = bf16[128,256]{1,0:T(8,128)(2,1)S(1)} custom-call(bf16[128,1024]{1,0:T(8,128)(2,1)S(1)} %carry_next.1.refs_0_.refs_4_, bf16[128,1024]{1,0:T(8,128)(2,1)} %collective-permute-done.9.refs_1_, bf16[128,1024]{1,0:T(8,128)(2,1)S(1)} %collective-permute-done.10.refs_2_, bf16[128,1024]{1,0:T(8,128)(2,1)S(1)} %collective-permute-done.11.refs_3_, ...), custom_call_target="tpu_custom_call" | custom-call | tf_op jit(solution)/shard_map/dnormed_back/pallas_call | solution.py:822
  100.0 0.7 collective-permute-start.14
  100.7 7.7 %compose_weights.1.refs_5_.refs_2_ = bf16[320,1280]{1,0:T(8,128)(2,1)S(1)} custom-call(bf16[256,4096]{1,0:T(8,128)(2,1)} %collective-permute-done.12.refs_4_.refs_0_, bf16[256,4096]{1,0:T(8,128)(2,1)} %collective-permute-done.13.refs_5_.refs_1_, bf16[4096,640]{1,0:T(8,128)(2,1)} %fusion.1.refs_6_.refs_2_.refs_12_, bf16[64,4096]{1,0:T(8,128)(2,1)S(1)} %bitcast.30), custom_call_target="tpu_custom_call" | custom-call | tf_op jit(solution)/shard_map/compose_weights/pallas_call | solution.py:833
  108.4 0.7 section_next.3
  109.1 2.6 %collective-permute-start.18 = (bf16[320,1280]{1,0:T(8,128)(2,1)S(1)}, bf16[320,1280]{1,0:T(8,128)(2,1)S(1)}, u32[]{:S(2)}, u32[]{:S(2)}) collective-permute-start(bf16[320,1280]{1,0:T(8,128)(2,1)S(1)} %compose_weights.1.refs_5_.refs_2_), channel_id=1, source_target_pairs={{8,9},{9,8},{10,11},{11,10},{12,13},{13,12},{14,15},{15,14},{16,17... | collective-permute-start | bytes 2457608 | tf_op jit(solution)/shard_map/ppermute | solution.py:705
  111.7 0.7 collective-permute-start.15
  112.4 0.7 collective-permute-start.16
  113.1 0.7 collective-permute-start.17
  113.8 0.8 send_back.2
  114.7 0.7 collective-permute-start.30
  115.4 1.3 collective-permute-start.19
  116.7 1.3 collective-permute-start.20
  118.0 1.3 collective-permute-start.21
  119.3 1.5 collective-permute-start.22
  120.8 3.0 %collective-permute-done.19.refs_0_ = bf16[128,640]{1,0:T(8,128)(2,1)S(1)} collective-permute-done((bf16[128,640]{1,0:T(8,128)(2,1)S(1)}, bf16[128,640]{1,0:T(8,128)(2,1)S(1)}, u32[]{:S(2)}, u32[]{:S(2)}) %collective-permute-start.19) | collective-permute-done | bytes 163872 | tf_op jit(solution)/shard_map/ppermute | solution.py:808
  123.8 5.8 %collective-permute-done.20.refs_1_ = bf16[128,640]{1,0:T(8,128)(2,1)S(1)} collective-permute-done((bf16[128,640]{1,0:T(8,128)(2,1)S(1)}, bf16[128,640]{1,0:T(8,128)(2,1)S(1)}, u32[]{:S(2)}, u32[]{:S(2)}) %collective-permute-start.20) | collective-permute-done | bytes 163872 | tf_op jit(solution)/shard_map/ppermute | solution.py:808
  129.6 4.5 %collective-permute-done.21.refs_2_ = bf16[128,640]{1,0:T(8,128)(2,1)S(1)} collective-permute-done((bf16[128,640]{1,0:T(8,128)(2,1)S(1)}, bf16[128,640]{1,0:T(8,128)(2,1)S(1)}, u32[]{:S(2)}, u32[]{:S(2)}) %collective-permute-start.21) | collective-permute-done | bytes 163872 | tf_op jit(solution)/shard_map/ppermute | solution.py:808
  134.1 3.7 %collective-permute-done.22.refs_3_ = bf16[128,640]{1,0:T(8,128)(2,1)S(1)} collective-permute-done((bf16[128,640]{1,0:T(8,128)(2,1)S(1)}, bf16[128,640]{1,0:T(8,128)(2,1)S(1)}, u32[]{:S(2)}, u32[]{:S(2)}) %collective-permute-start.22) | collective-permute-done | bytes 163872 | tf_op jit(solution)/shard_map/ppermute | solution.py:808
  137.7 1.3 section_next.4
  139.1 0.8 send_back.3
  139.9 2.1 %collective-permute-start.23 = (bf16[128,640]{1,0:T(8,128)(2,1)S(1)}, bf16[128,640]{1,0:T(8,128)(2,1)S(1)}, u32[]{:S(2)}, u32[]{:S(2)}) collective-permute-start(bf16[128,640]{1,0:T(8,128)(2,1)S(1)} %get-tuple-element.93), channel_id=1, source_target_pairs={{8,0},{10,2},{12,4},{14,6},{9,1},{11,3},{13,5},{15,7}} | collective-permute-start | bytes 491528 | tf_op jit(solution)/shard_map/ppermute | solution.py:808
  142.0 6.9 %collective-permute-start.24 = (bf16[128,640]{1,0:T(8,128)(2,1)S(1)}, bf16[128,640]{1,0:T(8,128)(2,1)S(1)}, u32[]{:S(2)}, u32[]{:S(2)}) collective-permute-start(bf16[128,640]{1,0:T(8,128)(2,1)S(1)} %get-tuple-element.94), channel_id=1, source_target_pairs={{8,6},{10,0},{12,2},{14,4},{9,7},{11,1},{13,3},{15,5}} | collective-permute-start | bytes 491528 | tf_op jit(solution)/shard_map/ppermute | solution.py:808
  148.9 1.3 collective-permute-start.25
  150.2 1.3 collective-permute-start.26
  151.5 3.8 %collective-permute-start.27 = (bf16[128,128]{1,0:T(8,128)(2,1)S(1)}, bf16[128,128]{1,0:T(8,128)(2,1)S(1)}, u32[]{:S(2)}, u32[]{:S(2)}) collective-permute-start(bf16[128,128]{1,0:T(8,128)(2,1)S(1)} %get-tuple-element.103), channel_id=1, source_target_pairs={{8,10},{10,12},{12,14},{14,8},{16,18},{18,20},{20,22},{22,16},{9,1... | collective-permute-start | bytes 98312 | tf_op jit(solution)/shard_map/ppermute | solution.py:773
  155.4 5.9 %collective-permute-start.28 = (bf16[128,128]{1,0:T(8,128)(2,1)S(1)}, bf16[128,128]{1,0:T(8,128)(2,1)S(1)}, u32[]{:S(2)}, u32[]{:S(2)}) collective-permute-start(bf16[128,128]{1,0:T(8,128)(2,1)S(1)} %get-tuple-element.104), channel_id=1, source_target_pairs={{8,12},{10,14},{12,8},{14,10},{16,20},{18,22},{20,16},{22,18},{9,1... | collective-permute-start | bytes 98312 | tf_op jit(solution)/shard_map/ppermute | solution.py:773
  161.3 1.9 collective-permute-start.29
  163.3 0.9 collective-permute-done.26.refs_3_
  164.1 1.8 section_next.5
  166.4 3.8 %project.3 = (bf16[128,1024]{1,0:T(8,128)(2,1)S(1)}, bf16[128,1024]{1,0:T(8,128)(2,1)S(1)}, bf16[128,1024]{1,0:T(8,128)(2,1)S(1)}, bf16[128,1024]{1,0:T(8,128)(2,1)S(1)}) custom-call(bf16[128,640]{1,0:T(8,128)(2,1)S(1)} %get-tuple-element.97.refs_0_, bf16[128,128]{1,0:T(8,128)(2,1)S(1)} %get-tuple-element.102.refs_1_, ...), custom_call_target="tpu_custom_call" | custom-call | tf_op jit(solution)/shard_map/project/pallas_call | solution.py:777
  170.2 3.4 %collective-permute-start.31 = (bf16[128,1024]{1,0:T(8,128)(2,1)S(1)}, bf16[128,1024]{1,0:T(8,128)(2,1)S(1)}, u32[]{:S(2)}, u32[]{:S(2)}) collective-permute-start(bf16[128,1024]{1,0:T(8,128)(2,1)S(1)} %get-tuple-element.112), channel_id=1, source_target_pairs={{0,2},{2,4},{4,6},{6,0},{8,10},{10,12},{12,14},{14,8},{16,18},{18,... | collective-permute-start | bytes 786440 | tf_op jit(solution)/shard_map/ppermute | solution.py:908
  173.6 3.0 %collective-permute-start.32 = (bf16[128,1024]{1,0:T(8,128)(2,1)S(1)}, bf16[128,1024]{1,0:T(8,128)(2,1)S(1)}, u32[]{:S(2)}, u32[]{:S(2)}) collective-permute-start(bf16[128,1024]{1,0:T(8,128)(2,1)S(1)} %get-tuple-element.113), channel_id=1, source_target_pairs={{0,4},{2,6},{4,0},{6,2},{8,12},{10,14},{12,8},{14,10},{16,20},{18,... | collective-permute-start | bytes 786440 | tf_op jit(solution)/shard_map/ppermute | solution.py:908
  176.6 3.4 %collective-permute-start.33 = (bf16[128,1024]{1,0:T(8,128)(2,1)S(1)}, bf16[128,1024]{1,0:T(8,128)(2,1)S(1)}, u32[]{:S(2)}, u32[]{:S(2)}) collective-permute-start(bf16[128,1024]{1,0:T(8,128)(2,1)S(1)} %get-tuple-element.114), channel_id=1, source_target_pairs={{0,6},{2,0},{4,2},{6,4},{8,14},{10,8},{12,10},{14,12},{16,22},{18,... | collective-permute-start | bytes 786440 | tf_op jit(solution)/shard_map/ppermute | solution.py:908
  180.0 14.0 %collective-permute-done.32.refs_2_ = bf16[128,1024]{1,0:T(8,128)(2,1)S(1)} collective-permute-done((bf16[128,1024]{1,0:T(8,128)(2,1)S(1)}, bf16[128,1024]{1,0:T(8,128)(2,1)S(1)}, u32[]{:S(2)}, u32[]{:S(2)}) %collective-permute-start.32) | collective-permute-done | bytes 262176 | tf_op jit(solution)/shard_map/ppermute | solution.py:908
  193.9 4.4 %collective-permute-done.33.refs_3_ = bf16[128,1024]{1,0:T(8,128)(2,1)S(1)} collective-permute-done((bf16[128,1024]{1,0:T(8,128)(2,1)S(1)}, bf16[128,1024]{1,0:T(8,128)(2,1)S(1)}, u32[]{:S(2)}, u32[]{:S(2)}) %collective-permute-start.33) | collective-permute-done | bytes 262176 | tf_op jit(solution)/shard_map/ppermute | solution.py:908
  198.3 0.9 carry_last.1
  (40 shorter events, 0.8 us)
Async XLA Ops:
  0.0 16.3 %collective-permute-start = (bf16[128,1024]{1,0:T(8,128)(2,1)}, bf16[128,1024]{1,0:T(8,128)(2,1)S(1)}, u32[]{:S(2)}, u32[]{:S(2)}) collective-permute-start(bf16[128,1024]{1,0:T(8,128)(2,1)} %refs_0_.1), channel_id=1, source_target_pairs={{24,26},{26,28},{28,30},{30,24},{25,27},{27,29},{29,31},{31,25}} | collective-permute-start | bytes 786440 | tf_op jit(solution)/shard_map/ppermute | solution.py:709
  0.7 18.7 %collective-permute-start.1 = (bf16[128,1024]{1,0:T(8,128)(2,1)}, bf16[128,1024]{1,0:T(8,128)(2,1)S(1)}, u32[]{:S(2)}, u32[]{:S(2)}) collective-permute-start(bf16[128,1024]{1,0:T(8,128)(2,1)} %refs_0_.1), channel_id=1, source_target_pairs={{24,28},{26,30},{28,24},{30,26},{25,29},{27,31},{29,25},{31,27}} | collective-permute-start | bytes 786440 | tf_op jit(solution)/shard_map/ppermute | solution.py:709
  1.4 18.0 %collective-permute-start.2 = (bf16[128,1024]{1,0:T(8,128)(2,1)}, bf16[128,1024]{1,0:T(8,128)(2,1)S(1)}, u32[]{:S(2)}, u32[]{:S(2)}) collective-permute-start(bf16[128,1024]{1,0:T(8,128)(2,1)} %refs_0_.1), channel_id=1, source_target_pairs={{24,30},{26,24},{28,26},{30,28},{25,31},{27,25},{29,27},{31,29}} | collective-permute-start | bytes 786440 | tf_op jit(solution)/shard_map/ppermute | solution.py:709
  2.0 95.6 %collective-permute-start.12 = (bf16[256,4096]{1,0:T(8,128)(2,1)}, bf16[256,4096]{1,0:T(8,128)(2,1)}, u32[]{:S(2)}, u32[]{:S(2)}) collective-permute-start(bf16[256,4096]{1,0:T(8,128)(2,1)} %bitcast.refs_4_), channel_id=1, source_target_pairs={{0,8},{1,13},{2,10},{3,15},{4,12},{5,9},{6,14},{7,11},{8,16},{9,21... | collective-permute-start | bytes 6291464 | tf_op jit(solution)/shard_map/ppermute | solution.py:711
  8.4 10.9 %copy-start.1 = (bf16[128,1024]{1,0:T(8,128)(2,1)S(1)}, bf16[128,1024]{1,0:T(8,128)(2,1)}, u32[]{:S(2)}) copy-start(bf16[128,1024]{1,0:T(8,128)(2,1)} %refs_0_.1) | copy-start | bytes 786436
  13.7 0.7 copy-start.2
  14.4 0.7 copy-start.4
  16.3 10.6 %copy-start.5 = (bf16[1,4,4096]{1,2,0:T(8,128)(2,1)S(1)}, bf16[1,4,4096]{1,2,0:T(8,128)(2,1)}, u32[]{:S(2)}) copy-start(bf16[1,4,4096]{1,2,0:T(8,128)(2,1)} %copy.18) | copy-start | bytes 98308
  23.0 74.7 %collective-permute-start.13 = (bf16[256,4096]{1,0:T(8,128)(2,1)}, bf16[256,4096]{1,0:T(8,128)(2,1)}, u32[]{:S(2)}, u32[]{:S(2)}) collective-permute-start(bf16[256,4096]{1,0:T(8,128)(2,1)} %bitcast.refs_4_), channel_id=1, source_target_pairs={{0,10},{1,15},{2,12},{3,9},{4,14},{5,11},{6,8},{7,13},{8,18},{9,23... | collective-permute-start | bytes 6291464 | tf_op jit(solution)/shard_map/ppermute | solution.py:792
  24.9 5.0 %collective-permute-start.3 = (bf16[128,128]{1,0:T(8,128)(2,1)S(1)}, bf16[128,128]{1,0:T(8,128)(2,1)S(1)}, u32[]{:S(2)}, u32[]{:S(2)}) collective-permute-start(bf16[128,128]{1,0:T(8,128)(2,1)S(1)} %get-tuple-element.70), channel_id=1, source_target_pairs={{24,26},{26,28},{28,30},{30,24},{25,27},{27,29},{29,31},{31,25}} | collective-permute-start | bytes 98312 | tf_op jit(solution)/shard_map/ppermute | solution.py:773
  25.6 4.4 %collective-permute-start.4 = (bf16[128,128]{1,0:T(8,128)(2,1)S(1)}, bf16[128,128]{1,0:T(8,128)(2,1)S(1)}, u32[]{:S(2)}, u32[]{:S(2)}) collective-permute-start(bf16[128,128]{1,0:T(8,128)(2,1)S(1)} %get-tuple-element.71), channel_id=1, source_target_pairs={{24,28},{26,30},{28,24},{30,26},{25,29},{27,31},{29,25},{31,27}} | collective-permute-start | bytes 98312 | tf_op jit(solution)/shard_map/ppermute | solution.py:773
  26.3 3.7 %collective-permute-start.5 = (bf16[128,128]{1,0:T(8,128)(2,1)S(1)}, bf16[128,128]{1,0:T(8,128)(2,1)S(1)}, u32[]{:S(2)}, u32[]{:S(2)}) collective-permute-start(bf16[128,128]{1,0:T(8,128)(2,1)S(1)} %get-tuple-element.72), channel_id=1, source_target_pairs={{24,30},{26,24},{28,26},{30,28},{25,31},{27,25},{29,27},{31,29}} | collective-permute-start | bytes 98312 | tf_op jit(solution)/shard_map/ppermute | solution.py:773
  26.9 3.0 %copy-start = (bf16[1,4096,2,32]{1,3,2,0:T(8,128)(2,1)S(1)}, bf16[1,4096,2,32]{1,3,2,0:T(8,128)(2,1)}, u32[]{:S(2)}) copy-start(bf16[1,4096,2,32]{1,3,2,0:T(8,128)(2,1)} %param.15) | copy-start | bytes 1572868
  33.9 2.1 %collective-permute-start.6 = (bf16[128,1024]{1,0:T(8,128)(2,1)S(1)}, bf16[128,1024]{1,0:T(8,128)(2,1)S(1)}, u32[]{:S(2)}, u32[]{:S(2)}) collective-permute-start(bf16[128,1024]{1,0:T(8,128)(2,1)S(1)} %get-tuple-element.76), channel_id=1, source_target_pairs={{24,26},{26,28},{28,30},{30,24},{25,27},{27,29},{29,31},{31,25}} | collective-permute-start | bytes 786440 | tf_op jit(solution)/shard_map/ppermute | solution.py:798
  34.6 1.4 collective-permute-start.7
  35.2 0.7 collective-permute-start.8
  36.1 2.7 %collective-permute-start.10 = (bf16[128,1024]{1,0:T(8,128)(2,1)S(1)}, bf16[128,1024]{1,0:T(8,128)(2,1)S(1)}, u32[]{:S(2)}, u32[]{:S(2)}) collective-permute-start(bf16[128,1024]{1,0:T(8,128)(2,1)S(1)} %carry_next.1.refs_0_.refs_4_), channel_id=1, source_target_pairs={{24,28},{26,30},{28,24},{30,26},{25,29},{27,31},{29,25},{31,27}} | collective-permute-start | bytes 786440 | tf_op jit(solution)/shard_map/ppermute | solution.py:821
  36.8 2.1 %collective-permute-start.11 = (bf16[128,1024]{1,0:T(8,128)(2,1)S(1)}, bf16[128,1024]{1,0:T(8,128)(2,1)S(1)}, u32[]{:S(2)}, u32[]{:S(2)}) collective-permute-start(bf16[128,1024]{1,0:T(8,128)(2,1)S(1)} %carry_next.1.refs_0_.refs_4_), channel_id=1, source_target_pairs={{24,30},{26,24},{28,26},{30,28},{25,31},{27,25},{29,27},{31,29}} | collective-permute-start | bytes 786440 | tf_op jit(solution)/shard_map/ppermute | solution.py:821
  37.5 1.4 collective-permute-start.9
  100.0 8.4 %collective-permute-start.14 = (bf16[128,256]{1,0:T(8,128)(2,1)S(1)}, bf16[128,256]{1,0:T(8,128)(2,1)S(1)}, u32[]{:S(2)}, u32[]{:S(2)}) collective-permute-start(bf16[128,256]{1,0:T(8,128)(2,1)S(1)} %dnormed_back.1), channel_id=1, source_target_pairs={{24,16},{26,18},{28,20},{30,22},{25,17},{27,19},{29,21},{31,23}} | collective-permute-start | bytes 196616 | tf_op jit(solution)/shard_map/ppermute | solution.py:831
  100.7 7.7 %copy-start.3 = (f32[1,4,256]{2,1,0:T(4,128)S(1)}, f32[1,4,256]{2,1,0:T(4,128)}, u32[]{:S(2)}) copy-start(f32[1,4,256]{2,1,0:T(4,128)} %param.18) | copy-start | bytes 12292
  109.1 4.7 %collective-permute-start.18 = (bf16[320,1280]{1,0:T(8,128)(2,1)S(1)}, bf16[320,1280]{1,0:T(8,128)(2,1)S(1)}, u32[]{:S(2)}, u32[]{:S(2)}) collective-permute-start(bf16[320,1280]{1,0:T(8,128)(2,1)S(1)} %compose_weights.1.refs_5_.refs_2_), channel_id=1, source_target_pairs={{8,9},{9,8},{10,11},{11,10},{12,13},{13,12},{14,15},{15,14},{16,17... | collective-permute-start | bytes 2457608 | tf_op jit(solution)/shard_map/ppermute | solution.py:705
  111.7 2.1 %collective-permute-start.15 = (bf16[64,2048]{1,0:T(8,128)(2,1)S(1)}, bf16[64,2048]{1,0:T(8,128)(2,1)S(1)}, u32[]{:S(2)}, u32[]{:S(2)}) collective-permute-start(bf16[64,2048]{1,0:T(8,128)(2,1)S(1)} %constant_dynamic-slice_fusion), channel_id=1, source_target_pairs={{0,6},{2,0},{4,2},{6,4},{1,7},{3,1},{5,3},{7,5}} | collective-permute-start | bytes 786440 | tf_op jit(solution)/shard_map/ppermute | solution.py:882
  112.4 1.4 collective-permute-start.16
  113.1 0.7 collective-permute-start.17
  114.7 51.8 %collective-permute-start.30 = (bf16[192,2048]{1,0:T(8,128)(2,1)S(1)}, bf16[192,2048]{1,0:T(8,128)(2,1)S(1)}, u32[]{:S(2)}, u32[]{:S(2)}) collective-permute-start(bf16[192,2048]{1,0:T(8,128)(2,1)S(1)} %get-tuple-element.110.refs_10_), channel_id=1, source_target_pairs={{0,1},{1,0},{2,3},{3,2},{4,5},{5,4},{6,7},{7,6}} | collective-permute-start | bytes 2359304 | tf_op jit(solution)/shard_map/ppermute | solution.py:705
  115.4 8.4 %collective-permute-start.19 = (bf16[128,640]{1,0:T(8,128)(2,1)S(1)}, bf16[128,640]{1,0:T(8,128)(2,1)S(1)}, u32[]{:S(2)}, u32[]{:S(2)}) collective-permute-start(bf16[128,640]{1,0:T(8,128)(2,1)S(1)} %get-tuple-element.87), channel_id=1, source_target_pairs={{16,8},{18,10},{20,12},{22,14},{17,9},{19,11},{21,13},{23,15}} | collective-permute-start | bytes 491528 | tf_op jit(solution)/shard_map/ppermute | solution.py:808
  116.7 12.9 %collective-permute-start.20 = (bf16[128,640]{1,0:T(8,128)(2,1)S(1)}, bf16[128,640]{1,0:T(8,128)(2,1)S(1)}, u32[]{:S(2)}, u32[]{:S(2)}) collective-permute-start(bf16[128,640]{1,0:T(8,128)(2,1)S(1)} %get-tuple-element.88), channel_id=1, source_target_pairs={{16,14},{18,8},{20,10},{22,12},{17,15},{19,9},{21,11},{23,13}} | collective-permute-start | bytes 491528 | tf_op jit(solution)/shard_map/ppermute | solution.py:808
  118.0 16.1 %collective-permute-start.21 = (bf16[128,640]{1,0:T(8,128)(2,1)S(1)}, bf16[128,640]{1,0:T(8,128)(2,1)S(1)}, u32[]{:S(2)}, u32[]{:S(2)}) collective-permute-start(bf16[128,640]{1,0:T(8,128)(2,1)S(1)} %get-tuple-element.89), channel_id=1, source_target_pairs={{16,12},{18,14},{20,8},{22,10},{17,13},{19,15},{21,9},{23,11}} | collective-permute-start | bytes 491528 | tf_op jit(solution)/shard_map/ppermute | solution.py:808
  119.3 18.5 %collective-permute-start.22 = (bf16[128,640]{1,0:T(8,128)(2,1)S(1)}, bf16[128,640]{1,0:T(8,128)(2,1)S(1)}, u32[]{:S(2)}, u32[]{:S(2)}) collective-permute-start(bf16[128,640]{1,0:T(8,128)(2,1)S(1)} %get-tuple-element.90), channel_id=1, source_target_pairs={{16,10},{18,12},{20,14},{22,8},{17,11},{19,13},{21,15},{23,9}} | collective-permute-start | bytes 491528 | tf_op jit(solution)/shard_map/ppermute | solution.py:808
  139.9 11.6 %collective-permute-start.23 = (bf16[128,640]{1,0:T(8,128)(2,1)S(1)}, bf16[128,640]{1,0:T(8,128)(2,1)S(1)}, u32[]{:S(2)}, u32[]{:S(2)}) collective-permute-start(bf16[128,640]{1,0:T(8,128)(2,1)S(1)} %get-tuple-element.93), channel_id=1, source_target_pairs={{8,0},{10,2},{12,4},{14,6},{9,1},{11,3},{13,5},{15,7}} | collective-permute-start | bytes 491528 | tf_op jit(solution)/shard_map/ppermute | solution.py:808
  142.0 13.3 %collective-permute-start.24 = (bf16[128,640]{1,0:T(8,128)(2,1)S(1)}, bf16[128,640]{1,0:T(8,128)(2,1)S(1)}, u32[]{:S(2)}, u32[]{:S(2)}) collective-permute-start(bf16[128,640]{1,0:T(8,128)(2,1)S(1)} %get-tuple-element.94), channel_id=1, source_target_pairs={{8,6},{10,0},{12,2},{14,4},{9,7},{11,1},{13,3},{15,5}} | collective-permute-start | bytes 491528 | tf_op jit(solution)/shard_map/ppermute | solution.py:808
  148.9 12.4 %collective-permute-start.25 = (bf16[128,640]{1,0:T(8,128)(2,1)S(1)}, bf16[128,640]{1,0:T(8,128)(2,1)S(1)}, u32[]{:S(2)}, u32[]{:S(2)}) collective-permute-start(bf16[128,640]{1,0:T(8,128)(2,1)S(1)} %get-tuple-element.95), channel_id=1, source_target_pairs={{8,4},{10,6},{12,0},{14,2},{9,5},{11,7},{13,1},{15,3}} | collective-permute-start | bytes 491528 | tf_op jit(solution)/shard_map/ppermute | solution.py:808
  150.2 13.9 %collective-permute-start.26 = (bf16[128,640]{1,0:T(8,128)(2,1)S(1)}, bf16[128,640]{1,0:T(8,128)(2,1)S(1)}, u32[]{:S(2)}, u32[]{:S(2)}) collective-permute-start(bf16[128,640]{1,0:T(8,128)(2,1)S(1)} %get-tuple-element.96), channel_id=1, source_target_pairs={{8,2},{10,4},{12,6},{14,0},{9,3},{11,5},{13,7},{15,1}} | collective-permute-start | bytes 491528 | tf_op jit(solution)/shard_map/ppermute | solution.py:808
  151.5 14.4 %collective-permute-start.27 = (bf16[128,128]{1,0:T(8,128)(2,1)S(1)}, bf16[128,128]{1,0:T(8,128)(2,1)S(1)}, u32[]{:S(2)}, u32[]{:S(2)}) collective-permute-start(bf16[128,128]{1,0:T(8,128)(2,1)S(1)} %get-tuple-element.103), channel_id=1, source_target_pairs={{8,10},{10,12},{12,14},{14,8},{16,18},{18,20},{20,22},{22,16},{9,1... | collective-permute-start | bytes 98312 | tf_op jit(solution)/shard_map/ppermute | solution.py:773
  155.4 10.5 %collective-permute-start.28 = (bf16[128,128]{1,0:T(8,128)(2,1)S(1)}, bf16[128,128]{1,0:T(8,128)(2,1)S(1)}, u32[]{:S(2)}, u32[]{:S(2)}) collective-permute-start(bf16[128,128]{1,0:T(8,128)(2,1)S(1)} %get-tuple-element.104), channel_id=1, source_target_pairs={{8,12},{10,14},{12,8},{14,10},{16,20},{18,22},{20,16},{22,18},{9,1... | collective-permute-start | bytes 98312 | tf_op jit(solution)/shard_map/ppermute | solution.py:773
  161.3 5.1 %collective-permute-start.29 = (bf16[128,128]{1,0:T(8,128)(2,1)S(1)}, bf16[128,128]{1,0:T(8,128)(2,1)S(1)}, u32[]{:S(2)}, u32[]{:S(2)}) collective-permute-start(bf16[128,128]{1,0:T(8,128)(2,1)S(1)} %get-tuple-element.105), channel_id=1, source_target_pairs={{8,14},{10,8},{12,10},{14,12},{16,22},{18,16},{20,18},{22,20},{9,1... | collective-permute-start | bytes 98312 | tf_op jit(solution)/shard_map/ppermute | solution.py:773
  170.2 9.8 %collective-permute-start.31 = (bf16[128,1024]{1,0:T(8,128)(2,1)S(1)}, bf16[128,1024]{1,0:T(8,128)(2,1)S(1)}, u32[]{:S(2)}, u32[]{:S(2)}) collective-permute-start(bf16[128,1024]{1,0:T(8,128)(2,1)S(1)} %get-tuple-element.112), channel_id=1, source_target_pairs={{0,2},{2,4},{4,6},{6,0},{8,10},{10,12},{12,14},{14,8},{16,18},{18,... | collective-permute-start | bytes 786440 | tf_op jit(solution)/shard_map/ppermute | solution.py:908
  173.6 20.4 %collective-permute-start.32 = (bf16[128,1024]{1,0:T(8,128)(2,1)S(1)}, bf16[128,1024]{1,0:T(8,128)(2,1)S(1)}, u32[]{:S(2)}, u32[]{:S(2)}) collective-permute-start(bf16[128,1024]{1,0:T(8,128)(2,1)S(1)} %get-tuple-element.113), channel_id=1, source_target_pairs={{0,4},{2,6},{4,0},{6,2},{8,12},{10,14},{12,8},{14,10},{16,20},{18,... | collective-permute-start | bytes 786440 | tf_op jit(solution)/shard_map/ppermute | solution.py:908
  176.6 21.7 %collective-permute-start.33 = (bf16[128,1024]{1,0:T(8,128)(2,1)S(1)}, bf16[128,1024]{1,0:T(8,128)(2,1)S(1)}, u32[]{:S(2)}, u32[]{:S(2)}) collective-permute-start(bf16[128,1024]{1,0:T(8,128)(2,1)S(1)} %get-tuple-element.114), channel_id=1, source_target_pairs={{0,6},{2,0},{4,2},{6,4},{8,14},{10,8},{12,10},{14,12},{16,22},{18,... | collective-permute-start | bytes 786440 | tf_op jit(solution)/shard_map/ppermute | solution.py:908

commit v5 on v4

--- a/solution.py
+++ b/solution.py
@@ -194,7 +194,7 @@
 BF16 = jnp.bfloat16
 F32 = jnp.float32
 SPACE = pltpu.VMEM
-VMEM_BYTES = 48 * 2**20
+VMEM_BYTES = 28 * 2**20
 
 
 def dot_nt(left, right, **options):
@@ -466,9 +466,11 @@
     state_ref, refs = refs[0], refs[1:]
     if final:
         own_ref, other_ref, refs = refs[0], refs[1], refs[2:]
-    cols_ref, refs = refs[0], refs[1:]
+    step_rows_ref, cols_ref, refs = refs[0], refs[1], refs[2:]
     outs, refs = refs[:chunks], refs[chunks:]
     cols, sems = refs
+    wide = cols.shape[2]
+    heads = step_rows_ref.shape[0]
     me = lax.axis_index("tensor")
     width = cols.shape[1]
     places = []
@@ -501,13 +503,16 @@
             place = pl.ds(pl.multiple_of(lax.rem(chunk, half) * width, width), width)
             held = jnp.where(mine, own_ref[:, place], other_ref[:, place])
             product = product + dot_nn(others, held)
+        product = product + dot_nn(main[:, wide : wide + heads], step_rows_ref[:, places[hop]])
         copies[hop].wait()
-        outs[hop][...] = (product + dot_nt(main, cols[hop])).astype(BF16)
+        outs[hop][...] = (product + dot_nt(main[:, :wide], cols[hop])).astype(BF16)
 
 
 def compose_kernel(half, *refs):
     rows, refs = refs[:half], refs[half:]
-    cols_ref, state_ref, joint_ref, main_sum, maps_sum = refs
+    cols_ref, step_rows_ref, state_ref, joint_ref, main_sum, maps_sum = refs
+    wide = cols_ref.shape[1]
+    heads = step_rows_ref.shape[0]
     step = pl.program_id(0)
     size = rows[0].shape[0]
     map_width = main_sum.shape[1]
@@ -517,16 +522,20 @@
     def _():
         stacked = jnp.concatenate([row[...] for row in rows], axis=0)
         main = dot_nn(stacked, cols_ref[...])
+        steps = dot_nt(stacked, step_rows_ref[...])
         maps = dot_nt(state_ref[...], stacked)
 
         @pl.when(step == 0)
         def _():
-            main_sum[...] = main
+            main_sum[:, :wide] = main
+            main_sum[:, wide:] = jnp.zeros_like(main_sum[:, wide:])
+            main_sum[:, wide : wide + heads] = steps
             maps_sum[...] = maps
 
         @pl.when(step > 0)
         def _():
-            main_sum[...] += main
+            main_sum[:, :wide] += main
+            main_sum[:, wide : wide + heads] += steps
             maps_sum[...] += maps
 
         @pl.when(step == pl.num_programs(0) - 1)
@@ -606,15 +615,21 @@
 
 def dnormed_kernel(chunks, *refs):
     incoming, refs = refs[:chunks], refs[chunks:]
-    *sources, out_ref = refs
+    *sources, out_ref, rows, sem = refs
     core = lax.axis_index("dp")
     last = lax.axis_index("pipe") == lax.axis_size("pipe") - 1
-    for lane, rows in enumerate(sources):
+    for lane, source in enumerate(sources):
 
         @pl.when(last & (core == lane))
         def _():
-            product = gathered_product(chunks, lax.axis_index("tensor"), incoming, rows)
-            out_ref[...] = product.astype(BF16)
+            copy = pltpu.make_async_copy(source, rows, sem)
+            copy.start()
+            copy.wait()
+
+    @pl.when(last)
+    def _():
+        product = gathered_product(chunks, lax.axis_index("tensor"), incoming, rows)
+        out_ref[...] = product.astype(BF16)
 
 
 def gathered_product(chunks, me, incoming, rows):
@@ -708,7 +723,7 @@
     for hop in range(1, chunks):
         incoming.append(lax.ppermute(output_grad, place, within(sections - 1, hop)))
 
-    rows = [lax.ppermute(weight_out[0], everywhere, rows_up(0))]
+    rows = [lax.ppermute(weight_out[0], everywhere, rows_up(hop)) for hop in range(half)]
     lanes = ((0, 0), (0, 128 - heads))
     by_head = jnp.pad(
         jnp.stack([step_bias[0], decay_log[0], skip_gain[0]]), ((0, 5), (0, 128 - heads))
@@ -749,10 +764,8 @@
     main_shape = jax.ShapeDtypeStruct((length, map_width), BF16)
     piece_shape = jax.ShapeDtypeStruct((length, 128), BF16)
     hbm = pl.BlockSpec(memory_space=pl.ANY)
-    step_cols, main_cols = after((weight_step[0], weight_main[0]), incoming[1])
-    step_cols = jnp.pad(step_cols.T, ((0, 0), (0, 128 - heads)))
-    main_cols = main_cols.reshape(model_width, -1)
-    cols = jnp.concatenate([main_cols, step_cols], axis=1)
+    main_cols = weight_main[0].reshape(model_width, -1)
+    step_rows = weight_step[0]
     residuals = residuals[:-1] + (after(by_head, main_cols),)
 
     main, *pieces = pl.pallas_call(
@@ -777,19 +790,17 @@
         return pl.pallas_call(
             lambda *refs: project_kernel(chunks, bool(others), *refs),
             out_shape=(message,) * chunks,
-            in_specs=whole(2 + chunks + len(newest) + len(others)) + [hbm],
+            in_specs=whole(3 + chunks + len(newest) + len(others)) + [hbm],
             out_specs=whole(chunks),
             scratch_shapes=[
-                pltpu.VMEM((chunks, width, map_width), BF16),
+                pltpu.VMEM((chunks, width, 2 * channels), BF16),
                 pltpu.SemaphoreType.DMA((chunks,)),
             ],
             compiler_params=kernel_params(),
             name="project",
-        )(main, *pieces, *newest, state_cols, *others, cols)
+        )(main, *pieces, *newest, state_cols, *others, step_rows, main_cols)
 
     pieces = share_state(pieces, [sections - 1])
-    for hop in range(1, half):
-        rows.append(lax.ppermute(after(weight_out[0], main), everywhere, rows_up(hop)))
     state_cols = after(weight_state[0], main).reshape(model_width, -1).T
     state_share = state_cols.shape[0]
     parts = project_call(main, pieces)
@@ -800,7 +811,6 @@
     grid_steps = 4
     depth = model_width // grid_steps
     rows_spec = pl.BlockSpec((channels, depth), lambda step: (0, step))
-    cols_spec = pl.BlockSpec((depth, map_width), lambda step: (step, 0))
     def pass_back(messages, active):
         moved = []
         for hop in range(chunks):
@@ -822,8 +832,12 @@
     dnormed = pl.pallas_call(
         lambda *refs: dnormed_kernel(chunks, *refs),
         out_shape=slice_out,
-        in_specs=whole(chunks + 2),
+        in_specs=whole(chunks) + [hbm] * 2,
         out_specs=pl.BlockSpec(memory_space=SPACE),
+        scratch_shapes=[
+            pltpu.VMEM((channels, model_width), BF16),
+            pltpu.SemaphoreType.DMA,
+        ],
         compiler_params=kernel_params(),
         name="dnormed_back",
     )(*exchanged, *rows)
@@ -835,7 +849,8 @@
         grid=(grid_steps,),
         out_shape=joint_shape,
         in_specs=[rows_spec] * half
-        + [cols_spec, pl.BlockSpec((state_share, depth), lambda step: (0, step))],
+        + [pl.BlockSpec((depth, 2 * channels), lambda step: (step, 0))]
+        + [pl.BlockSpec((count, depth), lambda step: (0, step)) for count in (heads, state_share)],
         out_specs=pl.BlockSpec(joint_shape.shape, lambda step: (0, 0)),
         scratch_shapes=[
             pltpu.VMEM((half * channels, map_width), F32),
@@ -843,7 +858,7 @@
         ],
         compiler_params=kernel_params(),
         name="compose_weights",
-    )(*rows[:-1], after(rows[-1], dnormed), cols, state_cols)
+    )(*rows[:-1], after(rows[-1], dnormed), main_cols, step_rows, state_cols)
 
     half_cols = lax.dynamic_slice_in_dim(
         after(state_cols, parts[0]), core * (model_width // 2), model_width // 2, 1

time: 202 us -> 197 us (0.975); the launches traced: 199 us -> 197 us
  starting transfers between devices: 60.2 us -> 65.2 us
  local copies, waits for them, and re-layouts: 10.2 us -> 6.76 us
  other arithmetic: 3.7 us -> 0.71 us
  Pallas kernels: 28.9 us -> 26.4 us
    unnamed x17 -> x40, local copies, waits for them, and re-layouts: 8.95 us -> 5.51 us
    concatenate x1 -> x0, other arithmetic: 2.99 us -> none  [relay_body(): cols = jnp.concatenate([main_cols, step_cols], axis=1)]
    pallas_call x2, Pallas kernels: 7.64 us -> 5.36 us  [project_call(): pl.pallas_call(lambda *refs: project_kernel(chunks, bool(others), *refs),...]
    ppermute x3, starting transfers between devices: 2.02 us -> 4.12 us  [relay_body(): incoming.append(lax.ppermute(output_grad, place, within(sections - 1, hop)))]
  transfers between devices with their start and end apart: 34 -> 34, of which waited for: 9 -> 7; matrix products, arithmetic and copies ran while one was open for 6% -> 4% of each run, Pallas kernels for 10% -> 10%
where the time goes in v5:
time: 197 us
  waiting for transfers between devices  96.7 us (49%)
  starting transfers between devices  65.2 us (33%)
  Pallas kernels  26.4 us (13%)
  local copies, waits for them, and re-layouts  6.76 us (3%)
    ppermute x2, waiting for transfers between devices, relay_body(): lax.ppermute(weight_out[0], everywhere, rows_up(hop))  60.4 us
    ppermute x3, waiting for transfers between devices, relay_body(): exchanged.append(lax.ppermute(parts[hop], place, pairs))  19.1 us
    ppermute x8, waiting for transfers between devices, pass_back(): moved.append(lax.ppermute(messages[hop], place, pairs))  17.2 us
    ppermute x8, starting transfers between devices, pass_back(): moved.append(lax.ppermute(messages[hop], place, pairs))  15.5 us
    ppermute x6, starting transfers between devices, share_state(): shared.append(lax.ppermute(pieces[hop], place, pairs))  15.5 us
    ppermute x3, starting transfers between devices, relay_body(): exchanged.append(lax.ppermute(parts[hop], place, pairs))  10.9 us
    ppermute x2, starting transfers between devices, relay_body(): lax.ppermute(weight_out[0], everywhere, rows_up(hop))  7.06 us
    pallas_call x1, Pallas kernels, relay_body(): pl.pallas_call(lambda *refs: compose_kernel(half, *refs), grid=(grid_step...  7 us
  transfers between devices with their start and end apart: 34, of which 7 were waited for; matrix products, arithmetic and copies ran while one was open for 4% of the time, Pallas kernels for 10%

profile of v5, /device:TPU:11, one launch (start us, length us, event | category | flops | bytes accessed | tf_op | source)
XLA Modules:
  0.0 196.5 jit_solution(2841653712677101755)
XLA Ops:
  0.0 5.1 %collective-permute-start.12 = (bf16[256,4096]{1,0:T(8,128)(2,1)}, bf16[256,4096]{1,0:T(8,128)(2,1)S(1)}, u32[]{:S(2)}, u32[]{:S(2)}) collective-permute-start(bf16[256,4096]{1,0:T(8,128)(2,1)} %bitcast.34), channel_id=1, source_target_pairs={{0,8},{1,13},{2,10},{3,15},{4,12},{5,9},{6,14},{7,11},{8,16},{9,21... | collective-permute-start | bytes 6291464 | tf_op jit(solution)/shard_map/ppermute | solution.py:726
  5.1 1.9 collective-permute-start.13
  7.1 1.4 collective-permute-start
  8.4 1.4 collective-permute-start.1
  9.8 1.4 collective-permute-start.2
  11.2 0.8 copy.17
  12.0 1.2 fusion
  13.2 0.7 select_maximum_fusion.refs_6_.refs_13_.refs_9_.refs_12_
  13.9 0.7 copy.28
  14.6 0.8 copy.27
  15.5 0.0 copy-start.16
  15.5 0.0 copy-start.15
  15.5 3.1 %copy.22 = bf16[512,8,2,256]{3,1,2,0:T(8,128)(2,1)S(1)} copy(bf16[512,8,2,256]{3,2,1,0:T(2,128)(2,1)} %bitcast.51) | data formatting | bytes 8388608
  18.7 1.2 forward_residuals.1
  19.9 0.0 copy-start.6
  20.0 3.5 %section_first.1 = (bf16[128,640]{1,0:T(8,128)(2,1)S(1)}, bf16[128,128]{1,0:T(8,128)(2,1)S(1)}, bf16[128,128]{1,0:T(8,128)(2,1)S(1)}, bf16[128,128]{1,0:T(8,128)(2,1)S(1)}, bf16[128,128]{1,0:T(8,128)(2,1)S(1)}) custom-call(bf16[128,1024]{1,0:T(8,128)(2,1)S(1)} %copy-done.15, bf16[128,1024]{1,0:T(8,128)(2,1)} %collective-permute-done.refs_1_, ...), custom_call_target="tpu_custom_call" | custom-call | tf_op jit(solution)/shard_map/section_first/pallas_call | solution.py:771
  23.5 0.7 collective-permute-start.3
  24.2 0.7 collective-permute-start.4
  24.8 0.7 collective-permute-start.5
  25.6 2.5 %project.2 = (bf16[128,1024]{1,0:T(8,128)(2,1)S(1)}, bf16[128,1024]{1,0:T(8,128)(2,1)S(1)}, bf16[128,1024]{1,0:T(8,128)(2,1)S(1)}, bf16[128,1024]{1,0:T(8,128)(2,1)S(1)}) custom-call(bf16[128,640]{1,0:T(8,128)(2,1)S(1)} %get-tuple-element.64.refs_0_, bf16[128,128]{1,0:T(8,128)(2,1)S(1)} %get-tuple-element.65.refs_1_, ...), custom_call_target="tpu_custom_call" | custom-call | tf_op jit(solution)/shard_map/project/pallas_call | solution.py:790
  28.1 0.7 collective-permute-start.6
  28.8 0.7 collective-permute-start.7
  29.5 0.7 collective-permute-start.8
  30.2 0.8 carry_next.1.refs_0_.refs_4_
  31.0 1.4 collective-permute-start.10
  32.4 1.4 collective-permute-start.11
  33.8 1.4 collective-permute-start.9
  35.2 60.4 %collective-permute-done.12.refs_4_.refs_0_ = bf16[256,4096]{1,0:T(8,128)(2,1)S(1)} collective-permute-done((bf16[256,4096]{1,0:T(8,128)(2,1)}, bf16[256,4096]{1,0:T(8,128)(2,1)S(1)}, u32[]{:S(2)}, u32[]{:S(2)}) %collective-permute-start.12) | collective-permute-done | bytes 2097184 | tf_op jit(solution)/shard_map/ppermute | solution.py:726
  95.6 1.2 dnormed_back.1
  96.8 0.7 collective-permute-start.14
  97.6 0.0 copy-start.7
  97.6 7.0 %compose_weights.1.refs_5_.refs_2_ = bf16[320,1280]{1,0:T(8,128)(2,1)S(1)} custom-call(bf16[256,4096]{1,0:T(8,128)(2,1)S(1)} %collective-permute-done.12.refs_4_.refs_0_, bf16[256,4096]{1,0:T(8,128)(2,1)} %collective-permute-done.13.refs_5_.refs_1_, bf16[4096,512]{1,0:T(8,128)(2,1)S(1)} %bitcast.28, bf16[4,4096]{1,0:T(4,128)(2,1)S(1)} %bitcast.38, ...), custom_call_target="tpu_custom_call" | custom-call | tf_op jit(solution)/shard_map/compose_weights/pallas_call | solution.py:847
  104.7 0.7 section_next.3
  105.4 2.5 %collective-permute-start.18 = (bf16[320,1280]{1,0:T(8,128)(2,1)S(1)}, bf16[320,1280]{1,0:T(8,128)(2,1)S(1)}, u32[]{:S(2)}, u32[]{:S(2)}) collective-permute-start(bf16[320,1280]{1,0:T(8,128)(2,1)S(1)} %compose_weights.1.refs_5_.refs_2_), channel_id=1, source_target_pairs={{8,9},{9,8},{10,11},{11,10},{12,13},{13,12},{14,15},{15,14},{16,17... | collective-permute-start | bytes 2457608 | tf_op jit(solution)/shard_map/ppermute | solution.py:720
  107.9 0.7 collective-permute-start.15
  108.6 0.7 collective-permute-start.16
  109.3 0.7 collective-permute-start.17
  110.0 0.8 send_back.2
  110.8 0.7 collective-permute-start.30
  111.6 1.3 collective-permute-start.19
  112.9 1.3 collective-permute-start.20
  114.2 1.3 collective-permute-start.21
  115.5 1.3 collective-permute-start.22
  116.8 4.4 %collective-permute-done.19.refs_0_ = bf16[128,640]{1,0:T(8,128)(2,1)S(1)} collective-permute-done((bf16[128,640]{1,0:T(8,128)(2,1)S(1)}, bf16[128,640]{1,0:T(8,128)(2,1)S(1)}, u32[]{:S(2)}, u32[]{:S(2)}) %collective-permute-start.19) | collective-permute-done | bytes 163872 | tf_op jit(solution)/shard_map/ppermute | solution.py:818
  121.2 4.7 %collective-permute-done.20.refs_1_ = bf16[128,640]{1,0:T(8,128)(2,1)S(1)} collective-permute-done((bf16[128,640]{1,0:T(8,128)(2,1)S(1)}, bf16[128,640]{1,0:T(8,128)(2,1)S(1)}, u32[]{:S(2)}, u32[]{:S(2)}) %collective-permute-start.20) | collective-permute-done | bytes 163872 | tf_op jit(solution)/shard_map/ppermute | solution.py:818
  125.9 4.5 %collective-permute-done.21.refs_2_ = bf16[128,640]{1,0:T(8,128)(2,1)S(1)} collective-permute-done((bf16[128,640]{1,0:T(8,128)(2,1)S(1)}, bf16[128,640]{1,0:T(8,128)(2,1)S(1)}, u32[]{:S(2)}, u32[]{:S(2)}) %collective-permute-start.21) | collective-permute-done | bytes 163872 | tf_op jit(solution)/shard_map/ppermute | solution.py:818
  130.4 3.5 %collective-permute-done.22.refs_3_ = bf16[128,640]{1,0:T(8,128)(2,1)S(1)} collective-permute-done((bf16[128,640]{1,0:T(8,128)(2,1)S(1)}, bf16[128,640]{1,0:T(8,128)(2,1)S(1)}, u32[]{:S(2)}, u32[]{:S(2)}) %collective-permute-start.22) | collective-permute-done | bytes 163872 | tf_op jit(solution)/shard_map/ppermute | solution.py:818
  133.9 1.3 section_next.4
  135.2 0.8 send_back.3
  136.1 1.3 collective-permute-start.23
  137.4 6.5 %collective-permute-start.24 = (bf16[128,640]{1,0:T(8,128)(2,1)S(1)}, bf16[128,640]{1,0:T(8,128)(2,1)S(1)}, u32[]{:S(2)}, u32[]{:S(2)}) collective-permute-start(bf16[128,640]{1,0:T(8,128)(2,1)S(1)} %get-tuple-element.88), channel_id=1, source_target_pairs={{8,6},{10,0},{12,2},{14,4},{9,7},{11,1},{13,3},{15,5}} | collective-permute-start | bytes 491528 | tf_op jit(solution)/shard_map/ppermute | solution.py:818
  143.9 1.3 collective-permute-start.25
  145.2 1.3 collective-permute-start.26
  146.5 8.3 %collective-permute-start.27 = (bf16[128,128]{1,0:T(8,128)(2,1)S(1)}, bf16[128,128]{1,0:T(8,128)(2,1)S(1)}, u32[]{:S(2)}, u32[]{:S(2)}) collective-permute-start(bf16[128,128]{1,0:T(8,128)(2,1)S(1)} %get-tuple-element.97), channel_id=1, source_target_pairs={{8,10},{10,12},{12,14},{14,8},{16,18},{18,20},{20,22},{22,16},{9,1... | collective-permute-start | bytes 98312 | tf_op jit(solution)/shard_map/ppermute | solution.py:786
  154.9 1.9 collective-permute-start.28
  156.8 3.3 %collective-permute-start.29 = (bf16[128,128]{1,0:T(8,128)(2,1)S(1)}, bf16[128,128]{1,0:T(8,128)(2,1)S(1)}, u32[]{:S(2)}, u32[]{:S(2)}) collective-permute-start(bf16[128,128]{1,0:T(8,128)(2,1)S(1)} %get-tuple-element.99), channel_id=1, source_target_pairs={{8,14},{10,8},{12,10},{14,12},{16,22},{18,16},{20,18},{22,20},{9,1... | collective-permute-start | bytes 98312 | tf_op jit(solution)/shard_map/ppermute | solution.py:786
  160.1 1.8 section_next.5
  161.9 2.9 %project.3 = (bf16[128,1024]{1,0:T(8,128)(2,1)S(1)}, bf16[128,1024]{1,0:T(8,128)(2,1)S(1)}, bf16[128,1024]{1,0:T(8,128)(2,1)S(1)}, bf16[128,1024]{1,0:T(8,128)(2,1)S(1)}) custom-call(bf16[128,640]{1,0:T(8,128)(2,1)S(1)} %get-tuple-element.91.refs_0_, bf16[128,128]{1,0:T(8,128)(2,1)S(1)} %get-tuple-element.96.refs_1_, ...), custom_call_target="tpu_custom_call" | custom-call | tf_op jit(solution)/shard_map/project/pallas_call | solution.py:790
  164.8 3.3 %collective-permute-start.31 = (bf16[128,1024]{1,0:T(8,128)(2,1)S(1)}, bf16[128,1024]{1,0:T(8,128)(2,1)S(1)}, u32[]{:S(2)}, u32[]{:S(2)}) collective-permute-start(bf16[128,1024]{1,0:T(8,128)(2,1)S(1)} %get-tuple-element.106), channel_id=1, source_target_pairs={{0,2},{2,4},{4,6},{6,0},{8,10},{10,12},{12,14},{14,8},{16,18},{18,... | collective-permute-start | bytes 786440 | tf_op jit(solution)/shard_map/ppermute | solution.py:923
  168.1 5.0 %collective-permute-start.32 = (bf16[128,1024]{1,0:T(8,128)(2,1)S(1)}, bf16[128,1024]{1,0:T(8,128)(2,1)S(1)}, u32[]{:S(2)}, u32[]{:S(2)}) collective-permute-start(bf16[128,1024]{1,0:T(8,128)(2,1)S(1)} %get-tuple-element.107), channel_id=1, source_target_pairs={{0,4},{2,6},{4,0},{6,2},{8,12},{10,14},{12,8},{14,10},{16,20},{18,... | collective-permute-start | bytes 786440 | tf_op jit(solution)/shard_map/ppermute | solution.py:923
  173.0 2.6 %collective-permute-start.33 = (bf16[128,1024]{1,0:T(8,128)(2,1)S(1)}, bf16[128,1024]{1,0:T(8,128)(2,1)S(1)}, u32[]{:S(2)}, u32[]{:S(2)}) collective-permute-start(bf16[128,1024]{1,0:T(8,128)(2,1)S(1)} %get-tuple-element.108), channel_id=1, source_target_pairs={{0,6},{2,0},{4,2},{6,4},{8,14},{10,8},{12,10},{14,12},{16,22},{18,... | collective-permute-start | bytes 786440 | tf_op jit(solution)/shard_map/ppermute | solution.py:923
  175.7 14.8 %collective-permute-done.32.refs_2_ = bf16[128,1024]{1,0:T(8,128)(2,1)S(1)} collective-permute-done((bf16[128,1024]{1,0:T(8,128)(2,1)S(1)}, bf16[128,1024]{1,0:T(8,128)(2,1)S(1)}, u32[]{:S(2)}, u32[]{:S(2)}) %collective-permute-start.32) | collective-permute-done | bytes 262176 | tf_op jit(solution)/shard_map/ppermute | solution.py:923
  190.4 4.3 %collective-permute-done.33.refs_3_ = bf16[128,1024]{1,0:T(8,128)(2,1)S(1)} collective-permute-done((bf16[128,1024]{1,0:T(8,128)(2,1)S(1)}, bf16[128,1024]{1,0:T(8,128)(2,1)S(1)}, u32[]{:S(2)}, u32[]{:S(2)}) %collective-permute-start.33) | collective-permute-done | bytes 262176 | tf_op jit(solution)/shard_map/ppermute | solution.py:923
  194.8 1.8 carry_last.1
  (62 shorter events, 0.2 us)
Async XLA Ops:
  0.0 95.6 %collective-permute-start.12 = (bf16[256,4096]{1,0:T(8,128)(2,1)}, bf16[256,4096]{1,0:T(8,128)(2,1)S(1)}, u32[]{:S(2)}, u32[]{:S(2)}) collective-permute-start(bf16[256,4096]{1,0:T(8,128)(2,1)} %bitcast.34), channel_id=1, source_target_pairs={{0,8},{1,13},{2,10},{3,15},{4,12},{5,9},{6,14},{7,11},{8,16},{9,21... | collective-permute-start | bytes 6291464 | tf_op jit(solution)/shard_map/ppermute | solution.py:726
  5.1 90.5 %collective-permute-start.13 = (bf16[256,4096]{1,0:T(8,128)(2,1)}, bf16[256,4096]{1,0:T(8,128)(2,1)}, u32[]{:S(2)}, u32[]{:S(2)}) collective-permute-start(bf16[256,4096]{1,0:T(8,128)(2,1)} %bitcast.35), channel_id=1, source_target_pairs={{0,10},{1,15},{2,12},{3,9},{4,14},{5,11},{6,8},{7,13},{8,18},{9,23... | collective-permute-start | bytes 6291464 | tf_op jit(solution)/shard_map/ppermute | solution.py:726
  7.1 12.8 %collective-permute-start = (bf16[128,1024]{1,0:T(8,128)(2,1)}, bf16[128,1024]{1,0:T(8,128)(2,1)}, u32[]{:S(2)}, u32[]{:S(2)}) collective-permute-start(bf16[128,1024]{1,0:T(8,128)(2,1)} %refs_0_.1), channel_id=1, source_target_pairs={{24,26},{26,28},{28,30},{30,24},{25,27},{27,29},{29,31},{31,25}} | collective-permute-start | bytes 786440 | tf_op jit(solution)/shard_map/ppermute | solution.py:724
  8.4 11.5 %collective-permute-start.1 = (bf16[128,1024]{1,0:T(8,128)(2,1)}, bf16[128,1024]{1,0:T(8,128)(2,1)}, u32[]{:S(2)}, u32[]{:S(2)}) collective-permute-start(bf16[128,1024]{1,0:T(8,128)(2,1)} %refs_0_.1), channel_id=1, source_target_pairs={{24,28},{26,30},{28,24},{30,26},{25,29},{27,31},{29,25},{31,27}} | collective-permute-start | bytes 786440 | tf_op jit(solution)/shard_map/ppermute | solution.py:724
  9.8 10.1 %collective-permute-start.2 = (bf16[128,1024]{1,0:T(8,128)(2,1)}, bf16[128,1024]{1,0:T(8,128)(2,1)}, u32[]{:S(2)}, u32[]{:S(2)}) collective-permute-start(bf16[128,1024]{1,0:T(8,128)(2,1)} %refs_0_.1), channel_id=1, source_target_pairs={{24,30},{26,24},{28,26},{30,28},{25,31},{27,25},{29,27},{31,29}} | collective-permute-start | bytes 786440 | tf_op jit(solution)/shard_map/ppermute | solution.py:724
  15.5 3.2 %copy-start.16 = (f32[1,4,256]{2,1,0:T(4,128)S(1)}, f32[1,4,256]{2,1,0:T(4,128)}, u32[]{:S(2)}) copy-start(f32[1,4,256]{2,1,0:T(4,128)} %param.18) | copy-start | bytes 12292
  15.5 3.2 %copy-start.17 = (f32[1,256]{1,0:T(1,128)S(1)}, f32[1,256]{1,0:T(1,128)}, u32[]{:S(2)}) copy-start(f32[1,256]{1,0:T(1,128)} %refs_7_.1) | copy-start | bytes 3076
  15.5 4.4 %copy-start.8 = (bf16[1,256,4096]{2,1,0:T(8,128)(2,1)S(1)}, bf16[1,256,4096]{2,1,0:T(8,128)(2,1)}, u32[]{:S(2)}) copy-start(bf16[1,256,4096]{2,1,0:T(8,128)(2,1)} %param.17) | copy-start | bytes 6291460
  15.5 4.4 %copy-start.15 = (bf16[128,1024]{1,0:T(8,128)(2,1)S(1)}, bf16[128,1024]{1,0:T(8,128)(2,1)}, u32[]{:S(2)}) copy-start(bf16[128,1024]{1,0:T(8,128)(2,1)} %refs_0_.1) | copy-start | bytes 786436
  18.6 6.9 %copy-start = (bf16[512,8,2,256]{3,1,2,0:T(8,128)(2,1)}, bf16[512,8,2,256]{3,1,2,0:T(8,128)(2,1)S(1)}, u32[]{:S(2)}) copy-start(bf16[512,8,2,256]{3,1,2,0:T(8,128)(2,1)S(1)} %copy.22) | copy-start | bytes 12582916
  19.9 3.6 %copy-start.2 = (f32[2,128,512]{2,1,0:T(8,128)}, f32[2,128,512]{2,1,0:T(8,128)S(1)}, u32[]{:S(2)}) copy-start(f32[2,128,512]{2,1,0:T(8,128)S(1)} %get-tuple-element.58.refs_6_.refs_2_.refs_5_) | copy-start | bytes 1572868
  19.9 3.6 %copy-start.6 = (bf16[128,512]{1,0:T(8,128)(2,1)}, bf16[128,512]{1,0:T(8,128)(2,1)S(1)}, u32[]{:S(2)}) copy-start(bf16[128,512]{1,0:T(8,128)(2,1)S(1)} %get-tuple-element.59.refs_7_.refs_3_.refs_6_) | copy-start | bytes 393220
  19.9 3.6 %copy-start.9 = (bf16[2,128,128]{2,1,0:T(8,128)(2,1)}, bf16[2,128,128]{2,1,0:T(8,128)(2,1)S(1)}, u32[]{:S(2)}) copy-start(bf16[2,128,128]{2,1,0:T(8,128)(2,1)S(1)} %get-tuple-element.61.refs_9_.refs_5_.refs_8_) | copy-start | bytes 196612
  19.9 3.6 %copy-start.11 = (f32[128,128]{1,0:T(8,128)}, f32[128,128]{1,0:T(8,128)S(1)}, u32[]{:S(2)}) copy-start(f32[128,128]{1,0:T(8,128)S(1)} %get-tuple-element.62.refs_10_.refs_6_.refs_9_) | copy-start | bytes 196612
  19.9 5.6 %copy-start.4 = (bf16[1,4096,2,32]{1,3,2,0:T(8,128)(2,1)S(1)}, bf16[1,4096,2,32]{1,3,2,0:T(8,128)(2,1)}, u32[]{:S(2)}) copy-start(bf16[1,4096,2,32]{1,3,2,0:T(8,128)(2,1)} %param.15) | copy-start | bytes 1572868
  20.0 5.6 %copy-start.13 = (bf16[1,4,4096]{2,1,0:T(4,128)(2,1)S(1)}, bf16[1,4,4096]{2,1,0:T(4,128)(2,1)}, u32[]{:S(2)}) copy-start(bf16[1,4,4096]{2,1,0:T(4,128)(2,1)} %param.16) | copy-start | bytes 98308
  23.5 2.0 %collective-permute-start.3 = (bf16[128,128]{1,0:T(8,128)(2,1)S(1)}, bf16[128,128]{1,0:T(8,128)(2,1)S(1)}, u32[]{:S(2)}, u32[]{:S(2)}) collective-permute-start(bf16[128,128]{1,0:T(8,128)(2,1)S(1)} %get-tuple-element.66), channel_id=1, source_target_pairs={{24,26},{26,28},{28,30},{30,24},{25,27},{27,29},{29,31},{31,25}} | collective-permute-start | bytes 98312 | tf_op jit(solution)/shard_map/ppermute | solution.py:786
  24.2 1.4 collective-permute-start.4
  24.8 0.7 collective-permute-start.5
  28.1 2.1 %collective-permute-start.6 = (bf16[128,1024]{1,0:T(8,128)(2,1)S(1)}, bf16[128,1024]{1,0:T(8,128)(2,1)S(1)}, u32[]{:S(2)}, u32[]{:S(2)}) collective-permute-start(bf16[128,1024]{1,0:T(8,128)(2,1)S(1)} %get-tuple-element.71), channel_id=1, source_target_pairs={{24,26},{26,28},{28,30},{30,24},{25,27},{27,29},{29,31},{31,25}} | collective-permute-start | bytes 786440 | tf_op jit(solution)/shard_map/ppermute | solution.py:809
  28.8 1.4 collective-permute-start.7
  29.5 0.7 collective-permute-start.8
  31.0 4.1 %collective-permute-start.10 = (bf16[128,1024]{1,0:T(8,128)(2,1)}, bf16[128,1024]{1,0:T(8,128)(2,1)}, u32[]{:S(2)}, u32[]{:S(2)}) collective-permute-start(bf16[128,1024]{1,0:T(8,128)(2,1)} %carry_next.1.refs_0_.refs_4_), channel_id=1, source_target_pairs={{24,28},{26,30},{28,24},{30,26},{25,29},{27,31},{29,25},{31,27}} | collective-permute-start | bytes 786440 | tf_op jit(solution)/shard_map/ppermute | solution.py:831
  32.4 2.8 %collective-permute-start.11 = (bf16[128,1024]{1,0:T(8,128)(2,1)}, bf16[128,1024]{1,0:T(8,128)(2,1)}, u32[]{:S(2)}, u32[]{:S(2)}) collective-permute-start(bf16[128,1024]{1,0:T(8,128)(2,1)} %carry_next.1.refs_0_.refs_4_), channel_id=1, source_target_pairs={{24,30},{26,24},{28,26},{30,28},{25,31},{27,25},{29,27},{31,29}} | collective-permute-start | bytes 786440 | tf_op jit(solution)/shard_map/ppermute | solution.py:831
  33.8 1.4 collective-permute-start.9
  35.1 62.4 %copy-start.5 = (bf16[1,4096,2,32]{1,3,2,0:T(8,128)(2,1)S(1)}, bf16[1,4096,2,32]{1,3,2,0:T(8,128)(2,1)}, u32[]{:S(2)}) copy-start(bf16[1,4096,2,32]{1,3,2,0:T(8,128)(2,1)} %param.15) | copy-start | bytes 1572868
  35.1 62.4 %copy-start.1 = (bf16[512,8,2,256]{3,1,2,0:T(8,128)(2,1)S(1)}, bf16[512,8,2,256]{3,1,2,0:T(8,128)(2,1)}, u32[]{:S(2)}) copy-start(bf16[512,8,2,256]{3,1,2,0:T(8,128)(2,1)} %copy-done) | copy-start | bytes 12582916
  35.1 62.4 %copy-start.14 = (bf16[1,4,4096]{2,1,0:T(4,128)(2,1)S(1)}, bf16[1,4,4096]{2,1,0:T(4,128)(2,1)}, u32[]{:S(2)}) copy-start(bf16[1,4,4096]{2,1,0:T(4,128)(2,1)} %param.16) | copy-start | bytes 98308
  96.8 7.8 %collective-permute-start.14 = (bf16[128,256]{1,0:T(8,128)(2,1)S(1)}, bf16[128,256]{1,0:T(8,128)(2,1)S(1)}, u32[]{:S(2)}, u32[]{:S(2)}) collective-permute-start(bf16[128,256]{1,0:T(8,128)(2,1)S(1)} %dnormed_back.1), channel_id=1, source_target_pairs={{24,16},{26,18},{28,20},{30,22},{25,17},{27,19},{29,21},{31,23}} | collective-permute-start | bytes 196616 | tf_op jit(solution)/shard_map/ppermute | solution.py:845
  97.6 7.1 %copy-start.3 = (f32[2,128,512]{2,1,0:T(8,128)S(1)}, f32[2,128,512]{2,1,0:T(8,128)}, u32[]{:S(2)}) copy-start(f32[2,128,512]{2,1,0:T(8,128)} %copy-done.2) | copy-start | bytes 1572868
  97.6 7.1 %copy-start.7 = (bf16[128,512]{1,0:T(8,128)(2,1)S(1)}, bf16[128,512]{1,0:T(8,128)(2,1)}, u32[]{:S(2)}) copy-start(bf16[128,512]{1,0:T(8,128)(2,1)} %copy-done.6) | copy-start | bytes 393220
  97.6 7.1 %copy-start.10 = (bf16[2,128,128]{2,1,0:T(8,128)(2,1)S(1)}, bf16[2,128,128]{2,1,0:T(8,128)(2,1)}, u32[]{:S(2)}) copy-start(bf16[2,128,128]{2,1,0:T(8,128)(2,1)} %copy-done.9) | copy-start | bytes 196612
  97.6 7.1 %copy-start.12 = (f32[128,128]{1,0:T(8,128)S(1)}, f32[128,128]{1,0:T(8,128)}, u32[]{:S(2)}) copy-start(f32[128,128]{1,0:T(8,128)} %copy-done.11) | copy-start | bytes 196612
  105.4 4.6 %collective-permute-start.18 = (bf16[320,1280]{1,0:T(8,128)(2,1)S(1)}, bf16[320,1280]{1,0:T(8,128)(2,1)S(1)}, u32[]{:S(2)}, u32[]{:S(2)}) collective-permute-start(bf16[320,1280]{1,0:T(8,128)(2,1)S(1)} %compose_weights.1.refs_5_.refs_2_), channel_id=1, source_target_pairs={{8,9},{9,8},{10,11},{11,10},{12,13},{13,12},{14,15},{15,14},{16,17... | collective-permute-start | bytes 2457608 | tf_op jit(solution)/shard_map/ppermute | solution.py:720
  107.9 2.1 %collective-permute-start.15 = (bf16[64,2048]{1,0:T(8,128)(2,1)S(1)}, bf16[64,2048]{1,0:T(8,128)(2,1)S(1)}, u32[]{:S(2)}, u32[]{:S(2)}) collective-permute-start(bf16[64,2048]{1,0:T(8,128)(2,1)S(1)} %constant_dynamic-slice_fusion), channel_id=1, source_target_pairs={{0,6},{2,0},{4,2},{6,4},{1,7},{3,1},{5,3},{7,5}} | collective-permute-start | bytes 786440 | tf_op jit(solution)/shard_map/ppermute | solution.py:897
  108.6 1.4 collective-permute-start.16
  109.3 0.7 collective-permute-start.17
  110.8 51.1 %collective-permute-start.30 = (bf16[192,2048]{1,0:T(8,128)(2,1)S(1)}, bf16[192,2048]{1,0:T(8,128)(2,1)S(1)}, u32[]{:S(2)}, u32[]{:S(2)}) collective-permute-start(bf16[192,2048]{1,0:T(8,128)(2,1)S(1)} %get-tuple-element.104.refs_10_), channel_id=1, source_target_pairs={{0,1},{1,0},{2,3},{3,2},{4,5},{5,4},{6,7},{7,6}} | collective-permute-start | bytes 2359304 | tf_op jit(solution)/shard_map/ppermute | solution.py:720
  111.6 9.6 %collective-permute-start.19 = (bf16[128,640]{1,0:T(8,128)(2,1)S(1)}, bf16[128,640]{1,0:T(8,128)(2,1)S(1)}, u32[]{:S(2)}, u32[]{:S(2)}) collective-permute-start(bf16[128,640]{1,0:T(8,128)(2,1)S(1)} %get-tuple-element.81), channel_id=1, source_target_pairs={{16,8},{18,10},{20,12},{22,14},{17,9},{19,11},{21,13},{23,15}} | collective-permute-start | bytes 491528 | tf_op jit(solution)/shard_map/ppermute | solution.py:818
  112.9 13.0 %collective-permute-start.20 = (bf16[128,640]{1,0:T(8,128)(2,1)S(1)}, bf16[128,640]{1,0:T(8,128)(2,1)S(1)}, u32[]{:S(2)}, u32[]{:S(2)}) collective-permute-start(bf16[128,640]{1,0:T(8,128)(2,1)S(1)} %get-tuple-element.82), channel_id=1, source_target_pairs={{16,14},{18,8},{20,10},{22,12},{17,15},{19,9},{21,11},{23,13}} | collective-permute-start | bytes 491528 | tf_op jit(solution)/shard_map/ppermute | solution.py:818
  114.2 16.2 %collective-permute-start.21 = (bf16[128,640]{1,0:T(8,128)(2,1)S(1)}, bf16[128,640]{1,0:T(8,128)(2,1)S(1)}, u32[]{:S(2)}, u32[]{:S(2)}) collective-permute-start(bf16[128,640]{1,0:T(8,128)(2,1)S(1)} %get-tuple-element.83), channel_id=1, source_target_pairs={{16,12},{18,14},{20,8},{22,10},{17,13},{19,15},{21,9},{23,11}} | collective-permute-start | bytes 491528 | tf_op jit(solution)/shard_map/ppermute | solution.py:818
  115.5 18.4 %collective-permute-start.22 = (bf16[128,640]{1,0:T(8,128)(2,1)S(1)}, bf16[128,640]{1,0:T(8,128)(2,1)S(1)}, u32[]{:S(2)}, u32[]{:S(2)}) collective-permute-start(bf16[128,640]{1,0:T(8,128)(2,1)S(1)} %get-tuple-element.84), channel_id=1, source_target_pairs={{16,10},{18,12},{20,14},{22,8},{17,11},{19,13},{21,15},{23,9}} | collective-permute-start | bytes 491528 | tf_op jit(solution)/shard_map/ppermute | solution.py:818
  136.1 10.4 %collective-permute-start.23 = (bf16[128,640]{1,0:T(8,128)(2,1)S(1)}, bf16[128,640]{1,0:T(8,128)(2,1)S(1)}, u32[]{:S(2)}, u32[]{:S(2)}) collective-permute-start(bf16[128,640]{1,0:T(8,128)(2,1)S(1)} %get-tuple-element.87), channel_id=1, source_target_pairs={{8,0},{10,2},{12,4},{14,6},{9,1},{11,3},{13,5},{15,7}} | collective-permute-start | bytes 491528 | tf_op jit(solution)/shard_map/ppermute | solution.py:818
  137.4 17.5 %collective-permute-start.24 = (bf16[128,640]{1,0:T(8,128)(2,1)S(1)}, bf16[128,640]{1,0:T(8,128)(2,1)S(1)}, u32[]{:S(2)}, u32[]{:S(2)}) collective-permute-start(bf16[128,640]{1,0:T(8,128)(2,1)S(1)} %get-tuple-element.88), channel_id=1, source_target_pairs={{8,6},{10,0},{12,2},{14,4},{9,7},{11,1},{13,3},{15,5}} | collective-permute-start | bytes 491528 | tf_op jit(solution)/shard_map/ppermute | solution.py:818
  143.9 12.9 %collective-permute-start.25 = (bf16[128,640]{1,0:T(8,128)(2,1)S(1)}, bf16[128,640]{1,0:T(8,128)(2,1)S(1)}, u32[]{:S(2)}, u32[]{:S(2)}) collective-permute-start(bf16[128,640]{1,0:T(8,128)(2,1)S(1)} %get-tuple-element.89), channel_id=1, source_target_pairs={{8,4},{10,6},{12,0},{14,2},{9,5},{11,7},{13,1},{15,3}} | collective-permute-start | bytes 491528 | tf_op jit(solution)/shard_map/ppermute | solution.py:818
  145.2 14.9 %collective-permute-start.26 = (bf16[128,640]{1,0:T(8,128)(2,1)S(1)}, bf16[128,640]{1,0:T(8,128)(2,1)S(1)}, u32[]{:S(2)}, u32[]{:S(2)}) collective-permute-start(bf16[128,640]{1,0:T(8,128)(2,1)S(1)} %get-tuple-element.90), channel_id=1, source_target_pairs={{8,2},{10,4},{12,6},{14,0},{9,3},{11,5},{13,7},{15,1}} | collective-permute-start | bytes 491528 | tf_op jit(solution)/shard_map/ppermute | solution.py:818
  146.5 15.4 %collective-permute-start.27 = (bf16[128,128]{1,0:T(8,128)(2,1)S(1)}, bf16[128,128]{1,0:T(8,128)(2,1)S(1)}, u32[]{:S(2)}, u32[]{:S(2)}) collective-permute-start(bf16[128,128]{1,0:T(8,128)(2,1)S(1)} %get-tuple-element.97), channel_id=1, source_target_pairs={{8,10},{10,12},{12,14},{14,8},{16,18},{18,20},{20,22},{22,16},{9,1... | collective-permute-start | bytes 98312 | tf_op jit(solution)/shard_map/ppermute | solution.py:786
  154.9 7.0 %collective-permute-start.28 = (bf16[128,128]{1,0:T(8,128)(2,1)S(1)}, bf16[128,128]{1,0:T(8,128)(2,1)S(1)}, u32[]{:S(2)}, u32[]{:S(2)}) collective-permute-start(bf16[128,128]{1,0:T(8,128)(2,1)S(1)} %get-tuple-element.98), channel_id=1, source_target_pairs={{8,12},{10,14},{12,8},{14,10},{16,20},{18,22},{20,16},{22,18},{9,1... | collective-permute-start | bytes 98312 | tf_op jit(solution)/shard_map/ppermute | solution.py:786
  156.8 5.1 %collective-permute-start.29 = (bf16[128,128]{1,0:T(8,128)(2,1)S(1)}, bf16[128,128]{1,0:T(8,128)(2,1)S(1)}, u32[]{:S(2)}, u32[]{:S(2)}) collective-permute-start(bf16[128,128]{1,0:T(8,128)(2,1)S(1)} %get-tuple-element.99), channel_id=1, source_target_pairs={{8,14},{10,8},{12,10},{14,12},{16,22},{18,16},{20,18},{22,20},{9,1... | collective-permute-start | bytes 98312 | tf_op jit(solution)/shard_map/ppermute | solution.py:786
  164.8 10.9 %collective-permute-start.31 = (bf16[128,1024]{1,0:T(8,128)(2,1)S(1)}, bf16[128,1024]{1,0:T(8,128)(2,1)S(1)}, u32[]{:S(2)}, u32[]{:S(2)}) collective-permute-start(bf16[128,1024]{1,0:T(8,128)(2,1)S(1)} %get-tuple-element.106), channel_id=1, source_target_pairs={{0,2},{2,4},{4,6},{6,0},{8,10},{10,12},{12,14},{14,8},{16,18},{18,... | collective-permute-start | bytes 786440 | tf_op jit(solution)/shard_map/ppermute | solution.py:923
  168.1 22.4 %collective-permute-start.32 = (bf16[128,1024]{1,0:T(8,128)(2,1)S(1)}, bf16[128,1024]{1,0:T(8,128)(2,1)S(1)}, u32[]{:S(2)}, u32[]{:S(2)}) collective-permute-start(bf16[128,1024]{1,0:T(8,128)(2,1)S(1)} %get-tuple-element.107), channel_id=1, source_target_pairs={{0,4},{2,6},{4,0},{6,2},{8,12},{10,14},{12,8},{14,10},{16,20},{18,... | collective-permute-start | bytes 786440 | tf_op jit(solution)/shard_map/ppermute | solution.py:923
  173.0 21.7 %collective-permute-start.33 = (bf16[128,1024]{1,0:T(8,128)(2,1)S(1)}, bf16[128,1024]{1,0:T(8,128)(2,1)S(1)}, u32[]{:S(2)}, u32[]{:S(2)}) collective-permute-start(bf16[128,1024]{1,0:T(8,128)(2,1)S(1)} %get-tuple-element.108), channel_id=1, source_target_pairs={{0,6},{2,0},{4,2},{6,4},{8,14},{10,8},{12,10},{14,12},{16,22},{18,... | collective-permute-start | bytes 786440 | tf_op jit(solution)/shard_map/ppermute | solution.py:923

commit v6 on v5

--- a/solution.py
+++ b/solution.py
@@ -425,7 +425,7 @@
     for message in incoming[1:]:
         dnormed = dnormed + message[:, :channels].astype(F32)
     states = residuals[4].shape[2] * 2
-    joined = count > 1
+    joined = incoming[0].shape[1] > channels
     if joined:
         place = slice(channels, channels + states)
         state = incoming[0][:, place].astype(F32)
@@ -439,14 +439,14 @@
             halves = [incoming[hop][start : start + share, place] for start in (0, share)]
             dnormed = dnormed + jnp.concatenate([dot_nn(piece, half) for half in halves], axis=1)
     main, state = mixer_back(heads, dnormed, residuals)
-    if joined:
+    if count > 1:
         done = lax.axis_index("pipe") > active
         main = jnp.where(done, refs[0][...], main)
         state = jnp.where(done, refs[1][...], state)
         refs = refs[2:]
     refs[0][...] = main
     refs[1][...] = state
-    if joined:
+    if count > 1:
         for ref, piece in zip(refs[2:], picked_members(chunks, state)):
             ref[...] = piece
 
@@ -556,18 +556,11 @@
     ]
 
 
-def send_kernel(chunks, count, main_ref, state_ref, *refs):
-    others, refs = refs[:count], refs[count:]
+def send_kernel(chunks, ahead, main_ref, state_ref, *refs):
+    others, refs = refs[: chunks - 1], refs[chunks - 1 :]
     sources, refs = refs[:2], refs[2:]
-    outs, others_ref, held, sems = refs[:chunks], refs[chunks], refs[chunks + 1 : -1], refs[-1]
-    if count:
-
-        @pl.when(lax.axis_index("pipe") == 0)
-        def _():
-            for index, other in enumerate(others):
-                size = other.shape[0]
-                others_ref[index * size : (index + 1) * size, :] = other[...]
-
+    outs, refs = refs[:chunks], refs[chunks:]
+    held, sems = refs[-3:-1], refs[-1]
     half = chunks // 2
     map_width = main_ref.shape[1]
     states = state_ref.shape[1]
@@ -579,7 +572,18 @@
     ]
     for copy in copies:
         copy.start()
+    if ahead:
+        stack_ref, map_ref = refs[:2]
+
+        @pl.when(lax.axis_index("pipe") == 0)
+        def _():
+            for index, other in enumerate(others):
+                stack_ref[index * share : (index + 1) * share, :] = other[...]
+
     main = main_ref[...]
+    state = state_ref[...]
+    if not ahead:
+        pieces = picked_members(chunks, state)
     for copy in copies:
         copy.wait()
 
@@ -594,23 +598,27 @@
 
     total = by_hop(chunks, terms(held[0]), terms(held[1]))
     kept = by_hop(chunks, maps(held[0]), maps(held[1]))
+    if not ahead:
+        for hop in range(chunks):
+            total[hop] = total[hop] + dot_nn(pieces[0][:, :share], kept[hop])
+        for away, other in enumerate(others, 1):
+            term = dot_nn(pieces[away][:, :share], other[...])
+            for hop in range(chunks):
+                start = (hop + away) % chunks * size
+                total[hop] = total[hop] + term[:, start : start + size]
     for hop in range(chunks):
         outs[hop][:, :size] = total[hop].astype(BF16)
-        outs[hop][:, size : size + states] = state_ref[...]
-        for part in range(2):
-            outs[hop][part * share : (part + 1) * share, size + states :] = kept[hop][
-                :, part * (size // 2) : (part + 1) * (size // 2)
-            ]
-
-
-def carry_kernel(chunks, last, *refs):
-    carry = sum_pieces(refs[:chunks], refs[0].shape[1])
-    if last:
-        done_ref, out_ref = refs[chunks:]
-        is_last = lax.axis_index("pipe") == lax.axis_size("pipe") - 1
-        out_ref[0] = jnp.where(is_last, done_ref[...], carry)
-    else:
-        refs[-1][...] = carry
+        if ahead:
+            map_ref[:, hop * size : (hop + 1) * size] = kept[hop]
+            outs[hop][:, size : size + states] = state
+            for part in range(2):
+                outs[hop][part * share : (part + 1) * share, size + states :] = kept[hop][
+                    :, part * (size // 2) : (part + 1) * (size // 2)
+                ]
+
+
+def carry_kernel(chunks, *refs):
+    refs[-1][...] = sum_pieces(refs[:chunks], refs[0].shape[1])
 
 
 def dnormed_kernel(chunks, *refs):
@@ -808,7 +816,7 @@
     for hop in range(1, chunks):
         exchanged.append(lax.ppermute(parts[hop], place, within(sections - 1, hop)))
 
-    grid_steps = 4
+    grid_steps = 2
     depth = model_width // grid_steps
     rows_spec = pl.BlockSpec((channels, depth), lambda step: (0, step))
     def pass_back(messages, active):
@@ -819,7 +827,7 @@
         return moved
 
     result = pl.pallas_call(
-        lambda *refs: carry_kernel(chunks, False, *refs),
+        lambda *refs: carry_kernel(chunks, *refs),
         out_shape=message,
         in_specs=whole(chunks),
         out_specs=pl.BlockSpec(memory_space=SPACE),
@@ -890,28 +898,35 @@
             break
         if joint_other is None:
             joint_other = swap(after(joint, kept[0]), range(1, sections - 1))
-        state_others = []
-        if active == sections - 2:
+        ahead = active == sections - 2
+        if ahead:
             late = after(half_cols, kept[0])
-            state_others = [
+            others = [
                 lax.ppermute(late, place, within(0, chunks - away)) for away in range(1, chunks)
             ]
-        count = len(state_others)
-        others_shape = jax.ShapeDtypeStruct((count * state_share, model_width // 2), BF16)
-        *messages, state_others = pl.pallas_call(
-            lambda *refs: send_kernel(chunks, count, *refs),
-            out_shape=(joined,) * chunks + (others_shape if count else piece_shape,),
-            in_specs=whole(2 + count) + [hbm] * 2,
-            out_specs=whole(chunks + 1),
+            stack = jax.ShapeDtypeStruct(((chunks - 1) * state_share, model_width // 2), BF16)
+            state_map = jax.ShapeDtypeStruct((state_share, chunks * channels), BF16)
+            outs = (joined,) * chunks + (stack, state_map)
+        else:
+            outs = (slice_out,) * chunks
+        messages = pl.pallas_call(
+            lambda *refs: send_kernel(chunks, ahead, *refs),
+            out_shape=outs,
+            in_specs=whole(2 + len(others)) + [hbm] * 2,
+            out_specs=whole(len(outs)),
             scratch_shapes=[pltpu.VMEM(joint_shape.shape, BF16)] * 2
             + [pltpu.SemaphoreType.DMA((2,))],
             compiler_params=kernel_params(),
-            name="send_back",
-        )(*kept, *state_others, joint, joint_other)
+            name="send_ahead" if ahead else "send_back",
+        )(*kept, *others, joint, joint_other)
         incoming = pass_back(messages, active)
-        if active == sections - 2:
-            shared = (state_others, swap(state_others, [0]))
-        if active == 1:
+        if ahead:
+            stack, late = messages[chunks], after(messages[chunks + 1], incoming[0])
+            others = [
+                lax.ppermute(late, place, within(1, chunks - away)) for away in range(1, chunks)
+            ]
+        else:
+            shared = (stack, swap(after(stack, messages[0]), [0]))
             summed = share_state(after(pieces, incoming[0]), range(1, sections - 1))
 
     parts = project_call(kept[0], summed, pieces, shared)
@@ -921,14 +936,10 @@
         for source in range(sections - 1):
             pairs += within(source, hop)
         exchanged.append(lax.ppermute(parts[hop], place, pairs))
-    return pl.pallas_call(
-        lambda *refs: carry_kernel(chunks, True, *refs),
-        out_shape=jax.ShapeDtypeStruct((1, length, width), BF16),
-        in_specs=whole(chunks + 1),
-        out_specs=pl.BlockSpec(memory_space=SPACE),
-        compiler_params=kernel_params(),
-        name="carry_last",
-    )(*exchanged, result)
+    total = exchanged[0].astype(F32)
+    for part in exchanged[1:]:
+        total = total + part.astype(F32)
+    return jnp.where(section == sections - 1, result, total.astype(BF16))[None]
 
 
 def solution(mesh):

time: 197 us -> 194 us (0.985)
  waiting for transfers between devices: 96.7 us -> 86.9 us
  starting transfers between devices: 65.2 us -> 71.7 us
  Pallas kernels: 26.4 us -> 24 us
    ppermute x0 -> x3, starting transfers between devices: none -> 13.9 us  [relay_body(): lax.ppermute(late, place, within(1, chunks - away))]
    ppermute x8, waiting for transfers between devices: 17.2 us -> 4.96 us  [pass_back(): moved.append(lax.ppermute(messages[hop], place, pairs))]
    ppermute x6, starting transfers between devices: 15.5 us -> 11.3 us  [share_state(): shared.append(lax.ppermute(pieces[hop], place, pairs))]
    ppermute x0 -> x3, waiting for transfers between devices: none -> 3.17 us  [relay_body(): lax.ppermute(late, place, within(1, chunks - away))]
    ppermute x8, starting transfers between devices: 15.5 us -> 12.7 us  [pass_back(): moved.append(lax.ppermute(messages[hop], place, pairs))]
    pallas_call x4 -> x3, Pallas kernels: 4.28 us -> 2.93 us  [the longest x2 2.1 us: relay_body(): pl.pallas_call(lambda *refs: send_kernel(chunks, ahead, *refs), out_shape...]
  transfers between devices with their start and end apart: 34 -> 37, of which waited for: 7 -> 6; matrix products, arithmetic and copies ran while one was open for 4% -> 4% of each run, Pallas kernels for 10% -> 9%
where the time goes in v6:
time: 194 us; the launch traced here: 192 us
  waiting for transfers between devices  86.9 us (45%)
  starting transfers between devices  71.7 us (37%)
  Pallas kernels  24 us (12%)
  local copies, waits for them, and re-layouts  6.75 us (3%)
    ppermute x2, waiting for transfers between devices, relay_body(): lax.ppermute(weight_out[0], everywhere, rows_up(hop))  60.5 us
    ppermute x3, waiting for transfers between devices, relay_body(): exchanged.append(lax.ppermute(parts[hop], place, pairs))  17.6 us
    ppermute x3, starting transfers between devices, relay_body(): lax.ppermute(late, place, within(1, chunks - away))  13.9 us
    ppermute x8, starting transfers between devices, pass_back(): moved.append(lax.ppermute(messages[hop], place, pairs))  12.7 us
    ppermute x6, starting transfers between devices, share_state(): shared.append(lax.ppermute(pieces[hop], place, pairs))  11.3 us
    ppermute x3, starting transfers between devices, relay_body(): exchanged.append(lax.ppermute(parts[hop], place, pairs))  10.7 us
    ppermute x2, starting transfers between devices, relay_body(): lax.ppermute(weight_out[0], everywhere, rows_up(hop))  7.06 us
    pallas_call x1, Pallas kernels, relay_body(): pl.pallas_call(lambda *refs: compose_kernel(half, *refs), grid=(grid_step...  6.45 us
  transfers between devices with their start and end apart: 37, of which 6 were waited for; matrix products, arithmetic and copies ran while one was open for 4% of the time, Pallas kernels for 9%

profile of v6, /device:TPU:11, one launch (start us, length us, event | category | flops | bytes accessed | tf_op | source)
XLA Modules:
  0.0 191.8 jit_solution(17657686653137046939)
XLA Ops:
  0.0 5.1 %collective-permute-start.12 = (bf16[256,4096]{1,0:T(8,128)(2,1)}, bf16[256,4096]{1,0:T(8,128)(2,1)S(1)}, u32[]{:S(2)}, u32[]{:S(2)}) collective-permute-start(bf16[256,4096]{1,0:T(8,128)(2,1)} %bitcast.36), channel_id=1, source_target_pairs={{0,8},{1,13},{2,10},{3,15},{4,12},{5,9},{6,14},{7,11},{8,16},{9,21... | collective-permute-start | bytes 6291464 | tf_op jit(solution)/shard_map/ppermute | solution.py:734
  5.1 1.9 %collective-permute-start.13 = (bf16[256,4096]{1,0:T(8,128)(2,1)}, bf16[256,4096]{1,0:T(8,128)(2,1)}, u32[]{:S(2)}, u32[]{:S(2)}) collective-permute-start(bf16[256,4096]{1,0:T(8,128)(2,1)} %bitcast.37), channel_id=1, source_target_pairs={{0,10},{1,15},{2,12},{3,9},{4,14},{5,11},{6,8},{7,13},{8,18},{9,23... | collective-permute-start | bytes 6291464 | tf_op jit(solution)/shard_map/ppermute | solution.py:734
  7.1 1.4 collective-permute-start
  8.4 1.4 collective-permute-start.1
  9.8 1.4 collective-permute-start.2
  11.2 0.8 copy.17
  12.0 1.2 fusion.2
  13.2 0.7 select_maximum_fusion.refs_6_.refs_13_.refs_9_.refs_12_
  13.9 0.8 copy.27
  14.8 0.7 copy.28
  15.5 3.1 %copy.22 = bf16[512,8,2,256]{3,1,2,0:T(8,128)(2,1)S(1)} copy(bf16[512,8,2,256]{3,2,1,0:T(2,128)(2,1)} %bitcast.53) | data formatting | bytes 8388608
  18.6 1.2 forward_residuals.1
  19.9 0.0 copy-start.4
  19.9 0.0 copy-start.13
  19.9 3.5 %section_first.1 = (bf16[128,640]{1,0:T(8,128)(2,1)S(1)}, bf16[128,128]{1,0:T(8,128)(2,1)S(1)}, bf16[128,128]{1,0:T(8,128)(2,1)S(1)}, bf16[128,128]{1,0:T(8,128)(2,1)S(1)}, bf16[128,128]{1,0:T(8,128)(2,1)S(1)}) custom-call(bf16[128,1024]{1,0:T(8,128)(2,1)S(1)} %copy-done.15, bf16[128,1024]{1,0:T(8,128)(2,1)} %collective-permute-done.refs_1_, ...), custom_call_target="tpu_custom_call" | custom-call | tf_op jit(solution)/shard_map/section_first/pallas_call | solution.py:779
  23.5 0.7 collective-permute-start.3
  24.1 0.7 collective-permute-start.4
  24.8 0.7 collective-permute-start.5
  25.5 2.5 %project.2 = (bf16[128,1024]{1,0:T(8,128)(2,1)S(1)}, bf16[128,1024]{1,0:T(8,128)(2,1)S(1)}, bf16[128,1024]{1,0:T(8,128)(2,1)S(1)}, bf16[128,1024]{1,0:T(8,128)(2,1)S(1)}) custom-call(bf16[128,640]{1,0:T(8,128)(2,1)S(1)} %get-tuple-element.67.refs_0_, bf16[128,128]{1,0:T(8,128)(2,1)S(1)} %get-tuple-element.68.refs_1_, ...), custom_call_target="tpu_custom_call" | custom-call | tf_op jit(solution)/shard_map/project/pallas_call | solution.py:798
  28.1 0.7 collective-permute-start.6
  28.7 0.7 collective-permute-start.7
  29.4 0.7 collective-permute-start.8
  30.1 0.8 carry_next.1.refs_0_
  31.0 1.4 collective-permute-start.9
  32.3 1.4 collective-permute-start.10
  33.7 1.4 collective-permute-start.11
  35.1 60.5 %collective-permute-done.12.refs_4_.refs_0_ = bf16[256,4096]{1,0:T(8,128)(2,1)S(1)} collective-permute-done((bf16[256,4096]{1,0:T(8,128)(2,1)}, bf16[256,4096]{1,0:T(8,128)(2,1)S(1)}, u32[]{:S(2)}, u32[]{:S(2)}) %collective-permute-start.12) | collective-permute-done | bytes 2097184 | tf_op jit(solution)/shard_map/ppermute | solution.py:734
  95.6 1.2 dnormed_back.1
  96.8 0.7 collective-permute-start.14
  97.6 6.5 %compose_weights.1.refs_5_ = bf16[320,1280]{1,0:T(8,128)(2,1)S(1)} custom-call(bf16[256,4096]{1,0:T(8,128)(2,1)S(1)} %collective-permute-done.12.refs_4_.refs_0_, bf16[256,4096]{1,0:T(8,128)(2,1)} %collective-permute-done.13.refs_5_.refs_1_, bf16[4096,512]{1,0:T(8,128)(2,1)S(1)} %bitcast.30, bf16[4,4096]{1,0:T(4,128)(2,1)S(1)} %bitcast.40, ...), custom_call_target="tpu_custom_call" | custom-call | tf_op jit(solution)/shard_map/compose_weights/pallas_call | solution.py:855
  104.1 0.7 section_next.3
  104.8 2.5 %collective-permute-start.18 = (bf16[320,1280]{1,0:T(8,128)(2,1)S(1)}, bf16[320,1280]{1,0:T(8,128)(2,1)S(1)}, u32[]{:S(2)}, u32[]{:S(2)}) collective-permute-start(bf16[320,1280]{1,0:T(8,128)(2,1)S(1)} %compose_weights.1.refs_5_), channel_id=1, source_target_pairs={{8,9},{9,8},{10,11},{11,10},{12,13},{13,12},{14,15},{15,14},{16,17... | collective-permute-start | bytes 2457608 | tf_op jit(solution)/shard_map/ppermute | solution.py:728
  107.4 0.7 collective-permute-start.15
  108.1 0.7 collective-permute-start.16
  108.7 0.7 collective-permute-start.17
  109.5 0.8 send_ahead.1
  110.3 1.3 collective-permute-start.19
  111.6 1.3 collective-permute-start.20
  112.9 1.3 collective-permute-start.21
  114.2 1.3 collective-permute-start.22
  115.5 4.9 %collective-permute-done.19.refs_0_ = bf16[128,640]{1,0:T(8,128)(2,1)S(1)} collective-permute-done((bf16[128,640]{1,0:T(8,128)(2,1)S(1)}, bf16[128,640]{1,0:T(8,128)(2,1)S(1)}, u32[]{:S(2)}, u32[]{:S(2)}) %collective-permute-start.19) | collective-permute-done | bytes 163872 | tf_op jit(solution)/shard_map/ppermute | solution.py:826
  120.4 1.9 collective-permute-start.23
  122.4 9.9 %collective-permute-start.24 = (bf16[64,1024]{1,0:T(8,128)(2,1)S(1)}, bf16[64,1024]{1,0:T(8,128)(2,1)S(1)}, u32[]{:S(2)}, u32[]{:S(2)}) collective-permute-start(bf16[64,1024]{1,0:T(8,128)(2,1)S(1)} %get-tuple-element.91), channel_id=1, source_target_pairs={{8,12},{10,14},{12,8},{14,10},{9,13},{11,15},{13,9},{15,11}} | collective-permute-start | bytes 393224 | tf_op jit(solution)/shard_map/ppermute | solution.py:926
  132.3 2.1 %collective-permute-start.25 = (bf16[64,1024]{1,0:T(8,128)(2,1)S(1)}, bf16[64,1024]{1,0:T(8,128)(2,1)S(1)}, u32[]{:S(2)}, u32[]{:S(2)}) collective-permute-start(bf16[64,1024]{1,0:T(8,128)(2,1)S(1)} %get-tuple-element.91), channel_id=1, source_target_pairs={{8,10},{10,12},{12,14},{14,8},{9,11},{11,13},{13,15},{15,9}} | collective-permute-start | bytes 393224 | tf_op jit(solution)/shard_map/ppermute | solution.py:926
  134.4 1.3 section_next.4
  135.7 3.2 %collective-permute-done.25.refs_4_ = bf16[64,1024]{1,0:T(8,128)(2,1)S(1)} collective-permute-done((bf16[64,1024]{1,0:T(8,128)(2,1)S(1)}, bf16[64,1024]{1,0:T(8,128)(2,1)S(1)}, u32[]{:S(2)}, u32[]{:S(2)}) %collective-permute-start.25) | collective-permute-done | bytes 131104 | tf_op jit(solution)/shard_map/ppermute | solution.py:926
  138.9 1.3 send_back.1
  140.2 0.7 collective-permute-start.33
  140.9 1.3 collective-permute-start.26
  142.2 3.6 %collective-permute-start.27 = (bf16[128,256]{1,0:T(8,128)(2,1)S(1)}, bf16[128,256]{1,0:T(8,128)(2,1)S(1)}, u32[]{:S(2)}, u32[]{:S(2)}) collective-permute-start(bf16[128,256]{1,0:T(8,128)(2,1)S(1)} %get-tuple-element.93), channel_id=1, source_target_pairs={{8,6},{10,0},{12,2},{14,4},{9,7},{11,1},{13,3},{15,5}} | collective-permute-start | bytes 196616 | tf_op jit(solution)/shard_map/ppermute | solution.py:826
  145.8 1.3 collective-permute-start.28
  147.1 1.3 collective-permute-start.29
  148.5 3.1 %collective-permute-start.30 = (bf16[128,128]{1,0:T(8,128)(2,1)S(1)}, bf16[128,128]{1,0:T(8,128)(2,1)S(1)}, u32[]{:S(2)}, u32[]{:S(2)}) collective-permute-start(bf16[128,128]{1,0:T(8,128)(2,1)S(1)} %get-tuple-element.102), channel_id=1, source_target_pairs={{8,10},{10,12},{12,14},{14,8},{16,18},{18,20},{20,22},{22,16},{9,1... | collective-permute-start | bytes 98312 | tf_op jit(solution)/shard_map/ppermute | solution.py:794
  151.6 3.1 %collective-permute-start.31 = (bf16[128,128]{1,0:T(8,128)(2,1)S(1)}, bf16[128,128]{1,0:T(8,128)(2,1)S(1)}, u32[]{:S(2)}, u32[]{:S(2)}) collective-permute-start(bf16[128,128]{1,0:T(8,128)(2,1)S(1)} %get-tuple-element.103), channel_id=1, source_target_pairs={{8,12},{10,14},{12,8},{14,10},{16,20},{18,22},{20,16},{22,18},{9,1... | collective-permute-start | bytes 98312 | tf_op jit(solution)/shard_map/ppermute | solution.py:794
  154.7 3.1 %collective-permute-start.32 = (bf16[128,128]{1,0:T(8,128)(2,1)S(1)}, bf16[128,128]{1,0:T(8,128)(2,1)S(1)}, u32[]{:S(2)}, u32[]{:S(2)}) collective-permute-start(bf16[128,128]{1,0:T(8,128)(2,1)S(1)} %get-tuple-element.104), channel_id=1, source_target_pairs={{8,14},{10,8},{12,10},{14,12},{16,22},{18,16},{20,18},{22,20},{9,1... | collective-permute-start | bytes 98312 | tf_op jit(solution)/shard_map/ppermute | solution.py:794
  157.8 1.4 section_next.5
  159.2 0.6 collective-permute-done.32.refs_4_
  159.8 2.8 %project.3 = (bf16[128,1024]{1,0:T(8,128)(2,1)S(1)}, bf16[128,1024]{1,0:T(8,128)(2,1)S(1)}, bf16[128,1024]{1,0:T(8,128)(2,1)S(1)}, bf16[128,1024]{1,0:T(8,128)(2,1)S(1)}) custom-call(bf16[128,640]{1,0:T(8,128)(2,1)S(1)} %get-tuple-element.96.refs_0_, bf16[128,128]{1,0:T(8,128)(2,1)S(1)} %get-tuple-element.101.refs_1_, ...), custom_call_target="tpu_custom_call" | custom-call | tf_op jit(solution)/shard_map/project/pallas_call | solution.py:798
  162.6 2.9 %collective-permute-start.36 = (bf16[128,1024]{1,0:T(8,128)(2,1)S(1)}, bf16[128,1024]{1,0:T(8,128)(2,1)S(1)}, u32[]{:S(2)}, u32[]{:S(2)}) collective-permute-start(bf16[128,1024]{1,0:T(8,128)(2,1)S(1)} %get-tuple-element.114), channel_id=1, source_target_pairs={{0,6},{2,0},{4,2},{6,4},{8,14},{10,8},{12,10},{14,12},{16,22},{18,... | collective-permute-start | bytes 786440 | tf_op jit(solution)/shard_map/ppermute | solution.py:938
  165.5 3.5 %collective-permute-start.35 = (bf16[128,1024]{1,0:T(8,128)(2,1)S(1)}, bf16[128,1024]{1,0:T(8,128)(2,1)S(1)}, u32[]{:S(2)}, u32[]{:S(2)}) collective-permute-start(bf16[128,1024]{1,0:T(8,128)(2,1)S(1)} %get-tuple-element.113), channel_id=1, source_target_pairs={{0,4},{2,6},{4,0},{6,2},{8,12},{10,14},{12,8},{14,10},{16,20},{18,... | collective-permute-start | bytes 786440 | tf_op jit(solution)/shard_map/ppermute | solution.py:938
  169.0 4.3 %collective-permute-start.34 = (bf16[128,1024]{1,0:T(8,128)(2,1)S(1)}, bf16[128,1024]{1,0:T(8,128)(2,1)S(1)}, u32[]{:S(2)}, u32[]{:S(2)}) collective-permute-start(bf16[128,1024]{1,0:T(8,128)(2,1)S(1)} %get-tuple-element.112), channel_id=1, source_target_pairs={{0,2},{2,4},{4,6},{6,0},{8,10},{10,12},{12,14},{14,8},{16,18},{18,... | collective-permute-start | bytes 786440 | tf_op jit(solution)/shard_map/ppermute | solution.py:938
  173.3 12.0 %collective-permute-done.35 = bf16[128,1024]{1,0:T(8,128)(2,1)S(1)} collective-permute-done((bf16[128,1024]{1,0:T(8,128)(2,1)S(1)}, bf16[128,1024]{1,0:T(8,128)(2,1)S(1)}, u32[]{:S(2)}, u32[]{:S(2)}) %collective-permute-start.35) | collective-permute-done | bytes 262176 | tf_op jit(solution)/shard_map/ppermute | solution.py:938
  185.3 5.6 %collective-permute-done.34 = bf16[128,1024]{1,0:T(8,128)(2,1)S(1)} collective-permute-done((bf16[128,1024]{1,0:T(8,128)(2,1)S(1)}, bf16[128,1024]{1,0:T(8,128)(2,1)S(1)}, u32[]{:S(2)}, u32[]{:S(2)}) %collective-permute-start.34) | collective-permute-done | bytes 262176 | tf_op jit(solution)/shard_map/ppermute | solution.py:938
  190.9 0.9 fusion.1
  (68 shorter events, 0.2 us)
Async XLA Ops:
  0.0 95.6 %collective-permute-start.12 = (bf16[256,4096]{1,0:T(8,128)(2,1)}, bf16[256,4096]{1,0:T(8,128)(2,1)S(1)}, u32[]{:S(2)}, u32[]{:S(2)}) collective-permute-start(bf16[256,4096]{1,0:T(8,128)(2,1)} %bitcast.36), channel_id=1, source_target_pairs={{0,8},{1,13},{2,10},{3,15},{4,12},{5,9},{6,14},{7,11},{8,16},{9,21... | collective-permute-start | bytes 6291464 | tf_op jit(solution)/shard_map/ppermute | solution.py:734
  5.1 90.5 %collective-permute-start.13 = (bf16[256,4096]{1,0:T(8,128)(2,1)}, bf16[256,4096]{1,0:T(8,128)(2,1)}, u32[]{:S(2)}, u32[]{:S(2)}) collective-permute-start(bf16[256,4096]{1,0:T(8,128)(2,1)} %bitcast.37), channel_id=1, source_target_pairs={{0,10},{1,15},{2,12},{3,9},{4,14},{5,11},{6,8},{7,13},{8,18},{9,23... | collective-permute-start | bytes 6291464 | tf_op jit(solution)/shard_map/ppermute | solution.py:734
  7.1 12.8 %collective-permute-start = (bf16[128,1024]{1,0:T(8,128)(2,1)}, bf16[128,1024]{1,0:T(8,128)(2,1)}, u32[]{:S(2)}, u32[]{:S(2)}) collective-permute-start(bf16[128,1024]{1,0:T(8,128)(2,1)} %refs_0_.1), channel_id=1, source_target_pairs={{24,26},{26,28},{28,30},{30,24},{25,27},{27,29},{29,31},{31,25}} | collective-permute-start | bytes 786440 | tf_op jit(solution)/shard_map/ppermute | solution.py:732
  8.4 11.4 %collective-permute-start.1 = (bf16[128,1024]{1,0:T(8,128)(2,1)}, bf16[128,1024]{1,0:T(8,128)(2,1)}, u32[]{:S(2)}, u32[]{:S(2)}) collective-permute-start(bf16[128,1024]{1,0:T(8,128)(2,1)} %refs_0_.1), channel_id=1, source_target_pairs={{24,28},{26,30},{28,24},{30,26},{25,29},{27,31},{29,25},{31,27}} | collective-permute-start | bytes 786440 | tf_op jit(solution)/shard_map/ppermute | solution.py:732
  9.8 10.1 %collective-permute-start.2 = (bf16[128,1024]{1,0:T(8,128)(2,1)}, bf16[128,1024]{1,0:T(8,128)(2,1)}, u32[]{:S(2)}, u32[]{:S(2)}) collective-permute-start(bf16[128,1024]{1,0:T(8,128)(2,1)} %refs_0_.1), channel_id=1, source_target_pairs={{24,30},{26,24},{28,26},{30,28},{25,31},{27,25},{29,27},{31,29}} | collective-permute-start | bytes 786440 | tf_op jit(solution)/shard_map/ppermute | solution.py:732
  15.5 3.1 %copy-start.16 = (f32[1,4,256]{2,1,0:T(4,128)S(1)}, f32[1,4,256]{2,1,0:T(4,128)}, u32[]{:S(2)}) copy-start(f32[1,4,256]{2,1,0:T(4,128)} %param.18) | copy-start | bytes 12292
  15.5 3.1 %copy-start.17 = (f32[1,256]{1,0:T(1,128)S(1)}, f32[1,256]{1,0:T(1,128)}, u32[]{:S(2)}) copy-start(f32[1,256]{1,0:T(1,128)} %refs_7_.1) | copy-start | bytes 3076
  15.5 4.4 %copy-start.6 = (bf16[1,256,4096]{2,1,0:T(8,128)(2,1)S(1)}, bf16[1,256,4096]{2,1,0:T(8,128)(2,1)}, u32[]{:S(2)}) copy-start(bf16[1,256,4096]{2,1,0:T(8,128)(2,1)} %param.17) | copy-start | bytes 6291460
  15.5 4.4 %copy-start.15 = (bf16[128,1024]{1,0:T(8,128)(2,1)S(1)}, bf16[128,1024]{1,0:T(8,128)(2,1)}, u32[]{:S(2)}) copy-start(bf16[128,1024]{1,0:T(8,128)(2,1)} %refs_0_.1) | copy-start | bytes 786436
  18.6 6.9 %copy-start = (bf16[512,8,2,256]{3,1,2,0:T(8,128)(2,1)}, bf16[512,8,2,256]{3,1,2,0:T(8,128)(2,1)S(1)}, u32[]{:S(2)}) copy-start(bf16[512,8,2,256]{3,1,2,0:T(8,128)(2,1)S(1)} %copy.22) | copy-start | bytes 12582916
  19.8 3.6 %copy-start.2 = (f32[2,128,512]{2,1,0:T(8,128)}, f32[2,128,512]{2,1,0:T(8,128)S(1)}, u32[]{:S(2)}) copy-start(f32[2,128,512]{2,1,0:T(8,128)S(1)} %get-tuple-element.61.refs_6_.refs_2_.refs_5_) | copy-start | bytes 1572868
  19.8 3.6 %copy-start.7 = (bf16[128,512]{1,0:T(8,128)(2,1)}, bf16[128,512]{1,0:T(8,128)(2,1)S(1)}, u32[]{:S(2)}) copy-start(bf16[128,512]{1,0:T(8,128)(2,1)S(1)} %get-tuple-element.62.refs_7_.refs_3_.refs_6_) | copy-start | bytes 393220
  19.8 3.6 %copy-start.9 = (bf16[2,128,128]{2,1,0:T(8,128)(2,1)}, bf16[2,128,128]{2,1,0:T(8,128)(2,1)S(1)}, u32[]{:S(2)}) copy-start(bf16[2,128,128]{2,1,0:T(8,128)(2,1)S(1)} %get-tuple-element.64.refs_9_.refs_5_.refs_8_) | copy-start | bytes 196612
  19.9 3.6 %copy-start.11 = (f32[128,128]{1,0:T(8,128)}, f32[128,128]{1,0:T(8,128)S(1)}, u32[]{:S(2)}) copy-start(f32[128,128]{1,0:T(8,128)S(1)} %get-tuple-element.65.refs_10_.refs_6_.refs_9_) | copy-start | bytes 196612
  19.9 5.6 %copy-start.4 = (bf16[1,4096,2,32]{1,3,2,0:T(8,128)(2,1)S(1)}, bf16[1,4096,2,32]{1,3,2,0:T(8,128)(2,1)}, u32[]{:S(2)}) copy-start(bf16[1,4096,2,32]{1,3,2,0:T(8,128)(2,1)} %param.15) | copy-start | bytes 1572868
  19.9 5.6 %copy-start.13 = (bf16[1,4,4096]{2,1,0:T(4,128)(2,1)S(1)}, bf16[1,4,4096]{2,1,0:T(4,128)(2,1)}, u32[]{:S(2)}) copy-start(bf16[1,4,4096]{2,1,0:T(4,128)(2,1)} %param.16) | copy-start | bytes 98308
  23.5 2.0 %collective-permute-start.3 = (bf16[128,128]{1,0:T(8,128)(2,1)S(1)}, bf16[128,128]{1,0:T(8,128)(2,1)S(1)}, u32[]{:S(2)}, u32[]{:S(2)}) collective-permute-start(bf16[128,128]{1,0:T(8,128)(2,1)S(1)} %get-tuple-element.69), channel_id=1, source_target_pairs={{24,26},{26,28},{28,30},{30,24},{25,27},{27,29},{29,31},{31,25}} | collective-permute-start | bytes 98312 | tf_op jit(solution)/shard_map/ppermute | solution.py:794
  24.1 1.4 collective-permute-start.4
  24.8 0.7 collective-permute-start.5
  28.1 2.1 %collective-permute-start.6 = (bf16[128,1024]{1,0:T(8,128)(2,1)S(1)}, bf16[128,1024]{1,0:T(8,128)(2,1)S(1)}, u32[]{:S(2)}, u32[]{:S(2)}) collective-permute-start(bf16[128,1024]{1,0:T(8,128)(2,1)S(1)} %get-tuple-element.74), channel_id=1, source_target_pairs={{24,26},{26,28},{28,30},{30,24},{25,27},{27,29},{29,31},{31,25}} | collective-permute-start | bytes 786440 | tf_op jit(solution)/shard_map/ppermute | solution.py:817
  28.7 1.4 collective-permute-start.7
  29.4 0.7 collective-permute-start.8
  31.0 4.1 %collective-permute-start.9 = (bf16[128,1024]{1,0:T(8,128)(2,1)}, bf16[128,1024]{1,0:T(8,128)(2,1)}, u32[]{:S(2)}, u32[]{:S(2)}) collective-permute-start(bf16[128,1024]{1,0:T(8,128)(2,1)} %carry_next.1.refs_0_), channel_id=1, source_target_pairs={{24,26},{26,28},{28,30},{30,24},{25,27},{27,29},{29,31},{31,25}} | collective-permute-start | bytes 786440 | tf_op jit(solution)/shard_map/ppermute | solution.py:839
  32.3 2.8 %collective-permute-start.10 = (bf16[128,1024]{1,0:T(8,128)(2,1)}, bf16[128,1024]{1,0:T(8,128)(2,1)}, u32[]{:S(2)}, u32[]{:S(2)}) collective-permute-start(bf16[128,1024]{1,0:T(8,128)(2,1)} %carry_next.1.refs_0_), channel_id=1, source_target_pairs={{24,28},{26,30},{28,24},{30,26},{25,29},{27,31},{29,25},{31,27}} | collective-permute-start | bytes 786440 | tf_op jit(solution)/shard_map/ppermute | solution.py:839
  33.7 1.4 collective-permute-start.11
  35.1 62.4 %copy-start.5 = (bf16[1,4096,2,32]{1,3,2,0:T(8,128)(2,1)S(1)}, bf16[1,4096,2,32]{1,3,2,0:T(8,128)(2,1)}, u32[]{:S(2)}) copy-start(bf16[1,4096,2,32]{1,3,2,0:T(8,128)(2,1)} %param.15) | copy-start | bytes 1572868
  35.1 62.4 %copy-start.1 = (bf16[512,8,2,256]{3,1,2,0:T(8,128)(2,1)S(1)}, bf16[512,8,2,256]{3,1,2,0:T(8,128)(2,1)}, u32[]{:S(2)}) copy-start(bf16[512,8,2,256]{3,1,2,0:T(8,128)(2,1)} %copy-done) | copy-start | bytes 12582916
  35.1 62.5 %copy-start.14 = (bf16[1,4,4096]{2,1,0:T(4,128)(2,1)S(1)}, bf16[1,4,4096]{2,1,0:T(4,128)(2,1)}, u32[]{:S(2)}) copy-start(bf16[1,4,4096]{2,1,0:T(4,128)(2,1)} %param.16) | copy-start | bytes 98308
  96.8 7.2 %collective-permute-start.14 = (bf16[128,256]{1,0:T(8,128)(2,1)S(1)}, bf16[128,256]{1,0:T(8,128)(2,1)S(1)}, u32[]{:S(2)}, u32[]{:S(2)}) collective-permute-start(bf16[128,256]{1,0:T(8,128)(2,1)S(1)} %dnormed_back.1), channel_id=1, source_target_pairs={{24,16},{26,18},{28,20},{30,22},{25,17},{27,19},{29,21},{31,23}} | collective-permute-start | bytes 196616 | tf_op jit(solution)/shard_map/ppermute | solution.py:853
  97.6 6.5 %copy-start.3 = (f32[2,128,512]{2,1,0:T(8,128)S(1)}, f32[2,128,512]{2,1,0:T(8,128)}, u32[]{:S(2)}) copy-start(f32[2,128,512]{2,1,0:T(8,128)} %copy-done.2) | copy-start | bytes 1572868
  97.6 6.5 %copy-start.8 = (bf16[128,512]{1,0:T(8,128)(2,1)S(1)}, bf16[128,512]{1,0:T(8,128)(2,1)}, u32[]{:S(2)}) copy-start(bf16[128,512]{1,0:T(8,128)(2,1)} %copy-done.7) | copy-start | bytes 393220
  97.6 6.5 %copy-start.10 = (bf16[2,128,128]{2,1,0:T(8,128)(2,1)S(1)}, bf16[2,128,128]{2,1,0:T(8,128)(2,1)}, u32[]{:S(2)}) copy-start(bf16[2,128,128]{2,1,0:T(8,128)(2,1)} %copy-done.9) | copy-start | bytes 196612
  97.6 6.5 %copy-start.12 = (f32[128,128]{1,0:T(8,128)S(1)}, f32[128,128]{1,0:T(8,128)}, u32[]{:S(2)}) copy-start(f32[128,128]{1,0:T(8,128)} %copy-done.11) | copy-start | bytes 196612
  104.8 4.6 %collective-permute-start.18 = (bf16[320,1280]{1,0:T(8,128)(2,1)S(1)}, bf16[320,1280]{1,0:T(8,128)(2,1)S(1)}, u32[]{:S(2)}, u32[]{:S(2)}) collective-permute-start(bf16[320,1280]{1,0:T(8,128)(2,1)S(1)} %compose_weights.1.refs_5_), channel_id=1, source_target_pairs={{8,9},{9,8},{10,11},{11,10},{12,13},{13,12},{14,15},{15,14},{16,17... | collective-permute-start | bytes 2457608 | tf_op jit(solution)/shard_map/ppermute | solution.py:728
  107.4 2.1 %collective-permute-start.15 = (bf16[64,2048]{1,0:T(8,128)(2,1)S(1)}, bf16[64,2048]{1,0:T(8,128)(2,1)S(1)}, u32[]{:S(2)}, u32[]{:S(2)}) collective-permute-start(bf16[64,2048]{1,0:T(8,128)(2,1)S(1)} %constant_dynamic-slice_fusion), channel_id=1, source_target_pairs={{0,6},{2,0},{4,2},{6,4},{1,7},{3,1},{5,3},{7,5}} | collective-permute-start | bytes 786440 | tf_op jit(solution)/shard_map/ppermute | solution.py:905
  108.1 1.4 collective-permute-start.16
  108.7 0.7 collective-permute-start.17
  110.3 10.1 %collective-permute-start.19 = (bf16[128,640]{1,0:T(8,128)(2,1)S(1)}, bf16[128,640]{1,0:T(8,128)(2,1)S(1)}, u32[]{:S(2)}, u32[]{:S(2)}) collective-permute-start(bf16[128,640]{1,0:T(8,128)(2,1)S(1)} %get-tuple-element.84), channel_id=1, source_target_pairs={{16,8},{18,10},{20,12},{22,14},{17,9},{19,11},{21,13},{23,15}} | collective-permute-start | bytes 491528 | tf_op jit(solution)/shard_map/ppermute | solution.py:826
  111.6 20.7 %collective-permute-start.20 = (bf16[128,640]{1,0:T(8,128)(2,1)S(1)}, bf16[128,640]{1,0:T(8,128)(2,1)S(1)}, u32[]{:S(2)}, u32[]{:S(2)}) collective-permute-start(bf16[128,640]{1,0:T(8,128)(2,1)S(1)} %get-tuple-element.85), channel_id=1, source_target_pairs={{16,14},{18,8},{20,10},{22,12},{17,15},{19,9},{21,11},{23,13}} | collective-permute-start | bytes 491528 | tf_op jit(solution)/shard_map/ppermute | solution.py:826
  112.9 21.5 %collective-permute-start.21 = (bf16[128,640]{1,0:T(8,128)(2,1)S(1)}, bf16[128,640]{1,0:T(8,128)(2,1)S(1)}, u32[]{:S(2)}, u32[]{:S(2)}) collective-permute-start(bf16[128,640]{1,0:T(8,128)(2,1)S(1)} %get-tuple-element.86), channel_id=1, source_target_pairs={{16,12},{18,14},{20,8},{22,10},{17,13},{19,15},{21,9},{23,11}} | collective-permute-start | bytes 491528 | tf_op jit(solution)/shard_map/ppermute | solution.py:826
  114.2 20.2 %collective-permute-start.22 = (bf16[128,640]{1,0:T(8,128)(2,1)S(1)}, bf16[128,640]{1,0:T(8,128)(2,1)S(1)}, u32[]{:S(2)}, u32[]{:S(2)}) collective-permute-start(bf16[128,640]{1,0:T(8,128)(2,1)S(1)} %get-tuple-element.87), channel_id=1, source_target_pairs={{16,10},{18,12},{20,14},{22,8},{17,11},{19,13},{21,15},{23,9}} | collective-permute-start | bytes 491528 | tf_op jit(solution)/shard_map/ppermute | solution.py:826
  120.4 15.3 %collective-permute-start.23 = (bf16[64,1024]{1,0:T(8,128)(2,1)S(1)}, bf16[64,1024]{1,0:T(8,128)(2,1)S(1)}, u32[]{:S(2)}, u32[]{:S(2)}) collective-permute-start(bf16[64,1024]{1,0:T(8,128)(2,1)S(1)} %get-tuple-element.91), channel_id=1, source_target_pairs={{8,14},{10,8},{12,10},{14,12},{9,15},{11,9},{13,11},{15,13}} | collective-permute-start | bytes 393224 | tf_op jit(solution)/shard_map/ppermute | solution.py:926
  122.4 13.4 %collective-permute-start.24 = (bf16[64,1024]{1,0:T(8,128)(2,1)S(1)}, bf16[64,1024]{1,0:T(8,128)(2,1)S(1)}, u32[]{:S(2)}, u32[]{:S(2)}) collective-permute-start(bf16[64,1024]{1,0:T(8,128)(2,1)S(1)} %get-tuple-element.91), channel_id=1, source_target_pairs={{8,12},{10,14},{12,8},{14,10},{9,13},{11,15},{13,9},{15,11}} | collective-permute-start | bytes 393224 | tf_op jit(solution)/shard_map/ppermute | solution.py:926
  132.3 6.6 %collective-permute-start.25 = (bf16[64,1024]{1,0:T(8,128)(2,1)S(1)}, bf16[64,1024]{1,0:T(8,128)(2,1)S(1)}, u32[]{:S(2)}, u32[]{:S(2)}) collective-permute-start(bf16[64,1024]{1,0:T(8,128)(2,1)S(1)} %get-tuple-element.91), channel_id=1, source_target_pairs={{8,10},{10,12},{12,14},{14,8},{9,11},{11,13},{13,15},{15,9}} | collective-permute-start | bytes 393224 | tf_op jit(solution)/shard_map/ppermute | solution.py:926
  140.2 19.6 %collective-permute-start.33 = (bf16[192,2048]{1,0:T(8,128)(2,1)S(1)}, bf16[192,2048]{1,0:T(8,128)(2,1)S(1)}, u32[]{:S(2)}, u32[]{:S(2)}) collective-permute-start(bf16[192,2048]{1,0:T(8,128)(2,1)S(1)} %get-tuple-element.110.refs_10_), channel_id=1, source_target_pairs={{0,1},{1,0},{2,3},{3,2},{4,5},{5,4},{6,7},{7,6}} | collective-permute-start | bytes 2359304 | tf_op jit(solution)/shard_map/ppermute | solution.py:728
  140.9 7.5 %collective-permute-start.26 = (bf16[128,256]{1,0:T(8,128)(2,1)S(1)}, bf16[128,256]{1,0:T(8,128)(2,1)S(1)}, u32[]{:S(2)}, u32[]{:S(2)}) collective-permute-start(bf16[128,256]{1,0:T(8,128)(2,1)S(1)} %get-tuple-element.92), channel_id=1, source_target_pairs={{8,0},{10,2},{12,4},{14,6},{9,1},{11,3},{13,5},{15,7}} | collective-permute-start | bytes 196616 | tf_op jit(solution)/shard_map/ppermute | solution.py:826
  142.2 9.3 %collective-permute-start.27 = (bf16[128,256]{1,0:T(8,128)(2,1)S(1)}, bf16[128,256]{1,0:T(8,128)(2,1)S(1)}, u32[]{:S(2)}, u32[]{:S(2)}) collective-permute-start(bf16[128,256]{1,0:T(8,128)(2,1)S(1)} %get-tuple-element.93), channel_id=1, source_target_pairs={{8,6},{10,0},{12,2},{14,4},{9,7},{11,1},{13,3},{15,5}} | collective-permute-start | bytes 196616 | tf_op jit(solution)/shard_map/ppermute | solution.py:826
  145.8 8.8 %collective-permute-start.28 = (bf16[128,256]{1,0:T(8,128)(2,1)S(1)}, bf16[128,256]{1,0:T(8,128)(2,1)S(1)}, u32[]{:S(2)}, u32[]{:S(2)}) collective-permute-start(bf16[128,256]{1,0:T(8,128)(2,1)S(1)} %get-tuple-element.94), channel_id=1, source_target_pairs={{8,4},{10,6},{12,0},{14,2},{9,5},{11,7},{13,1},{15,3}} | collective-permute-start | bytes 196616 | tf_op jit(solution)/shard_map/ppermute | solution.py:826
  147.1 10.6 %collective-permute-start.29 = (bf16[128,256]{1,0:T(8,128)(2,1)S(1)}, bf16[128,256]{1,0:T(8,128)(2,1)S(1)}, u32[]{:S(2)}, u32[]{:S(2)}) collective-permute-start(bf16[128,256]{1,0:T(8,128)(2,1)S(1)} %get-tuple-element.95), channel_id=1, source_target_pairs={{8,2},{10,4},{12,6},{14,0},{9,3},{11,5},{13,7},{15,1}} | collective-permute-start | bytes 196616 | tf_op jit(solution)/shard_map/ppermute | solution.py:826
  148.5 10.7 %collective-permute-start.30 = (bf16[128,128]{1,0:T(8,128)(2,1)S(1)}, bf16[128,128]{1,0:T(8,128)(2,1)S(1)}, u32[]{:S(2)}, u32[]{:S(2)}) collective-permute-start(bf16[128,128]{1,0:T(8,128)(2,1)S(1)} %get-tuple-element.102), channel_id=1, source_target_pairs={{8,10},{10,12},{12,14},{14,8},{16,18},{18,20},{20,22},{22,16},{9,1... | collective-permute-start | bytes 98312 | tf_op jit(solution)/shard_map/ppermute | solution.py:794
  151.6 7.6 %collective-permute-start.31 = (bf16[128,128]{1,0:T(8,128)(2,1)S(1)}, bf16[128,128]{1,0:T(8,128)(2,1)S(1)}, u32[]{:S(2)}, u32[]{:S(2)}) collective-permute-start(bf16[128,128]{1,0:T(8,128)(2,1)S(1)} %get-tuple-element.103), channel_id=1, source_target_pairs={{8,12},{10,14},{12,8},{14,10},{16,20},{18,22},{20,16},{22,18},{9,1... | collective-permute-start | bytes 98312 | tf_op jit(solution)/shard_map/ppermute | solution.py:794
  154.7 5.1 %collective-permute-start.32 = (bf16[128,128]{1,0:T(8,128)(2,1)S(1)}, bf16[128,128]{1,0:T(8,128)(2,1)S(1)}, u32[]{:S(2)}, u32[]{:S(2)}) collective-permute-start(bf16[128,128]{1,0:T(8,128)(2,1)S(1)} %get-tuple-element.104), channel_id=1, source_target_pairs={{8,14},{10,8},{12,10},{14,12},{16,22},{18,16},{20,18},{22,20},{9,1... | collective-permute-start | bytes 98312 | tf_op jit(solution)/shard_map/ppermute | solution.py:794
  162.6 10.7 %collective-permute-start.36 = (bf16[128,1024]{1,0:T(8,128)(2,1)S(1)}, bf16[128,1024]{1,0:T(8,128)(2,1)S(1)}, u32[]{:S(2)}, u32[]{:S(2)}) collective-permute-start(bf16[128,1024]{1,0:T(8,128)(2,1)S(1)} %get-tuple-element.114), channel_id=1, source_target_pairs={{0,6},{2,0},{4,2},{6,4},{8,14},{10,8},{12,10},{14,12},{16,22},{18,... | collective-permute-start | bytes 786440 | tf_op jit(solution)/shard_map/ppermute | solution.py:938
  165.5 19.8 %collective-permute-start.35 = (bf16[128,1024]{1,0:T(8,128)(2,1)S(1)}, bf16[128,1024]{1,0:T(8,128)(2,1)S(1)}, u32[]{:S(2)}, u32[]{:S(2)}) collective-permute-start(bf16[128,1024]{1,0:T(8,128)(2,1)S(1)} %get-tuple-element.113), channel_id=1, source_target_pairs={{0,4},{2,6},{4,0},{6,2},{8,12},{10,14},{12,8},{14,10},{16,20},{18,... | collective-permute-start | bytes 786440 | tf_op jit(solution)/shard_map/ppermute | solution.py:938
  169.0 21.9 %collective-permute-start.34 = (bf16[128,1024]{1,0:T(8,128)(2,1)S(1)}, bf16[128,1024]{1,0:T(8,128)(2,1)S(1)}, u32[]{:S(2)}, u32[]{:S(2)}) collective-permute-start(bf16[128,1024]{1,0:T(8,128)(2,1)S(1)} %get-tuple-element.112), channel_id=1, source_target_pairs={{0,2},{2,4},{4,6},{6,0},{8,10},{10,12},{12,14},{14,8},{16,18},{18,... | collective-permute-start | bytes 786440 | tf_op jit(solution)/shard_map/ppermute | solution.py:938

commit v7 on v6

--- a/solution.py
+++ b/solution.py
@@ -502,7 +502,7 @@
             mine = chunk // half == core
             place = pl.ds(pl.multiple_of(lax.rem(chunk, half) * width, width), width)
             held = jnp.where(mine, own_ref[:, place], other_ref[:, place])
-            product = product + dot_nn(others, held)
+            product = product + jnp.where(first, dot_nn(others, held), 0.0)
         product = product + dot_nn(main[:, wide : wide + heads], step_rows_ref[:, places[hop]])
         copies[hop].wait()
         outs[hop][...] = (product + dot_nt(main[:, :wide], cols[hop])).astype(BF16)
@@ -727,9 +727,18 @@
                 pairs.append((start, start ^ 1))
         return lax.ppermute(value, everywhere, pairs)
 
-    incoming = [output_grad]
-    for hop in range(1, chunks):
-        incoming.append(lax.ppermute(output_grad, place, within(sections - 1, hop)))
+    far_first = sorted(range(1, chunks), key=lambda hop: -min(hop, chunks - hop))
+
+    def exchange(values, sections_in):
+        moved = [values[0]] * chunks
+        for hop in far_first:
+            pairs = []
+            for source in sections_in:
+                pairs += within(source, hop)
+            moved[hop] = lax.ppermute(values[hop], place, pairs)
+        return moved
+
+    incoming = exchange([output_grad] * chunks, [sections - 1])
 
     rows = [lax.ppermute(weight_out[0], everywhere, rows_up(hop)) for hop in range(half)]
     lanes = ((0, 0), (0, 128 - heads))
@@ -785,15 +794,6 @@
         name="section_first",
     )(*incoming, weight_out[0], *residuals)
 
-    def share_state(pieces, sections_in):
-        shared = [pieces[0]]
-        for hop in range(1, chunks):
-            pairs = []
-            for source in sections_in:
-                pairs += within(source, hop)
-            shared.append(lax.ppermute(pieces[hop], place, pairs))
-        return shared
-
     def project_call(main, pieces, newest=(), others=()):
         return pl.pallas_call(
             lambda *refs: project_kernel(chunks, bool(others), *refs),
@@ -808,13 +808,11 @@
             name="project",
         )(main, *pieces, *newest, state_cols, *others, step_rows, main_cols)
 
-    pieces = share_state(pieces, [sections - 1])
+    pieces = exchange(pieces, [sections - 1])
     state_cols = after(weight_state[0], main).reshape(model_width, -1).T
     state_share = state_cols.shape[0]
     parts = project_call(main, pieces)
-    exchanged = [parts[0]]
-    for hop in range(1, chunks):
-        exchanged.append(lax.ppermute(parts[hop], place, within(sections - 1, hop)))
+    exchanged = exchange(parts, [sections - 1])
 
     grid_steps = 2
     depth = model_width // grid_steps
@@ -834,9 +832,7 @@
         compiler_params=kernel_params(),
         name="carry_next",
     )(*exchanged)
-    exchanged = [result]
-    for hop in range(1, chunks):
-        exchanged.append(lax.ppermute(result, place, within(sections - 1, hop)))
+    exchanged = exchange([result] * chunks, [sections - 1])
     dnormed = pl.pallas_call(
         lambda *refs: dnormed_kernel(chunks, *refs),
         out_shape=slice_out,
@@ -927,15 +923,10 @@
             ]
         else:
             shared = (stack, swap(after(stack, messages[0]), [0]))
-            summed = share_state(after(pieces, incoming[0]), range(1, sections - 1))
+            summed = exchange(after(pieces, incoming[0]), range(1, sections - 1))
 
     parts = project_call(kept[0], summed, pieces, shared)
-    exchanged = [parts[0]]
-    for hop in range(1, chunks):
-        pairs = []
-        for source in range(sections - 1):
-            pairs += within(source, hop)
-        exchanged.append(lax.ppermute(parts[hop], place, pairs))
+    exchanged = exchange(parts, range(sections - 1))
     total = exchanged[0].astype(F32)
     for part in exchanged[1:]:
         total = total + part.astype(F32)

time: 194 us -> 194 us (level)
  no operation moved by 1% of the time
where the time goes in v7:
time: 194 us; the launch traced here: 192 us
  waiting for transfers between devices  86.9 us (45%)
  starting transfers between devices  71.7 us (37%)
  Pallas kernels  24.1 us (12%)
  local copies, waits for them, and re-layouts  6.75 us (3%)
    ppermute x2, waiting for transfers between devices, relay_body(): lax.ppermute(weight_out[0], everywhere, rows_up(hop))  60.5 us
    ppermute x18, starting transfers between devices, exchange(): moved[hop] = lax.ppermute(values[hop], place, pairs)  32.2 us
    ppermute x18, waiting for transfers between devices, exchange(): moved[hop] = lax.ppermute(values[hop], place, pairs)  18.2 us
    ppermute x3, starting transfers between devices, relay_body(): lax.ppermute(late, place, within(1, chunks - away))  13.9 us
    ppermute x8, starting transfers between devices, pass_back(): moved.append(lax.ppermute(messages[hop], place, pairs))  12.7 us
    ppermute x2, starting transfers between devices, relay_body(): lax.ppermute(weight_out[0], everywhere, rows_up(hop))  7.06 us
    pallas_call x1, Pallas kernels, relay_body(): pl.pallas_call(lambda *refs: compose_kernel(half, *refs), grid=(grid_step...  6.45 us
    unnamed x40, local copies, waits for them, and re-layouts  5.5 us
  transfers between devices with their start and end apart: 37, of which 6 were waited for; matrix products, arithmetic and copies ran while one was open for 4% of the time, Pallas kernels for 9%

profile of v7, /device:TPU:11, one launch (start us, length us, event | category | flops | bytes accessed | tf_op | source)
XLA Modules:
  0.0 191.9 jit_solution(17082850430242271404)
XLA Ops:
  0.0 5.1 %collective-permute-start.12 = (bf16[256,4096]{1,0:T(8,128)(2,1)}, bf16[256,4096]{1,0:T(8,128)(2,1)S(1)}, u32[]{:S(2)}, u32[]{:S(2)}) collective-permute-start(bf16[256,4096]{1,0:T(8,128)(2,1)} %bitcast.36), channel_id=1, source_target_pairs={{0,8},{1,13},{2,10},{3,15},{4,12},{5,9},{6,14},{7,11},{8,16},{9,21... | collective-permute-start | bytes 6291464 | tf_op jit(solution)/shard_map/ppermute | solution.py:743
  5.1 1.9 %collective-permute-start.13 = (bf16[256,4096]{1,0:T(8,128)(2,1)}, bf16[256,4096]{1,0:T(8,128)(2,1)}, u32[]{:S(2)}, u32[]{:S(2)}) collective-permute-start(bf16[256,4096]{1,0:T(8,128)(2,1)} %bitcast.37), channel_id=1, source_target_pairs={{0,10},{1,15},{2,12},{3,9},{4,14},{5,11},{6,8},{7,13},{8,18},{9,23... | collective-permute-start | bytes 6291464 | tf_op jit(solution)/shard_map/ppermute | solution.py:743
  7.1 1.4 collective-permute-start
  8.4 1.4 collective-permute-start.1
  9.8 1.4 collective-permute-start.2
  11.2 0.8 copy.17
  12.0 1.2 fusion.2
  13.2 0.7 select_maximum_fusion.refs_6_.refs_13_.refs_9_.refs_12_
  13.9 0.8 copy.27
  14.8 0.7 copy.28
  15.5 3.1 %copy.22 = bf16[512,8,2,256]{3,1,2,0:T(8,128)(2,1)S(1)} copy(bf16[512,8,2,256]{3,2,1,0:T(2,128)(2,1)} %bitcast.53) | data formatting | bytes 8388608
  18.6 1.2 forward_residuals.1
  19.9 0.0 copy-start.4
  19.9 0.0 copy-start.13
  19.9 3.5 %section_first.1 = (bf16[128,640]{1,0:T(8,128)(2,1)S(1)}, bf16[128,128]{1,0:T(8,128)(2,1)S(1)}, bf16[128,128]{1,0:T(8,128)(2,1)S(1)}, bf16[128,128]{1,0:T(8,128)(2,1)S(1)}, bf16[128,128]{1,0:T(8,128)(2,1)S(1)}) custom-call(bf16[128,1024]{1,0:T(8,128)(2,1)S(1)} %copy-done.15, bf16[128,1024]{1,0:T(8,128)(2,1)} %collective-permute-done.refs_1_, ...), custom_call_target="tpu_custom_call" | custom-call | tf_op jit(solution)/shard_map/section_first/pallas_call | solution.py:788
  23.5 0.7 collective-permute-start.3
  24.1 0.7 collective-permute-start.4
  24.8 0.7 collective-permute-start.5
  25.5 2.5 %project.2 = (bf16[128,1024]{1,0:T(8,128)(2,1)S(1)}, bf16[128,1024]{1,0:T(8,128)(2,1)S(1)}, bf16[128,1024]{1,0:T(8,128)(2,1)S(1)}, bf16[128,1024]{1,0:T(8,128)(2,1)S(1)}) custom-call(bf16[128,640]{1,0:T(8,128)(2,1)S(1)} %get-tuple-element.67.refs_0_, bf16[128,128]{1,0:T(8,128)(2,1)S(1)} %get-tuple-element.68.refs_1_, ...), custom_call_target="tpu_custom_call" | custom-call | tf_op jit(solution)/shard_map/project/pallas_call | solution.py:798
  28.1 0.7 collective-permute-start.6
  28.7 0.7 collective-permute-start.7
  29.4 0.7 collective-permute-start.8
  30.1 0.8 carry_next.1.refs_0_
  31.0 1.4 collective-permute-start.9
  32.3 1.4 collective-permute-start.10
  33.7 1.4 collective-permute-start.11
  35.1 60.5 %collective-permute-done.12.refs_4_.refs_0_ = bf16[256,4096]{1,0:T(8,128)(2,1)S(1)} collective-permute-done((bf16[256,4096]{1,0:T(8,128)(2,1)}, bf16[256,4096]{1,0:T(8,128)(2,1)S(1)}, u32[]{:S(2)}, u32[]{:S(2)}) %collective-permute-start.12) | collective-permute-done | bytes 2097184 | tf_op jit(solution)/shard_map/ppermute | solution.py:743
  95.6 1.2 dnormed_back.1
  96.8 0.7 collective-permute-start.14
  97.6 6.5 %compose_weights.1.refs_5_ = bf16[320,1280]{1,0:T(8,128)(2,1)S(1)} custom-call(bf16[256,4096]{1,0:T(8,128)(2,1)S(1)} %collective-permute-done.12.refs_4_.refs_0_, bf16[256,4096]{1,0:T(8,128)(2,1)} %collective-permute-done.13.refs_5_.refs_1_, bf16[4096,512]{1,0:T(8,128)(2,1)S(1)} %bitcast.30, bf16[4,4096]{1,0:T(4,128)(2,1)S(1)} %bitcast.40, ...), custom_call_target="tpu_custom_call" | custom-call | tf_op jit(solution)/shard_map/compose_weights/pallas_call | solution.py:851
  104.1 0.7 section_next.3
  104.8 2.5 %collective-permute-start.18 = (bf16[320,1280]{1,0:T(8,128)(2,1)S(1)}, bf16[320,1280]{1,0:T(8,128)(2,1)S(1)}, u32[]{:S(2)}, u32[]{:S(2)}) collective-permute-start(bf16[320,1280]{1,0:T(8,128)(2,1)S(1)} %compose_weights.1.refs_5_), channel_id=1, source_target_pairs={{8,9},{9,8},{10,11},{11,10},{12,13},{13,12},{14,15},{15,14},{16,17... | collective-permute-start | bytes 2457608 | tf_op jit(solution)/shard_map/ppermute | solution.py:728
  107.4 0.7 collective-permute-start.15
  108.1 0.7 collective-permute-start.16
  108.7 0.7 collective-permute-start.17
  109.5 0.8 send_ahead.1
  110.3 1.3 collective-permute-start.19
  111.6 1.3 collective-permute-start.20
  112.9 1.3 collective-permute-start.21
  114.2 1.3 collective-permute-start.22
  115.5 4.9 %collective-permute-done.19.refs_0_ = bf16[128,640]{1,0:T(8,128)(2,1)S(1)} collective-permute-done((bf16[128,640]{1,0:T(8,128)(2,1)S(1)}, bf16[128,640]{1,0:T(8,128)(2,1)S(1)}, u32[]{:S(2)}, u32[]{:S(2)}) %collective-permute-start.19) | collective-permute-done | bytes 163872 | tf_op jit(solution)/shard_map/ppermute | solution.py:824
  120.4 1.9 collective-permute-start.23
  122.4 9.9 %collective-permute-start.24 = (bf16[64,1024]{1,0:T(8,128)(2,1)S(1)}, bf16[64,1024]{1,0:T(8,128)(2,1)S(1)}, u32[]{:S(2)}, u32[]{:S(2)}) collective-permute-start(bf16[64,1024]{1,0:T(8,128)(2,1)S(1)} %get-tuple-element.91), channel_id=1, source_target_pairs={{8,12},{10,14},{12,8},{14,10},{9,13},{11,15},{13,9},{15,11}} | collective-permute-start | bytes 393224 | tf_op jit(solution)/shard_map/ppermute | solution.py:922
  132.3 2.1 %collective-permute-start.25 = (bf16[64,1024]{1,0:T(8,128)(2,1)S(1)}, bf16[64,1024]{1,0:T(8,128)(2,1)S(1)}, u32[]{:S(2)}, u32[]{:S(2)}) collective-permute-start(bf16[64,1024]{1,0:T(8,128)(2,1)S(1)} %get-tuple-element.91), channel_id=1, source_target_pairs={{8,10},{10,12},{12,14},{14,8},{9,11},{11,13},{13,15},{15,9}} | collective-permute-start | bytes 393224 | tf_op jit(solution)/shard_map/ppermute | solution.py:922
  134.4 1.3 section_next.4
  135.7 3.2 %collective-permute-done.25.refs_4_ = bf16[64,1024]{1,0:T(8,128)(2,1)S(1)} collective-permute-done((bf16[64,1024]{1,0:T(8,128)(2,1)S(1)}, bf16[64,1024]{1,0:T(8,128)(2,1)S(1)}, u32[]{:S(2)}, u32[]{:S(2)}) %collective-permute-start.25) | collective-permute-done | bytes 131104 | tf_op jit(solution)/shard_map/ppermute | solution.py:922
  138.9 1.3 send_back.1
  140.2 0.7 collective-permute-start.33
  140.9 1.3 collective-permute-start.26
  142.2 3.6 %collective-permute-start.27 = (bf16[128,256]{1,0:T(8,128)(2,1)S(1)}, bf16[128,256]{1,0:T(8,128)(2,1)S(1)}, u32[]{:S(2)}, u32[]{:S(2)}) collective-permute-start(bf16[128,256]{1,0:T(8,128)(2,1)S(1)} %get-tuple-element.93), channel_id=1, source_target_pairs={{8,6},{10,0},{12,2},{14,4},{9,7},{11,1},{13,3},{15,5}} | collective-permute-start | bytes 196616 | tf_op jit(solution)/shard_map/ppermute | solution.py:824
  145.8 1.3 collective-permute-start.28
  147.1 1.3 collective-permute-start.29
  148.5 3.1 %collective-permute-start.30 = (bf16[128,128]{1,0:T(8,128)(2,1)S(1)}, bf16[128,128]{1,0:T(8,128)(2,1)S(1)}, u32[]{:S(2)}, u32[]{:S(2)}) collective-permute-start(bf16[128,128]{1,0:T(8,128)(2,1)S(1)} %get-tuple-element.102), channel_id=1, source_target_pairs={{8,10},{10,12},{12,14},{14,8},{16,18},{18,20},{20,22},{22,16},{9,1... | collective-permute-start | bytes 98312 | tf_op jit(solution)/shard_map/ppermute | solution.py:738
  151.6 3.1 %collective-permute-start.31 = (bf16[128,128]{1,0:T(8,128)(2,1)S(1)}, bf16[128,128]{1,0:T(8,128)(2,1)S(1)}, u32[]{:S(2)}, u32[]{:S(2)}) collective-permute-start(bf16[128,128]{1,0:T(8,128)(2,1)S(1)} %get-tuple-element.103), channel_id=1, source_target_pairs={{8,12},{10,14},{12,8},{14,10},{16,20},{18,22},{20,16},{22,18},{9,1... | collective-permute-start | bytes 98312 | tf_op jit(solution)/shard_map/ppermute | solution.py:738
  154.7 3.1 %collective-permute-start.32 = (bf16[128,128]{1,0:T(8,128)(2,1)S(1)}, bf16[128,128]{1,0:T(8,128)(2,1)S(1)}, u32[]{:S(2)}, u32[]{:S(2)}) collective-permute-start(bf16[128,128]{1,0:T(8,128)(2,1)S(1)} %get-tuple-element.104), channel_id=1, source_target_pairs={{8,14},{10,8},{12,10},{14,12},{16,22},{18,16},{20,18},{22,20},{9,1... | collective-permute-start | bytes 98312 | tf_op jit(solution)/shard_map/ppermute | solution.py:738
  157.8 1.4 section_next.5
  159.2 0.6 collective-permute-done.32.refs_4_
  159.8 2.8 %project.3 = (bf16[128,1024]{1,0:T(8,128)(2,1)S(1)}, bf16[128,1024]{1,0:T(8,128)(2,1)S(1)}, bf16[128,1024]{1,0:T(8,128)(2,1)S(1)}, bf16[128,1024]{1,0:T(8,128)(2,1)S(1)}) custom-call(bf16[128,640]{1,0:T(8,128)(2,1)S(1)} %get-tuple-element.96.refs_0_, bf16[128,128]{1,0:T(8,128)(2,1)S(1)} %get-tuple-element.101.refs_1_, ...), custom_call_target="tpu_custom_call" | custom-call | tf_op jit(solution)/shard_map/project/pallas_call | solution.py:798
  162.6 2.9 %collective-permute-start.36 = (bf16[128,1024]{1,0:T(8,128)(2,1)S(1)}, bf16[128,1024]{1,0:T(8,128)(2,1)S(1)}, u32[]{:S(2)}, u32[]{:S(2)}) collective-permute-start(bf16[128,1024]{1,0:T(8,128)(2,1)S(1)} %get-tuple-element.114), channel_id=1, source_target_pairs={{0,6},{2,0},{4,2},{6,4},{8,14},{10,8},{12,10},{14,12},{16,22},{18,... | collective-permute-start | bytes 786440 | tf_op jit(solution)/shard_map/ppermute | solution.py:738
  165.5 3.5 %collective-permute-start.35 = (bf16[128,1024]{1,0:T(8,128)(2,1)S(1)}, bf16[128,1024]{1,0:T(8,128)(2,1)S(1)}, u32[]{:S(2)}, u32[]{:S(2)}) collective-permute-start(bf16[128,1024]{1,0:T(8,128)(2,1)S(1)} %get-tuple-element.113), channel_id=1, source_target_pairs={{0,4},{2,6},{4,0},{6,2},{8,12},{10,14},{12,8},{14,10},{16,20},{18,... | collective-permute-start | bytes 786440 | tf_op jit(solution)/shard_map/ppermute | solution.py:738
  169.0 4.3 %collective-permute-start.34 = (bf16[128,1024]{1,0:T(8,128)(2,1)S(1)}, bf16[128,1024]{1,0:T(8,128)(2,1)S(1)}, u32[]{:S(2)}, u32[]{:S(2)}) collective-permute-start(bf16[128,1024]{1,0:T(8,128)(2,1)S(1)} %get-tuple-element.112), channel_id=1, source_target_pairs={{0,2},{2,4},{4,6},{6,0},{8,10},{10,12},{12,14},{14,8},{16,18},{18,... | collective-permute-start | bytes 786440 | tf_op jit(solution)/shard_map/ppermute | solution.py:738
  173.3 12.0 %collective-permute-done.35 = bf16[128,1024]{1,0:T(8,128)(2,1)S(1)} collective-permute-done((bf16[128,1024]{1,0:T(8,128)(2,1)S(1)}, bf16[128,1024]{1,0:T(8,128)(2,1)S(1)}, u32[]{:S(2)}, u32[]{:S(2)}) %collective-permute-start.35) | collective-permute-done | bytes 262176 | tf_op jit(solution)/shard_map/ppermute | solution.py:738
  185.3 5.6 %collective-permute-done.34 = bf16[128,1024]{1,0:T(8,128)(2,1)S(1)} collective-permute-done((bf16[128,1024]{1,0:T(8,128)(2,1)S(1)}, bf16[128,1024]{1,0:T(8,128)(2,1)S(1)}, u32[]{:S(2)}, u32[]{:S(2)}) %collective-permute-start.34) | collective-permute-done | bytes 262176 | tf_op jit(solution)/shard_map/ppermute | solution.py:738
  190.9 0.9 fusion.1
  (68 shorter events, 0.2 us)
Async XLA Ops:
  0.0 95.6 %collective-permute-start.12 = (bf16[256,4096]{1,0:T(8,128)(2,1)}, bf16[256,4096]{1,0:T(8,128)(2,1)S(1)}, u32[]{:S(2)}, u32[]{:S(2)}) collective-permute-start(bf16[256,4096]{1,0:T(8,128)(2,1)} %bitcast.36), channel_id=1, source_target_pairs={{0,8},{1,13},{2,10},{3,15},{4,12},{5,9},{6,14},{7,11},{8,16},{9,21... | collective-permute-start | bytes 6291464 | tf_op jit(solution)/shard_map/ppermute | solution.py:743
  5.1 90.5 %collective-permute-start.13 = (bf16[256,4096]{1,0:T(8,128)(2,1)}, bf16[256,4096]{1,0:T(8,128)(2,1)}, u32[]{:S(2)}, u32[]{:S(2)}) collective-permute-start(bf16[256,4096]{1,0:T(8,128)(2,1)} %bitcast.37), channel_id=1, source_target_pairs={{0,10},{1,15},{2,12},{3,9},{4,14},{5,11},{6,8},{7,13},{8,18},{9,23... | collective-permute-start | bytes 6291464 | tf_op jit(solution)/shard_map/ppermute | solution.py:743
  7.1 12.8 %collective-permute-start = (bf16[128,1024]{1,0:T(8,128)(2,1)}, bf16[128,1024]{1,0:T(8,128)(2,1)}, u32[]{:S(2)}, u32[]{:S(2)}) collective-permute-start(bf16[128,1024]{1,0:T(8,128)(2,1)} %refs_0_.1), channel_id=1, source_target_pairs={{24,26},{26,28},{28,30},{30,24},{25,27},{27,29},{29,31},{31,25}} | collective-permute-start | bytes 786440 | tf_op jit(solution)/shard_map/ppermute | solution.py:738
  8.4 11.4 %collective-permute-start.1 = (bf16[128,1024]{1,0:T(8,128)(2,1)}, bf16[128,1024]{1,0:T(8,128)(2,1)}, u32[]{:S(2)}, u32[]{:S(2)}) collective-permute-start(bf16[128,1024]{1,0:T(8,128)(2,1)} %refs_0_.1), channel_id=1, source_target_pairs={{24,28},{26,30},{28,24},{30,26},{25,29},{27,31},{29,25},{31,27}} | collective-permute-start | bytes 786440 | tf_op jit(solution)/shard_map/ppermute | solution.py:738
  9.8 10.1 %collective-permute-start.2 = (bf16[128,1024]{1,0:T(8,128)(2,1)}, bf16[128,1024]{1,0:T(8,128)(2,1)}, u32[]{:S(2)}, u32[]{:S(2)}) collective-permute-start(bf16[128,1024]{1,0:T(8,128)(2,1)} %refs_0_.1), channel_id=1, source_target_pairs={{24,30},{26,24},{28,26},{30,28},{25,31},{27,25},{29,27},{31,29}} | collective-permute-start | bytes 786440 | tf_op jit(solution)/shard_map/ppermute | solution.py:738
  15.5 3.1 %copy-start.16 = (f32[1,4,256]{2,1,0:T(4,128)S(1)}, f32[1,4,256]{2,1,0:T(4,128)}, u32[]{:S(2)}) copy-start(f32[1,4,256]{2,1,0:T(4,128)} %param.18) | copy-start | bytes 12292
  15.5 3.1 %copy-start.17 = (f32[1,256]{1,0:T(1,128)S(1)}, f32[1,256]{1,0:T(1,128)}, u32[]{:S(2)}) copy-start(f32[1,256]{1,0:T(1,128)} %refs_7_.1) | copy-start | bytes 3076
  15.5 4.4 %copy-start.6 = (bf16[1,256,4096]{2,1,0:T(8,128)(2,1)S(1)}, bf16[1,256,4096]{2,1,0:T(8,128)(2,1)}, u32[]{:S(2)}) copy-start(bf16[1,256,4096]{2,1,0:T(8,128)(2,1)} %param.17) | copy-start | bytes 6291460
  15.5 4.4 %copy-start.15 = (bf16[128,1024]{1,0:T(8,128)(2,1)S(1)}, bf16[128,1024]{1,0:T(8,128)(2,1)}, u32[]{:S(2)}) copy-start(bf16[128,1024]{1,0:T(8,128)(2,1)} %refs_0_.1) | copy-start | bytes 786436
  18.6 6.9 %copy-start = (bf16[512,8,2,256]{3,1,2,0:T(8,128)(2,1)}, bf16[512,8,2,256]{3,1,2,0:T(8,128)(2,1)S(1)}, u32[]{:S(2)}) copy-start(bf16[512,8,2,256]{3,1,2,0:T(8,128)(2,1)S(1)} %copy.22) | copy-start | bytes 12582916
  19.8 3.6 %copy-start.2 = (f32[2,128,512]{2,1,0:T(8,128)}, f32[2,128,512]{2,1,0:T(8,128)S(1)}, u32[]{:S(2)}) copy-start(f32[2,128,512]{2,1,0:T(8,128)S(1)} %get-tuple-element.61.refs_6_.refs_2_.refs_5_) | copy-start | bytes 1572868
  19.8 3.6 %copy-start.7 = (bf16[128,512]{1,0:T(8,128)(2,1)}, bf16[128,512]{1,0:T(8,128)(2,1)S(1)}, u32[]{:S(2)}) copy-start(bf16[128,512]{1,0:T(8,128)(2,1)S(1)} %get-tuple-element.62.refs_7_.refs_3_.refs_6_) | copy-start | bytes 393220
  19.8 3.6 %copy-start.9 = (bf16[2,128,128]{2,1,0:T(8,128)(2,1)}, bf16[2,128,128]{2,1,0:T(8,128)(2,1)S(1)}, u32[]{:S(2)}) copy-start(bf16[2,128,128]{2,1,0:T(8,128)(2,1)S(1)} %get-tuple-element.64.refs_9_.refs_5_.refs_8_) | copy-start | bytes 196612
  19.9 3.6 %copy-start.11 = (f32[128,128]{1,0:T(8,128)}, f32[128,128]{1,0:T(8,128)S(1)}, u32[]{:S(2)}) copy-start(f32[128,128]{1,0:T(8,128)S(1)} %get-tuple-element.65.refs_10_.refs_6_.refs_9_) | copy-start | bytes 196612
  19.9 5.6 %copy-start.4 = (bf16[1,4096,2,32]{1,3,2,0:T(8,128)(2,1)S(1)}, bf16[1,4096,2,32]{1,3,2,0:T(8,128)(2,1)}, u32[]{:S(2)}) copy-start(bf16[1,4096,2,32]{1,3,2,0:T(8,128)(2,1)} %param.15) | copy-start | bytes 1572868
  19.9 5.6 %copy-start.13 = (bf16[1,4,4096]{2,1,0:T(4,128)(2,1)S(1)}, bf16[1,4,4096]{2,1,0:T(4,128)(2,1)}, u32[]{:S(2)}) copy-start(bf16[1,4,4096]{2,1,0:T(4,128)(2,1)} %param.16) | copy-start | bytes 98308
  23.5 2.0 %collective-permute-start.3 = (bf16[128,128]{1,0:T(8,128)(2,1)S(1)}, bf16[128,128]{1,0:T(8,128)(2,1)S(1)}, u32[]{:S(2)}, u32[]{:S(2)}) collective-permute-start(bf16[128,128]{1,0:T(8,128)(2,1)S(1)} %get-tuple-element.69), channel_id=1, source_target_pairs={{24,26},{26,28},{28,30},{30,24},{25,27},{27,29},{29,31},{31,25}} | collective-permute-start | bytes 98312 | tf_op jit(solution)/shard_map/ppermute | solution.py:738
  24.1 1.4 collective-permute-start.4
  24.8 0.7 collective-permute-start.5
  28.1 2.1 %collective-permute-start.6 = (bf16[128,1024]{1,0:T(8,128)(2,1)S(1)}, bf16[128,1024]{1,0:T(8,128)(2,1)S(1)}, u32[]{:S(2)}, u32[]{:S(2)}) collective-permute-start(bf16[128,1024]{1,0:T(8,128)(2,1)S(1)} %get-tuple-element.74), channel_id=1, source_target_pairs={{24,26},{26,28},{28,30},{30,24},{25,27},{27,29},{29,31},{31,25}} | collective-permute-start | bytes 786440 | tf_op jit(solution)/shard_map/ppermute | solution.py:738
  28.7 1.4 collective-permute-start.7
  29.4 0.7 collective-permute-start.8
  31.0 4.1 %collective-permute-start.9 = (bf16[128,1024]{1,0:T(8,128)(2,1)}, bf16[128,1024]{1,0:T(8,128)(2,1)}, u32[]{:S(2)}, u32[]{:S(2)}) collective-permute-start(bf16[128,1024]{1,0:T(8,128)(2,1)} %carry_next.1.refs_0_), channel_id=1, source_target_pairs={{24,26},{26,28},{28,30},{30,24},{25,27},{27,29},{29,31},{31,25}} | collective-permute-start | bytes 786440 | tf_op jit(solution)/shard_map/ppermute | solution.py:738
  32.3 2.8 %collective-permute-start.10 = (bf16[128,1024]{1,0:T(8,128)(2,1)}, bf16[128,1024]{1,0:T(8,128)(2,1)}, u32[]{:S(2)}, u32[]{:S(2)}) collective-permute-start(bf16[128,1024]{1,0:T(8,128)(2,1)} %carry_next.1.refs_0_), channel_id=1, source_target_pairs={{24,28},{26,30},{28,24},{30,26},{25,29},{27,31},{29,25},{31,27}} | collective-permute-start | bytes 786440 | tf_op jit(solution)/shard_map/ppermute | solution.py:738
  33.7 1.4 collective-permute-start.11
  35.1 62.4 %copy-start.5 = (bf16[1,4096,2,32]{1,3,2,0:T(8,128)(2,1)S(1)}, bf16[1,4096,2,32]{1,3,2,0:T(8,128)(2,1)}, u32[]{:S(2)}) copy-start(bf16[1,4096,2,32]{1,3,2,0:T(8,128)(2,1)} %param.15) | copy-start | bytes 1572868
  35.1 62.4 %copy-start.1 = (bf16[512,8,2,256]{3,1,2,0:T(8,128)(2,1)S(1)}, bf16[512,8,2,256]{3,1,2,0:T(8,128)(2,1)}, u32[]{:S(2)}) copy-start(bf16[512,8,2,256]{3,1,2,0:T(8,128)(2,1)} %copy-done) | copy-start | bytes 12582916
  35.1 62.5 %copy-start.14 = (bf16[1,4,4096]{2,1,0:T(4,128)(2,1)S(1)}, bf16[1,4,4096]{2,1,0:T(4,128)(2,1)}, u32[]{:S(2)}) copy-start(bf16[1,4,4096]{2,1,0:T(4,128)(2,1)} %param.16) | copy-start | bytes 98308
  96.8 7.2 %collective-permute-start.14 = (bf16[128,256]{1,0:T(8,128)(2,1)S(1)}, bf16[128,256]{1,0:T(8,128)(2,1)S(1)}, u32[]{:S(2)}, u32[]{:S(2)}) collective-permute-start(bf16[128,256]{1,0:T(8,128)(2,1)S(1)} %dnormed_back.1), channel_id=1, source_target_pairs={{24,16},{26,18},{28,20},{30,22},{25,17},{27,19},{29,21},{31,23}} | collective-permute-start | bytes 196616 | tf_op jit(solution)/shard_map/ppermute | solution.py:849
  97.6 6.5 %copy-start.3 = (f32[2,128,512]{2,1,0:T(8,128)S(1)}, f32[2,128,512]{2,1,0:T(8,128)}, u32[]{:S(2)}) copy-start(f32[2,128,512]{2,1,0:T(8,128)} %copy-done.2) | copy-start | bytes 1572868
  97.6 6.5 %copy-start.8 = (bf16[128,512]{1,0:T(8,128)(2,1)S(1)}, bf16[128,512]{1,0:T(8,128)(2,1)}, u32[]{:S(2)}) copy-start(bf16[128,512]{1,0:T(8,128)(2,1)} %copy-done.7) | copy-start | bytes 393220
  97.6 6.5 %copy-start.10 = (bf16[2,128,128]{2,1,0:T(8,128)(2,1)S(1)}, bf16[2,128,128]{2,1,0:T(8,128)(2,1)}, u32[]{:S(2)}) copy-start(bf16[2,128,128]{2,1,0:T(8,128)(2,1)} %copy-done.9) | copy-start | bytes 196612
  97.6 6.5 %copy-start.12 = (f32[128,128]{1,0:T(8,128)S(1)}, f32[128,128]{1,0:T(8,128)}, u32[]{:S(2)}) copy-start(f32[128,128]{1,0:T(8,128)} %copy-done.11) | copy-start | bytes 196612
  104.8 4.6 %collective-permute-start.18 = (bf16[320,1280]{1,0:T(8,128)(2,1)S(1)}, bf16[320,1280]{1,0:T(8,128)(2,1)S(1)}, u32[]{:S(2)}, u32[]{:S(2)}) collective-permute-start(bf16[320,1280]{1,0:T(8,128)(2,1)S(1)} %compose_weights.1.refs_5_), channel_id=1, source_target_pairs={{8,9},{9,8},{10,11},{11,10},{12,13},{13,12},{14,15},{15,14},{16,17... | collective-permute-start | bytes 2457608 | tf_op jit(solution)/shard_map/ppermute | solution.py:728
  107.4 2.1 %collective-permute-start.15 = (bf16[64,2048]{1,0:T(8,128)(2,1)S(1)}, bf16[64,2048]{1,0:T(8,128)(2,1)S(1)}, u32[]{:S(2)}, u32[]{:S(2)}) collective-permute-start(bf16[64,2048]{1,0:T(8,128)(2,1)S(1)} %constant_dynamic-slice_fusion), channel_id=1, source_target_pairs={{0,6},{2,0},{4,2},{6,4},{1,7},{3,1},{5,3},{7,5}} | collective-permute-start | bytes 786440 | tf_op jit(solution)/shard_map/ppermute | solution.py:901
  108.1 1.4 collective-permute-start.16
  108.7 0.7 collective-permute-start.17
  110.3 10.1 %collective-permute-start.19 = (bf16[128,640]{1,0:T(8,128)(2,1)S(1)}, bf16[128,640]{1,0:T(8,128)(2,1)S(1)}, u32[]{:S(2)}, u32[]{:S(2)}) collective-permute-start(bf16[128,640]{1,0:T(8,128)(2,1)S(1)} %get-tuple-element.84), channel_id=1, source_target_pairs={{16,8},{18,10},{20,12},{22,14},{17,9},{19,11},{21,13},{23,15}} | collective-permute-start | bytes 491528 | tf_op jit(solution)/shard_map/ppermute | solution.py:824
  111.6 20.7 %collective-permute-start.20 = (bf16[128,640]{1,0:T(8,128)(2,1)S(1)}, bf16[128,640]{1,0:T(8,128)(2,1)S(1)}, u32[]{:S(2)}, u32[]{:S(2)}) collective-permute-start(bf16[128,640]{1,0:T(8,128)(2,1)S(1)} %get-tuple-element.85), channel_id=1, source_target_pairs={{16,14},{18,8},{20,10},{22,12},{17,15},{19,9},{21,11},{23,13}} | collective-permute-start | bytes 491528 | tf_op jit(solution)/shard_map/ppermute | solution.py:824
  112.9 21.5 %collective-permute-start.21 = (bf16[128,640]{1,0:T(8,128)(2,1)S(1)}, bf16[128,640]{1,0:T(8,128)(2,1)S(1)}, u32[]{:S(2)}, u32[]{:S(2)}) collective-permute-start(bf16[128,640]{1,0:T(8,128)(2,1)S(1)} %get-tuple-element.86), channel_id=1, source_target_pairs={{16,12},{18,14},{20,8},{22,10},{17,13},{19,15},{21,9},{23,11}} | collective-permute-start | bytes 491528 | tf_op jit(solution)/shard_map/ppermute | solution.py:824
  114.2 20.2 %collective-permute-start.22 = (bf16[128,640]{1,0:T(8,128)(2,1)S(1)}, bf16[128,640]{1,0:T(8,128)(2,1)S(1)}, u32[]{:S(2)}, u32[]{:S(2)}) collective-permute-start(bf16[128,640]{1,0:T(8,128)(2,1)S(1)} %get-tuple-element.87), channel_id=1, source_target_pairs={{16,10},{18,12},{20,14},{22,8},{17,11},{19,13},{21,15},{23,9}} | collective-permute-start | bytes 491528 | tf_op jit(solution)/shard_map/ppermute | solution.py:824
  120.4 15.3 %collective-permute-start.23 = (bf16[64,1024]{1,0:T(8,128)(2,1)S(1)}, bf16[64,1024]{1,0:T(8,128)(2,1)S(1)}, u32[]{:S(2)}, u32[]{:S(2)}) collective-permute-start(bf16[64,1024]{1,0:T(8,128)(2,1)S(1)} %get-tuple-element.91), channel_id=1, source_target_pairs={{8,14},{10,8},{12,10},{14,12},{9,15},{11,9},{13,11},{15,13}} | collective-permute-start | bytes 393224 | tf_op jit(solution)/shard_map/ppermute | solution.py:922
  122.4 13.4 %collective-permute-start.24 = (bf16[64,1024]{1,0:T(8,128)(2,1)S(1)}, bf16[64,1024]{1,0:T(8,128)(2,1)S(1)}, u32[]{:S(2)}, u32[]{:S(2)}) collective-permute-start(bf16[64,1024]{1,0:T(8,128)(2,1)S(1)} %get-tuple-element.91), channel_id=1, source_target_pairs={{8,12},{10,14},{12,8},{14,10},{9,13},{11,15},{13,9},{15,11}} | collective-permute-start | bytes 393224 | tf_op jit(solution)/shard_map/ppermute | solution.py:922
  132.3 6.6 %collective-permute-start.25 = (bf16[64,1024]{1,0:T(8,128)(2,1)S(1)}, bf16[64,1024]{1,0:T(8,128)(2,1)S(1)}, u32[]{:S(2)}, u32[]{:S(2)}) collective-permute-start(bf16[64,1024]{1,0:T(8,128)(2,1)S(1)} %get-tuple-element.91), channel_id=1, source_target_pairs={{8,10},{10,12},{12,14},{14,8},{9,11},{11,13},{13,15},{15,9}} | collective-permute-start | bytes 393224 | tf_op jit(solution)/shard_map/ppermute | solution.py:922
  140.2 19.6 %collective-permute-start.33 = (bf16[192,2048]{1,0:T(8,128)(2,1)S(1)}, bf16[192,2048]{1,0:T(8,128)(2,1)S(1)}, u32[]{:S(2)}, u32[]{:S(2)}) collective-permute-start(bf16[192,2048]{1,0:T(8,128)(2,1)S(1)} %get-tuple-element.110.refs_10_), channel_id=1, source_target_pairs={{0,1},{1,0},{2,3},{3,2},{4,5},{5,4},{6,7},{7,6}} | collective-permute-start | bytes 2359304 | tf_op jit(solution)/shard_map/ppermute | solution.py:728
  140.9 7.5 %collective-permute-start.26 = (bf16[128,256]{1,0:T(8,128)(2,1)S(1)}, bf16[128,256]{1,0:T(8,128)(2,1)S(1)}, u32[]{:S(2)}, u32[]{:S(2)}) collective-permute-start(bf16[128,256]{1,0:T(8,128)(2,1)S(1)} %get-tuple-element.92), channel_id=1, source_target_pairs={{8,0},{10,2},{12,4},{14,6},{9,1},{11,3},{13,5},{15,7}} | collective-permute-start | bytes 196616 | tf_op jit(solution)/shard_map/ppermute | solution.py:824
  142.2 9.3 %collective-permute-start.27 = (bf16[128,256]{1,0:T(8,128)(2,1)S(1)}, bf16[128,256]{1,0:T(8,128)(2,1)S(1)}, u32[]{:S(2)}, u32[]{:S(2)}) collective-permute-start(bf16[128,256]{1,0:T(8,128)(2,1)S(1)} %get-tuple-element.93), channel_id=1, source_target_pairs={{8,6},{10,0},{12,2},{14,4},{9,7},{11,1},{13,3},{15,5}} | collective-permute-start | bytes 196616 | tf_op jit(solution)/shard_map/ppermute | solution.py:824
  145.8 8.8 %collective-permute-start.28 = (bf16[128,256]{1,0:T(8,128)(2,1)S(1)}, bf16[128,256]{1,0:T(8,128)(2,1)S(1)}, u32[]{:S(2)}, u32[]{:S(2)}) collective-permute-start(bf16[128,256]{1,0:T(8,128)(2,1)S(1)} %get-tuple-element.94), channel_id=1, source_target_pairs={{8,4},{10,6},{12,0},{14,2},{9,5},{11,7},{13,1},{15,3}} | collective-permute-start | bytes 196616 | tf_op jit(solution)/shard_map/ppermute | solution.py:824
  147.1 10.6 %collective-permute-start.29 = (bf16[128,256]{1,0:T(8,128)(2,1)S(1)}, bf16[128,256]{1,0:T(8,128)(2,1)S(1)}, u32[]{:S(2)}, u32[]{:S(2)}) collective-permute-start(bf16[128,256]{1,0:T(8,128)(2,1)S(1)} %get-tuple-element.95), channel_id=1, source_target_pairs={{8,2},{10,4},{12,6},{14,0},{9,3},{11,5},{13,7},{15,1}} | collective-permute-start | bytes 196616 | tf_op jit(solution)/shard_map/ppermute | solution.py:824
  148.5 10.7 %collective-permute-start.30 = (bf16[128,128]{1,0:T(8,128)(2,1)S(1)}, bf16[128,128]{1,0:T(8,128)(2,1)S(1)}, u32[]{:S(2)}, u32[]{:S(2)}) collective-permute-start(bf16[128,128]{1,0:T(8,128)(2,1)S(1)} %get-tuple-element.102), channel_id=1, source_target_pairs={{8,10},{10,12},{12,14},{14,8},{16,18},{18,20},{20,22},{22,16},{9,1... | collective-permute-start | bytes 98312 | tf_op jit(solution)/shard_map/ppermute | solution.py:738
  151.6 7.6 %collective-permute-start.31 = (bf16[128,128]{1,0:T(8,128)(2,1)S(1)}, bf16[128,128]{1,0:T(8,128)(2,1)S(1)}, u32[]{:S(2)}, u32[]{:S(2)}) collective-permute-start(bf16[128,128]{1,0:T(8,128)(2,1)S(1)} %get-tuple-element.103), channel_id=1, source_target_pairs={{8,12},{10,14},{12,8},{14,10},{16,20},{18,22},{20,16},{22,18},{9,1... | collective-permute-start | bytes 98312 | tf_op jit(solution)/shard_map/ppermute | solution.py:738
  154.7 5.1 %collective-permute-start.32 = (bf16[128,128]{1,0:T(8,128)(2,1)S(1)}, bf16[128,128]{1,0:T(8,128)(2,1)S(1)}, u32[]{:S(2)}, u32[]{:S(2)}) collective-permute-start(bf16[128,128]{1,0:T(8,128)(2,1)S(1)} %get-tuple-element.104), channel_id=1, source_target_pairs={{8,14},{10,8},{12,10},{14,12},{16,22},{18,16},{20,18},{22,20},{9,1... | collective-permute-start | bytes 98312 | tf_op jit(solution)/shard_map/ppermute | solution.py:738
  162.6 10.7 %collective-permute-start.36 = (bf16[128,1024]{1,0:T(8,128)(2,1)S(1)}, bf16[128,1024]{1,0:T(8,128)(2,1)S(1)}, u32[]{:S(2)}, u32[]{:S(2)}) collective-permute-start(bf16[128,1024]{1,0:T(8,128)(2,1)S(1)} %get-tuple-element.114), channel_id=1, source_target_pairs={{0,6},{2,0},{4,2},{6,4},{8,14},{10,8},{12,10},{14,12},{16,22},{18,... | collective-permute-start | bytes 786440 | tf_op jit(solution)/shard_map/ppermute | solution.py:738
  165.5 19.8 %collective-permute-start.35 = (bf16[128,1024]{1,0:T(8,128)(2,1)S(1)}, bf16[128,1024]{1,0:T(8,128)(2,1)S(1)}, u32[]{:S(2)}, u32[]{:S(2)}) collective-permute-start(bf16[128,1024]{1,0:T(8,128)(2,1)S(1)} %get-tuple-element.113), channel_id=1, source_target_pairs={{0,4},{2,6},{4,0},{6,2},{8,12},{10,14},{12,8},{14,10},{16,20},{18,... | collective-permute-start | bytes 786440 | tf_op jit(solution)/shard_map/ppermute | solution.py:738
  169.0 21.9 %collective-permute-start.34 = (bf16[128,1024]{1,0:T(8,128)(2,1)S(1)}, bf16[128,1024]{1,0:T(8,128)(2,1)S(1)}, u32[]{:S(2)}, u32[]{:S(2)}) collective-permute-start(bf16[128,1024]{1,0:T(8,128)(2,1)S(1)} %get-tuple-element.112), channel_id=1, source_target_pairs={{0,2},{2,4},{4,6},{6,0},{8,10},{10,12},{12,14},{14,8},{16,18},{18,... | collective-permute-start | bytes 786440 | tf_op jit(solution)/shard_map/ppermute | solution.py:738

commit v8 on v7

--- a/solution.py
+++ b/solution.py
@@ -522,8 +522,10 @@
     def _():
         stacked = jnp.concatenate([row[...] for row in rows], axis=0)
         main = dot_nn(stacked, cols_ref[...])
-        steps = dot_nt(stacked, step_rows_ref[...])
-        maps = dot_nt(state_ref[...], stacked)
+        small = jnp.concatenate([state_ref[...], step_rows_ref[...]], axis=0)
+        product = dot_nt(stacked, small)
+        maps = product[:, : state_ref.shape[0]]
+        steps = product[:, state_ref.shape[0] :]
 
         @pl.when(step == 0)
         def _():
@@ -544,7 +546,7 @@
                 joint_ref[:size, hop * map_width : (hop + 1) * map_width] = main_sum[
                     hop * size : (hop + 1) * size, :
                 ].astype(BF16)
-            joint_ref[size:, : half * size] = maps_sum[...].astype(BF16)
+            joint_ref[size:, : half * size] = maps_sum[...].T.astype(BF16)
 
 
 def by_hop(chunks, own, other):
@@ -858,7 +860,7 @@
         out_specs=pl.BlockSpec(joint_shape.shape, lambda step: (0, 0)),
         scratch_shapes=[
             pltpu.VMEM((half * channels, map_width), F32),
-            pltpu.VMEM((state_share, half * channels), F32),
+            pltpu.VMEM((half * channels, state_share), F32),
         ],
         compiler_params=kernel_params(),
         name="compose_weights",
@@ -918,9 +920,7 @@
         incoming = pass_back(messages, active)
         if ahead:
             stack, late = messages[chunks], after(messages[chunks + 1], incoming[0])
-            others = [
-                lax.ppermute(late, place, within(1, chunks - away)) for away in range(1, chunks)
-            ]
+            others = exchange([late] * chunks, [1])[:0:-1]
         else:
             shared = (stack, swap(after(stack, messages[0]), [0]))
             summed = exchange(after(pieces, incoming[0]), range(1, sections - 1))

time: 194 us -> 194 us (level)
  the two profiles are of different devices: /device:TPU:11 before, /device:TPU:18 now
where the time goes in v8:
time: 194 us; the launch traced here: 193 us
  waiting for transfers between devices  88.1 us (45%)
  starting transfers between devices  72.2 us (37%)
  Pallas kernels  23.1 us (12%)
  local copies, waits for them, and re-layouts  6.75 us (3%)
    ppermute x2, waiting for transfers between devices, relay_body(): lax.ppermute(weight_out[0], everywhere, rows_up(hop))  63.2 us
    ppermute x21, starting transfers between devices, exchange(): moved[hop] = lax.ppermute(values[hop], place, pairs)  48.7 us
    ppermute x21, waiting for transfers between devices, exchange(): moved[hop] = lax.ppermute(values[hop], place, pairs)  14.3 us
    ppermute x8, waiting for transfers between devices, pass_back(): moved.append(lax.ppermute(messages[hop], place, pairs))  10.4 us
    ppermute x8, starting transfers between devices, pass_back(): moved.append(lax.ppermute(messages[hop], place, pairs))  10.3 us
    ppermute x2, starting transfers between devices, relay_body(): lax.ppermute(weight_out[0], everywhere, rows_up(hop))  7.8 us
    pallas_call x1, Pallas kernels, relay_body(): pl.pallas_call(lambda *refs: compose_kernel(half, *refs), grid=(grid_step...  5.5 us
    unnamed x40, local copies, waits for them, and re-layouts  5.5 us
  transfers between devices with their start and end apart: 37, of which 9 were waited for; matrix products, arithmetic and copies ran while one was open for 4% of the time, Pallas kernels for 8%

profile of v8, /device:TPU:18, one launch (start us, length us, event | category | flops | bytes accessed | tf_op | source)
XLA Modules:
  0.0 192.6 jit_solution(6779661055036096855)
XLA Ops:
  0.0 3.4 %collective-permute-start.12 = (bf16[256,4096]{1,0:T(8,128)(2,1)}, bf16[256,4096]{1,0:T(8,128)(2,1)S(1)}, u32[]{:S(2)}, u32[]{:S(2)}) collective-permute-start(bf16[256,4096]{1,0:T(8,128)(2,1)} %bitcast.36), channel_id=1, source_target_pairs={{0,8},{1,13},{2,10},{3,15},{4,12},{5,9},{6,14},{7,11},{8,16},{9,21... | collective-permute-start | bytes 6291464 | tf_op jit(solution)/shard_map/ppermute | solution.py:745
  3.4 4.4 %collective-permute-start.13 = (bf16[256,4096]{1,0:T(8,128)(2,1)}, bf16[256,4096]{1,0:T(8,128)(2,1)}, u32[]{:S(2)}, u32[]{:S(2)}) collective-permute-start(bf16[256,4096]{1,0:T(8,128)(2,1)} %bitcast.37), channel_id=1, source_target_pairs={{0,10},{1,15},{2,12},{3,9},{4,14},{5,11},{6,8},{7,13},{8,18},{9,23... | collective-permute-start | bytes 6291464 | tf_op jit(solution)/shard_map/ppermute | solution.py:745
  7.8 1.4 collective-permute-start
  9.2 1.4 collective-permute-start.1
  10.6 1.4 collective-permute-start.2
  11.9 0.8 copy.17
  12.8 1.2 fusion.2
  14.0 0.7 select_maximum_fusion.refs_6_.refs_13_.refs_9_.refs_12_
  14.7 0.8 copy.27
  15.5 0.7 copy.28
  16.2 3.1 %copy.22 = bf16[512,8,2,256]{3,1,2,0:T(8,128)(2,1)S(1)} copy(bf16[512,8,2,256]{3,2,1,0:T(2,128)(2,1)} %bitcast.53) | data formatting | bytes 8388608
  19.4 1.2 forward_residuals.1
  20.7 3.5 %section_first.1 = (bf16[128,640]{1,0:T(8,128)(2,1)S(1)}, bf16[128,128]{1,0:T(8,128)(2,1)S(1)}, bf16[128,128]{1,0:T(8,128)(2,1)S(1)}, bf16[128,128]{1,0:T(8,128)(2,1)S(1)}, bf16[128,128]{1,0:T(8,128)(2,1)S(1)}) custom-call(bf16[128,1024]{1,0:T(8,128)(2,1)S(1)} %copy-done.15, bf16[128,1024]{1,0:T(8,128)(2,1)} %collective-permute-done.refs_1_, ...), custom_call_target="tpu_custom_call" | custom-call | tf_op jit(solution)/shard_map/section_first/pallas_call | solution.py:790
  24.2 0.7 collective-permute-start.3
  24.9 0.7 collective-permute-start.4
  25.6 0.7 collective-permute-start.5
  26.3 2.5 %project.2 = (bf16[128,1024]{1,0:T(8,128)(2,1)S(1)}, bf16[128,1024]{1,0:T(8,128)(2,1)S(1)}, bf16[128,1024]{1,0:T(8,128)(2,1)S(1)}, bf16[128,1024]{1,0:T(8,128)(2,1)S(1)}) custom-call(bf16[128,640]{1,0:T(8,128)(2,1)S(1)} %get-tuple-element.67.refs_0_, bf16[128,128]{1,0:T(8,128)(2,1)S(1)} %get-tuple-element.68.refs_1_, ...), custom_call_target="tpu_custom_call" | custom-call | tf_op jit(solution)/shard_map/project/pallas_call | solution.py:800
  28.8 0.7 collective-permute-start.6
  29.5 0.7 collective-permute-start.7
  30.2 0.7 collective-permute-start.8
  30.9 0.8 carry_next.1.refs_0_
  31.7 1.4 collective-permute-start.9
  33.1 1.4 collective-permute-start.10
  34.5 1.4 collective-permute-start.11
  35.9 57.9 %collective-permute-done.12.refs_4_.refs_0_ = bf16[256,4096]{1,0:T(8,128)(2,1)S(1)} collective-permute-done((bf16[256,4096]{1,0:T(8,128)(2,1)}, bf16[256,4096]{1,0:T(8,128)(2,1)S(1)}, u32[]{:S(2)}, u32[]{:S(2)}) %collective-permute-start.12) | collective-permute-done | bytes 2097184 | tf_op jit(solution)/shard_map/ppermute | solution.py:745
  93.8 5.4 %collective-permute-done.13.refs_5_.refs_1_ = bf16[256,4096]{1,0:T(8,128)(2,1)} collective-permute-done((bf16[256,4096]{1,0:T(8,128)(2,1)}, bf16[256,4096]{1,0:T(8,128)(2,1)}, u32[]{:S(2)}, u32[]{:S(2)}) %collective-permute-start.13) | collective-permute-done | bytes 2097184 | tf_op jit(solution)/shard_map/ppermute | solution.py:745
  99.1 1.2 dnormed_back.1
  100.3 0.7 collective-permute-start.14
  101.1 5.5 %compose_weights.1.refs_5_ = bf16[320,1280]{1,0:T(8,128)(2,1)S(1)} custom-call(bf16[256,4096]{1,0:T(8,128)(2,1)S(1)} %collective-permute-done.12.refs_4_.refs_0_, bf16[256,4096]{1,0:T(8,128)(2,1)} %collective-permute-done.13.refs_5_.refs_1_, bf16[4096,512]{1,0:T(8,128)(2,1)S(1)} %bitcast.30, bf16[4,4096]{1,0:T(4,128)(2,1)S(1)} %bitcast.40, ...), custom_call_target="tpu_custom_call" | custom-call | tf_op jit(solution)/shard_map/compose_weights/pallas_call | solution.py:853
  106.7 0.7 section_next.3
  107.4 1.9 collective-permute-start.18
  109.3 0.7 collective-permute-start.15
  110.0 0.7 collective-permute-start.16
  110.7 0.7 collective-permute-start.17
  111.6 0.8 send_ahead.1
  112.4 1.3 collective-permute-start.19
  113.7 1.3 collective-permute-start.20
  115.0 1.3 collective-permute-start.21
  116.3 1.3 collective-permute-start.22
  117.6 10.4 %collective-permute-done.19.refs_0_ = bf16[128,640]{1,0:T(8,128)(2,1)S(1)} collective-permute-done((bf16[128,640]{1,0:T(8,128)(2,1)S(1)}, bf16[128,640]{1,0:T(8,128)(2,1)S(1)}, u32[]{:S(2)}, u32[]{:S(2)}) %collective-permute-start.19) | collective-permute-done | bytes 163872 | tf_op jit(solution)/shard_map/ppermute | solution.py:826
  128.0 1.9 collective-permute-start.23
  129.9 10.1 %collective-permute-start.24 = (bf16[64,1024]{1,0:T(8,128)(2,1)S(1)}, bf16[64,1024]{1,0:T(8,128)(2,1)S(1)}, u32[]{:S(2)}, u32[]{:S(2)}) collective-permute-start(bf16[64,1024]{1,0:T(8,128)(2,1)S(1)} %get-tuple-element.91), channel_id=1, source_target_pairs={{8,12},{10,14},{12,8},{14,10},{9,13},{11,15},{13,9},{15,11}} | collective-permute-start | bytes 393224 | tf_op jit(solution)/shard_map/ppermute | solution.py:740
  140.0 2.1 %collective-permute-start.25 = (bf16[64,1024]{1,0:T(8,128)(2,1)S(1)}, bf16[64,1024]{1,0:T(8,128)(2,1)S(1)}, u32[]{:S(2)}, u32[]{:S(2)}) collective-permute-start(bf16[64,1024]{1,0:T(8,128)(2,1)S(1)} %get-tuple-element.91), channel_id=1, source_target_pairs={{8,10},{10,12},{12,14},{14,8},{9,11},{11,13},{13,15},{15,9}} | collective-permute-start | bytes 393224 | tf_op jit(solution)/shard_map/ppermute | solution.py:740
  142.2 1.3 section_next.4
  143.5 3.4 %collective-permute-done.25.refs_4_ = bf16[64,1024]{1,0:T(8,128)(2,1)S(1)} collective-permute-done((bf16[64,1024]{1,0:T(8,128)(2,1)S(1)}, bf16[64,1024]{1,0:T(8,128)(2,1)S(1)}, u32[]{:S(2)}, u32[]{:S(2)}) %collective-permute-start.25) | collective-permute-done | bytes 131104 | tf_op jit(solution)/shard_map/ppermute | solution.py:740
  146.9 1.3 send_back.1
  148.2 0.7 collective-permute-start.33
  148.9 1.3 collective-permute-start.26
  150.2 1.3 collective-permute-start.27
  151.5 1.3 collective-permute-start.28
  152.8 1.3 collective-permute-start.29
  154.1 2.2 %collective-permute-start.30 = (bf16[128,128]{1,0:T(8,128)(2,1)S(1)}, bf16[128,128]{1,0:T(8,128)(2,1)S(1)}, u32[]{:S(2)}, u32[]{:S(2)}) collective-permute-start(bf16[128,128]{1,0:T(8,128)(2,1)S(1)} %get-tuple-element.102), channel_id=1, source_target_pairs={{8,10},{10,12},{12,14},{14,8},{16,18},{18,20},{20,22},{22,16},{9,1... | collective-permute-start | bytes 98312 | tf_op jit(solution)/shard_map/ppermute | solution.py:740
  156.3 4.7 %collective-permute-start.31 = (bf16[128,128]{1,0:T(8,128)(2,1)S(1)}, bf16[128,128]{1,0:T(8,128)(2,1)S(1)}, u32[]{:S(2)}, u32[]{:S(2)}) collective-permute-start(bf16[128,128]{1,0:T(8,128)(2,1)S(1)} %get-tuple-element.103), channel_id=1, source_target_pairs={{8,12},{10,14},{12,8},{14,10},{16,20},{18,22},{20,16},{22,18},{9,1... | collective-permute-start | bytes 98312 | tf_op jit(solution)/shard_map/ppermute | solution.py:740
  161.1 4.8 %collective-permute-start.32 = (bf16[128,128]{1,0:T(8,128)(2,1)S(1)}, bf16[128,128]{1,0:T(8,128)(2,1)S(1)}, u32[]{:S(2)}, u32[]{:S(2)}) collective-permute-start(bf16[128,128]{1,0:T(8,128)(2,1)S(1)} %get-tuple-element.104), channel_id=1, source_target_pairs={{8,14},{10,8},{12,10},{14,12},{16,22},{18,16},{20,18},{22,20},{9,1... | collective-permute-start | bytes 98312 | tf_op jit(solution)/shard_map/ppermute | solution.py:740
  165.9 1.4 section_next.5
  167.3 0.3 collective-permute-done.32.refs_4_
  167.6 2.8 %project.3 = (bf16[128,1024]{1,0:T(8,128)(2,1)S(1)}, bf16[128,1024]{1,0:T(8,128)(2,1)S(1)}, bf16[128,1024]{1,0:T(8,128)(2,1)S(1)}, bf16[128,1024]{1,0:T(8,128)(2,1)S(1)}) custom-call(bf16[128,640]{1,0:T(8,128)(2,1)S(1)} %get-tuple-element.96.refs_0_, bf16[128,128]{1,0:T(8,128)(2,1)S(1)} %get-tuple-element.101.refs_1_, ...), custom_call_target="tpu_custom_call" | custom-call | tf_op jit(solution)/shard_map/project/pallas_call | solution.py:800
  170.5 4.4 %collective-permute-start.36 = (bf16[128,1024]{1,0:T(8,128)(2,1)S(1)}, bf16[128,1024]{1,0:T(8,128)(2,1)S(1)}, u32[]{:S(2)}, u32[]{:S(2)}) collective-permute-start(bf16[128,1024]{1,0:T(8,128)(2,1)S(1)} %get-tuple-element.114), channel_id=1, source_target_pairs={{0,6},{2,0},{4,2},{6,4},{8,14},{10,8},{12,10},{14,12},{16,22},{18,... | collective-permute-start | bytes 786440 | tf_op jit(solution)/shard_map/ppermute | solution.py:740
  174.9 4.3 %collective-permute-start.35 = (bf16[128,1024]{1,0:T(8,128)(2,1)S(1)}, bf16[128,1024]{1,0:T(8,128)(2,1)S(1)}, u32[]{:S(2)}, u32[]{:S(2)}) collective-permute-start(bf16[128,1024]{1,0:T(8,128)(2,1)S(1)} %get-tuple-element.113), channel_id=1, source_target_pairs={{0,4},{2,6},{4,0},{6,2},{8,12},{10,14},{12,8},{14,10},{16,20},{18,... | collective-permute-start | bytes 786440 | tf_op jit(solution)/shard_map/ppermute | solution.py:740
  179.2 1.9 collective-permute-start.34
  181.1 1.8 collective-permute-done.36
  183.0 5.6 %collective-permute-done.35 = bf16[128,1024]{1,0:T(8,128)(2,1)S(1)} collective-permute-done((bf16[128,1024]{1,0:T(8,128)(2,1)S(1)}, bf16[128,1024]{1,0:T(8,128)(2,1)S(1)}, u32[]{:S(2)}, u32[]{:S(2)}) %collective-permute-start.35) | collective-permute-done | bytes 262176 | tf_op jit(solution)/shard_map/ppermute | solution.py:740
  188.6 3.1 %collective-permute-done.34 = bf16[128,1024]{1,0:T(8,128)(2,1)S(1)} collective-permute-done((bf16[128,1024]{1,0:T(8,128)(2,1)S(1)}, bf16[128,1024]{1,0:T(8,128)(2,1)S(1)}, u32[]{:S(2)}, u32[]{:S(2)}) %collective-permute-start.34) | collective-permute-done | bytes 262176 | tf_op jit(solution)/shard_map/ppermute | solution.py:740
  191.7 0.9 fusion.1
  (68 shorter events, 0.4 us)
Async XLA Ops:
  0.0 93.8 %collective-permute-start.12 = (bf16[256,4096]{1,0:T(8,128)(2,1)}, bf16[256,4096]{1,0:T(8,128)(2,1)S(1)}, u32[]{:S(2)}, u32[]{:S(2)}) collective-permute-start(bf16[256,4096]{1,0:T(8,128)(2,1)} %bitcast.36), channel_id=1, source_target_pairs={{0,8},{1,13},{2,10},{3,15},{4,12},{5,9},{6,14},{7,11},{8,16},{9,21... | collective-permute-start | bytes 6291464 | tf_op jit(solution)/shard_map/ppermute | solution.py:745
  3.4 95.7 %collective-permute-start.13 = (bf16[256,4096]{1,0:T(8,128)(2,1)}, bf16[256,4096]{1,0:T(8,128)(2,1)}, u32[]{:S(2)}, u32[]{:S(2)}) collective-permute-start(bf16[256,4096]{1,0:T(8,128)(2,1)} %bitcast.37), channel_id=1, source_target_pairs={{0,10},{1,15},{2,12},{3,9},{4,14},{5,11},{6,8},{7,13},{8,18},{9,23... | collective-permute-start | bytes 6291464 | tf_op jit(solution)/shard_map/ppermute | solution.py:745
  7.8 12.8 %collective-permute-start = (bf16[128,1024]{1,0:T(8,128)(2,1)}, bf16[128,1024]{1,0:T(8,128)(2,1)}, u32[]{:S(2)}, u32[]{:S(2)}) collective-permute-start(bf16[128,1024]{1,0:T(8,128)(2,1)} %refs_0_.1), channel_id=1, source_target_pairs={{24,26},{26,28},{28,30},{30,24},{25,27},{27,29},{29,31},{31,25}} | collective-permute-start | bytes 786440 | tf_op jit(solution)/shard_map/ppermute | solution.py:740
  9.2 11.4 %collective-permute-start.1 = (bf16[128,1024]{1,0:T(8,128)(2,1)}, bf16[128,1024]{1,0:T(8,128)(2,1)}, u32[]{:S(2)}, u32[]{:S(2)}) collective-permute-start(bf16[128,1024]{1,0:T(8,128)(2,1)} %refs_0_.1), channel_id=1, source_target_pairs={{24,28},{26,30},{28,24},{30,26},{25,29},{27,31},{29,25},{31,27}} | collective-permute-start | bytes 786440 | tf_op jit(solution)/shard_map/ppermute | solution.py:740
  10.6 10.1 %collective-permute-start.2 = (bf16[128,1024]{1,0:T(8,128)(2,1)}, bf16[128,1024]{1,0:T(8,128)(2,1)}, u32[]{:S(2)}, u32[]{:S(2)}) collective-permute-start(bf16[128,1024]{1,0:T(8,128)(2,1)} %refs_0_.1), channel_id=1, source_target_pairs={{24,30},{26,24},{28,26},{30,28},{25,31},{27,25},{29,27},{31,29}} | collective-permute-start | bytes 786440 | tf_op jit(solution)/shard_map/ppermute | solution.py:740
  16.2 3.1 %copy-start.16 = (f32[1,4,256]{2,1,0:T(4,128)S(1)}, f32[1,4,256]{2,1,0:T(4,128)}, u32[]{:S(2)}) copy-start(f32[1,4,256]{2,1,0:T(4,128)} %param.18) | copy-start | bytes 12292
  16.2 3.1 %copy-start.17 = (f32[1,256]{1,0:T(1,128)S(1)}, f32[1,256]{1,0:T(1,128)}, u32[]{:S(2)}) copy-start(f32[1,256]{1,0:T(1,128)} %refs_7_.1) | copy-start | bytes 3076
  16.2 4.4 %copy-start.6 = (bf16[1,256,4096]{2,1,0:T(8,128)(2,1)S(1)}, bf16[1,256,4096]{2,1,0:T(8,128)(2,1)}, u32[]{:S(2)}) copy-start(bf16[1,256,4096]{2,1,0:T(8,128)(2,1)} %param.17) | copy-start | bytes 6291460
  16.2 4.4 %copy-start.15 = (bf16[128,1024]{1,0:T(8,128)(2,1)S(1)}, bf16[128,1024]{1,0:T(8,128)(2,1)}, u32[]{:S(2)}) copy-start(bf16[128,1024]{1,0:T(8,128)(2,1)} %refs_0_.1) | copy-start | bytes 786436
  19.3 6.9 %copy-start = (bf16[512,8,2,256]{3,1,2,0:T(8,128)(2,1)}, bf16[512,8,2,256]{3,1,2,0:T(8,128)(2,1)S(1)}, u32[]{:S(2)}) copy-start(bf16[512,8,2,256]{3,1,2,0:T(8,128)(2,1)S(1)} %copy.22) | copy-start | bytes 12582916
  20.6 3.6 %copy-start.2 = (f32[2,128,512]{2,1,0:T(8,128)}, f32[2,128,512]{2,1,0:T(8,128)S(1)}, u32[]{:S(2)}) copy-start(f32[2,128,512]{2,1,0:T(8,128)S(1)} %get-tuple-element.61.refs_6_.refs_2_.refs_5_) | copy-start | bytes 1572868
  20.6 3.6 %copy-start.7 = (bf16[128,512]{1,0:T(8,128)(2,1)}, bf16[128,512]{1,0:T(8,128)(2,1)S(1)}, u32[]{:S(2)}) copy-start(bf16[128,512]{1,0:T(8,128)(2,1)S(1)} %get-tuple-element.62.refs_7_.refs_3_.refs_6_) | copy-start | bytes 393220
  20.6 3.6 %copy-start.9 = (bf16[2,128,128]{2,1,0:T(8,128)(2,1)}, bf16[2,128,128]{2,1,0:T(8,128)(2,1)S(1)}, u32[]{:S(2)}) copy-start(bf16[2,128,128]{2,1,0:T(8,128)(2,1)S(1)} %get-tuple-element.64.refs_9_.refs_5_.refs_8_) | copy-start | bytes 196612
  20.6 3.6 %copy-start.11 = (f32[128,128]{1,0:T(8,128)}, f32[128,128]{1,0:T(8,128)S(1)}, u32[]{:S(2)}) copy-start(f32[128,128]{1,0:T(8,128)S(1)} %get-tuple-element.65.refs_10_.refs_6_.refs_9_) | copy-start | bytes 196612
  20.7 5.6 %copy-start.4 = (bf16[1,4096,2,32]{1,3,2,0:T(8,128)(2,1)S(1)}, bf16[1,4096,2,32]{1,3,2,0:T(8,128)(2,1)}, u32[]{:S(2)}) copy-start(bf16[1,4096,2,32]{1,3,2,0:T(8,128)(2,1)} %param.15) | copy-start | bytes 1572868
  20.7 5.6 %copy-start.13 = (bf16[1,4,4096]{2,1,0:T(4,128)(2,1)S(1)}, bf16[1,4,4096]{2,1,0:T(4,128)(2,1)}, u32[]{:S(2)}) copy-start(bf16[1,4,4096]{2,1,0:T(4,128)(2,1)} %param.16) | copy-start | bytes 98308
  24.2 2.0 %collective-permute-start.3 = (bf16[128,128]{1,0:T(8,128)(2,1)S(1)}, bf16[128,128]{1,0:T(8,128)(2,1)S(1)}, u32[]{:S(2)}, u32[]{:S(2)}) collective-permute-start(bf16[128,128]{1,0:T(8,128)(2,1)S(1)} %get-tuple-element.69), channel_id=1, source_target_pairs={{24,26},{26,28},{28,30},{30,24},{25,27},{27,29},{29,31},{31,25}} | collective-permute-start | bytes 98312 | tf_op jit(solution)/shard_map/ppermute | solution.py:740
  24.9 1.4 collective-permute-start.4
  25.6 0.7 collective-permute-start.5
  28.8 2.1 %collective-permute-start.6 = (bf16[128,1024]{1,0:T(8,128)(2,1)S(1)}, bf16[128,1024]{1,0:T(8,128)(2,1)S(1)}, u32[]{:S(2)}, u32[]{:S(2)}) collective-permute-start(bf16[128,1024]{1,0:T(8,128)(2,1)S(1)} %get-tuple-element.74), channel_id=1, source_target_pairs={{24,26},{26,28},{28,30},{30,24},{25,27},{27,29},{29,31},{31,25}} | collective-permute-start | bytes 786440 | tf_op jit(solution)/shard_map/ppermute | solution.py:740
  29.5 1.4 collective-permute-start.7
  30.2 0.7 collective-permute-start.8
  31.7 4.1 %collective-permute-start.9 = (bf16[128,1024]{1,0:T(8,128)(2,1)}, bf16[128,1024]{1,0:T(8,128)(2,1)}, u32[]{:S(2)}, u32[]{:S(2)}) collective-permute-start(bf16[128,1024]{1,0:T(8,128)(2,1)} %carry_next.1.refs_0_), channel_id=1, source_target_pairs={{24,26},{26,28},{28,30},{30,24},{25,27},{27,29},{29,31},{31,25}} | collective-permute-start | bytes 786440 | tf_op jit(solution)/shard_map/ppermute | solution.py:740
  33.1 2.8 %collective-permute-start.10 = (bf16[128,1024]{1,0:T(8,128)(2,1)}, bf16[128,1024]{1,0:T(8,128)(2,1)}, u32[]{:S(2)}, u32[]{:S(2)}) collective-permute-start(bf16[128,1024]{1,0:T(8,128)(2,1)} %carry_next.1.refs_0_), channel_id=1, source_target_pairs={{24,28},{26,30},{28,24},{30,26},{25,29},{27,31},{29,25},{31,27}} | collective-permute-start | bytes 786440 | tf_op jit(solution)/shard_map/ppermute | solution.py:740
  34.5 1.4 collective-permute-start.11
  35.8 65.2 %copy-start.5 = (bf16[1,4096,2,32]{1,3,2,0:T(8,128)(2,1)S(1)}, bf16[1,4096,2,32]{1,3,2,0:T(8,128)(2,1)}, u32[]{:S(2)}) copy-start(bf16[1,4096,2,32]{1,3,2,0:T(8,128)(2,1)} %param.15) | copy-start | bytes 1572868
  35.8 65.2 %copy-start.1 = (bf16[512,8,2,256]{3,1,2,0:T(8,128)(2,1)S(1)}, bf16[512,8,2,256]{3,1,2,0:T(8,128)(2,1)}, u32[]{:S(2)}) copy-start(bf16[512,8,2,256]{3,1,2,0:T(8,128)(2,1)} %copy-done) | copy-start | bytes 12582916
  35.9 65.2 %copy-start.14 = (bf16[1,4,4096]{2,1,0:T(4,128)(2,1)S(1)}, bf16[1,4,4096]{2,1,0:T(4,128)(2,1)}, u32[]{:S(2)}) copy-start(bf16[1,4,4096]{2,1,0:T(4,128)(2,1)} %param.16) | copy-start | bytes 98308
  100.3 6.3 %collective-permute-start.14 = (bf16[128,256]{1,0:T(8,128)(2,1)S(1)}, bf16[128,256]{1,0:T(8,128)(2,1)S(1)}, u32[]{:S(2)}, u32[]{:S(2)}) collective-permute-start(bf16[128,256]{1,0:T(8,128)(2,1)S(1)} %dnormed_back.1), channel_id=1, source_target_pairs={{24,16},{26,18},{28,20},{30,22},{25,17},{27,19},{29,21},{31,23}} | collective-permute-start | bytes 196616 | tf_op jit(solution)/shard_map/ppermute | solution.py:851
  101.1 5.6 %copy-start.3 = (f32[2,128,512]{2,1,0:T(8,128)S(1)}, f32[2,128,512]{2,1,0:T(8,128)}, u32[]{:S(2)}) copy-start(f32[2,128,512]{2,1,0:T(8,128)} %copy-done.2) | copy-start | bytes 1572868
  101.1 5.6 %copy-start.8 = (bf16[128,512]{1,0:T(8,128)(2,1)S(1)}, bf16[128,512]{1,0:T(8,128)(2,1)}, u32[]{:S(2)}) copy-start(bf16[128,512]{1,0:T(8,128)(2,1)} %copy-done.7) | copy-start | bytes 393220
  101.1 5.6 %copy-start.10 = (bf16[2,128,128]{2,1,0:T(8,128)(2,1)S(1)}, bf16[2,128,128]{2,1,0:T(8,128)(2,1)}, u32[]{:S(2)}) copy-start(bf16[2,128,128]{2,1,0:T(8,128)(2,1)} %copy-done.9) | copy-start | bytes 196612
  101.1 5.6 %copy-start.12 = (f32[128,128]{1,0:T(8,128)S(1)}, f32[128,128]{1,0:T(8,128)}, u32[]{:S(2)}) copy-start(f32[128,128]{1,0:T(8,128)} %copy-done.11) | copy-start | bytes 196612
  107.4 4.2 %collective-permute-start.18 = (bf16[320,1280]{1,0:T(8,128)(2,1)S(1)}, bf16[320,1280]{1,0:T(8,128)(2,1)S(1)}, u32[]{:S(2)}, u32[]{:S(2)}) collective-permute-start(bf16[320,1280]{1,0:T(8,128)(2,1)S(1)} %compose_weights.1.refs_5_), channel_id=1, source_target_pairs={{8,9},{9,8},{10,11},{11,10},{12,13},{13,12},{14,15},{15,14},{16,17... | collective-permute-start | bytes 2457608 | tf_op jit(solution)/shard_map/ppermute | solution.py:730
  109.3 2.1 %collective-permute-start.15 = (bf16[64,2048]{1,0:T(8,128)(2,1)S(1)}, bf16[64,2048]{1,0:T(8,128)(2,1)S(1)}, u32[]{:S(2)}, u32[]{:S(2)}) collective-permute-start(bf16[64,2048]{1,0:T(8,128)(2,1)S(1)} %constant_dynamic-slice_fusion), channel_id=1, source_target_pairs={{0,6},{2,0},{4,2},{6,4},{1,7},{3,1},{5,3},{7,5}} | collective-permute-start | bytes 786440 | tf_op jit(solution)/shard_map/ppermute | solution.py:903
  110.0 1.4 collective-permute-start.16
  110.7 0.7 collective-permute-start.17
  112.4 15.6 %collective-permute-start.19 = (bf16[128,640]{1,0:T(8,128)(2,1)S(1)}, bf16[128,640]{1,0:T(8,128)(2,1)S(1)}, u32[]{:S(2)}, u32[]{:S(2)}) collective-permute-start(bf16[128,640]{1,0:T(8,128)(2,1)S(1)} %get-tuple-element.84), channel_id=1, source_target_pairs={{16,8},{18,10},{20,12},{22,14},{17,9},{19,11},{21,13},{23,15}} | collective-permute-start | bytes 491528 | tf_op jit(solution)/shard_map/ppermute | solution.py:826
  113.7 26.3 %collective-permute-start.20 = (bf16[128,640]{1,0:T(8,128)(2,1)S(1)}, bf16[128,640]{1,0:T(8,128)(2,1)S(1)}, u32[]{:S(2)}, u32[]{:S(2)}) collective-permute-start(bf16[128,640]{1,0:T(8,128)(2,1)S(1)} %get-tuple-element.85), channel_id=1, source_target_pairs={{16,14},{18,8},{20,10},{22,12},{17,15},{19,9},{21,11},{23,13}} | collective-permute-start | bytes 491528 | tf_op jit(solution)/shard_map/ppermute | solution.py:826
  115.0 27.1 %collective-permute-start.21 = (bf16[128,640]{1,0:T(8,128)(2,1)S(1)}, bf16[128,640]{1,0:T(8,128)(2,1)S(1)}, u32[]{:S(2)}, u32[]{:S(2)}) collective-permute-start(bf16[128,640]{1,0:T(8,128)(2,1)S(1)} %get-tuple-element.86), channel_id=1, source_target_pairs={{16,12},{18,14},{20,8},{22,10},{17,13},{19,15},{21,9},{23,11}} | collective-permute-start | bytes 491528 | tf_op jit(solution)/shard_map/ppermute | solution.py:826
  116.3 25.8 %collective-permute-start.22 = (bf16[128,640]{1,0:T(8,128)(2,1)S(1)}, bf16[128,640]{1,0:T(8,128)(2,1)S(1)}, u32[]{:S(2)}, u32[]{:S(2)}) collective-permute-start(bf16[128,640]{1,0:T(8,128)(2,1)S(1)} %get-tuple-element.87), channel_id=1, source_target_pairs={{16,10},{18,12},{20,14},{22,8},{17,11},{19,13},{21,15},{23,9}} | collective-permute-start | bytes 491528 | tf_op jit(solution)/shard_map/ppermute | solution.py:826
  128.0 15.5 %collective-permute-start.23 = (bf16[64,1024]{1,0:T(8,128)(2,1)S(1)}, bf16[64,1024]{1,0:T(8,128)(2,1)S(1)}, u32[]{:S(2)}, u32[]{:S(2)}) collective-permute-start(bf16[64,1024]{1,0:T(8,128)(2,1)S(1)} %get-tuple-element.91), channel_id=1, source_target_pairs={{8,14},{10,8},{12,10},{14,12},{9,15},{11,9},{13,11},{15,13}} | collective-permute-start | bytes 393224 | tf_op jit(solution)/shard_map/ppermute | solution.py:740
  129.9 13.6 %collective-permute-start.24 = (bf16[64,1024]{1,0:T(8,128)(2,1)S(1)}, bf16[64,1024]{1,0:T(8,128)(2,1)S(1)}, u32[]{:S(2)}, u32[]{:S(2)}) collective-permute-start(bf16[64,1024]{1,0:T(8,128)(2,1)S(1)} %get-tuple-element.91), channel_id=1, source_target_pairs={{8,12},{10,14},{12,8},{14,10},{9,13},{11,15},{13,9},{15,11}} | collective-permute-start | bytes 393224 | tf_op jit(solution)/shard_map/ppermute | solution.py:740
  140.0 6.9 %collective-permute-start.25 = (bf16[64,1024]{1,0:T(8,128)(2,1)S(1)}, bf16[64,1024]{1,0:T(8,128)(2,1)S(1)}, u32[]{:S(2)}, u32[]{:S(2)}) collective-permute-start(bf16[64,1024]{1,0:T(8,128)(2,1)S(1)} %get-tuple-element.91), channel_id=1, source_target_pairs={{8,10},{10,12},{12,14},{14,8},{9,11},{11,13},{13,15},{15,9}} | collective-permute-start | bytes 393224 | tf_op jit(solution)/shard_map/ppermute | solution.py:740
  148.2 19.5 %collective-permute-start.33 = (bf16[192,2048]{1,0:T(8,128)(2,1)S(1)}, bf16[192,2048]{1,0:T(8,128)(2,1)S(1)}, u32[]{:S(2)}, u32[]{:S(2)}) collective-permute-start(bf16[192,2048]{1,0:T(8,128)(2,1)S(1)} %get-tuple-element.110.refs_10_), channel_id=1, source_target_pairs={{0,1},{1,0},{2,3},{3,2},{4,5},{5,4},{6,7},{7,6}} | collective-permute-start | bytes 2359304 | tf_op jit(solution)/shard_map/ppermute | solution.py:730
  148.9 5.2 %collective-permute-start.26 = (bf16[128,256]{1,0:T(8,128)(2,1)S(1)}, bf16[128,256]{1,0:T(8,128)(2,1)S(1)}, u32[]{:S(2)}, u32[]{:S(2)}) collective-permute-start(bf16[128,256]{1,0:T(8,128)(2,1)S(1)} %get-tuple-element.92), channel_id=1, source_target_pairs={{8,0},{10,2},{12,4},{14,6},{9,1},{11,3},{13,5},{15,7}} | collective-permute-start | bytes 196616 | tf_op jit(solution)/shard_map/ppermute | solution.py:826
  150.2 6.1 %collective-permute-start.27 = (bf16[128,256]{1,0:T(8,128)(2,1)S(1)}, bf16[128,256]{1,0:T(8,128)(2,1)S(1)}, u32[]{:S(2)}, u32[]{:S(2)}) collective-permute-start(bf16[128,256]{1,0:T(8,128)(2,1)S(1)} %get-tuple-element.93), channel_id=1, source_target_pairs={{8,6},{10,0},{12,2},{14,4},{9,7},{11,1},{13,3},{15,5}} | collective-permute-start | bytes 196616 | tf_op jit(solution)/shard_map/ppermute | solution.py:826
  151.5 9.6 %collective-permute-start.28 = (bf16[128,256]{1,0:T(8,128)(2,1)S(1)}, bf16[128,256]{1,0:T(8,128)(2,1)S(1)}, u32[]{:S(2)}, u32[]{:S(2)}) collective-permute-start(bf16[128,256]{1,0:T(8,128)(2,1)S(1)} %get-tuple-element.94), channel_id=1, source_target_pairs={{8,4},{10,6},{12,0},{14,2},{9,5},{11,7},{13,1},{15,3}} | collective-permute-start | bytes 196616 | tf_op jit(solution)/shard_map/ppermute | solution.py:826
  152.8 13.1 %collective-permute-start.29 = (bf16[128,256]{1,0:T(8,128)(2,1)S(1)}, bf16[128,256]{1,0:T(8,128)(2,1)S(1)}, u32[]{:S(2)}, u32[]{:S(2)}) collective-permute-start(bf16[128,256]{1,0:T(8,128)(2,1)S(1)} %get-tuple-element.95), channel_id=1, source_target_pairs={{8,2},{10,4},{12,6},{14,0},{9,3},{11,5},{13,7},{15,1}} | collective-permute-start | bytes 196616 | tf_op jit(solution)/shard_map/ppermute | solution.py:826
  154.1 13.2 %collective-permute-start.30 = (bf16[128,128]{1,0:T(8,128)(2,1)S(1)}, bf16[128,128]{1,0:T(8,128)(2,1)S(1)}, u32[]{:S(2)}, u32[]{:S(2)}) collective-permute-start(bf16[128,128]{1,0:T(8,128)(2,1)S(1)} %get-tuple-element.102), channel_id=1, source_target_pairs={{8,10},{10,12},{12,14},{14,8},{16,18},{18,20},{20,22},{22,16},{9,1... | collective-permute-start | bytes 98312 | tf_op jit(solution)/shard_map/ppermute | solution.py:740
  156.3 11.0 %collective-permute-start.31 = (bf16[128,128]{1,0:T(8,128)(2,1)S(1)}, bf16[128,128]{1,0:T(8,128)(2,1)S(1)}, u32[]{:S(2)}, u32[]{:S(2)}) collective-permute-start(bf16[128,128]{1,0:T(8,128)(2,1)S(1)} %get-tuple-element.103), channel_id=1, source_target_pairs={{8,12},{10,14},{12,8},{14,10},{16,20},{18,22},{20,16},{22,18},{9,1... | collective-permute-start | bytes 98312 | tf_op jit(solution)/shard_map/ppermute | solution.py:740
  161.1 6.6 %collective-permute-start.32 = (bf16[128,128]{1,0:T(8,128)(2,1)S(1)}, bf16[128,128]{1,0:T(8,128)(2,1)S(1)}, u32[]{:S(2)}, u32[]{:S(2)}) collective-permute-start(bf16[128,128]{1,0:T(8,128)(2,1)S(1)} %get-tuple-element.104), channel_id=1, source_target_pairs={{8,14},{10,8},{12,10},{14,12},{16,22},{18,16},{20,18},{22,20},{9,1... | collective-permute-start | bytes 98312 | tf_op jit(solution)/shard_map/ppermute | solution.py:740
  170.5 12.5 %collective-permute-start.36 = (bf16[128,1024]{1,0:T(8,128)(2,1)S(1)}, bf16[128,1024]{1,0:T(8,128)(2,1)S(1)}, u32[]{:S(2)}, u32[]{:S(2)}) collective-permute-start(bf16[128,1024]{1,0:T(8,128)(2,1)S(1)} %get-tuple-element.114), channel_id=1, source_target_pairs={{0,6},{2,0},{4,2},{6,4},{8,14},{10,8},{12,10},{14,12},{16,22},{18,... | collective-permute-start | bytes 786440 | tf_op jit(solution)/shard_map/ppermute | solution.py:740
  174.9 13.7 %collective-permute-start.35 = (bf16[128,1024]{1,0:T(8,128)(2,1)S(1)}, bf16[128,1024]{1,0:T(8,128)(2,1)S(1)}, u32[]{:S(2)}, u32[]{:S(2)}) collective-permute-start(bf16[128,1024]{1,0:T(8,128)(2,1)S(1)} %get-tuple-element.113), channel_id=1, source_target_pairs={{0,4},{2,6},{4,0},{6,2},{8,12},{10,14},{12,8},{14,10},{16,20},{18,... | collective-permute-start | bytes 786440 | tf_op jit(solution)/shard_map/ppermute | solution.py:740
  179.2 12.5 %collective-permute-start.34 = (bf16[128,1024]{1,0:T(8,128)(2,1)S(1)}, bf16[128,1024]{1,0:T(8,128)(2,1)S(1)}, u32[]{:S(2)}, u32[]{:S(2)}) collective-permute-start(bf16[128,1024]{1,0:T(8,128)(2,1)S(1)} %get-tuple-element.112), channel_id=1, source_target_pairs={{0,2},{2,4},{4,6},{6,0},{8,10},{10,12},{12,14},{14,8},{16,18},{18,... | collective-permute-start | bytes 786440 | tf_op jit(solution)/shard_map/ppermute | solution.py:740
